TPU v7x, 512 devices: a whole 4x4x16 slice. The times are simulated.
512 devices in a mesh: dp: 64 (over z, x), mp: 8 (over y, core).
Axes of the slice: x: 4, y: 4, z: 16, core: 2. Of those that a mesh axis runs over, the one named last changes fastest.
Arguments:
- activations: bfloat16 [8, 512, 16384], P(None, 'mp', 'dp'), may hold values from -16 to 16
- out_grads: bfloat16 [16384, 6144], P('dp'), may hold values from -16 to 16
- owners: int32 [96], replicated, may hold values from 0 to 63, as said below
- live_rows: int32 [96], replicated, may hold values from 64 to 512
- left_stat: float32 [64, 2, 512, 512], P('dp', None, 'mp'), may hold values from -6 to 6
- right_stat: float32 [64, 2, 512, 512], P('dp', None, 'mp'), may hold values from -6 to 6
- left_root: bfloat16 [64, 2, 512, 512], P('dp', None, 'mp'), may hold values from -1 to 2
- right_root: bfloat16 [64, 2, 512, 512], P('dp', None, 'mp'), may hold values from -1 to 2
- grad_acc: float32 [64, 2, 512, 512], P('dp', None, 'mp'), may hold values from 0.05 to 2
Outputs:
- left_new: float32 [64, 2, 512, 512], P('dp', None, 'mp')
- right_new: float32 [64, 2, 512, 512], P('dp', None, 'mp')
- acc_new: float32 [64, 2, 512, 512], P('dp', None, 'mp')
- directions: bfloat16 [64, 2, 512, 512], P('dp')
Inputs may be any that keep to these rules, and one draw needn't show every extreme that they name: `owners`: no owner index appears more than 2 times, and some owner appears exactly 2 times.
All inputs are finite; a program needn't handle non-finite values.
Results may differ from a plain program's by a relative error of at most 0.0064.
Values may be sent and summed in bfloat16 or wider, within the bound.
No kernel may reach another device: no remote copies, remote signals or barrier semaphores. Data moves between devices by JAX's collectives and lax.ppermute only.
A program may use at most 128 MiB of HBM per device.

v0:
```python
import jax
import jax.numpy as jnp
from jax import lax
from jax.sharding import PartitionSpec as P

STAT_DECAY = 0.9
GRAFT_EPS = 1e-06


def slot_targets(owners, slot_count):
    block_count = owners.shape[0]
    same_owner = owners[:, None] == owners[None, :]
    earlier = lax.broadcasted_iota(jnp.int32, (block_count, block_count), 1) < lax.broadcasted_iota(
        jnp.int32, (block_count, block_count), 0
    )
    ranked = jnp.sum(jnp.where(same_owner & earlier, 1, 0), axis=1).astype(jnp.int32)
    return owners * slot_count + ranked


def body(
    activations,
    out_grads,
    owners,
    live_rows,
    left_stat,
    right_stat,
    left_root,
    right_root,
    grad_acc,
):
    dp_count = lax.axis_size("dp")
    row_count = activations.shape[1]
    block_size = left_stat.shape[3]
    slot_count = left_stat.shape[1]
    block_count = owners.shape[0]
    column_blocks = out_grads.shape[1] // block_size
    tok_count = out_grads.shape[0]
    my_owner = lax.axis_index("dp")
    my_rows = lax.axis_index("mp") * row_count
    grads_blocks = out_grads.reshape(tok_count, column_blocks, block_size)
    partial_value = jnp.einsum(
        "irt,tjc->ijrc", activations, grads_blocks, preferred_element_type=jnp.float32
    )
    partial_half = partial_value.reshape(block_count, row_count, block_size).astype(jnp.bfloat16)
    targets = slot_targets(owners, slot_count)
    outgoing = (
        jnp.zeros((dp_count * slot_count, row_count, block_size), jnp.bfloat16)
        .at[targets]
        .set(partial_half)
    )
    outgoing = outgoing.reshape(dp_count, slot_count, row_count, block_size)
    incoming = lax.all_to_all(outgoing, "dp", split_axis=0, concat_axis=0, tiled=True)
    grad_mine = jnp.sum(incoming, axis=0, dtype=jnp.float32)
    wanted = my_owner * slot_count + lax.broadcasted_iota(jnp.int32, (slot_count, block_count), 0)
    matched = targets[None, :] == wanted
    occupied = jnp.any(matched, axis=1)
    live_mine = jnp.sum(jnp.where(matched, live_rows[None, :], 0), axis=1)
    row_ids = my_rows + lax.broadcasted_iota(jnp.int32, (slot_count, row_count, 1), 1)
    row_mask = row_ids < live_mine[:, None, None]
    grad_mine = jnp.where(row_mask, grad_mine, 0.0)
    grad_half = grad_mine.astype(jnp.bfloat16)
    root_full = lax.all_gather(right_root[0], "mp", axis=1, tiled=True)
    rows_in = lax.all_gather(grad_half, "mp", axis=1, tiled=True)
    left_cols = jnp.einsum("sak,snk->san", grad_half, rows_in, preferred_element_type=jnp.float32)
    own_cols = lax.dynamic_slice_in_dim(rows_in, my_rows, row_count, 2)
    right_rows = jnp.einsum("snc,snk->sck", own_cols, rows_in, preferred_element_type=jnp.float32)
    left_cols, right_rows = (left_cols, right_rows)
    prod_rows = jnp.einsum("snk,sjk->snj", rows_in, root_full, preferred_element_type=jnp.float32)
    half_round = prod_rows.astype(jnp.bfloat16)
    raw_dir = jnp.einsum(
        "sak,skj->saj", left_root[0], half_round, preferred_element_type=jnp.float32
    )
    raw_dir = jnp.where(row_mask, raw_dir, 0.0)
    left_old = left_stat[0]
    right_old = right_stat[0]
    left_next = jnp.where(
        occupied[:, None, None],
        STAT_DECAY * left_old + (1.0 - STAT_DECAY) * left_cols / block_size,
        left_old,
    )
    right_next = jnp.where(
        occupied[:, None, None],
        STAT_DECAY * right_old + (1.0 - STAT_DECAY) * right_rows / block_size,
        right_old,
    )
    acc_next = grad_acc[0] + grad_mine * grad_mine
    grafted = grad_mine / (jnp.sqrt(acc_next) + GRAFT_EPS)
    graft_sq, raw_sq = lax.psum(
        (jnp.sum(grafted * grafted, axis=(1, 2)), jnp.sum(raw_dir * raw_dir, axis=(1, 2))), "mp"
    )
    factor = jnp.sqrt(graft_sq) / jnp.sqrt(raw_sq + GRAFT_EPS)
    dir_rows = jnp.where(occupied[:, None, None], factor[:, None, None] * raw_dir, 0.0).astype(
        jnp.bfloat16
    )
    dir_full = lax.all_gather(dir_rows, "mp", axis=1, tiled=True)
    return (left_next[None], right_next[None], acc_next[None], dir_full[None])


def solution(mesh):
    placed = (
        P(None, "mp", "dp"),
        P("dp", None),
        P(),
        P(),
        P("dp", None, "mp", None),
        P("dp", None, "mp", None),
        P("dp", None, "mp", None),
        P("dp", None, "mp", None),
        P("dp", None, "mp", None),
    )
    return jax.shard_map(
        body,
        mesh=mesh,
        in_specs=placed,
        out_specs=(
            P("dp", None, "mp", None),
            P("dp", None, "mp", None),
            P("dp", None, "mp", None),
            P("dp", None, None, None),
        ),
        check_vma=False,
    )
```

profile of v0, /device:TPU:1, one launch (start us, length us, event | category | flops | bytes accessed | tf_op | source)
XLA Modules:
  0.0 513.4 jit_solution(6025200444740684222)
XLA Ops:
  7.2 0.0 copy-start
  7.2 0.9 select_reduce_fusion
  8.1 0.7 compare_select_fusion
  8.8 3.2 copy.19
  11.9 0.0 copy-done
  11.9 1.8 convert_bitcast_fusion
  13.8 3.4 copy.21
  17.2 4.3 broadcast_in_dim.96
  21.4 17.7 %scatter_fusion = bf16[128,64,512]{2,1,0:T(8,128)(2,1)} fusion(bf16[128,64,512]{2,1,0:T(8,128)(2,1)} %broadcast_in_dim.96, s32[96]{0:T(128)S(1)} %get-tuple-element.6, bf16[96,64,512]{2,1,0:T(8,128)(2,1)} %bitcast.64), kind=kCustom, calls=%fused_computation | custom fusion | bytes 18874752 | tf_op jit(solution)/shard_map/scatter | solution.py:49
  39.2 0.0 copy-start.6
  39.2 19.5 %all-to-all-start = ((bf16[64,2,64,512]{3,2,1,0:T(8,128)(2,1)}), bf16[64,2,64,512]{3,2,1,0:T(8,128)(2,1)}, u32[]{:S(2)}, u32[]{:S(2)}) async-start(bf16[64,2,64,512]{3,2,1,0:T(8,128)(2,1)} %bitcast.63), calls=%async_computation | async-start | bytes 16777216 | tf_op jit(solution)/shard_map/all_to_all | solution.py:52
  58.7 0.0 copy-start.3
  58.7 0.0 copy-start.7
  58.7 0.0 all-gather.9.cloned.1.call-start
  58.8 0.7 all-gather.9.cloned.1.call-update
  59.4 0.0 all-gather.5.cloned.1.call-start
  59.5 0.0 copy-done.6
  59.5 0.2 fusion.22
  59.7 0.1 broadcast_compare_fusion
  59.8 0.0 copy-start.5
  59.8 0.0 copy-start.4
  59.8 359.5 %all-to-all-done = bf16[64,2,64,512]{3,2,1,0:T(8,128)(2,1)} async-done(((bf16[64,2,64,512]{3,2,1,0:T(8,128)(2,1)}), bf16[64,2,64,512]{3,2,1,0:T(8,128)(2,1)}, u32[]{:S(2)}, u32[]{:S(2)}) %all-to-all-start) | async-done | bytes 8388640 | tf_op jit(solution)/shard_map/all_to_all | solution.py:52
  419.3 4.8 convert_reduce_fusion
  424.1 0.7 select_convert_fusion.1
  424.8 0.0 copy-start.2
  424.8 0.0 all-gather.5.cloned.1.call-update
  424.9 0.0 all-gather.7.cloned.1.call-start
  424.9 0.2 compare_reduce_fusion
  425.1 0.0 copy-done.3
  425.1 0.3 fusion.18
  425.4 0.0 all-gather.9.cloned.1.call-done
  425.4 32.4 %all-gather.5.cloned.1.call-done = bf16[2,512,512]{2,1,0:T(8,128)(2,1)} async-done(((bf16[2,64,512]{2,1,0:T(8,128)(2,1)}), bf16[2,512,512]{2,1,0:T(8,128)(2,1)}) %all-gather.5.cloned.1.call-update) | async-done | bytes 1048592 | tf_op jit(solution)/shard_map/all_gather | solution.py:63
  457.8 0.0 copy-done.7
  457.8 0.0 copy-start.1
  457.9 2.6 multiply_reduce_fusion
  460.5 12.0 %all-reduce = (f32[2]{0:T(128)S(1)}, f32[2]{0:T(128)S(1)}) all-reduce(f32[2]{0:T(128)S(1)} %get-tuple-element.8, f32[2]{0:T(128)S(1)} %fusion.18), channel_id=1, replica_groups=mesh['dp'=64,'mp'=8] {'mp'}, use_global_device_ids=true, to_apply=%region_8.9 | all-reduce | flops 4 | bytes 32 | tf_op jit(solution)/shard_map/psum | solution.py:88
  472.5 0.8 fusion.19
  473.3 0.0 all-gather.7.cloned.1.call-update
  473.3 0.8 fusion.15
  474.1 0.0 copy-done.5
  474.1 2.5 fusion.4
  476.6 0.0 copy-done.4
  476.6 0.0 copy-done.2
  476.6 0.0 copy-done.1
  476.6 1.1 fusion.7
  477.8 26.9 %all-gather.7.cloned.1.call-done = bf16[2,512,512]{2,1,0:T(8,128)(2,1)} async-done(((bf16[2,64,512]{2,1,0:T(8,128)(2,1)}), bf16[2,512,512]{2,1,0:T(8,128)(2,1)}) %all-gather.7.cloned.1.call-update) | async-done | bytes 1048592 | tf_op jit(solution)/shard_map/all_gather | solution.py:95
  504.6 2.3 copy.29
  (3 shorter events, 0.0 us)
Async XLA Ops:
  7.2 4.8 copy-start
  39.2 20.4 %copy-start.6 = (s32[96]{0:T(128)S(1)}, s32[96]{0:T(128)}, u32[]{:S(2)}) copy-start(s32[96]{0:T(128)} %param.12) | copy-start | bytes 1156
  39.2 380.1 %all-to-all-start = ((bf16[64,2,64,512]{3,2,1,0:T(8,128)(2,1)}), bf16[64,2,64,512]{3,2,1,0:T(8,128)(2,1)}, u32[]{:S(2)}, u32[]{:S(2)}) async-start(bf16[64,2,64,512]{3,2,1,0:T(8,128)(2,1)} %bitcast.63), calls=%async_computation | async-start | bytes 16777216 | tf_op jit(solution)/shard_map/all_to_all | solution.py:52
  58.7 366.4 %copy-start.3 = (f32[1,2,64,512]{3,2,1,0:T(8,128)S(1)}, f32[1,2,64,512]{3,2,1,0:T(8,128)}, u32[]{:S(2)}) copy-start(f32[1,2,64,512]{3,2,1,0:T(8,128)} %param.17) | copy-start | bytes 786436
  58.7 399.1 %copy-start.7 = (bf16[1,2,64,512]{3,2,1,0:T(8,128)(2,1)S(1)}, bf16[1,2,64,512]{3,2,1,0:T(8,128)(2,1)}, u32[]{:S(2)}) copy-start(bf16[1,2,64,512]{3,2,1,0:T(8,128)(2,1)} %param.15) | copy-start | bytes 393220
  58.7 366.7 %all-gather.9.cloned.1.call-start = ((), (), s32[]{:S(2)}) async-start(), calls=%async_computation.3 | async-start | bytes 1179648 | tf_op jit(solution)/shard_map/all_gather | solution.py:62
  59.4 398.4 %all-gather.5.cloned.1.call-start = ((), (), s32[]{:S(2)}) async-start(), calls=%async_computation.1 | async-start | bytes 1179648 | tf_op jit(solution)/shard_map/all_gather | solution.py:63
  59.8 414.3 %copy-start.5 = (f32[1,2,64,512]{3,2,1,0:T(8,128)S(1)}, f32[1,2,64,512]{3,2,1,0:T(8,128)}, u32[]{:S(2)}) copy-start(f32[1,2,64,512]{3,2,1,0:T(8,128)} %param.14) | copy-start | bytes 786436
  59.8 416.8 %copy-start.4 = (f32[1,2,64,512]{3,2,1,0:T(8,128)S(1)}, f32[1,2,64,512]{3,2,1,0:T(8,128)}, u32[]{:S(2)}) copy-start(f32[1,2,64,512]{3,2,1,0:T(8,128)} %param.13) | copy-start | bytes 786436
  424.8 51.8 %copy-start.2 = (bf16[2,64,512]{2,1,0:T(8,128)(2,1)S(1)}, bf16[2,64,512]{2,1,0:T(8,128)(2,1)}, u32[]{:S(2)}) copy-start(bf16[2,64,512]{2,1,0:T(8,128)(2,1)} %select_convert_fusion.1) | copy-start | bytes 393220
  424.9 79.8 %all-gather.7.cloned.1.call-start = ((), (), s32[]{:S(2)}) async-start(), calls=%async_computation.2 | async-start | bytes 1179648 | tf_op jit(solution)/shard_map/all_gather | solution.py:95
  457.8 18.8 %copy-start.1 = (bf16[2,512,512]{2,1,0:T(8,128)(2,1)S(1)}, bf16[2,512,512]{2,1,0:T(8,128)(2,1)}, u32[]{:S(2)}) copy-start(bf16[2,512,512]{2,1,0:T(8,128)(2,1)} %all-gather.5.cloned.1.call-done) | copy-start | bytes 3145732
Sparse Core Ops, SparseCore 0:
  61.7 32.6 all-gather.8
  425.0 32.8 all-gather.4
  473.4 31.1 all-gather.6
where the time goes:
time: 514 us; the launch traced here: 513 us
  waiting for transfers between devices  420 us (82%)
  local copies, waits for them, and re-layouts  30.8 us (6%)
  starting transfers between devices  19.6 us (4%)
  between operations  13.9 us (3%)
  blocking collectives  12 us (2%)
  other arithmetic  9.47 us (2%)
  matrix products  8.12 us (2%)
    all_to_all x1, waiting for transfers between devices, body(): lax.all_to_all(outgoing, 'dp', split_axis=0, concat_axis=0, tiled=True)  359 us
    all_gather x1, waiting for transfers between devices, body(): rows_in = lax.all_gather(grad_half, 'mp', axis=1, tiled=True)  32.4 us
    all_gather x1, waiting for transfers between devices, body(): dir_full = lax.all_gather(dir_rows, 'mp', axis=1, tiled=True)  26.9 us
    all_to_all x1, starting transfers between devices, body(): lax.all_to_all(outgoing, 'dp', split_axis=0, concat_axis=0, tiled=True)  19.5 us
    scatter x1, local copies, waits for them, and re-layouts, body(): outgoing = jnp.zeros((dp_count * slot_count, row_count, block_size), jnp....  17.7 us
    psum x1, blocking collectives, body(): lax.psum((jnp.sum(grafted * grafted, axis=(1, 2)), jnp.sum(raw_dir * raw_...  12 us
  transfers between devices with their start and end apart: 4, of which 3 were waited for; matrix products, arithmetic and copies ran while one was open for 2% of the time, Pallas kernels for 0%

commit v1 on v0

v1 whole, which is shorter than its diff:
```python
import jax
import jax.numpy as jnp
from jax import lax
from jax.experimental import pallas as pl
from jax.experimental.pallas import tpu as pltpu
from jax.sharding import Mesh, PartitionSpec as P

STAT_DECAY = 0.9
GRAFT_EPS = 1e-06
HALF = jnp.bfloat16
WIDE = jnp.float32
NZ, NX, NC = 16, 4, 2
PARAMS = pltpu.CompilerParams(vmem_limit_bytes=24 * 1024 * 1024)


def slot_targets(owners, slot_count):
    block_count = owners.shape[0]
    same_owner = owners[:, None] == owners[None, :]
    earlier = lax.broadcasted_iota(jnp.int32, (block_count, block_count), 1) < lax.broadcasted_iota(
        jnp.int32, (block_count, block_count), 0
    )
    ranked = jnp.sum(jnp.where(same_owner & earlier, 1, 0), axis=1).astype(jnp.int32)
    return owners * slot_count + ranked


def ring(count, step):
    return [(i, (i + step) % count) for i in range(count)]


def iota(shape, dim):
    return lax.broadcasted_iota(jnp.int32, shape, dim)


def dot(a, b, dims=((1,), (0,))):
    return lax.dot_general(a, b, (dims, ((), ())), preferred_element_type=WIDE)


def order_rows(activations, place):
    block_rows, rows, toks = activations.shape
    part = block_rows // 2
    count = part * rows
    per_z = rows // NZ

    def kernel(place_ref, a_ref, o_ref):
        z, c = place_ref[0], place_ref[1]
        m, k = iota((count, count), 0), iota((count, count), 1)
        block = m % part
        row = (m // part) % per_z
        tail = m // (part * per_z)
        dist = 4 * (tail % 4) + 2 * ((tail // 4) % 2) + tail // 8
        for half in range(2):
            goal = jnp.bitwise_and(z + dist if half == 0 else z - dist, NZ - 1)
            pick = (block * rows + goal * per_z + row == k).astype(WIDE).astype(HALF)
            values = a_ref[half * part : (half + 1) * part].reshape(count, toks)
            moved = dot(pick, values).astype(HALF)
            turned = jnp.concatenate([moved[:, toks // 2 :], moved[:, : toks // 2]], axis=1)
            o_ref[half * count : (half + 1) * count, :] = jnp.where(c == 1, turned, moved)

    return pl.pallas_call(
        kernel,
        out_shape=jax.ShapeDtypeStruct((2 * count, toks), HALF),
        in_specs=[pl.BlockSpec(memory_space=pltpu.SMEM), pl.BlockSpec(memory_space=pltpu.VMEM)],
        out_specs=pl.BlockSpec(memory_space=pltpu.VMEM),
        compiler_params=PARAMS,
    )(place, activations)


def split_columns(out_grads, core):
    toks, columns = out_grads.shape
    half, width = toks // NC, columns // NX

    def kernel(core_ref, b_ref, o_ref):
        o_ref[0] = b_ref[...]

    return pl.pallas_call(
        kernel,
        out_shape=jax.ShapeDtypeStruct((NX, half, width), HALF),
        grid_spec=pltpu.PrefetchScalarGridSpec(
            num_scalar_prefetch=1,
            grid=(NX,),
            in_specs=[pl.BlockSpec((half, width), lambda i, core_ref: (core_ref[0], i))],
            out_specs=pl.BlockSpec((1, half, width), lambda i, core_ref: (i, 0, 0)),
        ),
        compiler_params=PARAMS,
    )(core, out_grads)


def partial_products(acts, mine, other):
    sources, rows, toks = acts.shape
    half, width = mine.shape[1:]
    tile = width // 6
    part = rows // 4

    def kernel(a_ref, m_ref, o_ref, ka_ref, sa_ref, kb_ref, sb_ref):
        total = None
        for s in range(sources):
            both = jnp.concatenate([m_ref[s], o_ref[s]], axis=0)
            term = dot(a_ref[s], both)
            total = term if total is None else total + term
        ka_ref[...] = total[:part]
        sa_ref[...] = total[part : 2 * part].astype(HALF)
        kb_ref[...] = total[2 * part : 3 * part]
        sb_ref[...] = total[3 * part :].astype(HALF)

    out_block = pl.BlockSpec((part, tile), lambda n: (0, n))
    return pl.pallas_call(
        kernel,
        grid=(6,),
        out_shape=[
            jax.ShapeDtypeStruct((part, width), WIDE),
            jax.ShapeDtypeStruct((part, width), HALF),
        ]
        * 2,
        in_specs=[
            pl.BlockSpec((sources, rows, toks), lambda n: (0, 0, 0)),
            pl.BlockSpec((sources, half, tile), lambda n: (0, 0, n)),
            pl.BlockSpec((sources, half, tile), lambda n: (0, 0, n)),
        ],
        out_specs=[out_block] * 4,
        compiler_params=PARAMS,
    )(acts, mine, other)


def pick_blocks(chosen, sums, block_size):
    sources, rows, width = sums.shape
    columns = width // block_size
    out_rows = chosen.shape[0]
    tile = out_rows // 2

    def kernel(p_ref, s_ref, o_ref):
        total = None
        for x in range(sources):
            for j in range(columns):
                at = (x * columns + j) * rows
                term = dot(p_ref[:, at : at + rows], s_ref[x, :, j * block_size : (j + 1) * block_size])
                total = term if total is None else total + term
        o_ref[...] = total.astype(HALF)

    return pl.pallas_call(
        kernel,
        grid=(2,),
        out_shape=jax.ShapeDtypeStruct((out_rows, block_size), HALF),
        in_specs=[
            pl.BlockSpec((tile, chosen.shape[1]), lambda n: (n, 0)),
            pl.BlockSpec(sums.shape, lambda n: (0, 0, 0)),
        ],
        out_specs=pl.BlockSpec((tile, block_size), lambda n: (n, 0)),
        compiler_params=PARAMS,
    )(chosen, sums)


def finish_sum(limits, pieces, acc):
    slots, rows, block_size = acc.shape
    per_z = rows // NZ
    total_rows = slots * rows
    piece_rows = pieces.shape[0]

    def kernel(lim_ref, p_ref, a_ref, g_ref, n_ref):
        m, k = iota((total_rows, piece_rows), 0), iota((total_rows, piece_rows), 1)
        row = k % per_z
        piece = (k // per_z) % 4
        slot = (k // (4 * per_z)) % slots
        source = k // (4 * per_z * slots)
        goal = jnp.bitwise_and(source + 4 * piece, NZ - 1)
        adds = (slot * rows + goal * per_z + row == m).astype(WIDE).astype(HALF)
        grad = dot(adds, p_ref[...])
        lane = iota((16, block_size), 1)
        extra_row = iota((16, block_size), 0)
        extra = jnp.zeros((16, block_size), WIDE)
        for s in range(slots):
            live = iota((rows, block_size), 0) < lim_ref[s]
            own = jnp.where(live, grad[s * rows : (s + 1) * rows], 0.0)
            new = a_ref[s] + own * own
            n_ref[s] = new
            grafted = own / (jnp.sqrt(new) + GRAFT_EPS)
            norm = jnp.sum(jnp.sum(grafted * grafted, axis=0, keepdims=True), axis=1, keepdims=True)
            high = norm.astype(HALF).astype(WIDE)
            middle = (norm - high).astype(HALF).astype(WIDE)
            low = norm - high - middle
            spread = jnp.where(lane == 0, high, jnp.where(lane == 1, middle, jnp.where(lane == 2, low, 0.0)))
            extra = jnp.where(extra_row == s, spread, extra)
            g_ref[s * rows : (s + 1) * rows, :] = own.astype(HALF)
        g_ref[total_rows:, :] = extra.astype(HALF)

    vmem = pl.BlockSpec(memory_space=pltpu.VMEM)
    return pl.pallas_call(
        kernel,
        out_shape=[
            jax.ShapeDtypeStruct((total_rows + 16, block_size), HALF),
            jax.ShapeDtypeStruct(acc.shape, WIDE),
        ],
        in_specs=[pl.BlockSpec(memory_space=pltpu.SMEM), vmem, vmem],
        out_specs=[vmem, vmem],
        compiler_params=PARAMS,
    )(limits, pieces, acc)


def update(facts, mine, other, left_root, right_root, left_stat, right_stat):
    ny = mine.shape[0]
    slots, rows, block_size = left_stat.shape
    all_rows = mine.shape[1]

    def kernel(f_ref, m_ref, o_ref, lr_ref, rr_ref, ls_ref, rs_ref, ln_ref, rn_ref, d_ref):
        s = pl.program_id(0)
        core, own_y, own_mp = f_ref[0], f_ref[1], f_ref[2]
        live, taken = f_ref[3 + s], f_ref[5 + s]
        at = pl.ds(pl.multiple_of(s * rows, rows), rows)
        parts = []
        norm = jnp.zeros((1, 1), WIDE)
        tail_row = iota((16, block_size), 0) == s
        for y in range(ny):
            a, b = m_ref[y, at, :], o_ref[y, at, :]
            parts += [jnp.where(core == 0, a, b), jnp.where(core == 0, b, a)]
            for ref in (m_ref, o_ref):
                tail = jnp.where(tail_row, ref[y, slots * rows : all_rows, :].astype(WIDE), 0.0)
                norm += jnp.sum(jnp.sum(tail, axis=0, keepdims=True), axis=1, keepdims=True)
        grad = jnp.concatenate(parts, axis=0)
        prod = dot(grad, rr_ref[0], ((1,), (1,))).astype(HALF)
        raw = dot(lr_ref[0], prod)
        raw = jnp.where(iota(raw.shape, 0) < live, raw, 0.0)
        raw_sq = jnp.sum(jnp.sum(raw * raw, axis=0, keepdims=True), axis=1, keepdims=True)
        factor = jnp.sqrt(norm) / jnp.sqrt(raw_sq + GRAFT_EPS)
        d_ref[0] = jnp.where(taken == 1, factor * raw, 0.0).astype(HALF)
        own = m_ref[own_y, at, :]
        left_cols = dot(own, grad, ((1,), (1,)))
        own_columns = (iota((block_size, rows), 0) == own_mp * rows + iota((block_size, rows), 1)).astype(WIDE)
        columns = dot(grad, own_columns.astype(HALF)).astype(HALF)
        right_rows = dot(columns, grad, ((0,), (0,)))
        for old_ref, value, new_ref in ((ls_ref, left_cols, ln_ref), (rs_ref, right_rows, rn_ref)):
            old = old_ref[0]
            fresh = STAT_DECAY * old + (1.0 - STAT_DECAY) * value / block_size
            new_ref[0] = jnp.where(taken == 1, fresh, old)

    whole = pl.BlockSpec((ny, all_rows, block_size), lambda s: (0, 0, 0))
    square = pl.BlockSpec((1, block_size, block_size), lambda s: (s, 0, 0))
    strip = pl.BlockSpec((1, rows, block_size), lambda s: (s, 0, 0))
    return pl.pallas_call(
        kernel,
        grid=(slots,),
        out_shape=[
            jax.ShapeDtypeStruct(left_stat.shape, WIDE),
            jax.ShapeDtypeStruct(right_stat.shape, WIDE),
            jax.ShapeDtypeStruct(left_root.shape, HALF),
        ],
        in_specs=[
            pl.BlockSpec(memory_space=pltpu.SMEM),
            whole,
            whole,
            square,
            square,
            strip,
            strip,
        ],
        out_specs=[strip, strip, square],
        compiler_params=PARAMS,
    )(facts, mine, other, left_root, right_root, left_stat, right_stat)


def body(
    activations,
    out_grads,
    owners,
    live_rows,
    left_stat,
    right_stat,
    left_root,
    right_root,
    grad_acc,
):
    z, x, y, c = (lax.axis_index(name) for name in ("z", "x", "y", "c"))
    block_rows, rows, toks = activations.shape
    block_size = left_stat.shape[3]
    slots = left_stat.shape[1]
    block_count = owners.shape[0]
    per_z = rows // NZ
    columns = out_grads.shape[1] // block_size // NX
    half_rows = block_rows // 2
    my_owner = z * NX + x
    my_mp = y * NC + c
    my_rows = my_mp * rows

    left_full = lax.all_gather(left_root[0], ("y", "c"), axis=1, tiled=True)
    right_full = lax.all_gather(right_root[0], ("y", "c"), axis=1, tiled=True)

    pieces = split_columns(out_grads, c.reshape(1).astype(jnp.int32))
    mine = lax.all_to_all(pieces, "x", 0, 0, tiled=True)
    other = lax.ppermute(mine, "c", ring(NC, 1))
    acts = order_rows(activations, jnp.stack([z, c]).astype(jnp.int32))
    acts, mine = lax.optimization_barrier((acts, mine))
    acts = lax.all_gather(acts, "x", axis=0, tiled=False)
    keep_a, send_a, keep_b, send_b = partial_products(acts, mine, other)

    for step in (1, 2):
        got_a = lax.ppermute(send_a, "z", ring(NZ, step))
        got_b = lax.ppermute(send_b, "z", ring(NZ, -step))
        keep_a, keep_b = keep_a + got_a, keep_b + got_b
        if step == 1:
            part = keep_a.shape[0] // 2
            send_a, send_b = keep_a[part:].astype(HALF), keep_b[part:].astype(HALF)
            keep_a, keep_b = keep_a[:part], keep_b[:part]
    sums = jnp.concatenate([keep_a, keep_b], axis=0).astype(HALF)
    sums = lax.all_gather(sums, "x", axis=0, tiled=False)

    targets = slot_targets(owners, slots)
    by_block = targets.reshape(2, half_rows, NX, columns).transpose(2, 3, 0, 1)[:, :, :, None, None, :]
    shape = (NX, columns, 2, 4, per_z, half_rows)
    owner = by_block // slots
    piece = iota(shape, 3)
    piece = jnp.where(iota(shape, 2) == 0, piece, (4 - piece) % 4)
    code = (((owner // NX) * slots + by_block % slots) * 4 + piece) * per_z + iota(shape, 4)
    code = jnp.where(owner % NX == x, code, -1).reshape(1, -1)
    out_rows = NZ * slots * 4 * per_z
    chosen = (code == iota((out_rows, 1), 0)).astype(HALF)

    picked = pick_blocks(chosen, sums, block_size).reshape(NZ, out_rows // NZ, block_size)
    arrived = lax.all_to_all(picked, "z", 0, 0, tiled=True).reshape(out_rows, block_size)

    wanted = my_owner * slots + iota((slots, block_count), 0)
    matched = targets[None, :] == wanted
    occupied = jnp.any(matched, axis=1).astype(jnp.int32)
    live_mine = jnp.sum(jnp.where(matched, live_rows[None, :], 0), axis=1).astype(jnp.int32)
    own_rows, acc_next = finish_sum(live_mine - my_rows, arrived, grad_acc[0])
    rows_mine = lax.all_gather(own_rows, "y", axis=0, tiled=False)
    rows_other = lax.ppermute(rows_mine, "c", ring(NC, 1))
    facts = jnp.concatenate([jnp.stack([c, y, my_mp]).astype(jnp.int32), live_mine, occupied])
    left_next, right_next, directions = update(
        facts, rows_mine, rows_other, left_full, right_full, left_stat[0], right_stat[0]
    )
    return (left_next[None], right_next[None], acc_next[None], directions[None])


def solution(mesh):
    dp, mp = mesh.devices.shape
    parts = Mesh(mesh.devices.reshape(NZ, NX, mp // NC, NC), ("z", "x", "y", "c"))
    owner, strip = ("z", "x"), ("y", "c")
    state = P(owner, None, strip, None)
    return jax.shard_map(
        body,
        mesh=parts,
        in_specs=(P(None, strip, owner), P(owner, None), P(), P(), state, state, state, state, state),
        out_specs=(state, state, state, P(owner, None, None, None)),
        check_vma=False,
    )
```

time: 514 us -> 221 us (0.43)
  waiting for transfers between devices: 420 us -> 117 us
  starting transfers between devices: 19.6 us -> 53.9 us
  local copies, waits for them, and re-layouts: 30.8 us -> 7.58 us
  Pallas kernels: 0 us -> 14.9 us
  matrix products: 8.12 us -> 0 us
  other arithmetic: 9.47 us -> 2.29 us
    all_to_all x1 -> x2, waiting for transfers between devices: 359 us -> 35.3 us  [the longest x1 22 us: body(): lax.all_to_all(picked, 'z', 0, 0, tiled=True).reshape(out_rows, block_size)]
    ppermute x0 -> x6, starting transfers between devices: none -> 36.6 us  [the longest x1 12.9 us: body(): rows_other = lax.ppermute(rows_mine, 'c', ring(NC, 1))]
    scatter x1 -> x0, local copies, waits for them, and re-layouts: 17.7 us -> none  [body(): outgoing = jnp.zeros((dp_count * slot_count, row_count, block_size), jnp....]
    ppermute x0 -> x6, waiting for transfers between devices: none -> 15.1 us  [the longest x2 11.9 us: body(): got_a = lax.ppermute(send_a, 'z', ring(NZ, step))]
    pallas_call x0 -> x6, Pallas kernels: none -> 14.9 us  [the longest x1 4.32 us: update(): pl.pallas_call(kernel, grid=(slots,), out_shape=[jax.ShapeDtypeStruct(lef...]
    psum x1 -> x0, blocking collectives: 12 us -> none  [body(): lax.psum((jnp.sum(grafted * grafted, axis=(1, 2)), jnp.sum(raw_dir * raw_...]
    all_gather x0 -> x1, blocking collectives: none -> 10.6 us  [body(): rows_mine = lax.all_gather(own_rows, 'y', axis=0, tiled=False)]
    dot_general x4 -> x0, matrix products: 8.12 us -> none  [the longest x1 2.64 us: body(): jnp.einsum('sak,skj->saj', left_root[0], half_round, preferred_element_ty...]
  transfers between devices with their start and end apart: 4 -> 12, of which waited for: 3 -> 8; matrix products, arithmetic and copies ran while one was open for 2% -> 1% of each run, Pallas kernels for 0% -> 3%
where the time goes in v1:
time: 221 us; the launch traced here: 220 us
  waiting for transfers between devices  117 us (53%)
  starting transfers between devices  53.9 us (24%)
  Pallas kernels  14.9 us (7%)
  between operations  14 us (6%)
  blocking collectives  10.6 us (5%)
  local copies, waits for them, and re-layouts  7.58 us (3%)
  other arithmetic  2.29 us (1%)
    all_gather x1, waiting for transfers between devices, body(): sums = lax.all_gather(sums, 'x', axis=0, tiled=False)  31.4 us
    all_gather x1, waiting for transfers between devices, body(): acts = lax.all_gather(acts, 'x', axis=0, tiled=False)  30.8 us
    all_to_all x1, waiting for transfers between devices, body(): lax.all_to_all(picked, 'z', 0, 0, tiled=True).reshape(out_rows, block_size)  22 us
    all_to_all x1, waiting for transfers between devices, body(): mine = lax.all_to_all(pieces, 'x', 0, 0, tiled=True)  13.3 us
    ppermute x1, starting transfers between devices, body(): rows_other = lax.ppermute(rows_mine, 'c', ring(NC, 1))  12.9 us
    all_to_all x1, starting transfers between devices, body(): lax.all_to_all(picked, 'z', 0, 0, tiled=True).reshape(out_rows, block_size)  12.1 us
    ppermute x2, waiting for transfers between devices, body(): got_a = lax.ppermute(send_a, 'z', ring(NZ, step))  11.9 us
    all_gather x1, blocking collectives, body(): rows_mine = lax.all_gather(own_rows, 'y', axis=0, tiled=False)  10.6 us
  transfers between devices with their start and end apart: 12, of which 8 were waited for; matrix products, arithmetic and copies ran while one was open for 1% of the time, Pallas kernels for 3%

profile of v1, /device:TPU:1, one launch (start us, length us, event | category | flops | bytes accessed | tf_op | source)
XLA Modules:
  0.0 220.2 jit_solution(2064250137320491333)
XLA Ops:
  7.2 1.9 copy-done
  9.1 1.8 shard_map.121
  10.9 5.0 %all-to-all-start = ((bf16[4,128,1536]{2,1,0:T(8,128)(2,1)}), bf16[4,128,1536]{2,1,0:T(8,128)(2,1)S(1)}, u32[]{:S(2)}, u32[]{:S(2)}) async-start(bf16[4,128,1536]{2,1,0:T(8,128)(2,1)} %shard_map.121), calls=%async_computation | async-start | bytes 3145728 | tf_op jit(solution)/shard_map/all_to_all | solution.py:286
  15.9 0.1 pad_add_fusion.place_ref
  15.9 1.5 shard_map.120
  17.5 13.3 %all-to-all-done.m_ref = bf16[4,128,1536]{2,1,0:T(8,128)(2,1)S(1)} async-done(((bf16[4,128,1536]{2,1,0:T(8,128)(2,1)}), bf16[4,128,1536]{2,1,0:T(8,128)(2,1)S(1)}, u32[]{:S(2)}, u32[]{:S(2)}) %all-to-all-start) | async-done | bytes 1572896 | tf_op jit(solution)/shard_map/all_to_all | solution.py:286
  30.7 0.0 all-gather.11.cloned.1.call-update
  30.8 0.0 all-gather.9.cloned.1.call-start
  30.8 8.7 %collective-permute-start = (bf16[4,128,1536]{2,1,0:T(8,128)(2,1)S(1)}, bf16[4,128,1536]{2,1,0:T(8,128)(2,1)S(1)}, u32[]{:S(2)}, u32[]{:S(2)}) collective-permute-start(bf16[4,128,1536]{2,1,0:T(8,128)(2,1)S(1)} %all-to-all-done.m_ref), channel_id=1, source_target_pairs={{0,1},{1,0},{2,3},{3,2},{4,5},{5,4},{6,7},{7,6},{8,9},{9,8},{10,11... | collective-permute-start | bytes 4718600 | tf_op jit(solution)/shard_map/ppermute | solution.py:287
  39.5 30.8 %all-gather.11.cloned.1.call-done = bf16[2048,256]{1,0:T(8,128)(2,1)} async-done(((bf16[512,256]{1,0:T(8,128)(2,1)}), bf16[2048,256]{1,0:T(8,128)(2,1)}) %all-gather.11.cloned.1.call-update) | async-done | bytes 1048592 | tf_op jit(solution)/shard_map/all_gather | solution.py:290
  70.4 1.2 copy-done.4
  71.6 3.1 %shard_map.122 = (f32[128,1536]{1,0:T(8,128)S(1)}, bf16[128,1536]{1,0:T(8,128)(2,1)S(1)}, f32[128,1536]{1,0:T(8,128)S(1)}, bf16[128,1536]{1,0:T(8,128)(2,1)S(1)}) custom-call(bf16[4,512,256]{2,1,0:T(8,128)(2,1)S(1)} %bitcast.52, bf16[4,128,1536]{2,1,0:T(8,128)(2,1)S(1)} %all-to-all-done.m_ref, bf16[4,128,1536]{2,1,0:T(8,128)(2,1)S(1)} %collective-permute-done.o_ref), custom_call_target="tpu_custom_call" | custom-call | tf_op jit(solution)/shard_map/pallas_call | solution.py:106
  74.7 3.2 %collective-permute-start.1 = (bf16[128,1536]{1,0:T(8,128)(2,1)S(1)}, bf16[128,1536]{1,0:T(8,128)(2,1)S(1)}, u32[]{:S(2)}, u32[]{:S(2)}) collective-permute-start(bf16[128,1536]{1,0:T(8,128)(2,1)S(1)} %get-tuple-element.18), channel_id=1, source_target_pairs={{0,32},{32,64},{64,96},{96,128},{128,160},{160,192},{192,224},{224... | collective-permute-start | bytes 1179656 | tf_op jit(solution)/shard_map/ppermute | solution.py:294
  77.9 4.4 %collective-permute-start.3 = (bf16[128,1536]{1,0:T(8,128)(2,1)S(1)}, bf16[128,1536]{1,0:T(8,128)(2,1)S(1)}, u32[]{:S(2)}, u32[]{:S(2)}) collective-permute-start(bf16[128,1536]{1,0:T(8,128)(2,1)S(1)} %get-tuple-element.20), channel_id=1, source_target_pairs={{0,480},{32,0},{64,32},{96,64},{128,96},{160,128},{192,160},{224,1... | collective-permute-start | bytes 1179656 | tf_op jit(solution)/shard_map/ppermute | solution.py:295
  82.3 5.9 %collective-permute-done.1 = bf16[128,1536]{1,0:T(8,128)(2,1)S(1)} collective-permute-done((bf16[128,1536]{1,0:T(8,128)(2,1)S(1)}, bf16[128,1536]{1,0:T(8,128)(2,1)S(1)}, u32[]{:S(2)}, u32[]{:S(2)}) %collective-permute-start.1) | collective-permute-done | bytes 393248 | tf_op jit(solution)/shard_map/ppermute | solution.py:294
  88.2 0.1 convert_add_fusion.1
  88.3 1.9 collective-permute-start.2
  90.3 0.1 convert_add_fusion
  90.4 5.5 %collective-permute-start.4 = (bf16[64,1536]{1,0:T(8,128)(2,1)S(1)}, bf16[64,1536]{1,0:T(8,128)(2,1)S(1)}, u32[]{:S(2)}, u32[]{:S(2)}) collective-permute-start(bf16[64,1536]{1,0:T(8,128)(2,1)S(1)} %slice.34), channel_id=1, source_target_pairs={{0,448},{32,480},{64,0},{96,32},{128,64},{160,96},{192,128},{224,1... | collective-permute-start | bytes 589832 | tf_op jit(solution)/shard_map/ppermute | solution.py:295
  95.9 6.0 %collective-permute-done.2 = bf16[64,1536]{1,0:T(8,128)(2,1)S(1)} collective-permute-done((bf16[64,1536]{1,0:T(8,128)(2,1)S(1)}, bf16[64,1536]{1,0:T(8,128)(2,1)S(1)}, u32[]{:S(2)}, u32[]{:S(2)}) %collective-permute-start.2) | collective-permute-done | bytes 196640 | tf_op jit(solution)/shard_map/ppermute | solution.py:294
  101.9 3.2 %collective-permute-done.4 = bf16[64,1536]{1,0:T(8,128)(2,1)S(1)} collective-permute-done((bf16[64,1536]{1,0:T(8,128)(2,1)S(1)}, bf16[64,1536]{1,0:T(8,128)(2,1)S(1)}, u32[]{:S(2)}, u32[]{:S(2)}) %collective-permute-start.4) | collective-permute-done | bytes 196640 | tf_op jit(solution)/shard_map/ppermute | solution.py:295
  105.1 0.8 pad_maximum_fusion
  105.9 0.0 all-gather.13.cloned.1.call-start
  105.9 0.7 all-gather.13.cloned.1.call-update
  106.7 0.2 select_reduce_fusion
  106.8 0.1 reshape.173
  107.0 0.1 copy.21
  107.1 0.1 fusion.9
  107.3 0.1 add_select_fusion
  107.4 0.2 reshape.180
  107.6 0.4 fusion.p_ref
  108.0 31.4 %all-gather.9.cloned.1.call-done.s_ref = bf16[4,128,1536]{2,1,0:T(8,128)(2,1)} async-done(((bf16[1,128,1536]{2,1,0:T(8,128)(2,1)}), bf16[4,128,1536]{2,1,0:T(8,128)(2,1)}) %all-gather.9.cloned.1.call-update) | async-done | bytes 1572880 | tf_op jit(solution)/shard_map/all_gather | solution.py:302
  139.5 1.4 copy-done.1
  140.9 2.6 %shard_map.123 = bf16[512,512]{1,0:T(8,128)(2,1)} custom-call(bf16[512,1536]{1,0:T(8,128)(2,1)S(1)} %fusion.p_ref, bf16[4,128,1536]{2,1,0:T(8,128)(2,1)S(1)} %copy-done.1), custom_call_target="tpu_custom_call" | custom-call | tf_op jit(solution)/shard_map/pallas_call | solution.py:139
  143.5 12.1 %all-to-all-start.1 = ((bf16[16,32,512]{2,1,0:T(8,128)(2,1)}), bf16[16,32,512]{2,1,0:T(8,128)(2,1)S(1)}, u32[]{:S(2)}, u32[]{:S(2)}) async-start(bf16[16,32,512]{2,1,0:T(8,128)(2,1)} %bitcast.8), calls=%async_computation.1 | async-start | bytes 1048576 | tf_op jit(solution)/shard_map/all_to_all | solution.py:316
  155.6 0.0 all-gather.15.cloned.1.call-start
  155.7 0.5 all-gather.15.cloned.1.call-update
  156.3 0.2 fusion.13
  156.4 22.0 %all-to-all-done.1 = bf16[16,32,512]{2,1,0:T(8,128)(2,1)S(1)} async-done(((bf16[16,32,512]{2,1,0:T(8,128)(2,1)}), bf16[16,32,512]{2,1,0:T(8,128)(2,1)S(1)}, u32[]{:S(2)}, u32[]{:S(2)}) %all-to-all-start.1) | async-done | bytes 524320 | tf_op jit(solution)/shard_map/all_to_all | solution.py:316
  178.5 1.6 shard_map.124
  180.0 10.6 %all-gather.1 = bf16[576,512]{1,0:T(8,128)(2,1)S(1)} all-gather(bf16[144,512]{1,0:T(8,128)(2,1)S(1)} %get-tuple-element.21), channel_id=3, replica_groups=mesh['z'=16,'x'=4,'y'=4,'c'=2] {'y'}, dimensions={0}, use_global_device_ids=true | all-gather | bytes 737280 | tf_op jit(solution)/shard_map/all_gather | solution.py:323
  190.7 12.9 %collective-permute-start.5 = (bf16[4,144,512]{2,1,0:T(8,128)(2,1)S(1)}, bf16[4,144,512]{2,1,0:T(8,128)(2,1)S(1)}, u32[]{:S(2)}, u32[]{:S(2)}) collective-permute-start(bf16[4,144,512]{2,1,0:T(8,128)(2,1)S(1)} %bitcast.47), channel_id=1, source_target_pairs={{0,1},{1,0},{2,3},{3,2},{4,5},{5,4},{6,7},{7,6},{8,9},{9,8},{10,11... | collective-permute-start | bytes 1769480 | tf_op jit(solution)/shard_map/ppermute | solution.py:324
  203.6 0.2 compare_reduce_fusion
  203.8 0.1 concatenate.18.f_ref
  203.9 3.0 %all-gather.15.cloned.1.call-done = bf16[1,2,512,512]{3,2,1,0:T(8,128)(2,1)} async-done(((bf16[1,2,64,512]{3,2,1,0:T(8,128)(2,1)}), bf16[1,2,512,512]{3,2,1,0:T(8,128)(2,1)}) %all-gather.15.cloned.1.call-update) | async-done | bytes 1048592 | tf_op jit(solution)/shard_map/all_gather | solution.py:283
  206.9 1.2 copy-done.2
  208.1 1.2 copy-done.3
  209.3 4.3 %shard_map.125 = (f32[2,64,512]{2,1,0:T(8,128)}, f32[2,64,512]{2,1,0:T(8,128)}, bf16[2,512,512]{2,1,0:T(8,128)(2,1)}) custom-call(s32[7]{0:T(128)S(1)} %concatenate.18.f_ref, bf16[4,144,512]{2,1,0:T(8,128)(2,1)S(1)} %bitcast.48, bf16[4,144,512]{2,1,0:T(8,128)(2,1)S(1)} %collective-permute-done.5.o_ref, bf16[2,512,512]{2,1,0:T(8,128)(2,1)S(1)} %bitcast.50, ...), custom_call_target="tpu_custom_call" | custom-call | tf_op jit(solution)/shard_map/pallas_call | solution.py:237
  (37 shorter events, 0.3 us)
Async XLA Ops:
  7.2 1.9 copy-start
  10.9 5.1 %copy-start.7 = (bf16[8,64,256]{2,1,0:T(8,128)(2,1)S(1)}, bf16[8,64,256]{2,1,0:T(8,128)(2,1)}, u32[]{:S(2)}) copy-start(bf16[8,64,256]{2,1,0:T(8,128)(2,1)} %a_ref.1) | copy-start | bytes 786436
  10.9 19.9 %all-to-all-start = ((bf16[4,128,1536]{2,1,0:T(8,128)(2,1)}), bf16[4,128,1536]{2,1,0:T(8,128)(2,1)S(1)}, u32[]{:S(2)}, u32[]{:S(2)}) async-start(bf16[4,128,1536]{2,1,0:T(8,128)(2,1)} %shard_map.121), calls=%async_computation | async-start | bytes 3145728 | tf_op jit(solution)/shard_map/all_to_all | solution.py:286
  15.9 54.5 %all-gather.11.cloned.1.call-start = ((), (), s32[]{:S(2)}) async-start(), calls=%async_computation.3 | async-start | bytes 1310720 | tf_op jit(solution)/shard_map/all_gather | solution.py:290
  30.8 108.7 %all-gather.9.cloned.1.call-start = ((), (), s32[]{:S(2)}) async-start(), calls=%async_computation.2 | async-start | bytes 1966080 | tf_op jit(solution)/shard_map/all_gather | solution.py:302
  30.8 39.6 %collective-permute-start = (bf16[4,128,1536]{2,1,0:T(8,128)(2,1)S(1)}, bf16[4,128,1536]{2,1,0:T(8,128)(2,1)S(1)}, u32[]{:S(2)}, u32[]{:S(2)}) collective-permute-start(bf16[4,128,1536]{2,1,0:T(8,128)(2,1)S(1)} %all-to-all-done.m_ref), channel_id=1, source_target_pairs={{0,1},{1,0},{2,3},{3,2},{4,5},{5,4},{6,7},{7,6},{8,9},{9,8},{10,11... | collective-permute-start | bytes 4718600 | tf_op jit(solution)/shard_map/ppermute | solution.py:287
  70.4 1.2 copy-start.4
  74.7 13.5 %collective-permute-start.1 = (bf16[128,1536]{1,0:T(8,128)(2,1)S(1)}, bf16[128,1536]{1,0:T(8,128)(2,1)S(1)}, u32[]{:S(2)}, u32[]{:S(2)}) collective-permute-start(bf16[128,1536]{1,0:T(8,128)(2,1)S(1)} %get-tuple-element.18), channel_id=1, source_target_pairs={{0,32},{32,64},{64,96},{96,128},{128,160},{160,192},{192,224},{224... | collective-permute-start | bytes 1179656 | tf_op jit(solution)/shard_map/ppermute | solution.py:294
  77.9 12.4 %collective-permute-start.3 = (bf16[128,1536]{1,0:T(8,128)(2,1)S(1)}, bf16[128,1536]{1,0:T(8,128)(2,1)S(1)}, u32[]{:S(2)}, u32[]{:S(2)}) collective-permute-start(bf16[128,1536]{1,0:T(8,128)(2,1)S(1)} %get-tuple-element.20), channel_id=1, source_target_pairs={{0,480},{32,0},{64,32},{96,64},{128,96},{160,128},{192,160},{224,1... | collective-permute-start | bytes 1179656 | tf_op jit(solution)/shard_map/ppermute | solution.py:295
  88.3 13.5 %collective-permute-start.2 = (bf16[64,1536]{1,0:T(8,128)(2,1)S(1)}, bf16[64,1536]{1,0:T(8,128)(2,1)S(1)}, u32[]{:S(2)}, u32[]{:S(2)}) collective-permute-start(bf16[64,1536]{1,0:T(8,128)(2,1)S(1)} %slice.35), channel_id=1, source_target_pairs={{0,64},{32,96},{64,128},{96,160},{128,192},{160,224},{192,256},{22... | collective-permute-start | bytes 589832 | tf_op jit(solution)/shard_map/ppermute | solution.py:294
  90.3 16.3 %copy-start.10 = (s32[96]{0:T(128)S(1)}, s32[96]{0:T(128)}, u32[]{:S(2)}) copy-start(s32[96]{0:T(128)} %param.11) | copy-start | bytes 1156
  90.4 14.7 %collective-permute-start.4 = (bf16[64,1536]{1,0:T(8,128)(2,1)S(1)}, bf16[64,1536]{1,0:T(8,128)(2,1)S(1)}, u32[]{:S(2)}, u32[]{:S(2)}) collective-permute-start(bf16[64,1536]{1,0:T(8,128)(2,1)S(1)} %slice.34), channel_id=1, source_target_pairs={{0,448},{32,480},{64,0},{96,32},{128,64},{160,96},{192,128},{224,1... | collective-permute-start | bytes 589832 | tf_op jit(solution)/shard_map/ppermute | solution.py:295
  105.9 98.0 %all-gather.13.cloned.1.call-start = ((), (), s32[]{:S(2)}) async-start(), calls=%async_computation.4 | async-start | bytes 1179648 | tf_op jit(solution)/shard_map/all_gather | solution.py:282
  139.5 1.4 copy-start.1
  140.9 15.4 %copy-start.9 = (s32[96]{0:T(128)S(1)}, s32[96]{0:T(128)}, u32[]{:S(2)}) copy-start(s32[96]{0:T(128)} %param.12) | copy-start | bytes 1156
  140.9 37.6 %copy-start.8 = (f32[1,2,64,512]{3,2,1,0:T(8,128)S(1)}, f32[1,2,64,512]{3,2,1,0:T(8,128)}, u32[]{:S(2)}) copy-start(f32[1,2,64,512]{3,2,1,0:T(8,128)} %param.17) | copy-start | bytes 786436
  143.5 63.4 %copy-start.5 = (f32[1,2,64,512]{3,2,1,0:T(8,128)S(1)}, f32[1,2,64,512]{3,2,1,0:T(8,128)}, u32[]{:S(2)}) copy-start(f32[1,2,64,512]{3,2,1,0:T(8,128)} %param.13) | copy-start | bytes 786436
  143.5 63.4 %copy-start.6 = (f32[1,2,64,512]{3,2,1,0:T(8,128)S(1)}, f32[1,2,64,512]{3,2,1,0:T(8,128)}, u32[]{:S(2)}) copy-start(f32[1,2,64,512]{3,2,1,0:T(8,128)} %param.14) | copy-start | bytes 786436
  143.5 35.0 %all-to-all-start.1 = ((bf16[16,32,512]{2,1,0:T(8,128)(2,1)}), bf16[16,32,512]{2,1,0:T(8,128)(2,1)S(1)}, u32[]{:S(2)}, u32[]{:S(2)}) async-start(bf16[16,32,512]{2,1,0:T(8,128)(2,1)} %bitcast.8), calls=%async_computation.1 | async-start | bytes 1048576 | tf_op jit(solution)/shard_map/all_to_all | solution.py:316
  155.6 51.2 %all-gather.15.cloned.1.call-start = ((), (), s32[]{:S(2)}) async-start(), calls=%async_computation.5 | async-start | bytes 1179648 | tf_op jit(solution)/shard_map/all_gather | solution.py:283
  190.7 16.2 %collective-permute-start.5 = (bf16[4,144,512]{2,1,0:T(8,128)(2,1)S(1)}, bf16[4,144,512]{2,1,0:T(8,128)(2,1)S(1)}, u32[]{:S(2)}, u32[]{:S(2)}) collective-permute-start(bf16[4,144,512]{2,1,0:T(8,128)(2,1)S(1)} %bitcast.47), channel_id=1, source_target_pairs={{0,1},{1,0},{2,3},{3,2},{4,5},{5,4},{6,7},{7,6},{8,9},{9,8},{10,11... | collective-permute-start | bytes 1769480 | tf_op jit(solution)/shard_map/ppermute | solution.py:324
  206.9 1.2 copy-start.2
  208.1 1.2 copy-start.3
Sparse Core Ops, SparseCore 0:
  30.9 39.4 all-gather.10
  106.0 33.3 all-gather.8
  141.6 31.8 all-gather.12
  175.5 31.3 all-gather.14

commit v2 on v1

v2 whole, which is shorter than its diff:
```python
import jax
import jax.numpy as jnp
from jax import lax
from jax.experimental import pallas as pl
from jax.experimental.pallas import tpu as pltpu
from jax.sharding import Mesh, PartitionSpec as P

STAT_DECAY = 0.9
GRAFT_EPS = 1e-06
HALF = jnp.bfloat16
WIDE = jnp.float32
NZ, NX, NC = 16, 4, 2
TILES = 6
Y_STEPS = (0, 1, 3, 2)
PARAMS = pltpu.CompilerParams(vmem_limit_bytes=16 * 1024 * 1024)


def slot_targets(owners, slot_count):
    block_count = owners.shape[0]
    same_owner = owners[:, None] == owners[None, :]
    earlier = lax.broadcasted_iota(jnp.int32, (block_count, block_count), 1) < lax.broadcasted_iota(
        jnp.int32, (block_count, block_count), 0
    )
    ranked = jnp.sum(jnp.where(same_owner & earlier, 1, 0), axis=1).astype(jnp.int32)
    return owners * slot_count + ranked


def ring(count, step):
    return [(i, (i + step) % count) for i in range(count)]


def iota(shape, dim):
    return lax.broadcasted_iota(jnp.int32, shape, dim)


def dot(a, b, dims=((1,), (0,))):
    return lax.dot_general(a, b, (dims, ((), ())), preferred_element_type=WIDE)


def prepare(activations, out_grads, place):
    block_rows, rows, toks = activations.shape
    part = block_rows // 2
    per_z = rows // NZ
    count = part * rows
    small = count // 2
    half = toks // NC
    width = out_grads.shape[1] // NX
    tile = width // TILES

    def kernel(place_ref, a_ref, b_ref, after_ref, before_ref, across_ref, acts, sems, row_sems):
        z, x, c = place_ref[0], place_ref[1], place_ref[2]
        targets = ((after_ref, 1), (before_ref, 3), (across_ref, 2))
        tok = pl.ds(pl.multiple_of(c * half, half), half)
        copies = []
        for i, (ref, step) in enumerate(targets):
            begin = jnp.bitwise_and(x + step, NX - 1) * width
            for n in range(TILES):
                at = pl.ds(pl.multiple_of(begin + n * tile, tile), tile)
                to = pl.ds(2 * count + n * half, half)
                copies.append(pltpu.make_async_copy(b_ref.at[tok, at], ref.at[to, :], sems.at[i, n]))
        for copy in copies:
            copy.start()
        m, k = iota((small, count), 0), iota((small, count), 1)
        block = m % part
        row = (m // part) % per_z
        tail = m // (part * per_z)
        high = 2 * (tail // 4) + 4 * ((tail // 2) % 2) + 8 * (tail % 2)
        for side in range(2):
            values = a_ref[side * part : (side + 1) * part].reshape(count, toks)
            for odd in range(2):
                dist = high + odd
                goal = jnp.bitwise_and(z + dist if side == 0 else z - dist, NZ - 1)
                pick = (block * rows + goal * per_z + row == k).astype(WIDE).astype(HALF)
                moved = dot(pick, values).astype(HALF)
                turned = jnp.concatenate([moved[:, half:], moved[:, :half]], axis=1)
                at = (1 - odd) * count + side * small
                acts[at : at + small, :] = jnp.where(c == 1, turned, moved)
        last = [
            pltpu.make_async_copy(acts, ref.at[pl.ds(0, 2 * count), :], row_sems.at[i])
            for i, (ref, _) in enumerate(targets)
        ]
        for copy in last:
            copy.start()
        for copy in copies + last:
            copy.wait()

    any_place = pl.BlockSpec(memory_space=pl.ANY)
    return pl.pallas_call(
        kernel,
        out_shape=[jax.ShapeDtypeStruct((2 * count + TILES * half, toks), HALF)] * 3,
        in_specs=[
            pl.BlockSpec(memory_space=pltpu.SMEM),
            pl.BlockSpec(memory_space=pltpu.VMEM),
            any_place,
        ],
        out_specs=[any_place] * 3,
        scratch_shapes=[
            pltpu.VMEM((2 * count, toks), HALF),
            pltpu.SemaphoreType.DMA((3, TILES)),
            pltpu.SemaphoreType.DMA((3,)),
        ],
        compiler_params=pltpu.CompilerParams(vmem_limit_bytes=60 * 1024 * 1024),
    )(place, activations, out_grads)


def partial_products(place, own, out_grads, arrived, swapped, odd):
    toks, tile = out_grads.shape[0], own.shape[1]
    half = toks // NC
    total_rows = own.shape[0] - TILES * half
    count = total_rows // 2
    kind = HALF if odd else WIDE

    def kernel(place_ref, *refs):
        rows_refs, mine, other, (one_ref, two_ref) = refs[:4], refs[4:8], refs[8:12], refs[12:]
        total = None
        for i in range(NX):
            term = dot(rows_refs[i][...], jnp.concatenate([mine[i][...], other[i][...]], axis=0))
            total = term if total is None else total + term
        one_ref[...] = total[: count // 2].astype(kind)
        two_ref[...] = total[count // 2 :].astype(kind)

    rows = pl.BlockSpec((count, tile), lambda n, place_ref: (0 if odd else 1, 0))
    columns = pl.BlockSpec((half, tile), lambda n, place_ref: (total_rows // half + n, 0))
    own_half = pl.BlockSpec((half, tile), lambda n, place_ref: (place_ref[2], place_ref[1] * TILES + n))
    other_half = pl.BlockSpec((half, tile), lambda n, place_ref: (1 - place_ref[2], place_ref[1] * TILES + n))
    return pl.pallas_call(
        kernel,
        out_shape=[jax.ShapeDtypeStruct((count // 2, TILES * tile), kind)] * 2,
        grid_spec=pltpu.PrefetchScalarGridSpec(
            num_scalar_prefetch=1,
            grid=(TILES,),
            in_specs=[rows] * 4 + [own_half] + [columns] * 3 + [other_half] + [columns] * 3,
            out_specs=[pl.BlockSpec((count // 2, tile), lambda n, place_ref: (0, n))] * 2,
        ),
        compiler_params=PARAMS,
    )(place, own, *arrived, out_grads, *arrived, out_grads, *swapped)


def pick_blocks(chosen, sums, block_size):
    sources, rows, width = sums.shape
    columns = width // block_size
    out_rows = chosen.shape[0]
    tile = out_rows // 2

    def kernel(p_ref, s_ref, o_ref):
        total = None
        for pair in range(sources // 2):
            depth = 2 * columns * rows
            pieces = [
                s_ref[x, :, j * block_size : (j + 1) * block_size]
                for x in (2 * pair, 2 * pair + 1)
                for j in range(columns)
            ]
            term = dot(p_ref[:, pair * depth : (pair + 1) * depth], jnp.concatenate(pieces, axis=0))
            total = term if total is None else total + term
        o_ref[...] = total.astype(HALF)

    return pl.pallas_call(
        kernel,
        grid=(2,),
        out_shape=jax.ShapeDtypeStruct((out_rows, block_size), HALF),
        in_specs=[
            pl.BlockSpec((tile, chosen.shape[1]), lambda n: (n, 0)),
            pl.BlockSpec(sums.shape, lambda n: (0, 0, 0)),
        ],
        out_specs=pl.BlockSpec((tile, block_size), lambda n: (n, 0)),
        compiler_params=PARAMS,
    )(chosen, sums)


def finish_sum(limits, pieces, acc):
    slots, rows, block_size = acc.shape
    per_z = rows // NZ
    total_rows = slots * rows
    piece_rows = pieces.shape[0]

    def kernel(lim_ref, p_ref, a_ref, g_ref, n_ref):
        m, k = iota((total_rows, piece_rows), 0), iota((total_rows, piece_rows), 1)
        row = k % per_z
        piece = (k // per_z) % 2
        slot = (k // (2 * per_z)) % slots
        source = k // (2 * per_z * slots)
        goal = jnp.bitwise_and(source + 8 * piece, NZ - 1)
        adds = (slot * rows + goal * per_z + row == m).astype(WIDE).astype(HALF)
        grad = dot(adds, p_ref[...])
        lane = iota((16, block_size), 1)
        extra_row = iota((16, block_size), 0)
        extra = jnp.zeros((16, block_size), WIDE)
        for s in range(slots):
            live = iota((rows, block_size), 0) < lim_ref[s]
            own = jnp.where(live, grad[s * rows : (s + 1) * rows], 0.0)
            new = a_ref[s] + own * own
            n_ref[s] = new
            grafted = own / (jnp.sqrt(new) + GRAFT_EPS)
            norm = jnp.sum(jnp.sum(grafted * grafted, axis=0, keepdims=True), axis=1, keepdims=True)
            high = norm.astype(HALF).astype(WIDE)
            middle = (norm - high).astype(HALF).astype(WIDE)
            low = norm - high - middle
            spread = jnp.where(lane == 0, high, jnp.where(lane == 1, middle, jnp.where(lane == 2, low, 0.0)))
            extra = jnp.where(extra_row == s, spread, extra)
            g_ref[s * rows : (s + 1) * rows, :] = own.astype(HALF)
        g_ref[total_rows:, :] = extra.astype(HALF)

    vmem = pl.BlockSpec(memory_space=pltpu.VMEM)
    return pl.pallas_call(
        kernel,
        out_shape=[
            jax.ShapeDtypeStruct((total_rows + 16, block_size), HALF),
            jax.ShapeDtypeStruct(acc.shape, WIDE),
        ],
        in_specs=[pl.BlockSpec(memory_space=pltpu.SMEM), vmem, vmem],
        out_specs=[vmem, vmem],
        compiler_params=PARAMS,
    )(limits, pieces, acc)


def update(facts, mine, other, roots_mine, roots_other, left_stat, right_stat):
    ny = mine.shape[0]
    slots, rows, block_size = left_stat.shape
    all_rows = mine.shape[1]

    def kernel(f_ref, m_ref, o_ref, *refs):
        root_refs, (t_ref, ls_ref, rs_ref, ln_ref, rn_ref, d_ref, roots) = refs[:ny], refs[ny:]
        s = pl.program_id(0)
        core, own_y, own_mp = f_ref[0], f_ref[1], f_ref[2]
        live, taken = f_ref[3 + s], f_ref[5 + s]
        at = pl.ds(pl.multiple_of(s * rows, rows), rows)
        for i, step in enumerate(Y_STEPS[:ny]):
            source = lax.rem(own_y + step, ny) * NC
            for ref, who in ((root_refs[i], core), (t_ref.at[i], 1 - core)):
                to = pl.ds(pl.multiple_of((source + who) * rows, rows), rows)
                for kind in range(2):
                    roots[kind, to, :] = ref[kind, 0]
        parts = []
        norm = jnp.zeros((1, 1), WIDE)
        tail_row = iota((16, block_size), 0) == s
        for y in range(ny):
            a, b = m_ref[y, at, :], o_ref[y, at, :]
            parts += [jnp.where(core == 0, a, b), jnp.where(core == 0, b, a)]
            for ref in (m_ref, o_ref):
                tail = jnp.where(tail_row, ref[y, slots * rows : all_rows, :].astype(WIDE), 0.0)
                norm += jnp.sum(jnp.sum(tail, axis=0, keepdims=True), axis=1, keepdims=True)
        grad = jnp.concatenate(parts, axis=0)
        prod = dot(grad, roots[1], ((1,), (1,))).astype(HALF)
        raw = dot(roots[0], prod)
        raw = jnp.where(iota(raw.shape, 0) < live, raw, 0.0)
        raw_sq = jnp.sum(jnp.sum(raw * raw, axis=0, keepdims=True), axis=1, keepdims=True)
        factor = jnp.sqrt(norm) / jnp.sqrt(raw_sq + GRAFT_EPS)
        d_ref[0] = jnp.where(taken == 1, factor * raw, 0.0).astype(HALF)
        own = m_ref[own_y, at, :]
        left_cols = dot(own, grad, ((1,), (1,)))
        own_columns = (iota((block_size, rows), 0) == own_mp * rows + iota((block_size, rows), 1)).astype(WIDE)
        columns = dot(grad, own_columns.astype(HALF)).astype(HALF)
        right_rows = dot(columns, grad, ((0,), (0,)))
        for old_ref, value, new_ref in ((ls_ref, left_cols, ln_ref), (rs_ref, right_rows, rn_ref)):
            old = old_ref[0]
            fresh = STAT_DECAY * old + (1.0 - STAT_DECAY) * value / block_size
            new_ref[0] = jnp.where(taken == 1, fresh, old)

    whole = pl.BlockSpec((ny, all_rows, block_size), lambda s: (0, 0, 0))
    square = pl.BlockSpec((1, block_size, block_size), lambda s: (s, 0, 0))
    strip = pl.BlockSpec((1, rows, block_size), lambda s: (s, 0, 0))
    return pl.pallas_call(
        kernel,
        grid=(slots,),
        out_shape=[
            jax.ShapeDtypeStruct(left_stat.shape, WIDE),
            jax.ShapeDtypeStruct(right_stat.shape, WIDE),
            jax.ShapeDtypeStruct((slots, block_size, block_size), HALF),
        ],
        in_specs=[pl.BlockSpec(memory_space=pltpu.SMEM), whole, whole]
        + [pl.BlockSpec((2, 1, rows, block_size), lambda s: (0, s, 0, 0))] * ny
        + [pl.BlockSpec((ny, 2, 1, rows, block_size), lambda s: (0, 0, s, 0, 0)), strip, strip],
        out_specs=[strip, strip, square],
        scratch_shapes=[pltpu.VMEM((2, block_size, block_size), HALF)],
        compiler_params=PARAMS,
    )(facts, mine, other, *roots_mine, roots_other, left_stat, right_stat)


def body(
    activations,
    out_grads,
    owners,
    live_rows,
    left_stat,
    right_stat,
    left_root,
    right_root,
    grad_acc,
):
    z, x, y, c = (lax.axis_index(name) for name in ("z", "x", "y", "c"))
    block_rows, rows, toks = activations.shape
    block_size = left_stat.shape[3]
    slots = left_stat.shape[1]
    block_count = owners.shape[0]
    per_z = rows // NZ
    columns = out_grads.shape[1] // block_size // NX
    half_rows = block_rows // 2
    my_owner = z * NX + x
    my_mp = y * NC + c
    my_rows = my_mp * rows

    place = jnp.stack([z, x, c]).astype(jnp.int32)
    pieces = prepare(activations, out_grads, place)
    arrived = [lax.ppermute(piece, "x", ring(NX, step)) for piece, step in zip(pieces, (1, -1, 2))]
    swapped = [lax.ppermute(piece, "c", ring(NC, 1)) for piece in arrived]
    send_a, send_b = partial_products(place, pieces[0], out_grads, arrived, swapped, True)
    keep_a, keep_b = partial_products(place, pieces[0], out_grads, arrived, swapped, False)

    for step in (1, 2, 4):
        got_a = lax.ppermute(send_a, "z", ring(NZ, step))
        got_b = lax.ppermute(send_b, "z", ring(NZ, -step))
        keep_a, keep_b = keep_a + got_a, keep_b + got_b
        if step < 4:
            part = keep_a.shape[0] // 2
            send_a, send_b = keep_a[part:].astype(HALF), keep_b[part:].astype(HALF)
            keep_a, keep_b = keep_a[:part], keep_b[:part]
    sums = jnp.concatenate([keep_a, keep_b], axis=0).astype(HALF)
    sums = lax.all_gather(sums, "x", axis=0, tiled=False)

    targets = slot_targets(owners, slots)
    by_block = targets.reshape(2, half_rows, NX, columns).transpose(2, 3, 0, 1)[:, :, :, None, None, :]
    shape = (NX, columns, 2, 2, per_z, half_rows)
    owner = by_block // slots
    code = (((owner // NX) * slots + by_block % slots) * 2 + iota(shape, 3)) * per_z + iota(shape, 4)
    code = jnp.where(owner % NX == x, code, -1).reshape(1, -1)
    out_rows = NZ * slots * 2 * per_z
    chosen = (code == iota((out_rows, 1), 0)).astype(HALF)

    picked = pick_blocks(chosen, sums, block_size).reshape(NZ, out_rows // NZ, block_size)
    picked, left_root, right_root = lax.optimization_barrier((picked, left_root, right_root))
    roots = jnp.concatenate([left_root, right_root], axis=0)
    ny = lax.axis_size("y")
    roots_mine = [roots] + [lax.ppermute(roots, "y", ring(ny, -step)) for step in Y_STEPS[1:ny]]
    roots_other = lax.ppermute(jnp.stack(roots_mine), "c", ring(NC, 1))
    arrived = lax.all_to_all(picked, "z", 0, 0, tiled=True).reshape(out_rows, block_size)

    wanted = my_owner * slots + iota((slots, block_count), 0)
    matched = targets[None, :] == wanted
    occupied = jnp.any(matched, axis=1).astype(jnp.int32)
    live_mine = jnp.sum(jnp.where(matched, live_rows[None, :], 0), axis=1).astype(jnp.int32)
    own_rows, acc_next = finish_sum(live_mine - my_rows, arrived, grad_acc[0])
    rows_mine = lax.all_gather(own_rows, "y", axis=0, tiled=False)
    rows_other = lax.ppermute(rows_mine, "c", ring(NC, 1))
    facts = jnp.concatenate([jnp.stack([c, y, my_mp]).astype(jnp.int32), live_mine, occupied])
    left_next, right_next, directions = update(
        facts, rows_mine, rows_other, roots_mine, roots_other, left_stat[0], right_stat[0]
    )
    return (left_next[None], right_next[None], acc_next[None], directions[None])


def solution(mesh):
    dp, mp = mesh.devices.shape
    parts = Mesh(mesh.devices.reshape(NZ, NX, mp // NC, NC), ("z", "x", "y", "c"))
    owner, strip = ("z", "x"), ("y", "c")
    state = P(owner, None, strip, None)
    return jax.shard_map(
        body,
        mesh=parts,
        in_specs=(P(None, strip, owner), P(owner, None), P(), P(), state, state, state, state, state),
        out_specs=(state, state, state, P(owner, None, None, None)),
        check_vma=False,
    )
```

time: 221 us -> 217 us (0.982)
  waiting for transfers between devices: 117 us -> 31.1 us
  Pallas kernels: 14.9 us -> 57 us
  starting transfers between devices: 53.9 us -> 93.3 us
  blocking collectives: 10.6 us -> 24 us
  between operations: 14 us -> 1.14 us
  local copies, waits for them, and re-layouts: 7.58 us -> 4.62 us
    all_gather x4 -> x0, waiting for transfers between devices: 65.2 us -> none  [the longest x1 31.4 us: body(): sums = lax.all_gather(sums, 'x', axis=0, tiled=False)]
    pallas_call x3, Pallas kernels: 6.44 us -> 49.6 us  [the longest x1 38.3 us: prepare(): pl.pallas_call(kernel, out_shape=[jax.ShapeDtypeStruct((2 * count + TILES...]
    ppermute x1 -> x10, starting transfers between devices: 8.7 us -> 46.8 us  [the longest x3 20 us: body(): swapped = [lax.ppermute(piece, 'c', ring(NC, 1)) for piece in arrived]]
    all_to_all x1, waiting for transfers between devices: 22 us -> 0.01 us  [body(): lax.all_to_all(picked, 'z', 0, 0, tiled=True).reshape(out_rows, block_size)]
    ppermute x1 -> x10, waiting for transfers between devices: 0.01 us -> 16.9 us  [the longest x3 7.86 us: body(): lax.ppermute(roots, 'y', ring(ny, -step))]
    all_to_all x1 -> x0, waiting for transfers between devices: 13.3 us -> none  [body(): mine = lax.all_to_all(pieces, 'x', 0, 0, tiled=True)]
    all_gather x0 -> x1, blocking collectives: none -> 13 us  [body(): sums = lax.all_gather(sums, 'x', axis=0, tiled=False)]
    ppermute x2 -> x3, starting transfers between devices: 9.88 us -> 22.4 us  [body(): got_b = lax.ppermute(send_b, 'z', ring(NZ, -step))]
  transfers between devices with their start and end apart: 12 -> 18, of which waited for: 8 -> 8; matrix products, arithmetic and copies ran while one was open for 1% -> 2% of each run, Pallas kernels for 3% -> 3%
where the time goes in v2:
time: 217 us; the launch traced here: 216 us
  starting transfers between devices  93.3 us (43%)
  Pallas kernels  57 us (26%)
  waiting for transfers between devices  31.1 us (14%)
  blocking collectives  24 us (11%)
  local copies, waits for them, and re-layouts  4.62 us (2%)
  other arithmetic  4.4 us (2%)
    pallas_call x1, Pallas kernels, prepare(): pl.pallas_call(kernel, out_shape=[jax.ShapeDtypeStruct((2 * count + TILES...  38.3 us
    ppermute x3, starting transfers between devices, body(): got_b = lax.ppermute(send_b, 'z', ring(NZ, -step))  22.4 us
    ppermute x3, starting transfers between devices, body(): swapped = [lax.ppermute(piece, 'c', ring(NC, 1)) for piece in arrived]  20 us
    all_gather x1, blocking collectives, body(): sums = lax.all_gather(sums, 'x', axis=0, tiled=False)  13 us
    ppermute x3, waiting for transfers between devices, body(): got_a = lax.ppermute(send_a, 'z', ring(NZ, step))  12.9 us
    pallas_call x2, Pallas kernels, partial_products(): pl.pallas_call(kernel, out_shape=[jax.ShapeDtypeStruct((count // 2, TILES...  11.3 us
    all_gather x1, blocking collectives, body(): rows_mine = lax.all_gather(own_rows, 'y', axis=0, tiled=False)  11 us
    ppermute x3, starting transfers between devices, body(): lax.ppermute(piece, 'x', ring(NX, step))  10.8 us
  transfers between devices with their start and end apart: 18, of which 8 were waited for; matrix products, arithmetic and copies ran while one was open for 2% of the time, Pallas kernels for 3%

profile of v2, /device:TPU:1, one launch (start us, length us, event | category | flops | bytes accessed | tf_op | source)
XLA Modules:
  0.0 215.6 jit_solution(2990225487684773710)
XLA Ops:
  0.7 0.6 pad_add_fusion.place_ref
  1.3 38.3 %shard_map.120 = (bf16[1280,256]{1,0:T(8,128)(2,1)}, bf16[1280,256]{1,0:T(8,128)(2,1)}, bf16[1280,256]{1,0:T(8,128)(2,1)}) custom-call(s32[3]{0:T(128)} %pad_add_fusion.place_ref, bf16[8,64,256]{2,1,0:T(8,128)(2,1)} %a_ref.1, bf16[256,6144]{1,0:T(8,128)(2,1)} %refs_8_.3), custom_call_target="tpu_custom_call" | custom-call | tf_op jit(solution)/shard_map/pallas_call | solution.py:88
  39.6 4.0 %collective-permute-start = (bf16[1280,256]{1,0:T(8,128)(2,1)}, bf16[1280,256]{1,0:T(8,128)(2,1)}, u32[]{:S(2)}, u32[]{:S(2)}) collective-permute-start(bf16[1280,256]{1,0:T(8,128)(2,1)} %get-tuple-element.19.refs_0_), channel_id=1, source_target_pairs={{0,8},{8,16},{16,24},{24,0},{1,9},{9,17},{17,25},{25,1},{2,10},{10... | collective-permute-start | bytes 1966088 | tf_op jit(solution)/shard_map/ppermute | solution.py:305
  43.5 3.2 %collective-permute-start.1 = (bf16[1280,256]{1,0:T(8,128)(2,1)}, bf16[1280,256]{1,0:T(8,128)(2,1)}, u32[]{:S(2)}, u32[]{:S(2)}) collective-permute-start(bf16[1280,256]{1,0:T(8,128)(2,1)} %get-tuple-element.20), channel_id=1, source_target_pairs={{0,24},{8,0},{16,8},{24,16},{1,25},{9,1},{17,9},{25,17},{2,26},{10... | collective-permute-start | bytes 1966088 | tf_op jit(solution)/shard_map/ppermute | solution.py:305
  46.7 3.6 %collective-permute-start.2 = (bf16[1280,256]{1,0:T(8,128)(2,1)}, bf16[1280,256]{1,0:T(8,128)(2,1)}, u32[]{:S(2)}, u32[]{:S(2)}) collective-permute-start(bf16[1280,256]{1,0:T(8,128)(2,1)} %get-tuple-element.21), channel_id=1, source_target_pairs={{0,16},{8,24},{16,0},{24,8},{1,17},{9,25},{17,1},{25,9},{2,18},{10... | collective-permute-start | bytes 1966088 | tf_op jit(solution)/shard_map/ppermute | solution.py:305
  50.4 0.2 select_reduce_fusion
  50.5 3.1 %collective-permute-done.refs_1_.refs_5_ = bf16[1280,256]{1,0:T(8,128)(2,1)} collective-permute-done((bf16[1280,256]{1,0:T(8,128)(2,1)}, bf16[1280,256]{1,0:T(8,128)(2,1)}, u32[]{:S(2)}, u32[]{:S(2)}) %collective-permute-start) | collective-permute-done | bytes 655392 | tf_op jit(solution)/shard_map/ppermute | solution.py:305
  53.6 12.1 %collective-permute-start.3 = (bf16[1280,256]{1,0:T(8,128)(2,1)}, bf16[1280,256]{1,0:T(8,128)(2,1)}, u32[]{:S(2)}, u32[]{:S(2)}) collective-permute-start(bf16[1280,256]{1,0:T(8,128)(2,1)} %collective-permute-done.refs_1_.refs_5_), channel_id=1, source_target_pairs={{0,1},{1,0},{2,3},{3,2},{4,5},{5,4},{6,7},{7,6},{8,9},{9,8},{10,11... | collective-permute-start | bytes 1966088 | tf_op jit(solution)/shard_map/ppermute | solution.py:306
  65.8 4.4 %collective-permute-start.4 = (bf16[1280,256]{1,0:T(8,128)(2,1)}, bf16[1280,256]{1,0:T(8,128)(2,1)}, u32[]{:S(2)}, u32[]{:S(2)}) collective-permute-start(bf16[1280,256]{1,0:T(8,128)(2,1)} %collective-permute-done.1.refs_2_.refs_6_), channel_id=1, source_target_pairs={{0,1},{1,0},{2,3},{3,2},{4,5},{5,4},{6,7},{7,6},{8,9},{9,8},{10,11... | collective-permute-start | bytes 1966088 | tf_op jit(solution)/shard_map/ppermute | solution.py:306
  70.2 4.3 %collective-permute-done.2.refs_3_.refs_7_ = bf16[1280,256]{1,0:T(8,128)(2,1)} collective-permute-done((bf16[1280,256]{1,0:T(8,128)(2,1)}, bf16[1280,256]{1,0:T(8,128)(2,1)}, u32[]{:S(2)}, u32[]{:S(2)}) %collective-permute-start.2) | collective-permute-done | bytes 655392 | tf_op jit(solution)/shard_map/ppermute | solution.py:305
  74.4 3.4 %collective-permute-start.5 = (bf16[1280,256]{1,0:T(8,128)(2,1)}, bf16[1280,256]{1,0:T(8,128)(2,1)}, u32[]{:S(2)}, u32[]{:S(2)}) collective-permute-start(bf16[1280,256]{1,0:T(8,128)(2,1)} %collective-permute-done.2.refs_3_.refs_7_), channel_id=1, source_target_pairs={{0,1},{1,0},{2,3},{3,2},{4,5},{5,4},{6,7},{7,6},{8,9},{9,8},{10,11... | collective-permute-start | bytes 1966088 | tf_op jit(solution)/shard_map/ppermute | solution.py:306
  77.9 0.1 reshape.141
  78.0 0.1 copy.21
  78.3 1.6 collective-permute-done.5.refs_11_
  80.0 1.1 copy-done.1
  81.0 6.0 %shard_map.122 = (bf16[128,1536]{1,0:T(8,128)(2,1)}, bf16[128,1536]{1,0:T(8,128)(2,1)S(1)}) custom-call(s32[3]{0:T(128)S(1)} %copy-done.6, bf16[1280,256]{1,0:T(8,128)(2,1)S(1)} %copy-done.1, bf16[1280,256]{1,0:T(8,128)(2,1)} %collective-permute-done.refs_1_.refs_5_, bf16[1280,256]{1,0:T(8,128)(2,1)} %collective-permute-done.1.refs_2_.refs_6_, ...), custom_call_target="tpu_custom_call" | custom-call | tf_op jit(solution)/shard_map/pallas_call | solution.py:126
  87.1 6.1 %collective-permute-start.6 = (bf16[128,1536]{1,0:T(8,128)(2,1)}, bf16[128,1536]{1,0:T(8,128)(2,1)}, u32[]{:S(2)}, u32[]{:S(2)}) collective-permute-start(bf16[128,1536]{1,0:T(8,128)(2,1)} %get-tuple-element.23), channel_id=1, source_target_pairs={{0,32},{32,64},{64,96},{96,128},{128,160},{160,192},{192,224},{224... | collective-permute-start | bytes 1179656 | tf_op jit(solution)/shard_map/ppermute | solution.py:311
  93.1 0.7 add_select_fusion
  93.8 1.0 select_n.49
  94.9 9.5 %collective-permute-start.9 = (bf16[128,1536]{1,0:T(8,128)(2,1)S(1)}, bf16[128,1536]{1,0:T(8,128)(2,1)S(1)}, u32[]{:S(2)}, u32[]{:S(2)}) collective-permute-start(bf16[128,1536]{1,0:T(8,128)(2,1)S(1)} %get-tuple-element.25), channel_id=1, source_target_pairs={{0,480},{32,0},{64,32},{96,64},{128,96},{160,128},{192,160},{224,1... | collective-permute-start | bytes 1179656 | tf_op jit(solution)/shard_map/ppermute | solution.py:312
  104.4 1.1 copy-done.2
  105.5 5.3 %shard_map.121 = (f32[128,1536]{1,0:T(8,128)S(1)}, f32[128,1536]{1,0:T(8,128)S(1)}) custom-call(s32[3]{0:T(128)S(1)} %copy-done.6, bf16[1280,256]{1,0:T(8,128)(2,1)S(1)} %copy-done.2, bf16[1280,256]{1,0:T(8,128)(2,1)} %collective-permute-done.refs_1_.refs_5_, bf16[1280,256]{1,0:T(8,128)(2,1)} %collective-permute-done.1.refs_2_.refs_6_, ...), custom_call_target="tpu_custom_call" | custom-call | tf_op jit(solution)/shard_map/pallas_call | solution.py:126
  110.8 1.1 convert_add_fusion.1
  111.9 1.9 collective-permute-start.7
  113.9 0.1 convert_add_fusion
  114.0 5.6 %collective-permute-start.10 = (bf16[64,1536]{1,0:T(8,128)(2,1)S(1)}, bf16[64,1536]{1,0:T(8,128)(2,1)S(1)}, u32[]{:S(2)}, u32[]{:S(2)}) collective-permute-start(bf16[64,1536]{1,0:T(8,128)(2,1)S(1)} %slice.60), channel_id=1, source_target_pairs={{0,448},{32,480},{64,0},{96,32},{128,64},{160,96},{192,128},{224,1... | collective-permute-start | bytes 589832 | tf_op jit(solution)/shard_map/ppermute | solution.py:312
  119.6 7.0 %collective-permute-done.7 = bf16[64,1536]{1,0:T(8,128)(2,1)S(1)} collective-permute-done((bf16[64,1536]{1,0:T(8,128)(2,1)S(1)}, bf16[64,1536]{1,0:T(8,128)(2,1)S(1)}, u32[]{:S(2)}, u32[]{:S(2)}) %collective-permute-start.7) | collective-permute-done | bytes 196640 | tf_op jit(solution)/shard_map/ppermute | solution.py:311
  126.7 1.9 collective-permute-start.8
  128.7 7.3 %collective-permute-start.11 = (bf16[32,1536]{1,0:T(8,128)(2,1)S(1)}, bf16[32,1536]{1,0:T(8,128)(2,1)S(1)}, u32[]{:S(2)}, u32[]{:S(2)}) collective-permute-start(bf16[32,1536]{1,0:T(8,128)(2,1)S(1)} %slice.62), channel_id=1, source_target_pairs={{0,384},{32,416},{64,448},{96,480},{128,0},{160,32},{192,64},{224,... | collective-permute-start | bytes 294920 | tf_op jit(solution)/shard_map/ppermute | solution.py:312
  136.0 5.9 %collective-permute-done.8 = bf16[32,1536]{1,0:T(8,128)(2,1)S(1)} collective-permute-done((bf16[32,1536]{1,0:T(8,128)(2,1)S(1)}, bf16[32,1536]{1,0:T(8,128)(2,1)S(1)}, u32[]{:S(2)}, u32[]{:S(2)}) %collective-permute-start.8) | collective-permute-done | bytes 98336 | tf_op jit(solution)/shard_map/ppermute | solution.py:311
  142.0 13.0 %all_gather.10.s_ref = bf16[4,64,1536]{2,1,0:T(8,128)(2,1)S(1)} all-gather(bf16[1,64,1536]{2,1,0:T(8,128)(2,1)S(1)} %pad_maximum_fusion.1), channel_id=1, replica_groups=mesh['z'=16,'x'=4,'y'=4,'c'=2] {'x'}, dimensions={0}, use_global_device_ids=true | all-gather | bytes 983040 | tf_op jit(solution)/shard_map/all_gather | solution.py:319
  155.0 1.3 shard_map.123
  156.3 9.6 %all-to-all-start = ((bf16[16,16,512]{2,1,0:T(8,128)(2,1)}), bf16[16,16,512]{2,1,0:T(8,128)(2,1)S(1)}, u32[]{:S(2)}, u32[]{:S(2)}) async-start(bf16[16,16,512]{2,1,0:T(8,128)(2,1)} %bitcast.8), calls=%async_computation | async-start | bytes 524288 | tf_op jit(solution)/shard_map/all_to_all | solution.py:336
  166.0 4.7 %collective-permute-start.13 = (bf16[2,2,64,512]{3,2,1,0:T(8,128)(2,1)S(1)}, bf16[2,2,64,512]{3,2,1,0:T(8,128)(2,1)S(1)}, u32[]{:S(2)}, u32[]{:S(2)}) collective-permute-start(bf16[2,2,64,512]{3,2,1,0:T(8,128)(2,1)S(1)} %constant_dynamic-update-slice_fusion.refs_0_), channel_id=1, source_target_pairs={{0,6},{2,0},{4,2},{6,4},{1,7},{3,1},{5,3},{7,5},{8,14},{10,8},{12,... | collective-permute-start | bytes 786440 | tf_op jit(solution)/shard_map/ppermute | solution.py:334
  170.6 1.9 collective-permute-start.14
  172.6 3.5 %collective-permute-start.15 = (bf16[2,2,64,512]{3,2,1,0:T(8,128)(2,1)S(1)}, bf16[2,2,64,512]{3,2,1,0:T(8,128)(2,1)S(1)}, u32[]{:S(2)}, u32[]{:S(2)}) collective-permute-start(bf16[2,2,64,512]{3,2,1,0:T(8,128)(2,1)S(1)} %constant_dynamic-update-slice_fusion.refs_0_), channel_id=1, source_target_pairs={{0,4},{2,6},{4,0},{6,2},{1,5},{3,7},{5,1},{7,3},{8,12},{10,14},{12... | collective-permute-start | bytes 786440 | tf_op jit(solution)/shard_map/ppermute | solution.py:334
  176.2 4.0 %collective-permute-done.14.refs_2_ = bf16[2,2,64,512]{3,2,1,0:T(8,128)(2,1)S(1)} collective-permute-done((bf16[2,2,64,512]{3,2,1,0:T(8,128)(2,1)S(1)}, bf16[2,2,64,512]{3,2,1,0:T(8,128)(2,1)S(1)}, u32[]{:S(2)}, u32[]{:S(2)}) %collective-permute-start.14) | collective-permute-done | bytes 262176 | tf_op jit(solution)/shard_map/ppermute | solution.py:334
  180.1 3.9 %collective-permute-done.15.refs_3_ = bf16[2,2,64,512]{3,2,1,0:T(8,128)(2,1)S(1)} collective-permute-done((bf16[2,2,64,512]{3,2,1,0:T(8,128)(2,1)S(1)}, bf16[2,2,64,512]{3,2,1,0:T(8,128)(2,1)S(1)}, u32[]{:S(2)}, u32[]{:S(2)}) %collective-permute-start.15) | collective-permute-done | bytes 262176 | tf_op jit(solution)/shard_map/ppermute | solution.py:334
  184.0 1.1 pad_maximum_fusion
  185.1 6.0 %collective-permute-start.16 = (bf16[4,2,2,64,512]{4,3,2,1,0:T(8,128)(2,1)}, bf16[4,2,2,64,512]{4,3,2,1,0:T(8,128)(2,1)S(1)}, u32[]{:S(2)}, u32[]{:S(2)}) collective-permute-start(bf16[4,2,2,64,512]{4,3,2,1,0:T(8,128)(2,1)} %pad_maximum_fusion), channel_id=1, source_target_pairs={{0,1},{1,0},{2,3},{3,2},{4,5},{5,4},{6,7},{7,6},{8,9},{9,8},{10,11... | collective-permute-start | bytes 3145736 | tf_op jit(solution)/shard_map/ppermute | solution.py:335
  191.1 0.2 fusion.13
  191.3 1.5 shard_map.124
  192.9 11.0 %all-gather = bf16[576,512]{1,0:T(8,128)(2,1)S(1)} all-gather(bf16[144,512]{1,0:T(8,128)(2,1)S(1)} %get-tuple-element.27), channel_id=2, replica_groups=mesh['z'=16,'x'=4,'y'=4,'c'=2] {'y'}, dimensions={0}, use_global_device_ids=true | all-gather | bytes 737280 | tf_op jit(solution)/shard_map/all_gather | solution.py:343
  203.9 4.6 %collective-permute-start.12 = (bf16[4,144,512]{2,1,0:T(8,128)(2,1)S(1)}, bf16[4,144,512]{2,1,0:T(8,128)(2,1)S(1)}, u32[]{:S(2)}, u32[]{:S(2)}) collective-permute-start(bf16[4,144,512]{2,1,0:T(8,128)(2,1)S(1)} %bitcast.49), channel_id=1, source_target_pairs={{0,1},{1,0},{2,3},{3,2},{4,5},{5,4},{6,7},{7,6},{8,9},{9,8},{10,11... | collective-permute-start | bytes 1769480 | tf_op jit(solution)/shard_map/ppermute | solution.py:344
  208.5 0.2 compare_reduce_fusion
  208.8 1.3 collective-permute-done.12.o_ref
  210.1 0.9 copy-done.4
  211.0 4.6 %shard_map.125 = (f32[2,64,512]{2,1,0:T(8,128)}, f32[2,64,512]{2,1,0:T(8,128)}, bf16[2,512,512]{2,1,0:T(8,128)(2,1)}) custom-call(s32[7]{0:T(128)S(1)} %concatenate.21.f_ref, bf16[4,144,512]{2,1,0:T(8,128)(2,1)S(1)} %bitcast.50, bf16[4,144,512]{2,1,0:T(8,128)(2,1)S(1)} %collective-permute-done.12.o_ref, ...), custom_call_target="tpu_custom_call" | custom-call | tf_op jit(solution)/shard_map/pallas_call | solution.py:263
  (50 shorter events, 0.6 us)
Async XLA Ops:
  0.6 79.3 %copy-start = (bf16[256,6144]{1,0:T(8,128)(2,1)S(1)}, bf16[256,6144]{1,0:T(8,128)(2,1)}, u32[]{:S(2)}) copy-start(bf16[256,6144]{1,0:T(8,128)(2,1)} %refs_8_.3) | copy-start | bytes 9437188
  0.6 49.7 %copy-start.10 = (s32[96]{0:T(128)S(1)}, s32[96]{0:T(128)}, u32[]{:S(2)}) copy-start(s32[96]{0:T(128)} %param.11) | copy-start | bytes 1156
  1.2 78.7 %copy-start.6 = (s32[3]{0:T(128)S(1)}, s32[3]{0:T(128)}, u32[]{:S(2)}) copy-start(s32[3]{0:T(128)} %pad_add_fusion.place_ref) | copy-start | bytes 40
  39.6 14.1 %collective-permute-start = (bf16[1280,256]{1,0:T(8,128)(2,1)}, bf16[1280,256]{1,0:T(8,128)(2,1)}, u32[]{:S(2)}, u32[]{:S(2)}) collective-permute-start(bf16[1280,256]{1,0:T(8,128)(2,1)} %get-tuple-element.19.refs_0_), channel_id=1, source_target_pairs={{0,8},{8,16},{16,24},{24,0},{1,9},{9,17},{17,25},{25,1},{2,10},{10... | collective-permute-start | bytes 1966088 | tf_op jit(solution)/shard_map/ppermute | solution.py:305
  43.5 22.2 %collective-permute-start.1 = (bf16[1280,256]{1,0:T(8,128)(2,1)}, bf16[1280,256]{1,0:T(8,128)(2,1)}, u32[]{:S(2)}, u32[]{:S(2)}) collective-permute-start(bf16[1280,256]{1,0:T(8,128)(2,1)} %get-tuple-element.20), channel_id=1, source_target_pairs={{0,24},{8,0},{16,8},{24,16},{1,25},{9,1},{17,9},{25,17},{2,26},{10... | collective-permute-start | bytes 1966088 | tf_op jit(solution)/shard_map/ppermute | solution.py:305
  46.7 27.7 %collective-permute-start.2 = (bf16[1280,256]{1,0:T(8,128)(2,1)}, bf16[1280,256]{1,0:T(8,128)(2,1)}, u32[]{:S(2)}, u32[]{:S(2)}) collective-permute-start(bf16[1280,256]{1,0:T(8,128)(2,1)} %get-tuple-element.21), channel_id=1, source_target_pairs={{0,16},{8,24},{16,0},{24,8},{1,17},{9,25},{17,1},{25,9},{2,18},{10... | collective-permute-start | bytes 1966088 | tf_op jit(solution)/shard_map/ppermute | solution.py:305
  53.6 24.7 %collective-permute-start.3 = (bf16[1280,256]{1,0:T(8,128)(2,1)}, bf16[1280,256]{1,0:T(8,128)(2,1)}, u32[]{:S(2)}, u32[]{:S(2)}) collective-permute-start(bf16[1280,256]{1,0:T(8,128)(2,1)} %collective-permute-done.refs_1_.refs_5_), channel_id=1, source_target_pairs={{0,1},{1,0},{2,3},{3,2},{4,5},{5,4},{6,7},{7,6},{8,9},{9,8},{10,11... | collective-permute-start | bytes 1966088 | tf_op jit(solution)/shard_map/ppermute | solution.py:306
  65.8 12.5 %collective-permute-start.4 = (bf16[1280,256]{1,0:T(8,128)(2,1)}, bf16[1280,256]{1,0:T(8,128)(2,1)}, u32[]{:S(2)}, u32[]{:S(2)}) collective-permute-start(bf16[1280,256]{1,0:T(8,128)(2,1)} %collective-permute-done.1.refs_2_.refs_6_), channel_id=1, source_target_pairs={{0,1},{1,0},{2,3},{3,2},{4,5},{5,4},{6,7},{7,6},{8,9},{9,8},{10,11... | collective-permute-start | bytes 1966088 | tf_op jit(solution)/shard_map/ppermute | solution.py:306
  74.4 5.5 %collective-permute-start.5 = (bf16[1280,256]{1,0:T(8,128)(2,1)}, bf16[1280,256]{1,0:T(8,128)(2,1)}, u32[]{:S(2)}, u32[]{:S(2)}) collective-permute-start(bf16[1280,256]{1,0:T(8,128)(2,1)} %collective-permute-done.2.refs_3_.refs_7_), channel_id=1, source_target_pairs={{0,1},{1,0},{2,3},{3,2},{4,5},{5,4},{6,7},{7,6},{8,9},{9,8},{10,11... | collective-permute-start | bytes 1966088 | tf_op jit(solution)/shard_map/ppermute | solution.py:306
  80.0 1.1 copy-start.1
  87.1 23.8 %collective-permute-start.6 = (bf16[128,1536]{1,0:T(8,128)(2,1)}, bf16[128,1536]{1,0:T(8,128)(2,1)}, u32[]{:S(2)}, u32[]{:S(2)}) collective-permute-start(bf16[128,1536]{1,0:T(8,128)(2,1)} %get-tuple-element.23), channel_id=1, source_target_pairs={{0,32},{32,64},{64,96},{96,128},{128,160},{160,192},{192,224},{224... | collective-permute-start | bytes 1179656 | tf_op jit(solution)/shard_map/ppermute | solution.py:311
  94.9 19.0 %collective-permute-start.9 = (bf16[128,1536]{1,0:T(8,128)(2,1)S(1)}, bf16[128,1536]{1,0:T(8,128)(2,1)S(1)}, u32[]{:S(2)}, u32[]{:S(2)}) collective-permute-start(bf16[128,1536]{1,0:T(8,128)(2,1)S(1)} %get-tuple-element.25), channel_id=1, source_target_pairs={{0,480},{32,0},{64,32},{96,64},{128,96},{160,128},{192,160},{224,1... | collective-permute-start | bytes 1179656 | tf_op jit(solution)/shard_map/ppermute | solution.py:312
  104.4 1.1 copy-start.2
  111.9 14.7 %collective-permute-start.7 = (bf16[64,1536]{1,0:T(8,128)(2,1)S(1)}, bf16[64,1536]{1,0:T(8,128)(2,1)S(1)}, u32[]{:S(2)}, u32[]{:S(2)}) collective-permute-start(bf16[64,1536]{1,0:T(8,128)(2,1)S(1)} %slice.61), channel_id=1, source_target_pairs={{0,64},{32,96},{64,128},{96,160},{128,192},{160,224},{192,256},{22... | collective-permute-start | bytes 589832 | tf_op jit(solution)/shard_map/ppermute | solution.py:311
  114.0 51.9 %copy-start.7 = (bf16[1,2,64,512]{3,2,1,0:T(8,128)(2,1)S(1)}, bf16[1,2,64,512]{3,2,1,0:T(8,128)(2,1)}, u32[]{:S(2)}) copy-start(bf16[1,2,64,512]{3,2,1,0:T(8,128)(2,1)} %param.15) | copy-start | bytes 393220
  114.0 51.9 %copy-start.8 = (bf16[1,2,64,512]{3,2,1,0:T(8,128)(2,1)S(1)}, bf16[1,2,64,512]{3,2,1,0:T(8,128)(2,1)}, u32[]{:S(2)}) copy-start(bf16[1,2,64,512]{3,2,1,0:T(8,128)(2,1)} %param.16) | copy-start | bytes 393220
  114.0 14.6 %collective-permute-start.10 = (bf16[64,1536]{1,0:T(8,128)(2,1)S(1)}, bf16[64,1536]{1,0:T(8,128)(2,1)S(1)}, u32[]{:S(2)}, u32[]{:S(2)}) collective-permute-start(bf16[64,1536]{1,0:T(8,128)(2,1)S(1)} %slice.60), channel_id=1, source_target_pairs={{0,448},{32,480},{64,0},{96,32},{128,64},{160,96},{192,128},{224,1... | collective-permute-start | bytes 589832 | tf_op jit(solution)/shard_map/ppermute | solution.py:312
  126.7 15.2 %collective-permute-start.8 = (bf16[32,1536]{1,0:T(8,128)(2,1)S(1)}, bf16[32,1536]{1,0:T(8,128)(2,1)S(1)}, u32[]{:S(2)}, u32[]{:S(2)}) collective-permute-start(bf16[32,1536]{1,0:T(8,128)(2,1)S(1)} %slice.63), channel_id=1, source_target_pairs={{0,128},{32,160},{64,192},{96,224},{128,256},{160,288},{192,320},{... | collective-permute-start | bytes 294920 | tf_op jit(solution)/shard_map/ppermute | solution.py:311
  128.7 13.3 %collective-permute-start.11 = (bf16[32,1536]{1,0:T(8,128)(2,1)S(1)}, bf16[32,1536]{1,0:T(8,128)(2,1)S(1)}, u32[]{:S(2)}, u32[]{:S(2)}) collective-permute-start(bf16[32,1536]{1,0:T(8,128)(2,1)S(1)} %slice.62), channel_id=1, source_target_pairs={{0,384},{32,416},{64,448},{96,480},{128,0},{160,32},{192,64},{224,... | collective-permute-start | bytes 294920 | tf_op jit(solution)/shard_map/ppermute | solution.py:312
  141.9 49.2 %copy-start.9 = (s32[96]{0:T(128)S(1)}, s32[96]{0:T(128)}, u32[]{:S(2)}) copy-start(s32[96]{0:T(128)} %param.12) | copy-start | bytes 1156
  141.9 49.4 %copy-start.5 = (f32[1,2,64,512]{3,2,1,0:T(8,128)S(1)}, f32[1,2,64,512]{3,2,1,0:T(8,128)}, u32[]{:S(2)}) copy-start(f32[1,2,64,512]{3,2,1,0:T(8,128)} %param.17) | copy-start | bytes 786436
  155.0 55.0 %copy-start.3 = (f32[1,2,64,512]{3,2,1,0:T(8,128)S(1)}, f32[1,2,64,512]{3,2,1,0:T(8,128)}, u32[]{:S(2)}) copy-start(f32[1,2,64,512]{3,2,1,0:T(8,128)} %param.13) | copy-start | bytes 786436
  156.3 35.0 %all-to-all-start = ((bf16[16,16,512]{2,1,0:T(8,128)(2,1)}), bf16[16,16,512]{2,1,0:T(8,128)(2,1)S(1)}, u32[]{:S(2)}, u32[]{:S(2)}) async-start(bf16[16,16,512]{2,1,0:T(8,128)(2,1)} %bitcast.8), calls=%async_computation | async-start | bytes 524288 | tf_op jit(solution)/shard_map/all_to_all | solution.py:336
  166.0 10.2 %collective-permute-start.13 = (bf16[2,2,64,512]{3,2,1,0:T(8,128)(2,1)S(1)}, bf16[2,2,64,512]{3,2,1,0:T(8,128)(2,1)S(1)}, u32[]{:S(2)}, u32[]{:S(2)}) collective-permute-start(bf16[2,2,64,512]{3,2,1,0:T(8,128)(2,1)S(1)} %constant_dynamic-update-slice_fusion.refs_0_), channel_id=1, source_target_pairs={{0,6},{2,0},{4,2},{6,4},{1,7},{3,1},{5,3},{7,5},{8,14},{10,8},{12,... | collective-permute-start | bytes 786440 | tf_op jit(solution)/shard_map/ppermute | solution.py:334
  170.6 9.5 %collective-permute-start.14 = (bf16[2,2,64,512]{3,2,1,0:T(8,128)(2,1)S(1)}, bf16[2,2,64,512]{3,2,1,0:T(8,128)(2,1)S(1)}, u32[]{:S(2)}, u32[]{:S(2)}) collective-permute-start(bf16[2,2,64,512]{3,2,1,0:T(8,128)(2,1)S(1)} %constant_dynamic-update-slice_fusion.refs_0_), channel_id=1, source_target_pairs={{0,2},{2,4},{4,6},{6,0},{1,3},{3,5},{5,7},{7,1},{8,10},{10,12},{12... | collective-permute-start | bytes 786440 | tf_op jit(solution)/shard_map/ppermute | solution.py:334
  172.6 11.4 %collective-permute-start.15 = (bf16[2,2,64,512]{3,2,1,0:T(8,128)(2,1)S(1)}, bf16[2,2,64,512]{3,2,1,0:T(8,128)(2,1)S(1)}, u32[]{:S(2)}, u32[]{:S(2)}) collective-permute-start(bf16[2,2,64,512]{3,2,1,0:T(8,128)(2,1)S(1)} %constant_dynamic-update-slice_fusion.refs_0_), channel_id=1, source_target_pairs={{0,4},{2,6},{4,0},{6,2},{1,5},{3,7},{5,1},{7,3},{8,12},{10,14},{12... | collective-permute-start | bytes 786440 | tf_op jit(solution)/shard_map/ppermute | solution.py:334
  185.1 23.6 %collective-permute-start.16 = (bf16[4,2,2,64,512]{4,3,2,1,0:T(8,128)(2,1)}, bf16[4,2,2,64,512]{4,3,2,1,0:T(8,128)(2,1)S(1)}, u32[]{:S(2)}, u32[]{:S(2)}) collective-permute-start(bf16[4,2,2,64,512]{4,3,2,1,0:T(8,128)(2,1)} %pad_maximum_fusion), channel_id=1, source_target_pairs={{0,1},{1,0},{2,3},{3,2},{4,5},{5,4},{6,7},{7,6},{8,9},{9,8},{10,11... | collective-permute-start | bytes 3145736 | tf_op jit(solution)/shard_map/ppermute | solution.py:335
  203.9 6.2 %collective-permute-start.12 = (bf16[4,144,512]{2,1,0:T(8,128)(2,1)S(1)}, bf16[4,144,512]{2,1,0:T(8,128)(2,1)S(1)}, u32[]{:S(2)}, u32[]{:S(2)}) collective-permute-start(bf16[4,144,512]{2,1,0:T(8,128)(2,1)S(1)} %bitcast.49), channel_id=1, source_target_pairs={{0,1},{1,0},{2,3},{3,2},{4,5},{5,4},{6,7},{7,6},{8,9},{9,8},{10,11... | collective-permute-start | bytes 1769480 | tf_op jit(solution)/shard_map/ppermute | solution.py:344
  210.1 1.0 copy-start.4

commit v3 on v2

--- a/solution.py
+++ b/solution.py
@@ -11,8 +11,9 @@
 WIDE = jnp.float32
 NZ, NX, NC = 16, 4, 2
 TILES = 6
+PREP_LIMIT = 60
 Y_STEPS = (0, 1, 3, 2)
-PARAMS = pltpu.CompilerParams(vmem_limit_bytes=16 * 1024 * 1024)
+PARAMS = pltpu.CompilerParams(vmem_limit_bytes=8 * 1024 * 1024)
 
 
 def slot_targets(owners, slot_count):
@@ -47,93 +48,93 @@
     width = out_grads.shape[1] // NX
     tile = width // TILES
 
-    def kernel(place_ref, a_ref, b_ref, after_ref, before_ref, across_ref, acts, sems, row_sems):
-        z, x, c = place_ref[0], place_ref[1], place_ref[2]
-        targets = ((after_ref, 1), (before_ref, 3), (across_ref, 2))
-        tok = pl.ds(pl.multiple_of(c * half, half), half)
-        copies = []
-        for i, (ref, step) in enumerate(targets):
-            begin = jnp.bitwise_and(x + step, NX - 1) * width
+    def kernel(place_ref, a_ref, b_ref, own_b_ref, *out_refs):
+        z, c, step = place_ref[0], place_ref[2], pl.program_id(0)
+        own_ref = out_refs[-1]
+
+        @pl.when(step == 0)
+        def _():
+            m, k = iota((small, count), 0), iota((small, count), 1)
+            block = m % part
+            row = (m // part) % per_z
+            tail = m // (part * per_z)
+            high = 2 * (tail // 4) + 4 * ((tail // 2) % 2) + 8 * (tail % 2)
+            for side in range(2):
+                values = a_ref[side * part : (side + 1) * part].reshape(count, toks)
+                for odd in range(2):
+                    dist = high + odd
+                    goal = jnp.bitwise_and(z + dist if side == 0 else z - dist, NZ - 1)
+                    pick = (block * rows + goal * per_z + row == k).astype(WIDE).astype(HALF)
+                    moved = dot(pick, values).astype(HALF)
+                    turned = jnp.concatenate([moved[:, half:], moved[:, :half]], axis=1)
+                    at = (1 - odd) * count + side * small
+                    for ref in out_refs:
+                        ref[at : at + small, :] = jnp.where(c == 1, turned, moved)
+
             for n in range(TILES):
-                at = pl.ds(pl.multiple_of(begin + n * tile, tile), tile)
-                to = pl.ds(2 * count + n * half, half)
-                copies.append(pltpu.make_async_copy(b_ref.at[tok, at], ref.at[to, :], sems.at[i, n]))
-        for copy in copies:
-            copy.start()
-        m, k = iota((small, count), 0), iota((small, count), 1)
-        block = m % part
-        row = (m // part) % per_z
-        tail = m // (part * per_z)
-        high = 2 * (tail // 4) + 4 * ((tail // 2) % 2) + 8 * (tail % 2)
-        for side in range(2):
-            values = a_ref[side * part : (side + 1) * part].reshape(count, toks)
-            for odd in range(2):
-                dist = high + odd
-                goal = jnp.bitwise_and(z + dist if side == 0 else z - dist, NZ - 1)
-                pick = (block * rows + goal * per_z + row == k).astype(WIDE).astype(HALF)
-                moved = dot(pick, values).astype(HALF)
-                turned = jnp.concatenate([moved[:, half:], moved[:, :half]], axis=1)
-                at = (1 - odd) * count + side * small
-                acts[at : at + small, :] = jnp.where(c == 1, turned, moved)
-        last = [
-            pltpu.make_async_copy(acts, ref.at[pl.ds(0, 2 * count), :], row_sems.at[i])
-            for i, (ref, _) in enumerate(targets)
-        ]
-        for copy in last:
-            copy.start()
-        for copy in copies + last:
-            copy.wait()
-
-    any_place = pl.BlockSpec(memory_space=pl.ANY)
-    return pl.pallas_call(
-        kernel,
-        out_shape=[jax.ShapeDtypeStruct((2 * count + TILES * half, toks), HALF)] * 3,
-        in_specs=[
-            pl.BlockSpec(memory_space=pltpu.SMEM),
-            pl.BlockSpec(memory_space=pltpu.VMEM),
-            any_place,
-        ],
-        out_specs=[any_place] * 3,
-        scratch_shapes=[
-            pltpu.VMEM((2 * count, toks), HALF),
-            pltpu.SemaphoreType.DMA((3, TILES)),
-            pltpu.SemaphoreType.DMA((3,)),
-        ],
-        compiler_params=pltpu.CompilerParams(vmem_limit_bytes=60 * 1024 * 1024),
-    )(place, activations, out_grads)
-
-
-def partial_products(place, own, out_grads, arrived, swapped, odd):
-    toks, tile = out_grads.shape[0], own.shape[1]
+                for side, who in enumerate((c, 1 - c)):
+                    at = 2 * count + (2 * n + side) * half
+                    tok = pl.ds(pl.multiple_of(who * half, half), half)
+                    own_ref[at : at + half, :] = own_b_ref[tok, n * tile : (n + 1) * tile]
+
+        for i, ref in enumerate(out_refs[:3]):
+
+            @pl.when(step == i)
+            def _():
+                for n in range(TILES):
+                    at = 2 * count + n * half
+                    ref[at : at + half, :] = b_ref[:, n * tile : (n + 1) * tile]
+
+    piece = (2 * count + TILES * half, toks)
+    own = (2 * count + TILES * toks, toks)
+    return pl.pallas_call(
+        kernel,
+        out_shape=[jax.ShapeDtypeStruct(shape, HALF) for shape in (piece, piece, piece, own)],
+        grid_spec=pltpu.PrefetchScalarGridSpec(
+            num_scalar_prefetch=1,
+            grid=(3,),
+            in_specs=[
+                pl.BlockSpec(activations.shape, lambda i, place_ref: (0, 0, 0)),
+                pl.BlockSpec((half, width), lambda i, place_ref: (place_ref[2], place_ref[3 + i])),
+                pl.BlockSpec((toks, width), lambda i, place_ref: (0, place_ref[1])),
+            ],
+            out_specs=[pl.BlockSpec(piece, lambda i, place_ref: (0, 0))] * 3
+            + [pl.BlockSpec(own, lambda i, place_ref: (0, 0))],
+        ),
+        compiler_params=pltpu.CompilerParams(vmem_limit_bytes=PREP_LIMIT * 1024 * 1024),
+    )(place, activations, out_grads, out_grads)
+
+
+def partial_products(own, arrived, swapped, odd):
+    toks = own.shape[1]
     half = toks // NC
-    total_rows = own.shape[0] - TILES * half
+    total_rows = own.shape[0] - TILES * toks
     count = total_rows // 2
     kind = HALF if odd else WIDE
-
-    def kernel(place_ref, *refs):
-        rows_refs, mine, other, (one_ref, two_ref) = refs[:4], refs[4:8], refs[8:12], refs[12:]
-        total = None
-        for i in range(NX):
-            term = dot(rows_refs[i][...], jnp.concatenate([mine[i][...], other[i][...]], axis=0))
-            total = term if total is None else total + term
-        one_ref[...] = total[: count // 2].astype(kind)
-        two_ref[...] = total[count // 2 :].astype(kind)
-
-    rows = pl.BlockSpec((count, tile), lambda n, place_ref: (0 if odd else 1, 0))
-    columns = pl.BlockSpec((half, tile), lambda n, place_ref: (total_rows // half + n, 0))
-    own_half = pl.BlockSpec((half, tile), lambda n, place_ref: (place_ref[2], place_ref[1] * TILES + n))
-    other_half = pl.BlockSpec((half, tile), lambda n, place_ref: (1 - place_ref[2], place_ref[1] * TILES + n))
-    return pl.pallas_call(
-        kernel,
-        out_shape=[jax.ShapeDtypeStruct((count // 2, TILES * tile), kind)] * 2,
-        grid_spec=pltpu.PrefetchScalarGridSpec(
-            num_scalar_prefetch=1,
-            grid=(TILES,),
-            in_specs=[rows] * 4 + [own_half] + [columns] * 3 + [other_half] + [columns] * 3,
-            out_specs=[pl.BlockSpec((count // 2, tile), lambda n, place_ref: (0, n))] * 2,
-        ),
+    group = 2
+
+    def kernel(*refs):
+        rows_refs, own_ref, mine, other, (one_ref, two_ref) = refs[:4], refs[4], refs[5:8], refs[8:11], refs[11:]
+        for n in range(group):
+            at = slice(n * half, (n + 1) * half)
+            total = dot(rows_refs[0][...], own_ref[n * toks : (n + 1) * toks, :])
+            for rows_ref, m_ref, o_ref in zip(rows_refs[1:], mine, other):
+                total += dot(rows_ref[...], jnp.concatenate([m_ref[at, :], o_ref[at, :]], axis=0))
+            to = slice(n * toks, (n + 1) * toks)
+            one_ref[:, to] = total[: count // 2].astype(kind)
+            two_ref[:, to] = total[count // 2 :].astype(kind)
+
+    rows = pl.BlockSpec((count, toks), lambda n: (0 if odd else 1, 0))
+    columns = pl.BlockSpec((group * half, toks), lambda n: (total_rows // (group * half) + n, 0))
+    own_columns = pl.BlockSpec((group * toks, toks), lambda n: (total_rows // (group * toks) + n, 0))
+    return pl.pallas_call(
+        kernel,
+        grid=(TILES // group,),
+        out_shape=[jax.ShapeDtypeStruct((count // 2, TILES * toks), kind)] * 2,
+        in_specs=[rows] * 4 + [own_columns] + [columns] * 6,
+        out_specs=[pl.BlockSpec((count // 2, group * toks), lambda n: (0, n))] * 2,
         compiler_params=PARAMS,
-    )(place, own, *arrived, out_grads, *arrived, out_grads, *swapped)
+    )(own, *arrived, own, *arrived, *swapped)
 
 
 def pick_blocks(chosen, sums, block_size):
@@ -300,12 +301,20 @@
     my_mp = y * NC + c
     my_rows = my_mp * rows
 
-    place = jnp.stack([z, x, c]).astype(jnp.int32)
-    pieces = prepare(activations, out_grads, place)
+    place = jnp.stack([z, x, c] + [jnp.bitwise_and(x + step, NX - 1) for step in (1, 3, 2)]).astype(jnp.int32)
+    *pieces, own = prepare(activations, out_grads, place)
     arrived = [lax.ppermute(piece, "x", ring(NX, step)) for piece, step in zip(pieces, (1, -1, 2))]
     swapped = [lax.ppermute(piece, "c", ring(NC, 1)) for piece in arrived]
-    send_a, send_b = partial_products(place, pieces[0], out_grads, arrived, swapped, True)
-    keep_a, keep_b = partial_products(place, pieces[0], out_grads, arrived, swapped, False)
+
+    first, left_root, right_root = lax.optimization_barrier((arrived[0], left_root, right_root))
+    roots = jnp.concatenate([left_root, right_root], axis=0)
+    ny = lax.axis_size("y")
+    roots_mine = [roots] + [lax.ppermute(roots, "y", ring(ny, -step)) for step in Y_STEPS[1:ny]]
+    arrived[0], *roots_mine = lax.optimization_barrier((first, *roots_mine))
+    roots_other = lax.ppermute(jnp.stack(roots_mine), "c", ring(NC, 1))
+
+    send_a, send_b = partial_products(own, arrived, swapped, True)
+    keep_a, keep_b = partial_products(own, arrived, swapped, False)
 
     for step in (1, 2, 4):
         got_a = lax.ppermute(send_a, "z", ring(NZ, step))
@@ -328,11 +337,6 @@
     chosen = (code == iota((out_rows, 1), 0)).astype(HALF)
 
     picked = pick_blocks(chosen, sums, block_size).reshape(NZ, out_rows // NZ, block_size)
-    picked, left_root, right_root = lax.optimization_barrier((picked, left_root, right_root))
-    roots = jnp.concatenate([left_root, right_root], axis=0)
-    ny = lax.axis_size("y")
-    roots_mine = [roots] + [lax.ppermute(roots, "y", ring(ny, -step)) for step in Y_STEPS[1:ny]]
-    roots_other = lax.ppermute(jnp.stack(roots_mine), "c", ring(NC, 1))
     arrived = lax.all_to_all(picked, "z", 0, 0, tiled=True).reshape(out_rows, block_size)
 
     wanted = my_owner * slots + iota((slots, block_count), 0)

time: 217 us -> 183 us (0.84)
  Pallas kernels: 57 us -> 19 us
  waiting for transfers between devices: 31.1 us -> 23.3 us
  starting transfers between devices: 93.3 us -> 97.7 us
  blocking collectives: 24 us -> 27.8 us
  local copies, waits for them, and re-layouts: 4.62 us -> 8.15 us
    pallas_call x3, Pallas kernels: 49.6 us -> 11.6 us  [the longest x2 6.5 us: partial_products(): pl.pallas_call(kernel, grid=(TILES // group,), out_shape=[jax.ShapeDtypeS...]
    ppermute x3, starting transfers between devices: 20 us -> 9.26 us  [body(): swapped = [lax.ppermute(piece, 'c', ring(NC, 1)) for piece in arrived]]
    ppermute x3, starting transfers between devices: 10.1 us -> 19.5 us  [body(): lax.ppermute(roots, 'y', ring(ny, -step))]
    ppermute x1, starting transfers between devices: 4.61 us -> 13.1 us  [body(): rows_other = lax.ppermute(rows_mine, 'c', ring(NC, 1))]
    ppermute x3, waiting for transfers between devices: 12.9 us -> 6.76 us  [body(): got_a = lax.ppermute(send_a, 'z', ring(NZ, step))]
    all_to_all x1, starting transfers between devices: 9.6 us -> 5.48 us  [body(): lax.all_to_all(picked, 'z', 0, 0, tiled=True).reshape(out_rows, block_size)]
    all_gather x1, blocking collectives: 13 us -> 17 us  [body(): sums = lax.all_gather(sums, 'x', axis=0, tiled=False)]
    ppermute x1, starting transfers between devices: 5.98 us -> 9.66 us  [body(): roots_other = lax.ppermute(jnp.stack(roots_mine), 'c', ring(NC, 1))]
  transfers between devices with their start and end apart: 18 -> 18, of which waited for: 8 -> 10; matrix products, arithmetic and copies ran while one was open for 2% -> 3% of each run, Pallas kernels for 3% -> 2%
where the time goes in v3:
time: 183 us; the launch traced here: 181 us
  starting transfers between devices  97.7 us (53%)
  blocking collectives  27.8 us (15%)
  waiting for transfers between devices  23.3 us (13%)
  Pallas kernels  19 us (10%)
  local copies, waits for them, and re-layouts  8.15 us (4%)
  other arithmetic  3.78 us (2%)
    ppermute x3, starting transfers between devices, body(): got_b = lax.ppermute(send_b, 'z', ring(NZ, -step))  21.5 us
    ppermute x3, starting transfers between devices, body(): lax.ppermute(roots, 'y', ring(ny, -step))  19.5 us
    all_gather x1, blocking collectives, body(): sums = lax.all_gather(sums, 'x', axis=0, tiled=False)  17 us
    ppermute x1, starting transfers between devices, body(): rows_other = lax.ppermute(rows_mine, 'c', ring(NC, 1))  13.1 us
    all_gather x1, blocking collectives, body(): rows_mine = lax.all_gather(own_rows, 'y', axis=0, tiled=False)  10.8 us
    ppermute x3, starting transfers between devices, body(): lax.ppermute(piece, 'x', ring(NX, step))  10.8 us
    ppermute x1, starting transfers between devices, body(): roots_other = lax.ppermute(jnp.stack(roots_mine), 'c', ring(NC, 1))  9.66 us
    ppermute x3, starting transfers between devices, body(): swapped = [lax.ppermute(piece, 'c', ring(NC, 1)) for piece in arrived]  9.26 us
  transfers between devices with their start and end apart: 18, of which 10 were waited for; matrix products, arithmetic and copies ran while one was open for 3% of the time, Pallas kernels for 2%

profile of v3, /device:TPU:1, one launch (start us, length us, event | category | flops | bytes accessed | tf_op | source)
XLA Modules:
  0.0 180.9 jit_solution(2420658021615032823)
XLA Ops:
  0.6 0.7 stack.51.place_ref
  1.3 5.1 %shard_map.120 = (bf16[1280,256]{1,0:T(8,128)(2,1)}, bf16[1280,256]{1,0:T(8,128)(2,1)}, bf16[1280,256]{1,0:T(8,128)(2,1)}, bf16[2048,256]{1,0:T(8,128)(2,1)}) custom-call(s32[6]{0:T(128)} %stack.51.place_ref, bf16[8,64,256]{2,1,0:T(8,128)(2,1)} %a_ref.1, bf16[256,6144]{1,0:T(8,128)(2,1)} %own_b_ref.1, bf16[256,6144]{1,0:T(8,128)(2,1)} %own_b_ref.1), custom_call_target="tpu_custom_call" | custom-call | tf_op jit(solution)/shard_map/pallas_call | solution.py:90
  6.5 3.9 %collective-permute-start = (bf16[1280,256]{1,0:T(8,128)(2,1)}, bf16[1280,256]{1,0:T(8,128)(2,1)S(1)}, u32[]{:S(2)}, u32[]{:S(2)}) collective-permute-start(bf16[1280,256]{1,0:T(8,128)(2,1)} %get-tuple-element.26), channel_id=1, source_target_pairs={{0,8},{8,16},{16,24},{24,0},{1,9},{9,17},{17,25},{25,1},{2,10},{10... | collective-permute-start | bytes 1966088 | tf_op jit(solution)/shard_map/ppermute | solution.py:306
  10.4 3.2 %collective-permute-start.4 = (bf16[1280,256]{1,0:T(8,128)(2,1)}, bf16[1280,256]{1,0:T(8,128)(2,1)S(1)}, u32[]{:S(2)}, u32[]{:S(2)}) collective-permute-start(bf16[1280,256]{1,0:T(8,128)(2,1)} %get-tuple-element.31), channel_id=1, source_target_pairs={{0,24},{8,0},{16,8},{24,16},{1,25},{9,1},{17,9},{25,17},{2,26},{10... | collective-permute-start | bytes 1966088 | tf_op jit(solution)/shard_map/ppermute | solution.py:306
  13.6 3.6 %collective-permute-start.5 = (bf16[1280,256]{1,0:T(8,128)(2,1)}, bf16[1280,256]{1,0:T(8,128)(2,1)S(1)}, u32[]{:S(2)}, u32[]{:S(2)}) collective-permute-start(bf16[1280,256]{1,0:T(8,128)(2,1)} %get-tuple-element.32), channel_id=1, source_target_pairs={{0,16},{8,24},{16,0},{24,8},{1,17},{9,25},{17,1},{25,9},{2,18},{10... | collective-permute-start | bytes 1966088 | tf_op jit(solution)/shard_map/ppermute | solution.py:306
  17.3 3.2 %collective-permute-done.refs_1_.refs_5_ = bf16[1280,256]{1,0:T(8,128)(2,1)S(1)} collective-permute-done((bf16[1280,256]{1,0:T(8,128)(2,1)}, bf16[1280,256]{1,0:T(8,128)(2,1)S(1)}, u32[]{:S(2)}, u32[]{:S(2)}) %collective-permute-start) | collective-permute-done | bytes 655392 | tf_op jit(solution)/shard_map/ppermute | solution.py:306
  20.5 10.6 %collective-permute-start.3 = (bf16[2,2,64,512]{3,2,1,0:T(8,128)(2,1)S(1)}, bf16[2,2,64,512]{3,2,1,0:T(8,128)(2,1)S(1)}, u32[]{:S(2)}, u32[]{:S(2)}) collective-permute-start(bf16[2,2,64,512]{3,2,1,0:T(8,128)(2,1)S(1)} %constant_dynamic-update-slice_fusion.refs_0_), channel_id=1, source_target_pairs={{0,4},{2,6},{4,0},{6,2},{1,5},{3,7},{5,1},{7,3},{8,12},{10,14},{12... | collective-permute-start | bytes 786440 | tf_op jit(solution)/shard_map/ppermute | solution.py:312
  31.3 3.9 %collective-permute-start.6 = (bf16[1280,256]{1,0:T(8,128)(2,1)S(1)}, bf16[1280,256]{1,0:T(8,128)(2,1)S(1)}, u32[]{:S(2)}, u32[]{:S(2)}) collective-permute-start(bf16[1280,256]{1,0:T(8,128)(2,1)S(1)} %collective-permute-done.refs_1_.refs_5_), channel_id=1, source_target_pairs={{0,1},{1,0},{2,3},{3,2},{4,5},{5,4},{6,7},{7,6},{8,9},{9,8},{10,11... | collective-permute-start | bytes 1966088 | tf_op jit(solution)/shard_map/ppermute | solution.py:307
  35.2 1.9 %collective-permute-start.7 = (bf16[1280,256]{1,0:T(8,128)(2,1)S(1)}, bf16[1280,256]{1,0:T(8,128)(2,1)}, u32[]{:S(2)}, u32[]{:S(2)}) collective-permute-start(bf16[1280,256]{1,0:T(8,128)(2,1)S(1)} %collective-permute-done.4.refs_2_.refs_6_), channel_id=1, source_target_pairs={{0,1},{1,0},{2,3},{3,2},{4,5},{5,4},{6,7},{7,6},{8,9},{9,8},{10,11... | collective-permute-start | bytes 1966088 | tf_op jit(solution)/shard_map/ppermute | solution.py:307
  37.1 4.1 %collective-permute-done.5.refs_3_.refs_7_ = bf16[1280,256]{1,0:T(8,128)(2,1)S(1)} collective-permute-done((bf16[1280,256]{1,0:T(8,128)(2,1)}, bf16[1280,256]{1,0:T(8,128)(2,1)S(1)}, u32[]{:S(2)}, u32[]{:S(2)}) %collective-permute-start.5) | collective-permute-done | bytes 655392 | tf_op jit(solution)/shard_map/ppermute | solution.py:306
  41.2 3.4 %collective-permute-start.8 = (bf16[1280,256]{1,0:T(8,128)(2,1)S(1)}, bf16[1280,256]{1,0:T(8,128)(2,1)}, u32[]{:S(2)}, u32[]{:S(2)}) collective-permute-start(bf16[1280,256]{1,0:T(8,128)(2,1)S(1)} %collective-permute-done.5.refs_3_.refs_7_), channel_id=1, source_target_pairs={{0,1},{1,0},{2,3},{3,2},{4,5},{5,4},{6,7},{7,6},{8,9},{9,8},{10,11... | collective-permute-start | bytes 1966088 | tf_op jit(solution)/shard_map/ppermute | solution.py:307
  45.0 5.5 %collective-permute-start.2 = (bf16[2,2,64,512]{3,2,1,0:T(8,128)(2,1)S(1)}, bf16[2,2,64,512]{3,2,1,0:T(8,128)(2,1)S(1)}, u32[]{:S(2)}, u32[]{:S(2)}) collective-permute-start(bf16[2,2,64,512]{3,2,1,0:T(8,128)(2,1)S(1)} %constant_dynamic-update-slice_fusion.refs_0_), channel_id=1, source_target_pairs={{0,2},{2,4},{4,6},{6,0},{1,3},{3,5},{5,7},{7,1},{8,10},{10,12},{12... | collective-permute-start | bytes 786440 | tf_op jit(solution)/shard_map/ppermute | solution.py:312
  50.4 3.4 %collective-permute-start.1 = (bf16[2,2,64,512]{3,2,1,0:T(8,128)(2,1)S(1)}, bf16[2,2,64,512]{3,2,1,0:T(8,128)(2,1)S(1)}, u32[]{:S(2)}, u32[]{:S(2)}) collective-permute-start(bf16[2,2,64,512]{3,2,1,0:T(8,128)(2,1)S(1)} %constant_dynamic-update-slice_fusion.refs_0_), channel_id=1, source_target_pairs={{0,6},{2,0},{4,2},{6,4},{1,7},{3,1},{5,3},{7,5},{8,14},{10,8},{12,... | collective-permute-start | bytes 786440 | tf_op jit(solution)/shard_map/ppermute | solution.py:312
  53.9 4.2 %collective-permute-done.2.refs_2_ = bf16[2,2,64,512]{3,2,1,0:T(8,128)(2,1)S(1)} collective-permute-done((bf16[2,2,64,512]{3,2,1,0:T(8,128)(2,1)S(1)}, bf16[2,2,64,512]{3,2,1,0:T(8,128)(2,1)S(1)}, u32[]{:S(2)}, u32[]{:S(2)}) %collective-permute-start.2) | collective-permute-done | bytes 262176 | tf_op jit(solution)/shard_map/ppermute | solution.py:312
  58.1 1.3 collective-permute-done.1.refs_1_
  59.4 0.9 copy-done.2
  60.3 1.2 copy-done
  61.5 1.1 copy-done.3
  62.6 3.6 %shard_map.122 = (bf16[128,1536]{1,0:T(8,128)(2,1)}, bf16[128,1536]{1,0:T(8,128)(2,1)S(1)}) custom-call(bf16[2048,256]{1,0:T(8,128)(2,1)S(1)} %copy-done, bf16[1280,256]{1,0:T(8,128)(2,1)S(1)} %collective-permute-done.refs_1_.refs_5_, bf16[1280,256]{1,0:T(8,128)(2,1)S(1)} %collective-permute-done.4.refs_2_.refs_6_, ...), custom_call_target="tpu_custom_call" | custom-call | tf_op jit(solution)/shard_map/pallas_call | solution.py:130
  66.2 0.8 copy-done.12
  67.0 3.5 %collective-permute-start.9 = (bf16[128,1536]{1,0:T(8,128)(2,1)}, bf16[128,1536]{1,0:T(8,128)(2,1)}, u32[]{:S(2)}, u32[]{:S(2)}) collective-permute-start(bf16[128,1536]{1,0:T(8,128)(2,1)} %get-tuple-element.34), channel_id=1, source_target_pairs={{0,32},{32,64},{64,96},{96,128},{128,160},{160,192},{192,224},{224... | collective-permute-start | bytes 1179656 | tf_op jit(solution)/shard_map/ppermute | solution.py:320
  70.5 0.7 add_select_fusion
  71.2 1.0 select_n.49
  72.3 9.5 %collective-permute-start.12 = (bf16[128,1536]{1,0:T(8,128)(2,1)}, bf16[128,1536]{1,0:T(8,128)(2,1)S(1)}, u32[]{:S(2)}, u32[]{:S(2)}) collective-permute-start(bf16[128,1536]{1,0:T(8,128)(2,1)} %copy-done.12), channel_id=1, source_target_pairs={{0,480},{32,0},{64,32},{96,64},{128,96},{160,128},{192,160},{224,1... | collective-permute-start | bytes 1179656 | tf_op jit(solution)/shard_map/ppermute | solution.py:321
  81.8 1.1 copy-done.4
  82.9 2.9 %shard_map.121 = (f32[128,1536]{1,0:T(8,128)S(1)}, f32[128,1536]{1,0:T(8,128)S(1)}) custom-call(bf16[2048,256]{1,0:T(8,128)(2,1)S(1)} %copy-done.1, bf16[1280,256]{1,0:T(8,128)(2,1)S(1)} %collective-permute-done.refs_1_.refs_5_, bf16[1280,256]{1,0:T(8,128)(2,1)S(1)} %collective-permute-done.4.refs_2_.refs_6_, ...), custom_call_target="tpu_custom_call" | custom-call | tf_op jit(solution)/shard_map/pallas_call | solution.py:130
  85.8 0.3 collective-permute-done.9
  86.1 1.1 convert_add_fusion.1
  87.2 1.9 %collective-permute-start.10 = (bf16[64,1536]{1,0:T(8,128)(2,1)S(1)}, bf16[64,1536]{1,0:T(8,128)(2,1)S(1)}, u32[]{:S(2)}, u32[]{:S(2)}) collective-permute-start(bf16[64,1536]{1,0:T(8,128)(2,1)S(1)} %slice.61), channel_id=1, source_target_pairs={{0,64},{32,96},{64,128},{96,160},{128,192},{160,224},{192,256},{22... | collective-permute-start | bytes 589832 | tf_op jit(solution)/shard_map/ppermute | solution.py:320
  89.3 5.6 %collective-permute-start.13 = (bf16[64,1536]{1,0:T(8,128)(2,1)S(1)}, bf16[64,1536]{1,0:T(8,128)(2,1)S(1)}, u32[]{:S(2)}, u32[]{:S(2)}) collective-permute-start(bf16[64,1536]{1,0:T(8,128)(2,1)S(1)} %slice.60), channel_id=1, source_target_pairs={{0,448},{32,480},{64,0},{96,32},{128,64},{160,96},{192,128},{224,1... | collective-permute-start | bytes 589832 | tf_op jit(solution)/shard_map/ppermute | solution.py:321
  94.9 3.4 %collective-permute-done.10 = bf16[64,1536]{1,0:T(8,128)(2,1)S(1)} collective-permute-done((bf16[64,1536]{1,0:T(8,128)(2,1)S(1)}, bf16[64,1536]{1,0:T(8,128)(2,1)S(1)}, u32[]{:S(2)}, u32[]{:S(2)}) %collective-permute-start.10) | collective-permute-done | bytes 196640 | tf_op jit(solution)/shard_map/ppermute | solution.py:320
  98.4 3.1 %collective-permute-start.11 = (bf16[32,1536]{1,0:T(8,128)(2,1)S(1)}, bf16[32,1536]{1,0:T(8,128)(2,1)S(1)}, u32[]{:S(2)}, u32[]{:S(2)}) collective-permute-start(bf16[32,1536]{1,0:T(8,128)(2,1)S(1)} %slice.63), channel_id=1, source_target_pairs={{0,128},{32,160},{64,192},{96,224},{128,256},{160,288},{192,320},{... | collective-permute-start | bytes 294920 | tf_op jit(solution)/shard_map/ppermute | solution.py:320
  101.6 6.4 %collective-permute-start.14 = (bf16[32,1536]{1,0:T(8,128)(2,1)S(1)}, bf16[32,1536]{1,0:T(8,128)(2,1)S(1)}, u32[]{:S(2)}, u32[]{:S(2)}) collective-permute-start(bf16[32,1536]{1,0:T(8,128)(2,1)S(1)} %slice.62), channel_id=1, source_target_pairs={{0,384},{32,416},{64,448},{96,480},{128,0},{160,32},{192,64},{224,... | collective-permute-start | bytes 294920 | tf_op jit(solution)/shard_map/ppermute | solution.py:321
  108.0 3.0 %collective-permute-done.11 = bf16[32,1536]{1,0:T(8,128)(2,1)S(1)} collective-permute-done((bf16[32,1536]{1,0:T(8,128)(2,1)S(1)}, bf16[32,1536]{1,0:T(8,128)(2,1)S(1)}, u32[]{:S(2)}, u32[]{:S(2)}) %collective-permute-start.11) | collective-permute-done | bytes 98336 | tf_op jit(solution)/shard_map/ppermute | solution.py:320
  111.0 0.6 collective-permute-done.14
  111.8 17.0 %all_gather.10.s_ref = bf16[4,64,1536]{2,1,0:T(8,128)(2,1)S(1)} all-gather(bf16[1,64,1536]{2,1,0:T(8,128)(2,1)S(1)} %pad_maximum_fusion.1), channel_id=1, replica_groups=mesh['z'=16,'x'=4,'y'=4,'c'=2] {'x'}, dimensions={0}, use_global_device_ids=true | all-gather | bytes 983040 | tf_op jit(solution)/shard_map/all_gather | solution.py:328
  128.7 1.3 shard_map.123
  130.0 5.5 %all-to-all-start = ((bf16[16,16,512]{2,1,0:T(8,128)(2,1)}), bf16[16,16,512]{2,1,0:T(8,128)(2,1)S(1)}, u32[]{:S(2)}, u32[]{:S(2)}) async-start(bf16[16,16,512]{2,1,0:T(8,128)(2,1)} %bitcast.11), calls=%async_computation | async-start | bytes 524288 | tf_op jit(solution)/shard_map/all_to_all | solution.py:340
  135.5 1.1 pad_maximum_fusion
  136.6 9.7 %collective-permute-start.16 = (bf16[4,2,2,64,512]{4,3,2,1,0:T(8,128)(2,1)}, bf16[4,2,2,64,512]{4,3,2,1,0:T(8,128)(2,1)S(1)}, u32[]{:S(2)}, u32[]{:S(2)}) collective-permute-start(bf16[4,2,2,64,512]{4,3,2,1,0:T(8,128)(2,1)} %pad_maximum_fusion), channel_id=1, source_target_pairs={{0,1},{1,0},{2,3},{3,2},{4,5},{5,4},{6,7},{7,6},{8,9},{9,8},{10,11... | collective-permute-start | bytes 3145736 | tf_op jit(solution)/shard_map/ppermute | solution.py:314
  146.5 1.8 all-to-all-done
  148.3 1.5 shard_map.124
  149.8 10.8 %all-gather = bf16[576,512]{1,0:T(8,128)(2,1)S(1)} all-gather(bf16[144,512]{1,0:T(8,128)(2,1)S(1)} %get-tuple-element.37), channel_id=2, replica_groups=mesh['z'=16,'x'=4,'y'=4,'c'=2] {'y'}, dimensions={0}, use_global_device_ids=true | all-gather | bytes 737280 | tf_op jit(solution)/shard_map/all_gather | solution.py:347
  160.6 13.1 %collective-permute-start.15 = (bf16[4,144,512]{2,1,0:T(8,128)(2,1)S(1)}, bf16[4,144,512]{2,1,0:T(8,128)(2,1)S(1)}, u32[]{:S(2)}, u32[]{:S(2)}) collective-permute-start(bf16[4,144,512]{2,1,0:T(8,128)(2,1)S(1)} %bitcast.52), channel_id=1, source_target_pairs={{0,1},{1,0},{2,3},{3,2},{4,5},{5,4},{6,7},{7,6},{8,9},{9,8},{10,11... | collective-permute-start | bytes 1769480 | tf_op jit(solution)/shard_map/ppermute | solution.py:348
  173.7 0.2 compare_reduce_fusion
  174.0 1.3 collective-permute-done.15.o_ref
  175.3 0.9 copy-done.10
  176.3 4.6 %shard_map.125 = (f32[2,64,512]{2,1,0:T(8,128)}, f32[2,64,512]{2,1,0:T(8,128)}, bf16[2,512,512]{2,1,0:T(8,128)(2,1)}) custom-call(s32[7]{0:T(128)S(1)} %concatenate.21.f_ref, bf16[4,144,512]{2,1,0:T(8,128)(2,1)S(1)} %bitcast.53, bf16[4,144,512]{2,1,0:T(8,128)(2,1)S(1)} %collective-permute-done.15.o_ref, ...), custom_call_target="tpu_custom_call" | custom-call | tf_op jit(solution)/shard_map/pallas_call | solution.py:264
  (62 shorter events, 1.3 us)
Async XLA Ops:
  1.3 19.1 %copy-start.13 = (bf16[1,2,64,512]{3,2,1,0:T(8,128)(2,1)S(1)}, bf16[1,2,64,512]{3,2,1,0:T(8,128)(2,1)}, u32[]{:S(2)}) copy-start(bf16[1,2,64,512]{3,2,1,0:T(8,128)(2,1)} %param.15) | copy-start | bytes 393220
  1.3 19.1 %copy-start.14 = (bf16[1,2,64,512]{3,2,1,0:T(8,128)(2,1)S(1)}, bf16[1,2,64,512]{3,2,1,0:T(8,128)(2,1)}, u32[]{:S(2)}) copy-start(bf16[1,2,64,512]{3,2,1,0:T(8,128)(2,1)} %param.16) | copy-start | bytes 393220
  1.3 29.8 %copy-start.16 = (s32[96]{0:T(128)S(1)}, s32[96]{0:T(128)}, u32[]{:S(2)}) copy-start(s32[96]{0:T(128)} %param.11) | copy-start | bytes 1156
  6.5 13.9 %collective-permute-start = (bf16[1280,256]{1,0:T(8,128)(2,1)}, bf16[1280,256]{1,0:T(8,128)(2,1)S(1)}, u32[]{:S(2)}, u32[]{:S(2)}) collective-permute-start(bf16[1280,256]{1,0:T(8,128)(2,1)} %get-tuple-element.26), channel_id=1, source_target_pairs={{0,8},{8,16},{16,24},{24,0},{1,9},{9,17},{17,25},{25,1},{2,10},{10... | collective-permute-start | bytes 1966088 | tf_op jit(solution)/shard_map/ppermute | solution.py:306
  10.4 24.8 %collective-permute-start.4 = (bf16[1280,256]{1,0:T(8,128)(2,1)}, bf16[1280,256]{1,0:T(8,128)(2,1)S(1)}, u32[]{:S(2)}, u32[]{:S(2)}) collective-permute-start(bf16[1280,256]{1,0:T(8,128)(2,1)} %get-tuple-element.31), channel_id=1, source_target_pairs={{0,24},{8,0},{16,8},{24,16},{1,25},{9,1},{17,9},{25,17},{2,26},{10... | collective-permute-start | bytes 1966088 | tf_op jit(solution)/shard_map/ppermute | solution.py:306
  13.6 27.6 %collective-permute-start.5 = (bf16[1280,256]{1,0:T(8,128)(2,1)}, bf16[1280,256]{1,0:T(8,128)(2,1)S(1)}, u32[]{:S(2)}, u32[]{:S(2)}) collective-permute-start(bf16[1280,256]{1,0:T(8,128)(2,1)} %get-tuple-element.32), channel_id=1, source_target_pairs={{0,16},{8,24},{16,0},{24,8},{1,17},{9,25},{17,1},{25,9},{2,18},{10... | collective-permute-start | bytes 1966088 | tf_op jit(solution)/shard_map/ppermute | solution.py:306
  20.5 30.0 %collective-permute-start.3 = (bf16[2,2,64,512]{3,2,1,0:T(8,128)(2,1)S(1)}, bf16[2,2,64,512]{3,2,1,0:T(8,128)(2,1)S(1)}, u32[]{:S(2)}, u32[]{:S(2)}) collective-permute-start(bf16[2,2,64,512]{3,2,1,0:T(8,128)(2,1)S(1)} %constant_dynamic-update-slice_fusion.refs_0_), channel_id=1, source_target_pairs={{0,4},{2,6},{4,0},{6,2},{1,5},{3,7},{5,1},{7,3},{8,12},{10,14},{12... | collective-permute-start | bytes 786440 | tf_op jit(solution)/shard_map/ppermute | solution.py:312
  31.3 28.1 %collective-permute-start.6 = (bf16[1280,256]{1,0:T(8,128)(2,1)S(1)}, bf16[1280,256]{1,0:T(8,128)(2,1)S(1)}, u32[]{:S(2)}, u32[]{:S(2)}) collective-permute-start(bf16[1280,256]{1,0:T(8,128)(2,1)S(1)} %collective-permute-done.refs_1_.refs_5_), channel_id=1, source_target_pairs={{0,1},{1,0},{2,3},{3,2},{4,5},{5,4},{6,7},{7,6},{8,9},{9,8},{10,11... | collective-permute-start | bytes 1966088 | tf_op jit(solution)/shard_map/ppermute | solution.py:307
  35.2 25.1 %collective-permute-start.7 = (bf16[1280,256]{1,0:T(8,128)(2,1)S(1)}, bf16[1280,256]{1,0:T(8,128)(2,1)}, u32[]{:S(2)}, u32[]{:S(2)}) collective-permute-start(bf16[1280,256]{1,0:T(8,128)(2,1)S(1)} %collective-permute-done.4.refs_2_.refs_6_), channel_id=1, source_target_pairs={{0,1},{1,0},{2,3},{3,2},{4,5},{5,4},{6,7},{7,6},{8,9},{9,8},{10,11... | collective-permute-start | bytes 1966088 | tf_op jit(solution)/shard_map/ppermute | solution.py:307
  41.2 19.0 %collective-permute-start.8 = (bf16[1280,256]{1,0:T(8,128)(2,1)S(1)}, bf16[1280,256]{1,0:T(8,128)(2,1)}, u32[]{:S(2)}, u32[]{:S(2)}) collective-permute-start(bf16[1280,256]{1,0:T(8,128)(2,1)S(1)} %collective-permute-done.5.refs_3_.refs_7_), channel_id=1, source_target_pairs={{0,1},{1,0},{2,3},{3,2},{4,5},{5,4},{6,7},{7,6},{8,9},{9,8},{10,11... | collective-permute-start | bytes 1966088 | tf_op jit(solution)/shard_map/ppermute | solution.py:307
  45.0 13.1 %collective-permute-start.2 = (bf16[2,2,64,512]{3,2,1,0:T(8,128)(2,1)S(1)}, bf16[2,2,64,512]{3,2,1,0:T(8,128)(2,1)S(1)}, u32[]{:S(2)}, u32[]{:S(2)}) collective-permute-start(bf16[2,2,64,512]{3,2,1,0:T(8,128)(2,1)S(1)} %constant_dynamic-update-slice_fusion.refs_0_), channel_id=1, source_target_pairs={{0,2},{2,4},{4,6},{6,0},{1,3},{3,5},{5,7},{7,1},{8,10},{10,12},{12... | collective-permute-start | bytes 786440 | tf_op jit(solution)/shard_map/ppermute | solution.py:312
  50.4 8.9 %collective-permute-start.1 = (bf16[2,2,64,512]{3,2,1,0:T(8,128)(2,1)S(1)}, bf16[2,2,64,512]{3,2,1,0:T(8,128)(2,1)S(1)}, u32[]{:S(2)}, u32[]{:S(2)}) collective-permute-start(bf16[2,2,64,512]{3,2,1,0:T(8,128)(2,1)S(1)} %constant_dynamic-update-slice_fusion.refs_0_), channel_id=1, source_target_pairs={{0,6},{2,0},{4,2},{6,4},{1,7},{3,1},{5,3},{7,5},{8,14},{10,8},{12,... | collective-permute-start | bytes 786440 | tf_op jit(solution)/shard_map/ppermute | solution.py:312
  58.1 2.2 %copy-start.5 = (bf16[2,2,64,512]{3,2,1,0:T(8,128)(2,1)}, bf16[2,2,64,512]{3,2,1,0:T(8,128)(2,1)S(1)}, u32[]{:S(2)}) copy-start(bf16[2,2,64,512]{3,2,1,0:T(8,128)(2,1)S(1)} %collective-permute-done.2.refs_2_) | copy-start | bytes 786436
  59.4 6.8 %copy-start.7 = (bf16[2,2,64,512]{3,2,1,0:T(8,128)(2,1)}, bf16[2,2,64,512]{3,2,1,0:T(8,128)(2,1)S(1)}, u32[]{:S(2)}) copy-start(bf16[2,2,64,512]{3,2,1,0:T(8,128)(2,1)S(1)} %collective-permute-done.1.refs_1_) | copy-start | bytes 786436
  59.4 0.9 copy-start.2
  60.3 1.2 copy-start
  61.5 1.1 copy-start.3
  62.6 19.2 %copy-start.1 = (bf16[2048,256]{1,0:T(8,128)(2,1)S(1)}, bf16[2048,256]{1,0:T(8,128)(2,1)}, u32[]{:S(2)}) copy-start(bf16[2048,256]{1,0:T(8,128)(2,1)} %get-tuple-element.25.refs_0_.refs_4_) | copy-start | bytes 3145732
  66.2 0.8 copy-start.12
  67.0 19.2 %collective-permute-start.9 = (bf16[128,1536]{1,0:T(8,128)(2,1)}, bf16[128,1536]{1,0:T(8,128)(2,1)}, u32[]{:S(2)}, u32[]{:S(2)}) collective-permute-start(bf16[128,1536]{1,0:T(8,128)(2,1)} %get-tuple-element.34), channel_id=1, source_target_pairs={{0,32},{32,64},{64,96},{96,128},{128,160},{160,192},{192,224},{224... | collective-permute-start | bytes 1179656 | tf_op jit(solution)/shard_map/ppermute | solution.py:320
  72.3 16.9 %collective-permute-start.12 = (bf16[128,1536]{1,0:T(8,128)(2,1)}, bf16[128,1536]{1,0:T(8,128)(2,1)S(1)}, u32[]{:S(2)}, u32[]{:S(2)}) collective-permute-start(bf16[128,1536]{1,0:T(8,128)(2,1)} %copy-done.12), channel_id=1, source_target_pairs={{0,480},{32,0},{64,32},{96,64},{128,96},{160,128},{192,160},{224,1... | collective-permute-start | bytes 1179656 | tf_op jit(solution)/shard_map/ppermute | solution.py:321
  81.8 1.1 copy-start.4
  87.2 11.1 %collective-permute-start.10 = (bf16[64,1536]{1,0:T(8,128)(2,1)S(1)}, bf16[64,1536]{1,0:T(8,128)(2,1)S(1)}, u32[]{:S(2)}, u32[]{:S(2)}) collective-permute-start(bf16[64,1536]{1,0:T(8,128)(2,1)S(1)} %slice.61), channel_id=1, source_target_pairs={{0,64},{32,96},{64,128},{96,160},{128,192},{160,224},{192,256},{22... | collective-permute-start | bytes 589832 | tf_op jit(solution)/shard_map/ppermute | solution.py:320
  89.3 46.2 %copy-start.6 = (bf16[2,2,64,512]{3,2,1,0:T(8,128)(2,1)S(1)}, bf16[2,2,64,512]{3,2,1,0:T(8,128)(2,1)}, u32[]{:S(2)}) copy-start(bf16[2,2,64,512]{3,2,1,0:T(8,128)(2,1)} %copy-done.5) | copy-start | bytes 786436
  89.3 46.2 %copy-start.8 = (bf16[2,2,64,512]{3,2,1,0:T(8,128)(2,1)S(1)}, bf16[2,2,64,512]{3,2,1,0:T(8,128)(2,1)}, u32[]{:S(2)}) copy-start(bf16[2,2,64,512]{3,2,1,0:T(8,128)(2,1)} %copy-done.7) | copy-start | bytes 786436
  89.3 12.2 %collective-permute-start.13 = (bf16[64,1536]{1,0:T(8,128)(2,1)S(1)}, bf16[64,1536]{1,0:T(8,128)(2,1)S(1)}, u32[]{:S(2)}, u32[]{:S(2)}) collective-permute-start(bf16[64,1536]{1,0:T(8,128)(2,1)S(1)} %slice.60), channel_id=1, source_target_pairs={{0,448},{32,480},{64,0},{96,32},{128,64},{160,96},{192,128},{224,1... | collective-permute-start | bytes 589832 | tf_op jit(solution)/shard_map/ppermute | solution.py:321
  98.4 12.6 %collective-permute-start.11 = (bf16[32,1536]{1,0:T(8,128)(2,1)S(1)}, bf16[32,1536]{1,0:T(8,128)(2,1)S(1)}, u32[]{:S(2)}, u32[]{:S(2)}) collective-permute-start(bf16[32,1536]{1,0:T(8,128)(2,1)S(1)} %slice.63), channel_id=1, source_target_pairs={{0,128},{32,160},{64,192},{96,224},{128,256},{160,288},{192,320},{... | collective-permute-start | bytes 294920 | tf_op jit(solution)/shard_map/ppermute | solution.py:320
  101.6 44.7 %copy-start.15 = (s32[96]{0:T(128)S(1)}, s32[96]{0:T(128)}, u32[]{:S(2)}) copy-start(s32[96]{0:T(128)} %param.12) | copy-start | bytes 1156
  101.6 46.7 %copy-start.11 = (f32[1,2,64,512]{3,2,1,0:T(8,128)S(1)}, f32[1,2,64,512]{3,2,1,0:T(8,128)}, u32[]{:S(2)}) copy-start(f32[1,2,64,512]{3,2,1,0:T(8,128)} %param.17) | copy-start | bytes 786436
  101.6 10.1 %collective-permute-start.14 = (bf16[32,1536]{1,0:T(8,128)(2,1)S(1)}, bf16[32,1536]{1,0:T(8,128)(2,1)S(1)}, u32[]{:S(2)}, u32[]{:S(2)}) collective-permute-start(bf16[32,1536]{1,0:T(8,128)(2,1)S(1)} %slice.62), channel_id=1, source_target_pairs={{0,384},{32,416},{64,448},{96,480},{128,0},{160,32},{192,64},{224,... | collective-permute-start | bytes 294920 | tf_op jit(solution)/shard_map/ppermute | solution.py:321
  111.7 63.6 %copy-start.9 = (f32[1,2,64,512]{3,2,1,0:T(8,128)S(1)}, f32[1,2,64,512]{3,2,1,0:T(8,128)}, u32[]{:S(2)}) copy-start(f32[1,2,64,512]{3,2,1,0:T(8,128)} %param.13) | copy-start | bytes 786436
  130.0 18.3 %all-to-all-start = ((bf16[16,16,512]{2,1,0:T(8,128)(2,1)}), bf16[16,16,512]{2,1,0:T(8,128)(2,1)S(1)}, u32[]{:S(2)}, u32[]{:S(2)}) async-start(bf16[16,16,512]{2,1,0:T(8,128)(2,1)} %bitcast.11), calls=%async_computation | async-start | bytes 524288 | tf_op jit(solution)/shard_map/all_to_all | solution.py:340
  136.6 37.4 %collective-permute-start.16 = (bf16[4,2,2,64,512]{4,3,2,1,0:T(8,128)(2,1)}, bf16[4,2,2,64,512]{4,3,2,1,0:T(8,128)(2,1)S(1)}, u32[]{:S(2)}, u32[]{:S(2)}) collective-permute-start(bf16[4,2,2,64,512]{4,3,2,1,0:T(8,128)(2,1)} %pad_maximum_fusion), channel_id=1, source_target_pairs={{0,1},{1,0},{2,3},{3,2},{4,5},{5,4},{6,7},{7,6},{8,9},{9,8},{10,11... | collective-permute-start | bytes 3145736 | tf_op jit(solution)/shard_map/ppermute | solution.py:314
  160.6 14.7 %collective-permute-start.15 = (bf16[4,144,512]{2,1,0:T(8,128)(2,1)S(1)}, bf16[4,144,512]{2,1,0:T(8,128)(2,1)S(1)}, u32[]{:S(2)}, u32[]{:S(2)}) collective-permute-start(bf16[4,144,512]{2,1,0:T(8,128)(2,1)S(1)} %bitcast.52), channel_id=1, source_target_pairs={{0,1},{1,0},{2,3},{3,2},{4,5},{5,4},{6,7},{7,6},{8,9},{9,8},{10,11... | collective-permute-start | bytes 1769480 | tf_op jit(solution)/shard_map/ppermute | solution.py:348
  175.3 1.0 copy-start.10

commit v4 on v3

--- a/solution.py
+++ b/solution.py
@@ -11,8 +11,7 @@
 WIDE = jnp.float32
 NZ, NX, NC = 16, 4, 2
 TILES = 6
-PREP_LIMIT = 60
-Y_STEPS = (0, 1, 3, 2)
+ROOMY = pltpu.CompilerParams(vmem_limit_bytes=60 * 1024 * 1024)
 PARAMS = pltpu.CompilerParams(vmem_limit_bytes=8 * 1024 * 1024)
 
 
@@ -48,9 +47,8 @@
     width = out_grads.shape[1] // NX
     tile = width // TILES
 
-    def kernel(place_ref, a_ref, b_ref, own_b_ref, *out_refs):
+    def kernel(place_ref, a_ref, b_ref, *out_refs):
         z, c, step = place_ref[0], place_ref[2], pl.program_id(0)
-        own_ref = out_refs[-1]
 
         @pl.when(step == 0)
         def _():
@@ -71,13 +69,7 @@
                     for ref in out_refs:
                         ref[at : at + small, :] = jnp.where(c == 1, turned, moved)
 
-            for n in range(TILES):
-                for side, who in enumerate((c, 1 - c)):
-                    at = 2 * count + (2 * n + side) * half
-                    tok = pl.ds(pl.multiple_of(who * half, half), half)
-                    own_ref[at : at + half, :] = own_b_ref[tok, n * tile : (n + 1) * tile]
-
-        for i, ref in enumerate(out_refs[:3]):
+        for i, ref in enumerate(out_refs):
 
             @pl.when(step == i)
             def _():
@@ -86,23 +78,53 @@
                     ref[at : at + half, :] = b_ref[:, n * tile : (n + 1) * tile]
 
     piece = (2 * count + TILES * half, toks)
-    own = (2 * count + TILES * toks, toks)
-    return pl.pallas_call(
-        kernel,
-        out_shape=[jax.ShapeDtypeStruct(shape, HALF) for shape in (piece, piece, piece, own)],
+    return pl.pallas_call(
+        kernel,
+        out_shape=[jax.ShapeDtypeStruct(piece, HALF)] * 3,
         grid_spec=pltpu.PrefetchScalarGridSpec(
             num_scalar_prefetch=1,
             grid=(3,),
             in_specs=[
                 pl.BlockSpec(activations.shape, lambda i, place_ref: (0, 0, 0)),
                 pl.BlockSpec((half, width), lambda i, place_ref: (place_ref[2], place_ref[3 + i])),
+            ],
+            out_specs=[pl.BlockSpec(piece, lambda i, place_ref: (0, 0))] * 3,
+        ),
+        compiler_params=ROOMY,
+    )(place, activations, out_grads)
+
+
+def own_part(piece, out_grads, place):
+    toks = out_grads.shape[0]
+    half = toks // NC
+    width = out_grads.shape[1] // NX
+    tile = width // TILES
+    count = piece.shape[0] - TILES * half
+
+    def kernel(place_ref, p_ref, b_ref, o_ref):
+        c = place_ref[2]
+        o_ref[:count, :] = p_ref[...]
+        for n in range(TILES):
+            for side, who in enumerate((c, 1 - c)):
+                at = count + (2 * n + side) * half
+                tok = pl.ds(pl.multiple_of(who * half, half), half)
+                o_ref[at : at + half, :] = b_ref[tok, n * tile : (n + 1) * tile]
+
+    own = (count + TILES * toks, tile)
+    return pl.pallas_call(
+        kernel,
+        out_shape=jax.ShapeDtypeStruct(own, HALF),
+        grid_spec=pltpu.PrefetchScalarGridSpec(
+            num_scalar_prefetch=1,
+            grid=(1,),
+            in_specs=[
+                pl.BlockSpec((count, tile), lambda i, place_ref: (0, 0)),
                 pl.BlockSpec((toks, width), lambda i, place_ref: (0, place_ref[1])),
             ],
-            out_specs=[pl.BlockSpec(piece, lambda i, place_ref: (0, 0))] * 3
-            + [pl.BlockSpec(own, lambda i, place_ref: (0, 0))],
+            out_specs=pl.BlockSpec(own, lambda i, place_ref: (0, 0)),
         ),
-        compiler_params=pltpu.CompilerParams(vmem_limit_bytes=PREP_LIMIT * 1024 * 1024),
-    )(place, activations, out_grads, out_grads)
+        compiler_params=ROOMY,
+    )(place, piece, out_grads)
 
 
 def partial_products(own, arrived, swapped, odd):
@@ -220,18 +242,17 @@
     slots, rows, block_size = left_stat.shape
     all_rows = mine.shape[1]
 
-    def kernel(f_ref, m_ref, o_ref, *refs):
-        root_refs, (t_ref, ls_ref, rs_ref, ln_ref, rn_ref, d_ref, roots) = refs[:ny], refs[ny:]
+    def kernel(f_ref, m_ref, o_ref, rm_ref, ro_ref, ls_ref, rs_ref, ln_ref, rn_ref, d_ref, roots):
         s = pl.program_id(0)
         core, own_y, own_mp = f_ref[0], f_ref[1], f_ref[2]
         live, taken = f_ref[3 + s], f_ref[5 + s]
         at = pl.ds(pl.multiple_of(s * rows, rows), rows)
-        for i, step in enumerate(Y_STEPS[:ny]):
-            source = lax.rem(own_y + step, ny) * NC
-            for ref, who in ((root_refs[i], core), (t_ref.at[i], 1 - core)):
+        for i in range(ny):
+            source = jnp.bitwise_xor(own_y, i) * NC
+            for ref, who in ((rm_ref, core), (ro_ref, 1 - core)):
                 to = pl.ds(pl.multiple_of((source + who) * rows, rows), rows)
                 for kind in range(2):
-                    roots[kind, to, :] = ref[kind, 0]
+                    roots[kind, to, :] = ref[i, kind, 0]
         parts = []
         norm = jnp.zeros((1, 1), WIDE)
         tail_row = iota((16, block_size), 0) == s
@@ -270,12 +291,12 @@
             jax.ShapeDtypeStruct((slots, block_size, block_size), HALF),
         ],
         in_specs=[pl.BlockSpec(memory_space=pltpu.SMEM), whole, whole]
-        + [pl.BlockSpec((2, 1, rows, block_size), lambda s: (0, s, 0, 0))] * ny
-        + [pl.BlockSpec((ny, 2, 1, rows, block_size), lambda s: (0, 0, s, 0, 0)), strip, strip],
+        + [pl.BlockSpec((ny, 2, 1, rows, block_size), lambda s: (0, 0, s, 0, 0))] * 2
+        + [strip, strip],
         out_specs=[strip, strip, square],
         scratch_shapes=[pltpu.VMEM((2, block_size, block_size), HALF)],
         compiler_params=PARAMS,
-    )(facts, mine, other, *roots_mine, roots_other, left_stat, right_stat)
+    )(facts, mine, other, roots_mine, roots_other, left_stat, right_stat)
 
 
 def body(
@@ -302,30 +323,18 @@
     my_rows = my_mp * rows
 
     place = jnp.stack([z, x, c] + [jnp.bitwise_and(x + step, NX - 1) for step in (1, 3, 2)]).astype(jnp.int32)
-    *pieces, own = prepare(activations, out_grads, place)
+    pieces = prepare(activations, out_grads, place)
     arrived = [lax.ppermute(piece, "x", ring(NX, step)) for piece, step in zip(pieces, (1, -1, 2))]
+    own = own_part(pieces[0], out_grads, place)
     swapped = [lax.ppermute(piece, "c", ring(NC, 1)) for piece in arrived]
 
-    first, left_root, right_root = lax.optimization_barrier((arrived[0], left_root, right_root))
-    roots = jnp.concatenate([left_root, right_root], axis=0)
+    own, left_root, right_root = lax.optimization_barrier((own, left_root, right_root))
     ny = lax.axis_size("y")
-    roots_mine = [roots] + [lax.ppermute(roots, "y", ring(ny, -step)) for step in Y_STEPS[1:ny]]
-    arrived[0], *roots_mine = lax.optimization_barrier((first, *roots_mine))
-    roots_other = lax.ppermute(jnp.stack(roots_mine), "c", ring(NC, 1))
-
-    send_a, send_b = partial_products(own, arrived, swapped, True)
-    keep_a, keep_b = partial_products(own, arrived, swapped, False)
-
-    for step in (1, 2, 4):
-        got_a = lax.ppermute(send_a, "z", ring(NZ, step))
-        got_b = lax.ppermute(send_b, "z", ring(NZ, -step))
-        keep_a, keep_b = keep_a + got_a, keep_b + got_b
-        if step < 4:
-            part = keep_a.shape[0] // 2
-            send_a, send_b = keep_a[part:].astype(HALF), keep_b[part:].astype(HALF)
-            keep_a, keep_b = keep_a[:part], keep_b[:part]
-    sums = jnp.concatenate([keep_a, keep_b], axis=0).astype(HALF)
-    sums = lax.all_gather(sums, "x", axis=0, tiled=False)
+    roots = jnp.stack([left_root[0], right_root[0]])[None]
+    for step in (1, 2):
+        if step < ny:
+            roots_from = lax.ppermute(roots, "y", [(i, i ^ step) for i in range(ny)])
+            roots = jnp.concatenate([roots, roots_from], axis=0)
 
     targets = slot_targets(owners, slots)
     by_block = targets.reshape(2, half_rows, NX, columns).transpose(2, 3, 0, 1)[:, :, :, None, None, :]
@@ -335,6 +344,27 @@
     code = jnp.where(owner % NX == x, code, -1).reshape(1, -1)
     out_rows = NZ * slots * 2 * per_z
     chosen = (code == iota((out_rows, 1), 0)).astype(HALF)
+    own, roots, chosen = lax.optimization_barrier((own, roots, chosen))
+    roots_other = lax.ppermute(roots, "c", ring(NC, 1))
+
+    sent = partial_products(own, arrived, swapped, True)
+    kept = partial_products(own, arrived, swapped, False)
+
+    sums = []
+    for way, out, keep in ((1, sent[0], kept[0]), (-1, sent[1], kept[1])):
+        got = [lax.ppermute(out, "z", ring(NZ, way))]
+        for step in (2, 4):
+            part = got[-1].shape[0] // 2
+            out = keep[part : 2 * part]
+            for rows_in in got:
+                out = out + rows_in[part : 2 * part]
+            got.append(lax.ppermute(out.astype(HALF), "z", ring(NZ, way * step)))
+        part = got[-1].shape[0]
+        total = keep[:part]
+        for rows_in in got:
+            total = total + rows_in[:part]
+        sums.append(total.astype(HALF))
+    sums = lax.all_gather(jnp.concatenate(sums, axis=0), "x", axis=0, tiled=False)
 
     picked = pick_blocks(chosen, sums, block_size).reshape(NZ, out_rows // NZ, block_size)
     arrived = lax.all_to_all(picked, "z", 0, 0, tiled=True).reshape(out_rows, block_size)
@@ -348,7 +378,7 @@
     rows_other = lax.ppermute(rows_mine, "c", ring(NC, 1))
     facts = jnp.concatenate([jnp.stack([c, y, my_mp]).astype(jnp.int32), live_mine, occupied])
     left_next, right_next, directions = update(
-        facts, rows_mine, rows_other, roots_mine, roots_other, left_stat[0], right_stat[0]
+        facts, rows_mine, rows_other, roots, roots_other, left_stat[0], right_stat[0]
     )
     return (left_next[None], right_next[None], acc_next[None], directions[None])
 

time: 183 us -> 173 us (0.945)
  starting transfers between devices: 97.7 us -> 87.1 us
  waiting for transfers between devices: 23.3 us -> 31.8 us
  blocking collectives: 27.8 us -> 22.7 us
  local copies, waits for them, and re-layouts: 8.15 us -> 4.31 us
    ppermute x10 -> x9, starting transfers between devices: 59.2 us -> 44.7 us  [the longest x4 16.8 us: body(): got.append(lax.ppermute(out.astype(HALF), 'z', ring(NZ, way * step)))]
    ppermute x10 -> x9, waiting for transfers between devices: 12.9 us -> 22.6 us  [the longest x4 15.8 us: body(): got.append(lax.ppermute(out.astype(HALF), 'z', ring(NZ, way * step)))]
    ppermute x3, waiting for transfers between devices: 7.29 us -> 1.29 us  [body(): lax.ppermute(piece, 'x', ring(NX, step))]
    unnamed x35 -> x18, local copies, waits for them, and re-layouts: 6.02 us -> 0.99 us
    all_to_all x1, waiting for transfers between devices: 1.76 us -> 6.59 us  [body(): lax.all_to_all(picked, 'z', 0, 0, tiled=True).reshape(out_rows, block_size)]
    all_gather x1, blocking collectives: 17 us -> 12.2 us  [body(): lax.all_gather(jnp.concatenate(sums, axis=0), 'x', axis=0, tiled=False)]
    ppermute x3, starting transfers between devices: 9.26 us -> 13.5 us  [body(): swapped = [lax.ppermute(piece, 'c', ring(NC, 1)) for piece in arrived]]
    concatenate x3, other arithmetic: 0.06 us -> 3 us  [the longest x2 2.98 us: body(): roots = jnp.concatenate([roots, roots_from], axis=0)]
  transfers between devices with their start and end apart: 18 -> 17, of which waited for: 10 -> 8; matrix products, arithmetic and copies ran while one was open for 3% -> 4% of each run, Pallas kernels for 2% -> 4%
where the time goes in v4:
time: 173 us; the launch traced here: 172 us
  starting transfers between devices  87.1 us (50%)
  waiting for transfers between devices  31.8 us (18%)
  blocking collectives  22.7 us (13%)
  Pallas kernels  20.7 us (12%)
  other arithmetic  4.65 us (3%)
  local copies, waits for them, and re-layouts  4.31 us (2%)
    ppermute x4, starting transfers between devices, body(): got.append(lax.ppermute(out.astype(HALF), 'z', ring(NZ, way * step)))  16.8 us
    ppermute x4, waiting for transfers between devices, body(): got.append(lax.ppermute(out.astype(HALF), 'z', ring(NZ, way * step)))  15.8 us
    ppermute x3, starting transfers between devices, body(): swapped = [lax.ppermute(piece, 'c', ring(NC, 1)) for piece in arrived]  13.5 us
    ppermute x2, starting transfers between devices, body(): got = [lax.ppermute(out, 'z', ring(NZ, way))]  13 us
    ppermute x1, starting transfers between devices, body(): rows_other = lax.ppermute(rows_mine, 'c', ring(NC, 1))  12.6 us
    all_gather x1, blocking collectives, body(): lax.all_gather(jnp.concatenate(sums, axis=0), 'x', axis=0, tiled=False)  12.2 us
    all_gather x1, blocking collectives, body(): rows_mine = lax.all_gather(own_rows, 'y', axis=0, tiled=False)  10.6 us
    ppermute x3, starting transfers between devices, body(): lax.ppermute(piece, 'x', ring(NX, step))  10.3 us
  transfers between devices with their start and end apart: 17, of which 8 were waited for; matrix products, arithmetic and copies ran while one was open for 4% of the time, Pallas kernels for 4%

profile of v4, /device:TPU:1, one launch (start us, length us, event | category | flops | bytes accessed | tf_op | source)
XLA Modules:
  0.0 172.3 jit_solution(1033172387776229781)
XLA Ops:
  0.6 0.6 stack.39.place_ref
  1.3 4.4 %shard_map.120 = (bf16[1280,256]{1,0:T(8,128)(2,1)}, bf16[1280,256]{1,0:T(8,128)(2,1)}, bf16[1280,256]{1,0:T(8,128)(2,1)}) custom-call(s32[6]{0:T(128)} %stack.39.place_ref, bf16[8,64,256]{2,1,0:T(8,128)(2,1)} %a_ref.1, bf16[256,6144]{1,0:T(8,128)(2,1)} %b_ref.3), custom_call_target="tpu_custom_call" | custom-call | tf_op jit(solution)/shard_map/pallas_call | solution.py:81
  5.6 5.3 %collective-permute-start.3 = (bf16[1280,256]{1,0:T(8,128)(2,1)}, bf16[1280,256]{1,0:T(8,128)(2,1)S(1)}, u32[]{:S(2)}, u32[]{:S(2)}) collective-permute-start(bf16[1280,256]{1,0:T(8,128)(2,1)} %get-tuple-element.28), channel_id=1, source_target_pairs={{0,24},{8,0},{16,8},{24,16},{1,25},{9,1},{17,9},{25,17},{2,26},{10... | collective-permute-start | bytes 1966088 | tf_op jit(solution)/shard_map/ppermute | solution.py:327
  11.0 2.4 %collective-permute-start.4 = (bf16[1280,256]{1,0:T(8,128)(2,1)}, bf16[1280,256]{1,0:T(8,128)(2,1)S(1)}, u32[]{:S(2)}, u32[]{:S(2)}) collective-permute-start(bf16[1280,256]{1,0:T(8,128)(2,1)} %get-tuple-element.29), channel_id=1, source_target_pairs={{0,16},{8,24},{16,0},{24,8},{1,17},{9,25},{17,1},{25,9},{2,18},{10... | collective-permute-start | bytes 1966088 | tf_op jit(solution)/shard_map/ppermute | solution.py:327
  13.4 2.5 %collective-permute-start.2 = (bf16[1280,256]{1,0:T(8,128)(2,1)}, bf16[1280,256]{1,0:T(8,128)(2,1)S(1)}, u32[]{:S(2)}, u32[]{:S(2)}) collective-permute-start(bf16[1280,256]{1,0:T(8,128)(2,1)} %get-tuple-element.22.p_ref), channel_id=1, source_target_pairs={{0,8},{8,16},{16,24},{24,0},{1,9},{9,17},{17,25},{25,1},{2,10},{10... | collective-permute-start | bytes 1966088 | tf_op jit(solution)/shard_map/ppermute | solution.py:327
  16.0 2.9 %shard_map.121.refs_0_.refs_4_ = bf16[2048,256]{1,0:T(8,128)(2,1)} custom-call(s32[6]{0:T(128)} %stack.39.place_ref, bf16[1280,256]{1,0:T(8,128)(2,1)} %get-tuple-element.22.p_ref, bf16[256,6144]{1,0:T(8,128)(2,1)} %b_ref.3), custom_call_target="tpu_custom_call" | custom-call | tf_op jit(solution)/shard_map/pallas_call | solution.py:114
  18.9 3.3 %collective-permute-start = (bf16[1,2,2,64,512]{4,3,2,1,0:T(8,128)(2,1)S(1)}, bf16[1,2,2,64,512]{4,3,2,1,0:T(8,128)(2,1)S(1)}, u32[]{:S(2)}, u32[]{:S(2)}) collective-permute-start(bf16[1,2,2,64,512]{4,3,2,1,0:T(8,128)(2,1)S(1)} %maximum_bitcast_fusion), channel_id=1, source_target_pairs={{0,2},{2,0},{4,6},{6,4},{1,3},{3,1},{5,7},{7,5},{8,10},{10,8},{12,... | collective-permute-start | bytes 786440 | tf_op jit(solution)/shard_map/ppermute | solution.py:336
  22.3 0.2 select_reduce_fusion
  22.5 0.7 reshape.110
  23.2 0.8 copy.19
  24.1 2.4 %collective-permute-done = bf16[1,2,2,64,512]{4,3,2,1,0:T(8,128)(2,1)S(1)} collective-permute-done((bf16[1,2,2,64,512]{4,3,2,1,0:T(8,128)(2,1)S(1)}, bf16[1,2,2,64,512]{4,3,2,1,0:T(8,128)(2,1)S(1)}, u32[]{:S(2)}, u32[]{:S(2)}) %collective-permute-start) | collective-permute-done | bytes 262176 | tf_op jit(solution)/shard_map/ppermute | solution.py:336
  26.5 0.8 pad_maximum_fusion.1
  27.3 5.6 %collective-permute-start.1 = (bf16[2,2,2,64,512]{4,3,2,1,0:T(8,128)(2,1)}, bf16[2,2,2,64,512]{4,3,2,1,0:T(8,128)(2,1)}, u32[]{:S(2)}, u32[]{:S(2)}) collective-permute-start(bf16[2,2,2,64,512]{4,3,2,1,0:T(8,128)(2,1)} %pad_maximum_fusion.1), channel_id=1, source_target_pairs={{0,4},{2,6},{4,0},{6,2},{1,5},{3,7},{5,1},{7,3},{8,12},{10,14},{12... | collective-permute-start | bytes 1572872 | tf_op jit(solution)/shard_map/ppermute | solution.py:336
  32.9 9.3 %collective-permute-start.6 = (bf16[1280,256]{1,0:T(8,128)(2,1)S(1)}, bf16[1280,256]{1,0:T(8,128)(2,1)}, u32[]{:S(2)}, u32[]{:S(2)}) collective-permute-start(bf16[1280,256]{1,0:T(8,128)(2,1)S(1)} %collective-permute-done.3.refs_2_.refs_6_), channel_id=1, source_target_pairs={{0,1},{1,0},{2,3},{3,2},{4,5},{5,4},{6,7},{7,6},{8,9},{9,8},{10,11... | collective-permute-start | bytes 1966088 | tf_op jit(solution)/shard_map/ppermute | solution.py:329
  42.2 1.9 %collective-permute-start.7 = (bf16[1280,256]{1,0:T(8,128)(2,1)S(1)}, bf16[1280,256]{1,0:T(8,128)(2,1)}, u32[]{:S(2)}, u32[]{:S(2)}) collective-permute-start(bf16[1280,256]{1,0:T(8,128)(2,1)S(1)} %collective-permute-done.4.refs_3_.refs_7_), channel_id=1, source_target_pairs={{0,1},{1,0},{2,3},{3,2},{4,5},{5,4},{6,7},{7,6},{8,9},{9,8},{10,11... | collective-permute-start | bytes 1966088 | tf_op jit(solution)/shard_map/ppermute | solution.py:329
  44.1 1.3 collective-permute-done.2.refs_1_.refs_5_
  45.4 2.3 %collective-permute-start.5 = (bf16[1280,256]{1,0:T(8,128)(2,1)S(1)}, bf16[1280,256]{1,0:T(8,128)(2,1)}, u32[]{:S(2)}, u32[]{:S(2)}) collective-permute-start(bf16[1280,256]{1,0:T(8,128)(2,1)S(1)} %collective-permute-done.2.refs_1_.refs_5_), channel_id=1, source_target_pairs={{0,1},{1,0},{2,3},{3,2},{4,5},{5,4},{6,7},{7,6},{8,9},{9,8},{10,11... | collective-permute-start | bytes 1966088 | tf_op jit(solution)/shard_map/ppermute | solution.py:329
  47.8 0.7 add_select_fusion
  48.5 1.0 select_n.49
  49.5 0.1 fusion.p_ref
  49.6 2.1 %pad_maximum_fusion.rm_ref = bf16[4,2,2,64,512]{4,3,2,1,0:T(8,128)(2,1)} fusion(bf16[2,2,2,64,512]{4,3,2,1,0:T(8,128)(2,1)} %collective-permute-done.1, bf16[1,2,2,64,512]{4,3,2,1,0:T(8,128)(2,1)S(1)} %collective-permute-done, bf16[1,2,2,64,512]{4,3,2,1,0:T(8,128)(2,1)S(1)} %maximum_bitcast_fusion), kind=kLoop, calls=%fused_computation | loop fusion | flops 1048576 | bytes 2097152 | tf_op jit(solution)/shard_map/concatenate | solution.py:337
  51.7 3.0 %shard_map.123 = (bf16[128,1536]{1,0:T(8,128)(2,1)S(1)}, bf16[128,1536]{1,0:T(8,128)(2,1)S(1)}) custom-call(bf16[2048,256]{1,0:T(8,128)(2,1)S(1)} %copy-done, bf16[1280,256]{1,0:T(8,128)(2,1)S(1)} %collective-permute-done.2.refs_1_.refs_5_, bf16[1280,256]{1,0:T(8,128)(2,1)S(1)} %collective-permute-done.3.refs_2_.refs_6_, ...), custom_call_target="tpu_custom_call" | custom-call | tf_op jit(solution)/shard_map/pallas_call | solution.py:152
  54.8 3.5 %collective-permute-start.8 = (bf16[128,1536]{1,0:T(8,128)(2,1)S(1)}, bf16[128,1536]{1,0:T(8,128)(2,1)S(1)}, u32[]{:S(2)}, u32[]{:S(2)}) collective-permute-start(bf16[128,1536]{1,0:T(8,128)(2,1)S(1)} %get-tuple-element.31), channel_id=1, source_target_pairs={{0,32},{32,64},{64,96},{96,128},{128,160},{160,192},{192,224},{224... | collective-permute-start | bytes 1179656 | tf_op jit(solution)/shard_map/ppermute | solution.py:355
  58.3 9.5 %collective-permute-start.11 = (bf16[128,1536]{1,0:T(8,128)(2,1)S(1)}, bf16[128,1536]{1,0:T(8,128)(2,1)S(1)}, u32[]{:S(2)}, u32[]{:S(2)}) collective-permute-start(bf16[128,1536]{1,0:T(8,128)(2,1)S(1)} %get-tuple-element.33), channel_id=1, source_target_pairs={{0,480},{32,0},{64,32},{96,64},{128,96},{160,128},{192,160},{224,1... | collective-permute-start | bytes 1179656 | tf_op jit(solution)/shard_map/ppermute | solution.py:355
  67.8 3.1 %shard_map.122 = (f32[128,1536]{1,0:T(8,128)S(1)}, f32[128,1536]{1,0:T(8,128)S(1)}) custom-call(bf16[2048,256]{1,0:T(8,128)(2,1)S(1)} %copy-done, bf16[1280,256]{1,0:T(8,128)(2,1)S(1)} %collective-permute-done.2.refs_1_.refs_5_, bf16[1280,256]{1,0:T(8,128)(2,1)S(1)} %collective-permute-done.3.refs_2_.refs_6_, ...), custom_call_target="tpu_custom_call" | custom-call | tf_op jit(solution)/shard_map/pallas_call | solution.py:152
  70.9 4.4 %collective-permute-done.8 = bf16[128,1536]{1,0:T(8,128)(2,1)S(1)} collective-permute-done((bf16[128,1536]{1,0:T(8,128)(2,1)S(1)}, bf16[128,1536]{1,0:T(8,128)(2,1)S(1)}, u32[]{:S(2)}, u32[]{:S(2)}) %collective-permute-start.8) | collective-permute-done | bytes 393248 | tf_op jit(solution)/shard_map/ppermute | solution.py:355
  75.3 1.9 %collective-permute-start.9 = (bf16[64,1536]{1,0:T(8,128)(2,1)S(1)}, bf16[64,1536]{1,0:T(8,128)(2,1)S(1)}, u32[]{:S(2)}, u32[]{:S(2)}) collective-permute-start(bf16[64,1536]{1,0:T(8,128)(2,1)S(1)} %add_convert_fusion.1), channel_id=1, source_target_pairs={{0,64},{32,96},{64,128},{96,160},{128,192},{160,224},{192,256},{22... | collective-permute-start | bytes 589832 | tf_op jit(solution)/shard_map/ppermute | solution.py:361
  77.3 0.0 copy-start.7
  77.3 5.6 %collective-permute-start.12 = (bf16[64,1536]{1,0:T(8,128)(2,1)S(1)}, bf16[64,1536]{1,0:T(8,128)(2,1)S(1)}, u32[]{:S(2)}, u32[]{:S(2)}) collective-permute-start(bf16[64,1536]{1,0:T(8,128)(2,1)S(1)} %add_convert_fusion), channel_id=1, source_target_pairs={{0,448},{32,480},{64,0},{96,32},{128,64},{160,96},{192,128},{224,1... | collective-permute-start | bytes 589832 | tf_op jit(solution)/shard_map/ppermute | solution.py:361
  82.9 6.4 %collective-permute-done.9 = bf16[64,1536]{1,0:T(8,128)(2,1)S(1)} collective-permute-done((bf16[64,1536]{1,0:T(8,128)(2,1)S(1)}, bf16[64,1536]{1,0:T(8,128)(2,1)S(1)}, u32[]{:S(2)}, u32[]{:S(2)}) %collective-permute-start.9) | collective-permute-done | bytes 196640 | tf_op jit(solution)/shard_map/ppermute | solution.py:361
  89.4 2.1 %collective-permute-start.10 = (bf16[32,1536]{1,0:T(8,128)(2,1)S(1)}, bf16[32,1536]{1,0:T(8,128)(2,1)S(1)}, u32[]{:S(2)}, u32[]{:S(2)}) collective-permute-start(bf16[32,1536]{1,0:T(8,128)(2,1)S(1)} %add_convert_fusion.5), channel_id=1, source_target_pairs={{0,128},{32,160},{64,192},{96,224},{128,256},{160,288},{192,320},{... | collective-permute-start | bytes 294920 | tf_op jit(solution)/shard_map/ppermute | solution.py:361
  91.5 7.3 %collective-permute-start.13 = (bf16[32,1536]{1,0:T(8,128)(2,1)S(1)}, bf16[32,1536]{1,0:T(8,128)(2,1)S(1)}, u32[]{:S(2)}, u32[]{:S(2)}) collective-permute-start(bf16[32,1536]{1,0:T(8,128)(2,1)S(1)} %add_convert_fusion.3), channel_id=1, source_target_pairs={{0,384},{32,416},{64,448},{96,480},{128,0},{160,32},{192,64},{224,... | collective-permute-start | bytes 294920 | tf_op jit(solution)/shard_map/ppermute | solution.py:361
  98.7 5.2 %collective-permute-done.10 = bf16[32,1536]{1,0:T(8,128)(2,1)S(1)} collective-permute-done((bf16[32,1536]{1,0:T(8,128)(2,1)S(1)}, bf16[32,1536]{1,0:T(8,128)(2,1)S(1)}, u32[]{:S(2)}, u32[]{:S(2)}) %collective-permute-start.10) | collective-permute-done | bytes 98336 | tf_op jit(solution)/shard_map/ppermute | solution.py:361
  104.0 4.2 %collective-permute-done.13 = bf16[32,1536]{1,0:T(8,128)(2,1)S(1)} collective-permute-done((bf16[32,1536]{1,0:T(8,128)(2,1)S(1)}, bf16[32,1536]{1,0:T(8,128)(2,1)S(1)}, u32[]{:S(2)}, u32[]{:S(2)}) %collective-permute-start.13) | collective-permute-done | bytes 98336 | tf_op jit(solution)/shard_map/ppermute | solution.py:361
  108.3 12.2 %all-gather = bf16[256,1536]{1,0:T(8,128)(2,1)S(1)} all-gather(bf16[64,1536]{1,0:T(8,128)(2,1)S(1)} %pad_maximum_fusion.2), channel_id=2, replica_groups=mesh['z'=16,'x'=4,'y'=4,'c'=2] {'x'}, dimensions={0}, use_global_device_ids=true | all-gather | bytes 983040 | tf_op jit(solution)/shard_map/all_gather | solution.py:367
  120.5 1.3 shard_map.124
  121.7 5.9 %all-to-all-start = ((bf16[16,16,512]{2,1,0:T(8,128)(2,1)}), bf16[16,16,512]{2,1,0:T(8,128)(2,1)S(1)}, u32[]{:S(2)}, u32[]{:S(2)}) async-start(bf16[16,16,512]{2,1,0:T(8,128)(2,1)} %bitcast.11), calls=%async_computation | async-start | bytes 524288 | tf_op jit(solution)/shard_map/all_to_all | solution.py:370
  127.7 5.9 %collective-permute-start.15 = (bf16[4,2,2,64,512]{4,3,2,1,0:T(8,128)(2,1)S(1)}, bf16[4,2,2,64,512]{4,3,2,1,0:T(8,128)(2,1)S(1)}, u32[]{:S(2)}, u32[]{:S(2)}) collective-permute-start(bf16[4,2,2,64,512]{4,3,2,1,0:T(8,128)(2,1)S(1)} %copy-done.1), channel_id=1, source_target_pairs={{0,1},{1,0},{2,3},{3,2},{4,5},{5,4},{6,7},{7,6},{8,9},{9,8},{10,11... | collective-permute-start | bytes 3145736 | tf_op jit(solution)/shard_map/ppermute | solution.py:348
  133.6 0.2 fusion.9
  133.8 6.6 %all-to-all-done = bf16[16,16,512]{2,1,0:T(8,128)(2,1)S(1)} async-done(((bf16[16,16,512]{2,1,0:T(8,128)(2,1)}), bf16[16,16,512]{2,1,0:T(8,128)(2,1)S(1)}, u32[]{:S(2)}, u32[]{:S(2)}) %all-to-all-start) | async-done | bytes 262176 | tf_op jit(solution)/shard_map/all_to_all | solution.py:370
  140.4 1.5 shard_map.125
  142.0 10.6 %all-gather.1 = bf16[576,512]{1,0:T(8,128)(2,1)S(1)} all-gather(bf16[144,512]{1,0:T(8,128)(2,1)S(1)} %get-tuple-element.34), channel_id=3, replica_groups=mesh['z'=16,'x'=4,'y'=4,'c'=2] {'y'}, dimensions={0}, use_global_device_ids=true | all-gather | bytes 737280 | tf_op jit(solution)/shard_map/all_gather | solution.py:377
  152.5 12.6 %collective-permute-start.14 = (bf16[4,144,512]{2,1,0:T(8,128)(2,1)S(1)}, bf16[4,144,512]{2,1,0:T(8,128)(2,1)S(1)}, u32[]{:S(2)}, u32[]{:S(2)}) collective-permute-start(bf16[4,144,512]{2,1,0:T(8,128)(2,1)S(1)} %bitcast.48), channel_id=1, source_target_pairs={{0,1},{1,0},{2,3},{3,2},{4,5},{5,4},{6,7},{7,6},{8,9},{9,8},{10,11... | collective-permute-start | bytes 1769480 | tf_op jit(solution)/shard_map/ppermute | solution.py:378
  165.2 0.2 compare_reduce_fusion
  165.4 0.1 concatenate.13.f_ref
  165.5 1.3 collective-permute-done.14.o_ref
  166.8 0.9 copy-done.3
  167.8 4.5 %shard_map.126 = (f32[2,64,512]{2,1,0:T(8,128)}, f32[2,64,512]{2,1,0:T(8,128)}, bf16[2,512,512]{2,1,0:T(8,128)(2,1)}) custom-call(s32[7]{0:T(128)S(1)} %concatenate.13.f_ref, bf16[4,144,512]{2,1,0:T(8,128)(2,1)S(1)} %bitcast.49, bf16[4,144,512]{2,1,0:T(8,128)(2,1)S(1)} %collective-permute-done.14.o_ref, bf16[4,2,2,64,512]{4,3,2,1,0:T(8,128)(2,1)S(1)} %copy-done.1, ...), custom_call_target="tpu_custom_call" | custom-call | tf_op jit(solution)/shard_map/pallas_call | solution.py:285
  (41 shorter events, 0.5 us)
Async XLA Ops:
  5.6 13.2 %copy-start.5 = (bf16[1,2,64,512]{3,2,1,0:T(8,128)(2,1)S(1)}, bf16[1,2,64,512]{3,2,1,0:T(8,128)(2,1)}, u32[]{:S(2)}) copy-start(bf16[1,2,64,512]{3,2,1,0:T(8,128)(2,1)} %param.16) | copy-start | bytes 393220
  5.6 13.2 %copy-start.6 = (bf16[1,2,64,512]{3,2,1,0:T(8,128)(2,1)S(1)}, bf16[1,2,64,512]{3,2,1,0:T(8,128)(2,1)}, u32[]{:S(2)}) copy-start(bf16[1,2,64,512]{3,2,1,0:T(8,128)(2,1)} %param.15) | copy-start | bytes 393220
  5.6 16.6 %copy-start.8 = (s32[96]{0:T(128)S(1)}, s32[96]{0:T(128)}, u32[]{:S(2)}) copy-start(s32[96]{0:T(128)} %param.11) | copy-start | bytes 1156
  5.6 27.2 %collective-permute-start.3 = (bf16[1280,256]{1,0:T(8,128)(2,1)}, bf16[1280,256]{1,0:T(8,128)(2,1)S(1)}, u32[]{:S(2)}, u32[]{:S(2)}) collective-permute-start(bf16[1280,256]{1,0:T(8,128)(2,1)} %get-tuple-element.28), channel_id=1, source_target_pairs={{0,24},{8,0},{16,8},{24,16},{1,25},{9,1},{17,9},{25,17},{2,26},{10... | collective-permute-start | bytes 1966088 | tf_op jit(solution)/shard_map/ppermute | solution.py:327
  11.0 31.2 %collective-permute-start.4 = (bf16[1280,256]{1,0:T(8,128)(2,1)}, bf16[1280,256]{1,0:T(8,128)(2,1)S(1)}, u32[]{:S(2)}, u32[]{:S(2)}) collective-permute-start(bf16[1280,256]{1,0:T(8,128)(2,1)} %get-tuple-element.29), channel_id=1, source_target_pairs={{0,16},{8,24},{16,0},{24,8},{1,17},{9,25},{17,1},{25,9},{2,18},{10... | collective-permute-start | bytes 1966088 | tf_op jit(solution)/shard_map/ppermute | solution.py:327
  13.4 32.0 %collective-permute-start.2 = (bf16[1280,256]{1,0:T(8,128)(2,1)}, bf16[1280,256]{1,0:T(8,128)(2,1)S(1)}, u32[]{:S(2)}, u32[]{:S(2)}) collective-permute-start(bf16[1280,256]{1,0:T(8,128)(2,1)} %get-tuple-element.22.p_ref), channel_id=1, source_target_pairs={{0,8},{8,16},{16,24},{24,0},{1,9},{9,17},{17,25},{25,1},{2,10},{10... | collective-permute-start | bytes 1966088 | tf_op jit(solution)/shard_map/ppermute | solution.py:327
  18.9 32.9 %copy-start = (bf16[2048,256]{1,0:T(8,128)(2,1)S(1)}, bf16[2048,256]{1,0:T(8,128)(2,1)}, u32[]{:S(2)}) copy-start(bf16[2048,256]{1,0:T(8,128)(2,1)} %shard_map.121.refs_0_.refs_4_) | copy-start | bytes 3145732
  18.9 7.5 %collective-permute-start = (bf16[1,2,2,64,512]{4,3,2,1,0:T(8,128)(2,1)S(1)}, bf16[1,2,2,64,512]{4,3,2,1,0:T(8,128)(2,1)S(1)}, u32[]{:S(2)}, u32[]{:S(2)}) collective-permute-start(bf16[1,2,2,64,512]{4,3,2,1,0:T(8,128)(2,1)S(1)} %maximum_bitcast_fusion), channel_id=1, source_target_pairs={{0,2},{2,0},{4,6},{6,4},{1,3},{3,1},{5,7},{7,5},{8,10},{10,8},{12,... | collective-permute-start | bytes 786440 | tf_op jit(solution)/shard_map/ppermute | solution.py:336
  27.3 22.3 %collective-permute-start.1 = (bf16[2,2,2,64,512]{4,3,2,1,0:T(8,128)(2,1)}, bf16[2,2,2,64,512]{4,3,2,1,0:T(8,128)(2,1)}, u32[]{:S(2)}, u32[]{:S(2)}) collective-permute-start(bf16[2,2,2,64,512]{4,3,2,1,0:T(8,128)(2,1)} %pad_maximum_fusion.1), channel_id=1, source_target_pairs={{0,4},{2,6},{4,0},{6,2},{1,5},{3,7},{5,1},{7,3},{8,12},{10,14},{12... | collective-permute-start | bytes 1572872 | tf_op jit(solution)/shard_map/ppermute | solution.py:336
  32.9 18.8 %collective-permute-start.6 = (bf16[1280,256]{1,0:T(8,128)(2,1)S(1)}, bf16[1280,256]{1,0:T(8,128)(2,1)}, u32[]{:S(2)}, u32[]{:S(2)}) collective-permute-start(bf16[1280,256]{1,0:T(8,128)(2,1)S(1)} %collective-permute-done.3.refs_2_.refs_6_), channel_id=1, source_target_pairs={{0,1},{1,0},{2,3},{3,2},{4,5},{5,4},{6,7},{7,6},{8,9},{9,8},{10,11... | collective-permute-start | bytes 1966088 | tf_op jit(solution)/shard_map/ppermute | solution.py:329
  42.2 9.5 %collective-permute-start.7 = (bf16[1280,256]{1,0:T(8,128)(2,1)S(1)}, bf16[1280,256]{1,0:T(8,128)(2,1)}, u32[]{:S(2)}, u32[]{:S(2)}) collective-permute-start(bf16[1280,256]{1,0:T(8,128)(2,1)S(1)} %collective-permute-done.4.refs_3_.refs_7_), channel_id=1, source_target_pairs={{0,1},{1,0},{2,3},{3,2},{4,5},{5,4},{6,7},{7,6},{8,9},{9,8},{10,11... | collective-permute-start | bytes 1966088 | tf_op jit(solution)/shard_map/ppermute | solution.py:329
  45.4 6.3 %collective-permute-start.5 = (bf16[1280,256]{1,0:T(8,128)(2,1)S(1)}, bf16[1280,256]{1,0:T(8,128)(2,1)}, u32[]{:S(2)}, u32[]{:S(2)}) collective-permute-start(bf16[1280,256]{1,0:T(8,128)(2,1)S(1)} %collective-permute-done.2.refs_1_.refs_5_), channel_id=1, source_target_pairs={{0,1},{1,0},{2,3},{3,2},{4,5},{5,4},{6,7},{7,6},{8,9},{9,8},{10,11... | collective-permute-start | bytes 1966088 | tf_op jit(solution)/shard_map/ppermute | solution.py:329
  54.8 20.5 %collective-permute-start.8 = (bf16[128,1536]{1,0:T(8,128)(2,1)S(1)}, bf16[128,1536]{1,0:T(8,128)(2,1)S(1)}, u32[]{:S(2)}, u32[]{:S(2)}) collective-permute-start(bf16[128,1536]{1,0:T(8,128)(2,1)S(1)} %get-tuple-element.31), channel_id=1, source_target_pairs={{0,32},{32,64},{64,96},{96,128},{128,160},{160,192},{192,224},{224... | collective-permute-start | bytes 1179656 | tf_op jit(solution)/shard_map/ppermute | solution.py:355
  58.3 18.9 %collective-permute-start.11 = (bf16[128,1536]{1,0:T(8,128)(2,1)S(1)}, bf16[128,1536]{1,0:T(8,128)(2,1)S(1)}, u32[]{:S(2)}, u32[]{:S(2)}) collective-permute-start(bf16[128,1536]{1,0:T(8,128)(2,1)S(1)} %get-tuple-element.33), channel_id=1, source_target_pairs={{0,480},{32,0},{64,32},{96,64},{128,96},{160,128},{192,160},{224,1... | collective-permute-start | bytes 1179656 | tf_op jit(solution)/shard_map/ppermute | solution.py:355
  75.3 14.0 %collective-permute-start.9 = (bf16[64,1536]{1,0:T(8,128)(2,1)S(1)}, bf16[64,1536]{1,0:T(8,128)(2,1)S(1)}, u32[]{:S(2)}, u32[]{:S(2)}) collective-permute-start(bf16[64,1536]{1,0:T(8,128)(2,1)S(1)} %add_convert_fusion.1), channel_id=1, source_target_pairs={{0,64},{32,96},{64,128},{96,160},{128,192},{160,224},{192,256},{22... | collective-permute-start | bytes 589832 | tf_op jit(solution)/shard_map/ppermute | solution.py:361
  77.3 50.4 %copy-start.1 = (bf16[4,2,2,64,512]{4,3,2,1,0:T(8,128)(2,1)S(1)}, bf16[4,2,2,64,512]{4,3,2,1,0:T(8,128)(2,1)}, u32[]{:S(2)}) copy-start(bf16[4,2,2,64,512]{4,3,2,1,0:T(8,128)(2,1)} %pad_maximum_fusion.rm_ref) | copy-start | bytes 3145732
  77.3 56.4 %copy-start.7 = (s32[96]{0:T(128)S(1)}, s32[96]{0:T(128)}, u32[]{:S(2)}) copy-start(s32[96]{0:T(128)} %param.12) | copy-start | bytes 1156
  77.3 63.2 %copy-start.4 = (f32[1,2,64,512]{3,2,1,0:T(8,128)S(1)}, f32[1,2,64,512]{3,2,1,0:T(8,128)}, u32[]{:S(2)}) copy-start(f32[1,2,64,512]{3,2,1,0:T(8,128)} %param.17) | copy-start | bytes 786436
  77.3 14.1 %collective-permute-start.12 = (bf16[64,1536]{1,0:T(8,128)(2,1)S(1)}, bf16[64,1536]{1,0:T(8,128)(2,1)S(1)}, u32[]{:S(2)}, u32[]{:S(2)}) collective-permute-start(bf16[64,1536]{1,0:T(8,128)(2,1)S(1)} %add_convert_fusion), channel_id=1, source_target_pairs={{0,448},{32,480},{64,0},{96,32},{128,64},{160,96},{192,128},{224,1... | collective-permute-start | bytes 589832 | tf_op jit(solution)/shard_map/ppermute | solution.py:361
  89.3 77.5 %copy-start.2 = (f32[1,2,64,512]{3,2,1,0:T(8,128)S(1)}, f32[1,2,64,512]{3,2,1,0:T(8,128)}, u32[]{:S(2)}) copy-start(f32[1,2,64,512]{3,2,1,0:T(8,128)} %param.13) | copy-start | bytes 786436
  89.4 14.6 %collective-permute-start.10 = (bf16[32,1536]{1,0:T(8,128)(2,1)S(1)}, bf16[32,1536]{1,0:T(8,128)(2,1)S(1)}, u32[]{:S(2)}, u32[]{:S(2)}) collective-permute-start(bf16[32,1536]{1,0:T(8,128)(2,1)S(1)} %add_convert_fusion.5), channel_id=1, source_target_pairs={{0,128},{32,160},{64,192},{96,224},{128,256},{160,288},{192,320},{... | collective-permute-start | bytes 294920 | tf_op jit(solution)/shard_map/ppermute | solution.py:361
  91.5 16.8 %collective-permute-start.13 = (bf16[32,1536]{1,0:T(8,128)(2,1)S(1)}, bf16[32,1536]{1,0:T(8,128)(2,1)S(1)}, u32[]{:S(2)}, u32[]{:S(2)}) collective-permute-start(bf16[32,1536]{1,0:T(8,128)(2,1)S(1)} %add_convert_fusion.3), channel_id=1, source_target_pairs={{0,384},{32,416},{64,448},{96,480},{128,0},{160,32},{192,64},{224,... | collective-permute-start | bytes 294920 | tf_op jit(solution)/shard_map/ppermute | solution.py:361
  121.7 18.7 %all-to-all-start = ((bf16[16,16,512]{2,1,0:T(8,128)(2,1)}), bf16[16,16,512]{2,1,0:T(8,128)(2,1)S(1)}, u32[]{:S(2)}, u32[]{:S(2)}) async-start(bf16[16,16,512]{2,1,0:T(8,128)(2,1)} %bitcast.11), calls=%async_computation | async-start | bytes 524288 | tf_op jit(solution)/shard_map/all_to_all | solution.py:370
  127.7 37.8 %collective-permute-start.15 = (bf16[4,2,2,64,512]{4,3,2,1,0:T(8,128)(2,1)S(1)}, bf16[4,2,2,64,512]{4,3,2,1,0:T(8,128)(2,1)S(1)}, u32[]{:S(2)}, u32[]{:S(2)}) collective-permute-start(bf16[4,2,2,64,512]{4,3,2,1,0:T(8,128)(2,1)S(1)} %copy-done.1), channel_id=1, source_target_pairs={{0,1},{1,0},{2,3},{3,2},{4,5},{5,4},{6,7},{7,6},{8,9},{9,8},{10,11... | collective-permute-start | bytes 3145736 | tf_op jit(solution)/shard_map/ppermute | solution.py:348
  152.5 14.3 %collective-permute-start.14 = (bf16[4,144,512]{2,1,0:T(8,128)(2,1)S(1)}, bf16[4,144,512]{2,1,0:T(8,128)(2,1)S(1)}, u32[]{:S(2)}, u32[]{:S(2)}) collective-permute-start(bf16[4,144,512]{2,1,0:T(8,128)(2,1)S(1)} %bitcast.48), channel_id=1, source_target_pairs={{0,1},{1,0},{2,3},{3,2},{4,5},{5,4},{6,7},{7,6},{8,9},{9,8},{10,11... | collective-permute-start | bytes 1769480 | tf_op jit(solution)/shard_map/ppermute | solution.py:378
  166.8 1.0 copy-start.3

commit v5 on v4

--- a/solution.py
+++ b/solution.py
@@ -47,49 +47,60 @@
     width = out_grads.shape[1] // NX
     tile = width // TILES
 
-    def kernel(place_ref, a_ref, b_ref, *out_refs):
-        z, c, step = place_ref[0], place_ref[2], pl.program_id(0)
-
-        @pl.when(step == 0)
-        def _():
-            m, k = iota((small, count), 0), iota((small, count), 1)
-            block = m % part
-            row = (m // part) % per_z
-            tail = m // (part * per_z)
-            high = 2 * (tail // 4) + 4 * ((tail // 2) % 2) + 8 * (tail % 2)
-            for side in range(2):
-                values = a_ref[side * part : (side + 1) * part].reshape(count, toks)
-                for odd in range(2):
-                    dist = high + odd
-                    goal = jnp.bitwise_and(z + dist if side == 0 else z - dist, NZ - 1)
-                    pick = (block * rows + goal * per_z + row == k).astype(WIDE).astype(HALF)
-                    moved = dot(pick, values).astype(HALF)
-                    turned = jnp.concatenate([moved[:, half:], moved[:, :half]], axis=1)
-                    at = (1 - odd) * count + side * small
-                    for ref in out_refs:
-                        ref[at : at + small, :] = jnp.where(c == 1, turned, moved)
-
-        for i, ref in enumerate(out_refs):
-
-            @pl.when(step == i)
-            def _():
-                for n in range(TILES):
-                    at = 2 * count + n * half
-                    ref[at : at + half, :] = b_ref[:, n * tile : (n + 1) * tile]
+    def kernel(place_ref, a_ref, b_ref, *refs):
+        out_refs, (held, sems, out_sems) = refs[:3], refs[3:]
+        z, c = place_ref[0], place_ref[2]
+        tok = pl.ds(pl.multiple_of(c * half, half), half)
+        copies = []
+        for i in range(3):
+            begin = place_ref[3 + i] * width
+            for n in range(TILES):
+                at = pl.ds(pl.multiple_of(begin + n * tile, tile), tile)
+                to = pl.ds(2 * count + n * half, half)
+                copies.append(pltpu.make_async_copy(b_ref.at[tok, at], held.at[i, to, :], sems.at[i, n]))
+        for copy in copies:
+            copy.start()
+        m, k = iota((small, count), 0), iota((small, count), 1)
+        block = m % part
+        row = (m // part) % per_z
+        tail = m // (part * per_z)
+        high = 2 * (tail // 4) + 4 * ((tail // 2) % 2) + 8 * (tail % 2)
+        for side in range(2):
+            values = a_ref[side * part : (side + 1) * part].reshape(count, toks)
+            for odd in range(2):
+                dist = high + odd
+                goal = jnp.bitwise_and(z + dist if side == 0 else z - dist, NZ - 1)
+                pick = (block * rows + goal * per_z + row == k).astype(WIDE).astype(HALF)
+                moved = dot(pick, values).astype(HALF)
+                turned = jnp.concatenate([moved[:, half:], moved[:, :half]], axis=1)
+                at = (1 - odd) * count + side * small
+                ordered = jnp.where(c == 1, turned, moved)
+                for i in range(3):
+                    held[i, at : at + small, :] = ordered
+        last = [pltpu.make_async_copy(held.at[i], out_refs[i], out_sems.at[i]) for i in range(3)]
+        for i in range(3):
+            for copy in copies[i * TILES : (i + 1) * TILES]:
+                copy.wait()
+            last[i].start()
+        for copy in last:
+            copy.wait()
 
     piece = (2 * count + TILES * half, toks)
+    any_place = pl.BlockSpec(memory_space=pl.ANY)
     return pl.pallas_call(
         kernel,
         out_shape=[jax.ShapeDtypeStruct(piece, HALF)] * 3,
-        grid_spec=pltpu.PrefetchScalarGridSpec(
-            num_scalar_prefetch=1,
-            grid=(3,),
-            in_specs=[
-                pl.BlockSpec(activations.shape, lambda i, place_ref: (0, 0, 0)),
-                pl.BlockSpec((half, width), lambda i, place_ref: (place_ref[2], place_ref[3 + i])),
-            ],
-            out_specs=[pl.BlockSpec(piece, lambda i, place_ref: (0, 0))] * 3,
-        ),
+        in_specs=[
+            pl.BlockSpec(memory_space=pltpu.SMEM),
+            pl.BlockSpec(memory_space=pltpu.VMEM),
+            any_place,
+        ],
+        out_specs=[any_place] * 3,
+        scratch_shapes=[
+            pltpu.VMEM((3, *piece), HALF),
+            pltpu.SemaphoreType.DMA((3, TILES)),
+            pltpu.SemaphoreType.DMA((3,)),
+        ],
         compiler_params=ROOMY,
     )(place, activations, out_grads)
 
@@ -325,17 +336,8 @@
     place = jnp.stack([z, x, c] + [jnp.bitwise_and(x + step, NX - 1) for step in (1, 3, 2)]).astype(jnp.int32)
     pieces = prepare(activations, out_grads, place)
     arrived = [lax.ppermute(piece, "x", ring(NX, step)) for piece, step in zip(pieces, (1, -1, 2))]
-    own = own_part(pieces[0], out_grads, place)
-    swapped = [lax.ppermute(piece, "c", ring(NC, 1)) for piece in arrived]
-
-    own, left_root, right_root = lax.optimization_barrier((own, left_root, right_root))
-    ny = lax.axis_size("y")
-    roots = jnp.stack([left_root[0], right_root[0]])[None]
-    for step in (1, 2):
-        if step < ny:
-            roots_from = lax.ppermute(roots, "y", [(i, i ^ step) for i in range(ny)])
-            roots = jnp.concatenate([roots, roots_from], axis=0)
-
+
+    piece_own, owners = lax.optimization_barrier((pieces[0], owners))
     targets = slot_targets(owners, slots)
     by_block = targets.reshape(2, half_rows, NX, columns).transpose(2, 3, 0, 1)[:, :, :, None, None, :]
     shape = (NX, columns, 2, 2, per_z, half_rows)
@@ -344,7 +346,18 @@
     code = jnp.where(owner % NX == x, code, -1).reshape(1, -1)
     out_rows = NZ * slots * 2 * per_z
     chosen = (code == iota((out_rows, 1), 0)).astype(HALF)
-    own, roots, chosen = lax.optimization_barrier((own, roots, chosen))
+    piece_own, chosen = lax.optimization_barrier((piece_own, chosen))
+    own = own_part(piece_own, out_grads, place)
+
+    own, left_root, right_root = lax.optimization_barrier((own, left_root, right_root))
+    ny = lax.axis_size("y")
+    roots = jnp.stack([left_root[0], right_root[0]])[None]
+    for step in (1, 2):
+        if step < ny:
+            came = lax.ppermute(roots, "y", [(i, i ^ step) for i in range(ny)])
+            roots = jnp.concatenate([roots, came], axis=0)
+    own, roots = lax.optimization_barrier((own, roots))
+    swapped = [lax.ppermute(piece, "c", ring(NC, 1)) for piece in arrived]
     roots_other = lax.ppermute(roots, "c", ring(NC, 1))
 
     sent = partial_products(own, arrived, swapped, True)

time: 173 us -> 167 us (0.965)
  starting transfers between devices: 87.1 us -> 93.6 us
  Pallas kernels: 20.7 us -> 17.1 us
  other arithmetic: 4.65 us -> 1.22 us
  local copies, waits for them, and re-layouts: 4.31 us -> 1.11 us
  waiting for transfers between devices: 31.8 us -> 29.4 us
    ppermute x4, waiting for transfers between devices: 15.8 us -> 9.75 us  [body(): got.append(lax.ppermute(out.astype(HALF), 'z', ring(NZ, way * step)))]
    all_to_all x1, starting transfers between devices: 5.9 us -> 11.5 us  [body(): lax.all_to_all(picked, 'z', 0, 0, tiled=True).reshape(out_rows, block_size)]
    pallas_call x2, Pallas kernels: 6.1 us -> 2.83 us  [partial_products(): pl.pallas_call(kernel, grid=(TILES // group,), out_shape=[jax.ShapeDtypeS...]
    concatenate x2, other arithmetic: 2.98 us -> 0.15 us  [body(): roots = jnp.concatenate([roots, came], axis=0)]
    ppermute x2, waiting for transfers between devices: 2.37 us -> 4.2 us  [body(): came = lax.ppermute(roots, 'y', [(i, i ^ step) for i in range(ny)])]
  transfers between devices with their start and end apart: 17 -> 17, of which waited for: 8 -> 8; matrix products, arithmetic and copies ran while one was open for 4% -> 1% of each run, Pallas kernels for 4% -> 4%
where the time goes in v5:
time: 167 us; the launch traced here: 166 us
  starting transfers between devices  93.6 us (56%)
  waiting for transfers between devices  29.4 us (18%)
  blocking collectives  22.3 us (13%)
  Pallas kernels  17.1 us (10%)
    ppermute x4, starting transfers between devices, body(): got.append(lax.ppermute(out.astype(HALF), 'z', ring(NZ, way * step)))  16.8 us
    ppermute x3, starting transfers between devices, body(): swapped = [lax.ppermute(piece, 'c', ring(NC, 1)) for piece in arrived]  13.5 us
    ppermute x2, starting transfers between devices, body(): got = [lax.ppermute(out, 'z', ring(NZ, way))]  13 us
    ppermute x1, starting transfers between devices, body(): rows_other = lax.ppermute(rows_mine, 'c', ring(NC, 1))  12.4 us
    all_to_all x1, starting transfers between devices, body(): lax.all_to_all(picked, 'z', 0, 0, tiled=True).reshape(out_rows, block_size)  11.5 us
    all_gather x1, blocking collectives, body(): lax.all_gather(jnp.concatenate(sums, axis=0), 'x', axis=0, tiled=False)  11.5 us
    all_gather x1, blocking collectives, body(): rows_mine = lax.all_gather(own_rows, 'y', axis=0, tiled=False)  10.8 us
    ppermute x3, starting transfers between devices, body(): lax.ppermute(piece, 'x', ring(NX, step))  10.3 us
  transfers between devices with their start and end apart: 17, of which 8 were waited for; matrix products, arithmetic and copies ran while one was open for 1% of the time, Pallas kernels for 4%

profile of v5, /device:TPU:1, one launch (start us, length us, event | category | flops | bytes accessed | tf_op | source)
XLA Modules:
  0.0 165.8 jit_solution(5605621493843617654)
XLA Ops:
  0.7 0.6 stack.39.place_ref
  1.2 3.5 %shard_map.120 = (bf16[1280,256]{1,0:T(8,128)(2,1)}, bf16[1280,256]{1,0:T(8,128)(2,1)}, bf16[1280,256]{1,0:T(8,128)(2,1)}) custom-call(s32[6]{0:T(128)} %stack.39.place_ref, bf16[8,64,256]{2,1,0:T(8,128)(2,1)} %a_ref.1, bf16[256,6144]{1,0:T(8,128)(2,1)} %b_ref.3), custom_call_target="tpu_custom_call" | custom-call | tf_op jit(solution)/shard_map/pallas_call | solution.py:90
  4.7 0.0 copy-start.4
  4.7 0.0 copy-start.5
  4.7 5.3 %collective-permute-start.3 = (bf16[1280,256]{1,0:T(8,128)(2,1)}, bf16[1280,256]{1,0:T(8,128)(2,1)S(1)}, u32[]{:S(2)}, u32[]{:S(2)}) collective-permute-start(bf16[1280,256]{1,0:T(8,128)(2,1)} %get-tuple-element.34), channel_id=1, source_target_pairs={{0,24},{8,0},{16,8},{24,16},{1,25},{9,1},{17,9},{25,17},{2,26},{10... | collective-permute-start | bytes 1966088 | tf_op jit(solution)/shard_map/ppermute | solution.py:338
  10.1 2.4 %collective-permute-start.4 = (bf16[1280,256]{1,0:T(8,128)(2,1)}, bf16[1280,256]{1,0:T(8,128)(2,1)S(1)}, u32[]{:S(2)}, u32[]{:S(2)}) collective-permute-start(bf16[1280,256]{1,0:T(8,128)(2,1)} %get-tuple-element.35), channel_id=1, source_target_pairs={{0,16},{8,24},{16,0},{24,8},{1,17},{9,25},{17,1},{25,9},{2,18},{10... | collective-permute-start | bytes 1966088 | tf_op jit(solution)/shard_map/ppermute | solution.py:338
  12.5 2.5 %collective-permute-start.2 = (bf16[1280,256]{1,0:T(8,128)(2,1)}, bf16[1280,256]{1,0:T(8,128)(2,1)S(1)}, u32[]{:S(2)}, u32[]{:S(2)}) collective-permute-start(bf16[1280,256]{1,0:T(8,128)(2,1)} %get-tuple-element.29.p_ref), channel_id=1, source_target_pairs={{0,8},{8,16},{16,24},{24,0},{1,9},{9,17},{17,25},{25,1},{2,10},{10... | collective-permute-start | bytes 1966088 | tf_op jit(solution)/shard_map/ppermute | solution.py:338
  15.1 0.2 select_reduce_fusion
  15.2 0.1 reshape.110
  15.4 0.1 copy.19
  15.7 0.1 select_n.49
  15.8 0.1 fusion.p_ref
  15.9 2.9 %shard_map.121.refs_0_.refs_4_ = bf16[2048,256]{1,0:T(8,128)(2,1)} custom-call(s32[6]{0:T(128)} %stack.39.place_ref, bf16[1280,256]{1,0:T(8,128)(2,1)} %get-tuple-element.29.p_ref, bf16[256,6144]{1,0:T(8,128)(2,1)} %b_ref.3), custom_call_target="tpu_custom_call" | custom-call | tf_op jit(solution)/shard_map/pallas_call | solution.py:125
  18.9 3.3 %collective-permute-start = (bf16[1,2,2,64,512]{4,3,2,1,0:T(8,128)(2,1)S(1)}, bf16[1,2,2,64,512]{4,3,2,1,0:T(8,128)(2,1)S(1)}, u32[]{:S(2)}, u32[]{:S(2)}) collective-permute-start(bf16[1,2,2,64,512]{4,3,2,1,0:T(8,128)(2,1)S(1)} %maximum_bitcast_fusion), channel_id=1, source_target_pairs={{0,2},{2,0},{4,6},{6,4},{1,3},{3,1},{5,7},{7,5},{8,10},{10,8},{12,... | collective-permute-start | bytes 786440 | tf_op jit(solution)/shard_map/ppermute | solution.py:357
  22.2 4.2 %collective-permute-done = bf16[1,2,2,64,512]{4,3,2,1,0:T(8,128)(2,1)S(1)} collective-permute-done((bf16[1,2,2,64,512]{4,3,2,1,0:T(8,128)(2,1)S(1)}, bf16[1,2,2,64,512]{4,3,2,1,0:T(8,128)(2,1)S(1)}, u32[]{:S(2)}, u32[]{:S(2)}) %collective-permute-start) | collective-permute-done | bytes 262176 | tf_op jit(solution)/shard_map/ppermute | solution.py:357
  26.4 0.1 pad_maximum_fusion.1
  26.5 5.6 %collective-permute-start.1 = (bf16[2,2,2,64,512]{4,3,2,1,0:T(8,128)(2,1)S(1)}, bf16[2,2,2,64,512]{4,3,2,1,0:T(8,128)(2,1)S(1)}, u32[]{:S(2)}, u32[]{:S(2)}) collective-permute-start(bf16[2,2,2,64,512]{4,3,2,1,0:T(8,128)(2,1)S(1)} %pad_maximum_fusion.1), channel_id=1, source_target_pairs={{0,4},{2,6},{4,0},{6,2},{1,5},{3,7},{5,1},{7,3},{8,12},{10,14},{12... | collective-permute-start | bytes 1572872 | tf_op jit(solution)/shard_map/ppermute | solution.py:357
  32.1 9.2 %collective-permute-start.6 = (bf16[1280,256]{1,0:T(8,128)(2,1)S(1)}, bf16[1280,256]{1,0:T(8,128)(2,1)S(1)}, u32[]{:S(2)}, u32[]{:S(2)}) collective-permute-start(bf16[1280,256]{1,0:T(8,128)(2,1)S(1)} %collective-permute-done.3.refs_2_.refs_6_), channel_id=1, source_target_pairs={{0,1},{1,0},{2,3},{3,2},{4,5},{5,4},{6,7},{7,6},{8,9},{9,8},{10,11... | collective-permute-start | bytes 1966088 | tf_op jit(solution)/shard_map/ppermute | solution.py:360
  41.3 1.9 %collective-permute-start.7 = (bf16[1280,256]{1,0:T(8,128)(2,1)S(1)}, bf16[1280,256]{1,0:T(8,128)(2,1)S(1)}, u32[]{:S(2)}, u32[]{:S(2)}) collective-permute-start(bf16[1280,256]{1,0:T(8,128)(2,1)S(1)} %collective-permute-done.4.refs_3_.refs_7_), channel_id=1, source_target_pairs={{0,1},{1,0},{2,3},{3,2},{4,5},{5,4},{6,7},{7,6},{8,9},{9,8},{10,11... | collective-permute-start | bytes 1966088 | tf_op jit(solution)/shard_map/ppermute | solution.py:360
  43.2 1.2 collective-permute-done.2.refs_1_.refs_5_
  44.4 2.4 %collective-permute-start.5 = (bf16[1280,256]{1,0:T(8,128)(2,1)S(1)}, bf16[1280,256]{1,0:T(8,128)(2,1)S(1)}, u32[]{:S(2)}, u32[]{:S(2)}) collective-permute-start(bf16[1280,256]{1,0:T(8,128)(2,1)S(1)} %collective-permute-done.2.refs_1_.refs_5_), channel_id=1, source_target_pairs={{0,1},{1,0},{2,3},{3,2},{4,5},{5,4},{6,7},{7,6},{8,9},{9,8},{10,11... | collective-permute-start | bytes 1966088 | tf_op jit(solution)/shard_map/ppermute | solution.py:360
  46.8 0.1 pad_maximum_fusion.rm_ref
  46.9 1.6 collective-permute-done.5.refs_8_
  48.5 1.4 shard_map.123
  49.9 3.5 %collective-permute-start.8 = (bf16[128,1536]{1,0:T(8,128)(2,1)S(1)}, bf16[128,1536]{1,0:T(8,128)(2,1)S(1)}, u32[]{:S(2)}, u32[]{:S(2)}) collective-permute-start(bf16[128,1536]{1,0:T(8,128)(2,1)S(1)} %get-tuple-element.37), channel_id=1, source_target_pairs={{0,32},{32,64},{64,96},{96,128},{128,160},{160,192},{192,224},{224... | collective-permute-start | bytes 1179656 | tf_op jit(solution)/shard_map/ppermute | solution.py:368
  53.5 9.5 %collective-permute-start.11 = (bf16[128,1536]{1,0:T(8,128)(2,1)S(1)}, bf16[128,1536]{1,0:T(8,128)(2,1)S(1)}, u32[]{:S(2)}, u32[]{:S(2)}) collective-permute-start(bf16[128,1536]{1,0:T(8,128)(2,1)S(1)} %get-tuple-element.39), channel_id=1, source_target_pairs={{0,480},{32,0},{64,32},{96,64},{128,96},{160,128},{192,160},{224,1... | collective-permute-start | bytes 1179656 | tf_op jit(solution)/shard_map/ppermute | solution.py:368
  63.0 1.4 shard_map.122
  64.4 5.8 %collective-permute-done.8 = bf16[128,1536]{1,0:T(8,128)(2,1)S(1)} collective-permute-done((bf16[128,1536]{1,0:T(8,128)(2,1)S(1)}, bf16[128,1536]{1,0:T(8,128)(2,1)S(1)}, u32[]{:S(2)}, u32[]{:S(2)}) %collective-permute-start.8) | collective-permute-done | bytes 393248 | tf_op jit(solution)/shard_map/ppermute | solution.py:368
  70.2 1.9 %collective-permute-start.9 = (bf16[64,1536]{1,0:T(8,128)(2,1)S(1)}, bf16[64,1536]{1,0:T(8,128)(2,1)S(1)}, u32[]{:S(2)}, u32[]{:S(2)}) collective-permute-start(bf16[64,1536]{1,0:T(8,128)(2,1)S(1)} %add_convert_fusion.1), channel_id=1, source_target_pairs={{0,64},{32,96},{64,128},{96,160},{128,192},{160,224},{192,256},{22... | collective-permute-start | bytes 589832 | tf_op jit(solution)/shard_map/ppermute | solution.py:374
  72.3 5.6 %collective-permute-start.12 = (bf16[64,1536]{1,0:T(8,128)(2,1)S(1)}, bf16[64,1536]{1,0:T(8,128)(2,1)S(1)}, u32[]{:S(2)}, u32[]{:S(2)}) collective-permute-start(bf16[64,1536]{1,0:T(8,128)(2,1)S(1)} %add_convert_fusion), channel_id=1, source_target_pairs={{0,448},{32,480},{64,0},{96,32},{128,64},{160,96},{192,128},{224,1... | collective-permute-start | bytes 589832 | tf_op jit(solution)/shard_map/ppermute | solution.py:374
  77.9 4.2 %collective-permute-done.9 = bf16[64,1536]{1,0:T(8,128)(2,1)S(1)} collective-permute-done((bf16[64,1536]{1,0:T(8,128)(2,1)S(1)}, bf16[64,1536]{1,0:T(8,128)(2,1)S(1)}, u32[]{:S(2)}, u32[]{:S(2)}) %collective-permute-start.9) | collective-permute-done | bytes 196640 | tf_op jit(solution)/shard_map/ppermute | solution.py:374
  82.1 3.1 %collective-permute-start.10 = (bf16[32,1536]{1,0:T(8,128)(2,1)S(1)}, bf16[32,1536]{1,0:T(8,128)(2,1)S(1)}, u32[]{:S(2)}, u32[]{:S(2)}) collective-permute-start(bf16[32,1536]{1,0:T(8,128)(2,1)S(1)} %add_convert_fusion.5), channel_id=1, source_target_pairs={{0,128},{32,160},{64,192},{96,224},{128,256},{160,288},{192,320},{... | collective-permute-start | bytes 294920 | tf_op jit(solution)/shard_map/ppermute | solution.py:374
  85.3 6.3 %collective-permute-start.13 = (bf16[32,1536]{1,0:T(8,128)(2,1)S(1)}, bf16[32,1536]{1,0:T(8,128)(2,1)S(1)}, u32[]{:S(2)}, u32[]{:S(2)}) collective-permute-start(bf16[32,1536]{1,0:T(8,128)(2,1)S(1)} %add_convert_fusion.3), channel_id=1, source_target_pairs={{0,384},{32,416},{64,448},{96,480},{128,0},{160,32},{192,64},{224,... | collective-permute-start | bytes 294920 | tf_op jit(solution)/shard_map/ppermute | solution.py:374
  91.5 5.5 %collective-permute-done.10 = bf16[32,1536]{1,0:T(8,128)(2,1)S(1)} collective-permute-done((bf16[32,1536]{1,0:T(8,128)(2,1)S(1)}, bf16[32,1536]{1,0:T(8,128)(2,1)S(1)}, u32[]{:S(2)}, u32[]{:S(2)}) %collective-permute-start.10) | collective-permute-done | bytes 98336 | tf_op jit(solution)/shard_map/ppermute | solution.py:374
  97.1 0.1 add_convert_fusion.4
  97.2 11.5 %all-gather = bf16[256,1536]{1,0:T(8,128)(2,1)S(1)} all-gather(bf16[64,1536]{1,0:T(8,128)(2,1)S(1)} %pad_maximum_fusion.2), channel_id=2, replica_groups=mesh['z'=16,'x'=4,'y'=4,'c'=2] {'x'}, dimensions={0}, use_global_device_ids=true | all-gather | bytes 983040 | tf_op jit(solution)/shard_map/all_gather | solution.py:380
  108.7 1.3 shard_map.124
  110.0 11.5 %all-to-all-start = ((bf16[16,16,512]{2,1,0:T(8,128)(2,1)}), bf16[16,16,512]{2,1,0:T(8,128)(2,1)S(1)}, u32[]{:S(2)}, u32[]{:S(2)}) async-start(bf16[16,16,512]{2,1,0:T(8,128)(2,1)} %bitcast.11), calls=%async_computation | async-start | bytes 524288 | tf_op jit(solution)/shard_map/all_to_all | solution.py:383
  121.5 7.1 %collective-permute-start.15 = (bf16[4,2,2,64,512]{4,3,2,1,0:T(8,128)(2,1)S(1)}, bf16[4,2,2,64,512]{4,3,2,1,0:T(8,128)(2,1)S(1)}, u32[]{:S(2)}, u32[]{:S(2)}) collective-permute-start(bf16[4,2,2,64,512]{4,3,2,1,0:T(8,128)(2,1)S(1)} %pad_maximum_fusion.rm_ref), channel_id=1, source_target_pairs={{0,1},{1,0},{2,3},{3,2},{4,5},{5,4},{6,7},{7,6},{8,9},{9,8},{10,11... | collective-permute-start | bytes 3145736 | tf_op jit(solution)/shard_map/ppermute | solution.py:361
  128.6 0.2 fusion.9
  128.8 5.4 %all-to-all-done = bf16[16,16,512]{2,1,0:T(8,128)(2,1)S(1)} async-done(((bf16[16,16,512]{2,1,0:T(8,128)(2,1)}), bf16[16,16,512]{2,1,0:T(8,128)(2,1)S(1)}, u32[]{:S(2)}, u32[]{:S(2)}) %all-to-all-start) | async-done | bytes 262176 | tf_op jit(solution)/shard_map/all_to_all | solution.py:383
  134.2 1.5 shard_map.125
  135.7 10.8 %all-gather.1 = bf16[576,512]{1,0:T(8,128)(2,1)S(1)} all-gather(bf16[144,512]{1,0:T(8,128)(2,1)S(1)} %get-tuple-element.40), channel_id=3, replica_groups=mesh['z'=16,'x'=4,'y'=4,'c'=2] {'y'}, dimensions={0}, use_global_device_ids=true | all-gather | bytes 737280 | tf_op jit(solution)/shard_map/all_gather | solution.py:390
  146.6 12.4 %collective-permute-start.14 = (bf16[4,144,512]{2,1,0:T(8,128)(2,1)S(1)}, bf16[4,144,512]{2,1,0:T(8,128)(2,1)}, u32[]{:S(2)}, u32[]{:S(2)}) collective-permute-start(bf16[4,144,512]{2,1,0:T(8,128)(2,1)S(1)} %bitcast.48), channel_id=1, source_target_pairs={{0,1},{1,0},{2,3},{3,2},{4,5},{5,4},{6,7},{7,6},{8,9},{9,8},{10,11... | collective-permute-start | bytes 1769480 | tf_op jit(solution)/shard_map/ppermute | solution.py:391
  158.9 0.2 compare_reduce_fusion
  159.1 0.1 concatenate.13.f_ref
  159.2 1.5 collective-permute-done.14.o_ref
  160.7 5.1 %shard_map.126 = (f32[2,64,512]{2,1,0:T(8,128)}, f32[2,64,512]{2,1,0:T(8,128)}, bf16[2,512,512]{2,1,0:T(8,128)(2,1)}) custom-call(s32[7]{0:T(128)S(1)} %concatenate.13.f_ref, bf16[4,144,512]{2,1,0:T(8,128)(2,1)S(1)} %bitcast.49, bf16[4,144,512]{2,1,0:T(8,128)(2,1)} %collective-permute-done.14.o_ref, bf16[4,2,2,64,512]{4,3,2,1,0:T(8,128)(2,1)S(1)} %pad_maximum_fusion.rm_ref, ...), custom_call_target="tpu_custom_call" | custom-call | tf_op jit(solution)/shard_map/pallas_call | solution.py:296
  (39 shorter events, 0.5 us)
Async XLA Ops:
  0.6 14.4 %copy-start.7 = (s32[96]{0:T(128)S(1)}, s32[96]{0:T(128)}, u32[]{:S(2)}) copy-start(s32[96]{0:T(128)} %param.11) | copy-start | bytes 1156
  4.7 14.1 %copy-start.4 = (bf16[1,2,64,512]{3,2,1,0:T(8,128)(2,1)S(1)}, bf16[1,2,64,512]{3,2,1,0:T(8,128)(2,1)}, u32[]{:S(2)}) copy-start(bf16[1,2,64,512]{3,2,1,0:T(8,128)(2,1)} %param.16) | copy-start | bytes 393220
  4.7 14.1 %copy-start.5 = (bf16[1,2,64,512]{3,2,1,0:T(8,128)(2,1)S(1)}, bf16[1,2,64,512]{3,2,1,0:T(8,128)(2,1)}, u32[]{:S(2)}) copy-start(bf16[1,2,64,512]{3,2,1,0:T(8,128)(2,1)} %param.15) | copy-start | bytes 393220
  4.7 27.3 %collective-permute-start.3 = (bf16[1280,256]{1,0:T(8,128)(2,1)}, bf16[1280,256]{1,0:T(8,128)(2,1)S(1)}, u32[]{:S(2)}, u32[]{:S(2)}) collective-permute-start(bf16[1280,256]{1,0:T(8,128)(2,1)} %get-tuple-element.34), channel_id=1, source_target_pairs={{0,24},{8,0},{16,8},{24,16},{1,25},{9,1},{17,9},{25,17},{2,26},{10... | collective-permute-start | bytes 1966088 | tf_op jit(solution)/shard_map/ppermute | solution.py:338
  10.1 31.2 %collective-permute-start.4 = (bf16[1280,256]{1,0:T(8,128)(2,1)}, bf16[1280,256]{1,0:T(8,128)(2,1)S(1)}, u32[]{:S(2)}, u32[]{:S(2)}) collective-permute-start(bf16[1280,256]{1,0:T(8,128)(2,1)} %get-tuple-element.35), channel_id=1, source_target_pairs={{0,16},{8,24},{16,0},{24,8},{1,17},{9,25},{17,1},{25,9},{2,18},{10... | collective-permute-start | bytes 1966088 | tf_op jit(solution)/shard_map/ppermute | solution.py:338
  12.5 31.9 %collective-permute-start.2 = (bf16[1280,256]{1,0:T(8,128)(2,1)}, bf16[1280,256]{1,0:T(8,128)(2,1)S(1)}, u32[]{:S(2)}, u32[]{:S(2)}) collective-permute-start(bf16[1280,256]{1,0:T(8,128)(2,1)} %get-tuple-element.29.p_ref), channel_id=1, source_target_pairs={{0,8},{8,16},{16,24},{24,0},{1,9},{9,17},{17,25},{25,1},{2,10},{10... | collective-permute-start | bytes 1966088 | tf_op jit(solution)/shard_map/ppermute | solution.py:338
  18.8 29.7 %copy-start = (bf16[2048,256]{1,0:T(8,128)(2,1)S(1)}, bf16[2048,256]{1,0:T(8,128)(2,1)}, u32[]{:S(2)}) copy-start(bf16[2048,256]{1,0:T(8,128)(2,1)} %shard_map.121.refs_0_.refs_4_) | copy-start | bytes 3145732
  18.9 7.5 %collective-permute-start = (bf16[1,2,2,64,512]{4,3,2,1,0:T(8,128)(2,1)S(1)}, bf16[1,2,2,64,512]{4,3,2,1,0:T(8,128)(2,1)S(1)}, u32[]{:S(2)}, u32[]{:S(2)}) collective-permute-start(bf16[1,2,2,64,512]{4,3,2,1,0:T(8,128)(2,1)S(1)} %maximum_bitcast_fusion), channel_id=1, source_target_pairs={{0,2},{2,0},{4,6},{6,4},{1,3},{3,1},{5,7},{7,5},{8,10},{10,8},{12,... | collective-permute-start | bytes 786440 | tf_op jit(solution)/shard_map/ppermute | solution.py:357
  26.5 20.3 %collective-permute-start.1 = (bf16[2,2,2,64,512]{4,3,2,1,0:T(8,128)(2,1)S(1)}, bf16[2,2,2,64,512]{4,3,2,1,0:T(8,128)(2,1)S(1)}, u32[]{:S(2)}, u32[]{:S(2)}) collective-permute-start(bf16[2,2,2,64,512]{4,3,2,1,0:T(8,128)(2,1)S(1)} %pad_maximum_fusion.1), channel_id=1, source_target_pairs={{0,4},{2,6},{4,0},{6,2},{1,5},{3,7},{5,1},{7,3},{8,12},{10,14},{12... | collective-permute-start | bytes 1572872 | tf_op jit(solution)/shard_map/ppermute | solution.py:357
  32.1 14.9 %collective-permute-start.6 = (bf16[1280,256]{1,0:T(8,128)(2,1)S(1)}, bf16[1280,256]{1,0:T(8,128)(2,1)S(1)}, u32[]{:S(2)}, u32[]{:S(2)}) collective-permute-start(bf16[1280,256]{1,0:T(8,128)(2,1)S(1)} %collective-permute-done.3.refs_2_.refs_6_), channel_id=1, source_target_pairs={{0,1},{1,0},{2,3},{3,2},{4,5},{5,4},{6,7},{7,6},{8,9},{9,8},{10,11... | collective-permute-start | bytes 1966088 | tf_op jit(solution)/shard_map/ppermute | solution.py:360
  41.3 5.6 %collective-permute-start.7 = (bf16[1280,256]{1,0:T(8,128)(2,1)S(1)}, bf16[1280,256]{1,0:T(8,128)(2,1)S(1)}, u32[]{:S(2)}, u32[]{:S(2)}) collective-permute-start(bf16[1280,256]{1,0:T(8,128)(2,1)S(1)} %collective-permute-done.4.refs_3_.refs_7_), channel_id=1, source_target_pairs={{0,1},{1,0},{2,3},{3,2},{4,5},{5,4},{6,7},{7,6},{8,9},{9,8},{10,11... | collective-permute-start | bytes 1966088 | tf_op jit(solution)/shard_map/ppermute | solution.py:360
  44.4 4.1 %collective-permute-start.5 = (bf16[1280,256]{1,0:T(8,128)(2,1)S(1)}, bf16[1280,256]{1,0:T(8,128)(2,1)S(1)}, u32[]{:S(2)}, u32[]{:S(2)}) collective-permute-start(bf16[1280,256]{1,0:T(8,128)(2,1)S(1)} %collective-permute-done.2.refs_1_.refs_5_), channel_id=1, source_target_pairs={{0,1},{1,0},{2,3},{3,2},{4,5},{5,4},{6,7},{7,6},{8,9},{9,8},{10,11... | collective-permute-start | bytes 1966088 | tf_op jit(solution)/shard_map/ppermute | solution.py:360
  49.9 20.3 %collective-permute-start.8 = (bf16[128,1536]{1,0:T(8,128)(2,1)S(1)}, bf16[128,1536]{1,0:T(8,128)(2,1)S(1)}, u32[]{:S(2)}, u32[]{:S(2)}) collective-permute-start(bf16[128,1536]{1,0:T(8,128)(2,1)S(1)} %get-tuple-element.37), channel_id=1, source_target_pairs={{0,32},{32,64},{64,96},{96,128},{128,160},{160,192},{192,224},{224... | collective-permute-start | bytes 1179656 | tf_op jit(solution)/shard_map/ppermute | solution.py:368
  53.5 18.7 %collective-permute-start.11 = (bf16[128,1536]{1,0:T(8,128)(2,1)S(1)}, bf16[128,1536]{1,0:T(8,128)(2,1)S(1)}, u32[]{:S(2)}, u32[]{:S(2)}) collective-permute-start(bf16[128,1536]{1,0:T(8,128)(2,1)S(1)} %get-tuple-element.39), channel_id=1, source_target_pairs={{0,480},{32,0},{64,32},{96,64},{128,96},{160,128},{192,160},{224,1... | collective-permute-start | bytes 1179656 | tf_op jit(solution)/shard_map/ppermute | solution.py:368
  70.2 11.8 %collective-permute-start.9 = (bf16[64,1536]{1,0:T(8,128)(2,1)S(1)}, bf16[64,1536]{1,0:T(8,128)(2,1)S(1)}, u32[]{:S(2)}, u32[]{:S(2)}) collective-permute-start(bf16[64,1536]{1,0:T(8,128)(2,1)S(1)} %add_convert_fusion.1), channel_id=1, source_target_pairs={{0,64},{32,96},{64,128},{96,160},{128,192},{160,224},{192,256},{22... | collective-permute-start | bytes 589832 | tf_op jit(solution)/shard_map/ppermute | solution.py:374
  72.2 56.4 %copy-start.6 = (s32[96]{0:T(128)S(1)}, s32[96]{0:T(128)}, u32[]{:S(2)}) copy-start(s32[96]{0:T(128)} %param.12) | copy-start | bytes 1156
  72.2 62.0 %copy-start.3 = (f32[1,2,64,512]{3,2,1,0:T(8,128)S(1)}, f32[1,2,64,512]{3,2,1,0:T(8,128)}, u32[]{:S(2)}) copy-start(f32[1,2,64,512]{3,2,1,0:T(8,128)} %param.17) | copy-start | bytes 786436
  72.3 13.0 %collective-permute-start.12 = (bf16[64,1536]{1,0:T(8,128)(2,1)S(1)}, bf16[64,1536]{1,0:T(8,128)(2,1)S(1)}, u32[]{:S(2)}, u32[]{:S(2)}) collective-permute-start(bf16[64,1536]{1,0:T(8,128)(2,1)S(1)} %add_convert_fusion), channel_id=1, source_target_pairs={{0,448},{32,480},{64,0},{96,32},{128,64},{160,96},{192,128},{224,1... | collective-permute-start | bytes 589832 | tf_op jit(solution)/shard_map/ppermute | solution.py:374
  82.1 78.6 %copy-start.1 = (f32[1,2,64,512]{3,2,1,0:T(8,128)S(1)}, f32[1,2,64,512]{3,2,1,0:T(8,128)}, u32[]{:S(2)}) copy-start(f32[1,2,64,512]{3,2,1,0:T(8,128)} %param.13) | copy-start | bytes 786436
  82.1 78.6 %copy-start.2 = (f32[1,2,64,512]{3,2,1,0:T(8,128)S(1)}, f32[1,2,64,512]{3,2,1,0:T(8,128)}, u32[]{:S(2)}) copy-start(f32[1,2,64,512]{3,2,1,0:T(8,128)} %param.14) | copy-start | bytes 786436
  82.1 14.9 %collective-permute-start.10 = (bf16[32,1536]{1,0:T(8,128)(2,1)S(1)}, bf16[32,1536]{1,0:T(8,128)(2,1)S(1)}, u32[]{:S(2)}, u32[]{:S(2)}) collective-permute-start(bf16[32,1536]{1,0:T(8,128)(2,1)S(1)} %add_convert_fusion.5), channel_id=1, source_target_pairs={{0,128},{32,160},{64,192},{96,224},{128,256},{160,288},{192,320},{... | collective-permute-start | bytes 294920 | tf_op jit(solution)/shard_map/ppermute | solution.py:374
  85.3 11.9 %collective-permute-start.13 = (bf16[32,1536]{1,0:T(8,128)(2,1)S(1)}, bf16[32,1536]{1,0:T(8,128)(2,1)S(1)}, u32[]{:S(2)}, u32[]{:S(2)}) collective-permute-start(bf16[32,1536]{1,0:T(8,128)(2,1)S(1)} %add_convert_fusion.3), channel_id=1, source_target_pairs={{0,384},{32,416},{64,448},{96,480},{128,0},{160,32},{192,64},{224,... | collective-permute-start | bytes 294920 | tf_op jit(solution)/shard_map/ppermute | solution.py:374
  110.0 24.3 %all-to-all-start = ((bf16[16,16,512]{2,1,0:T(8,128)(2,1)}), bf16[16,16,512]{2,1,0:T(8,128)(2,1)S(1)}, u32[]{:S(2)}, u32[]{:S(2)}) async-start(bf16[16,16,512]{2,1,0:T(8,128)(2,1)} %bitcast.11), calls=%async_computation | async-start | bytes 524288 | tf_op jit(solution)/shard_map/all_to_all | solution.py:383
  121.5 37.8 %collective-permute-start.15 = (bf16[4,2,2,64,512]{4,3,2,1,0:T(8,128)(2,1)S(1)}, bf16[4,2,2,64,512]{4,3,2,1,0:T(8,128)(2,1)S(1)}, u32[]{:S(2)}, u32[]{:S(2)}) collective-permute-start(bf16[4,2,2,64,512]{4,3,2,1,0:T(8,128)(2,1)S(1)} %pad_maximum_fusion.rm_ref), channel_id=1, source_target_pairs={{0,1},{1,0},{2,3},{3,2},{4,5},{5,4},{6,7},{7,6},{8,9},{9,8},{10,11... | collective-permute-start | bytes 3145736 | tf_op jit(solution)/shard_map/ppermute | solution.py:361
  146.6 14.1 %collective-permute-start.14 = (bf16[4,144,512]{2,1,0:T(8,128)(2,1)S(1)}, bf16[4,144,512]{2,1,0:T(8,128)(2,1)}, u32[]{:S(2)}, u32[]{:S(2)}) collective-permute-start(bf16[4,144,512]{2,1,0:T(8,128)(2,1)S(1)} %bitcast.48), channel_id=1, source_target_pairs={{0,1},{1,0},{2,3},{3,2},{4,5},{5,4},{6,7},{7,6},{8,9},{9,8},{10,11... | collective-permute-start | bytes 1769480 | tf_op jit(solution)/shard_map/ppermute | solution.py:391

commit v6 on v5

--- a/solution.py
+++ b/solution.py
@@ -11,6 +11,7 @@
 WIDE = jnp.float32
 NZ, NX, NC = 16, 4, 2
 TILES = 6
+CHUNKS = 2
 ROOMY = pltpu.CompilerParams(vmem_limit_bytes=60 * 1024 * 1024)
 PARAMS = pltpu.CompilerParams(vmem_limit_bytes=8 * 1024 * 1024)
 
@@ -138,13 +139,13 @@
     )(place, piece, out_grads)
 
 
-def partial_products(own, arrived, swapped, odd):
+def partial_products(own, arrived, swapped, odd, chunk):
     toks = own.shape[1]
     half = toks // NC
     total_rows = own.shape[0] - TILES * toks
     count = total_rows // 2
     kind = HALF if odd else WIDE
-    group = 2
+    group = TILES // CHUNKS
 
     def kernel(*refs):
         rows_refs, own_ref, mine, other, (one_ref, two_ref) = refs[:4], refs[4], refs[5:8], refs[8:11], refs[11:]
@@ -157,22 +158,24 @@
             one_ref[:, to] = total[: count // 2].astype(kind)
             two_ref[:, to] = total[count // 2 :].astype(kind)
 
+    def block(skip, size):
+        first = pl.Element(size)
+        return pl.BlockSpec((first, pl.Element(toks)), lambda n: (skip + chunk * size, 0))
+
     rows = pl.BlockSpec((count, toks), lambda n: (0 if odd else 1, 0))
-    columns = pl.BlockSpec((group * half, toks), lambda n: (total_rows // (group * half) + n, 0))
-    own_columns = pl.BlockSpec((group * toks, toks), lambda n: (total_rows // (group * toks) + n, 0))
-    return pl.pallas_call(
-        kernel,
-        grid=(TILES // group,),
-        out_shape=[jax.ShapeDtypeStruct((count // 2, TILES * toks), kind)] * 2,
-        in_specs=[rows] * 4 + [own_columns] + [columns] * 6,
-        out_specs=[pl.BlockSpec((count // 2, group * toks), lambda n: (0, n))] * 2,
+    return pl.pallas_call(
+        kernel,
+        grid=(1,),
+        out_shape=[jax.ShapeDtypeStruct((count // 2, group * toks), kind)] * 2,
+        in_specs=[rows] * 4 + [block(total_rows, group * toks)] + [block(total_rows, group * half)] * 6,
+        out_specs=[pl.BlockSpec((count // 2, group * toks), lambda n: (0, 0))] * 2,
         compiler_params=PARAMS,
     )(own, *arrived, own, *arrived, *swapped)
 
 
 def pick_blocks(chosen, sums, block_size):
-    sources, rows, width = sums.shape
-    columns = width // block_size
+    sources, rows, width = sums.shape[0], sums.shape[1] // CHUNKS, sums.shape[2]
+    columns = CHUNKS * width // block_size
     out_rows = chosen.shape[0]
     tile = out_rows // 2
 
@@ -180,11 +183,10 @@
         total = None
         for pair in range(sources // 2):
             depth = 2 * columns * rows
-            pieces = [
-                s_ref[x, :, j * block_size : (j + 1) * block_size]
-                for x in (2 * pair, 2 * pair + 1)
-                for j in range(columns)
-            ]
+            pieces = []
+            for x in (2 * pair, 2 * pair + 1):
+                whole = jnp.concatenate([s_ref[x, k * rows : (k + 1) * rows, :] for k in range(CHUNKS)], axis=1)
+                pieces += [whole[:, j * block_size : (j + 1) * block_size] for j in range(columns)]
             term = dot(p_ref[:, pair * depth : (pair + 1) * depth], jnp.concatenate(pieces, axis=0))
             total = term if total is None else total + term
         o_ref[...] = total.astype(HALF)
@@ -333,9 +335,9 @@
     my_mp = y * NC + c
     my_rows = my_mp * rows
 
-    place = jnp.stack([z, x, c] + [jnp.bitwise_and(x + step, NX - 1) for step in (1, 3, 2)]).astype(jnp.int32)
+    place = jnp.stack([z, x, c] + [jnp.bitwise_and(x + step, NX - 1) for step in (2, 3, 1)]).astype(jnp.int32)
     pieces = prepare(activations, out_grads, place)
-    arrived = [lax.ppermute(piece, "x", ring(NX, step)) for piece, step in zip(pieces, (1, -1, 2))]
+    arrived = [lax.ppermute(piece, "x", ring(NX, step)) for piece, step in zip(pieces, (2, -1, 1))]
 
     piece_own, owners = lax.optimization_barrier((pieces[0], owners))
     targets = slot_targets(owners, slots)
@@ -360,11 +362,10 @@
     swapped = [lax.ppermute(piece, "c", ring(NC, 1)) for piece in arrived]
     roots_other = lax.ppermute(roots, "c", ring(NC, 1))
 
-    sent = partial_products(own, arrived, swapped, True)
-    kept = partial_products(own, arrived, swapped, False)
-
-    sums = []
-    for way, out, keep in ((1, sent[0], kept[0]), (-1, sent[1], kept[1])):
+    sent = [partial_products(own, arrived, swapped, True, chunk) for chunk in range(CHUNKS)]
+    kept = [partial_products(own, arrived, swapped, False, chunk) for chunk in range(CHUNKS)]
+
+    def add_along(out, keep, way):
         got = [lax.ppermute(out, "z", ring(NZ, way))]
         for step in (2, 4):
             part = got[-1].shape[0] // 2
@@ -376,7 +377,9 @@
         total = keep[:part]
         for rows_in in got:
             total = total + rows_in[:part]
-        sums.append(total.astype(HALF))
+        return total.astype(HALF)
+
+    sums = [add_along(sent[k][i], kept[k][i], (1, -1)[i]) for k in range(CHUNKS) for i in range(2)]
     sums = lax.all_gather(jnp.concatenate(sums, axis=0), "x", axis=0, tiled=False)
 
     picked = pick_blocks(chosen, sums, block_size).reshape(NZ, out_rows // NZ, block_size)

time: 167 us -> 171 us (1.024)
  starting transfers between devices: 93.6 us -> 110 us
  waiting for transfers between devices: 29.4 us -> 17.5 us
    ppermute x6 -> x12, starting transfers between devices: 29.9 us -> 50.6 us  [the longest x8 31 us: add_along(): got.append(lax.ppermute(out.astype(HALF), 'z', ring(NZ, way * step)))]
    ppermute x6 -> x12, waiting for transfers between devices: 15.6 us -> 4.64 us  [the longest x8 4.63 us: add_along(): got.append(lax.ppermute(out.astype(HALF), 'z', ring(NZ, way * step)))]
    all_to_all x1, starting transfers between devices: 11.5 us -> 7.38 us  [body(): lax.all_to_all(picked, 'z', 0, 0, tiled=True).reshape(out_rows, block_size)]
    ppermute x3, starting transfers between devices: 13.5 us -> 9.9 us  [body(): swapped = [lax.ppermute(piece, 'c', ring(NC, 1)) for piece in arrived]]
    ppermute x1, starting transfers between devices: 7.14 us -> 9.25 us  [body(): roots_other = lax.ppermute(roots, 'c', ring(NC, 1))]
    all_to_all x1, waiting for transfers between devices: 5.4 us -> 3.38 us  [body(): lax.all_to_all(picked, 'z', 0, 0, tiled=True).reshape(out_rows, block_size)]
  transfers between devices with their start and end apart: 17 -> 23, of which waited for: 8 -> 6; matrix products, arithmetic and copies ran while one was open for 1% -> 1% of each run, Pallas kernels for 4% -> 4%
where the time goes in v6:
time: 171 us; the launch traced here: 170 us
  starting transfers between devices  110 us (64%)
  blocking collectives  22.6 us (13%)
  waiting for transfers between devices  17.5 us (10%)
  Pallas kernels  16.5 us (10%)
    ppermute x8, starting transfers between devices, add_along(): got.append(lax.ppermute(out.astype(HALF), 'z', ring(NZ, way * step)))  31 us
    ppermute x4, starting transfers between devices, add_along(): got = [lax.ppermute(out, 'z', ring(NZ, way))]  19.5 us
    ppermute x1, starting transfers between devices, body(): rows_other = lax.ppermute(rows_mine, 'c', ring(NC, 1))  12.9 us
    all_gather x1, blocking collectives, body(): lax.all_gather(jnp.concatenate(sums, axis=0), 'x', axis=0, tiled=False)  11.5 us
    all_gather x1, blocking collectives, body(): rows_mine = lax.all_gather(own_rows, 'y', axis=0, tiled=False)  11.1 us
    ppermute x3, starting transfers between devices, body(): lax.ppermute(piece, 'x', ring(NX, step))  10.9 us
    ppermute x3, starting transfers between devices, body(): swapped = [lax.ppermute(piece, 'c', ring(NC, 1)) for piece in arrived]  9.9 us
    ppermute x1, starting transfers between devices, body(): roots_other = lax.ppermute(roots, 'c', ring(NC, 1))  9.25 us
  transfers between devices with their start and end apart: 23, of which 6 were waited for; matrix products, arithmetic and copies ran while one was open for 1% of the time, Pallas kernels for 4%

profile of v6, /device:TPU:1, one launch (start us, length us, event | category | flops | bytes accessed | tf_op | source)
XLA Modules:
  0.0 170.1 jit_solution(5225771363677652716)
XLA Ops:
  0.7 0.7 stack.39.place_ref
  1.3 3.4 %shard_map.120 = (bf16[1280,256]{1,0:T(8,128)(2,1)}, bf16[1280,256]{1,0:T(8,128)(2,1)}, bf16[1280,256]{1,0:T(8,128)(2,1)}) custom-call(s32[6]{0:T(128)} %stack.39.place_ref, bf16[8,64,256]{2,1,0:T(8,128)(2,1)} %a_ref.1, bf16[256,6144]{1,0:T(8,128)(2,1)} %b_ref.3), custom_call_target="tpu_custom_call" | custom-call | tf_op jit(solution)/shard_map/pallas_call | solution.py:91
  4.8 5.6 %collective-permute-start.2 = (bf16[1280,256]{1,0:T(8,128)(2,1)}, bf16[1280,256]{1,0:T(8,128)(2,1)S(1)}, u32[]{:S(2)}, u32[]{:S(2)}) collective-permute-start(bf16[1280,256]{1,0:T(8,128)(2,1)} %get-tuple-element.33.p_ref), channel_id=1, source_target_pairs={{0,16},{8,24},{16,0},{24,8},{1,17},{9,25},{17,1},{25,9},{2,18},{10... | collective-permute-start | bytes 1966088 | tf_op jit(solution)/shard_map/ppermute | solution.py:340
  10.4 2.8 %collective-permute-start.3 = (bf16[1280,256]{1,0:T(8,128)(2,1)}, bf16[1280,256]{1,0:T(8,128)(2,1)S(1)}, u32[]{:S(2)}, u32[]{:S(2)}) collective-permute-start(bf16[1280,256]{1,0:T(8,128)(2,1)} %get-tuple-element.38), channel_id=1, source_target_pairs={{0,24},{8,0},{16,8},{24,16},{1,25},{9,1},{17,9},{25,17},{2,26},{10... | collective-permute-start | bytes 1966088 | tf_op jit(solution)/shard_map/ppermute | solution.py:340
  13.2 2.5 %collective-permute-start.4 = (bf16[1280,256]{1,0:T(8,128)(2,1)}, bf16[1280,256]{1,0:T(8,128)(2,1)S(1)}, u32[]{:S(2)}, u32[]{:S(2)}) collective-permute-start(bf16[1280,256]{1,0:T(8,128)(2,1)} %get-tuple-element.39), channel_id=1, source_target_pairs={{0,8},{8,16},{16,24},{24,0},{1,9},{9,17},{17,25},{25,1},{2,10},{10... | collective-permute-start | bytes 1966088 | tf_op jit(solution)/shard_map/ppermute | solution.py:340
  15.7 0.2 select_reduce_fusion
  15.9 0.1 reshape.110
  16.0 0.1 copy.19
  16.3 0.1 select_n.49
  16.5 2.9 %shard_map.121.refs_0_.refs_4_ = bf16[2048,256]{1,0:T(8,128)(2,1)} custom-call(s32[6]{0:T(128)} %stack.39.place_ref, bf16[1280,256]{1,0:T(8,128)(2,1)} %get-tuple-element.33.p_ref, bf16[256,6144]{1,0:T(8,128)(2,1)} %b_ref.3), custom_call_target="tpu_custom_call" | custom-call | tf_op jit(solution)/shard_map/pallas_call | solution.py:126
  19.5 3.3 %collective-permute-start = (bf16[1,2,2,64,512]{4,3,2,1,0:T(8,128)(2,1)S(1)}, bf16[1,2,2,64,512]{4,3,2,1,0:T(8,128)(2,1)S(1)}, u32[]{:S(2)}, u32[]{:S(2)}) collective-permute-start(bf16[1,2,2,64,512]{4,3,2,1,0:T(8,128)(2,1)S(1)} %maximum_bitcast_fusion), channel_id=1, source_target_pairs={{0,2},{2,0},{4,6},{6,4},{1,3},{3,1},{5,7},{7,5},{8,10},{10,8},{12,... | collective-permute-start | bytes 786440 | tf_op jit(solution)/shard_map/ppermute | solution.py:359
  22.9 4.2 %collective-permute-done = bf16[1,2,2,64,512]{4,3,2,1,0:T(8,128)(2,1)S(1)} collective-permute-done((bf16[1,2,2,64,512]{4,3,2,1,0:T(8,128)(2,1)S(1)}, bf16[1,2,2,64,512]{4,3,2,1,0:T(8,128)(2,1)S(1)}, u32[]{:S(2)}, u32[]{:S(2)}) %collective-permute-start) | collective-permute-done | bytes 262176 | tf_op jit(solution)/shard_map/ppermute | solution.py:359
  27.1 5.6 %collective-permute-start.1 = (bf16[2,2,2,64,512]{4,3,2,1,0:T(8,128)(2,1)S(1)}, bf16[2,2,2,64,512]{4,3,2,1,0:T(8,128)(2,1)S(1)}, u32[]{:S(2)}, u32[]{:S(2)}) collective-permute-start(bf16[2,2,2,64,512]{4,3,2,1,0:T(8,128)(2,1)S(1)} %pad_maximum_fusion.1), channel_id=1, source_target_pairs={{0,4},{2,6},{4,0},{6,2},{1,5},{3,7},{5,1},{7,3},{8,12},{10,14},{12... | collective-permute-start | bytes 1572872 | tf_op jit(solution)/shard_map/ppermute | solution.py:359
  32.7 4.6 %collective-permute-start.5 = (bf16[1280,256]{1,0:T(8,128)(2,1)S(1)}, bf16[1280,256]{1,0:T(8,128)(2,1)S(1)}, u32[]{:S(2)}, u32[]{:S(2)}) collective-permute-start(bf16[1280,256]{1,0:T(8,128)(2,1)S(1)} %collective-permute-done.2.refs_1_.refs_5_), channel_id=1, source_target_pairs={{0,1},{1,0},{2,3},{3,2},{4,5},{5,4},{6,7},{7,6},{8,9},{9,8},{10,11... | collective-permute-start | bytes 1966088 | tf_op jit(solution)/shard_map/ppermute | solution.py:362
  37.3 1.9 %collective-permute-done.3.refs_2_.refs_6_ = bf16[1280,256]{1,0:T(8,128)(2,1)S(1)} collective-permute-done((bf16[1280,256]{1,0:T(8,128)(2,1)}, bf16[1280,256]{1,0:T(8,128)(2,1)S(1)}, u32[]{:S(2)}, u32[]{:S(2)}) %collective-permute-start.3) | collective-permute-done | bytes 655392 | tf_op jit(solution)/shard_map/ppermute | solution.py:340
  39.2 3.3 %collective-permute-start.6 = (bf16[1280,256]{1,0:T(8,128)(2,1)S(1)}, bf16[1280,256]{1,0:T(8,128)(2,1)S(1)}, u32[]{:S(2)}, u32[]{:S(2)}) collective-permute-start(bf16[1280,256]{1,0:T(8,128)(2,1)S(1)} %collective-permute-done.3.refs_2_.refs_6_), channel_id=1, source_target_pairs={{0,1},{1,0},{2,3},{3,2},{4,5},{5,4},{6,7},{7,6},{8,9},{9,8},{10,11... | collective-permute-start | bytes 1966088 | tf_op jit(solution)/shard_map/ppermute | solution.py:362
  42.6 1.9 %collective-permute-start.7 = (bf16[1280,256]{1,0:T(8,128)(2,1)S(1)}, bf16[1280,256]{1,0:T(8,128)(2,1)S(1)}, u32[]{:S(2)}, u32[]{:S(2)}) collective-permute-start(bf16[1280,256]{1,0:T(8,128)(2,1)S(1)} %collective-permute-done.4.refs_3_.refs_7_), channel_id=1, source_target_pairs={{0,1},{1,0},{2,3},{3,2},{4,5},{5,4},{6,7},{7,6},{8,9},{9,8},{10,11... | collective-permute-start | bytes 1966088 | tf_op jit(solution)/shard_map/ppermute | solution.py:362
  44.5 0.1 pad_maximum_fusion.rm_ref
  44.6 1.9 %collective-permute-done.7.refs_10_ = bf16[1280,256]{1,0:T(8,128)(2,1)S(1)} collective-permute-done((bf16[1280,256]{1,0:T(8,128)(2,1)S(1)}, bf16[1280,256]{1,0:T(8,128)(2,1)S(1)}, u32[]{:S(2)}, u32[]{:S(2)}) %collective-permute-start.7) | collective-permute-done | bytes 655392 | tf_op jit(solution)/shard_map/ppermute | solution.py:362
  46.6 0.6 shard_map.125
  47.2 11.1 %collective-permute-start.17 = (bf16[128,768]{1,0:T(8,128)(2,1)S(1)}, bf16[128,768]{1,0:T(8,128)(2,1)S(1)}, u32[]{:S(2)}, u32[]{:S(2)}) collective-permute-start(bf16[128,768]{1,0:T(8,128)(2,1)S(1)} %get-tuple-element.47), channel_id=1, source_target_pairs={{0,480},{32,0},{64,32},{96,64},{128,96},{160,128},{192,160},{224,1... | collective-permute-start | bytes 589832 | tf_op jit(solution)/shard_map/ppermute | solution.py:369
  58.3 1.9 %collective-permute-start.14 = (bf16[128,768]{1,0:T(8,128)(2,1)S(1)}, bf16[128,768]{1,0:T(8,128)(2,1)S(1)}, u32[]{:S(2)}, u32[]{:S(2)}) collective-permute-start(bf16[128,768]{1,0:T(8,128)(2,1)S(1)} %get-tuple-element.45), channel_id=1, source_target_pairs={{0,32},{32,64},{64,96},{96,128},{128,160},{160,192},{192,224},{224... | collective-permute-start | bytes 589832 | tf_op jit(solution)/shard_map/ppermute | solution.py:369
  60.2 0.6 shard_map.123
  60.8 4.6 %collective-permute-start.11 = (bf16[128,768]{1,0:T(8,128)(2,1)S(1)}, bf16[128,768]{1,0:T(8,128)(2,1)S(1)}, u32[]{:S(2)}, u32[]{:S(2)}) collective-permute-start(bf16[128,768]{1,0:T(8,128)(2,1)S(1)} %get-tuple-element.43), channel_id=1, source_target_pairs={{0,480},{32,0},{64,32},{96,64},{128,96},{160,128},{192,160},{224,1... | collective-permute-start | bytes 589832 | tf_op jit(solution)/shard_map/ppermute | solution.py:369
  65.4 1.9 %collective-permute-start.8 = (bf16[128,768]{1,0:T(8,128)(2,1)S(1)}, bf16[128,768]{1,0:T(8,128)(2,1)S(1)}, u32[]{:S(2)}, u32[]{:S(2)}) collective-permute-start(bf16[128,768]{1,0:T(8,128)(2,1)S(1)} %get-tuple-element.41), channel_id=1, source_target_pairs={{0,32},{32,64},{64,96},{96,128},{128,160},{160,192},{192,224},{224... | collective-permute-start | bytes 589832 | tf_op jit(solution)/shard_map/ppermute | solution.py:369
  67.3 0.6 shard_map.124
  67.9 0.6 shard_map.122
  68.5 3.1 %collective-permute-start.18 = (bf16[64,768]{1,0:T(8,128)(2,1)S(1)}, bf16[64,768]{1,0:T(8,128)(2,1)S(1)}, u32[]{:S(2)}, u32[]{:S(2)}) collective-permute-start(bf16[64,768]{1,0:T(8,128)(2,1)S(1)} %add_convert_fusion), channel_id=1, source_target_pairs={{0,448},{32,480},{64,0},{96,32},{128,64},{160,96},{192,128},{224,1... | collective-permute-start | bytes 294920 | tf_op jit(solution)/shard_map/ppermute | solution.py:375
  71.7 3.1 %collective-permute-start.15 = (bf16[64,768]{1,0:T(8,128)(2,1)S(1)}, bf16[64,768]{1,0:T(8,128)(2,1)S(1)}, u32[]{:S(2)}, u32[]{:S(2)}) collective-permute-start(bf16[64,768]{1,0:T(8,128)(2,1)S(1)} %add_convert_fusion.1), channel_id=1, source_target_pairs={{0,64},{32,96},{64,128},{96,160},{128,192},{160,224},{192,256},{22... | collective-permute-start | bytes 294920 | tf_op jit(solution)/shard_map/ppermute | solution.py:375
  74.8 4.4 %collective-permute-start.12 = (bf16[64,768]{1,0:T(8,128)(2,1)S(1)}, bf16[64,768]{1,0:T(8,128)(2,1)S(1)}, u32[]{:S(2)}, u32[]{:S(2)}) collective-permute-start(bf16[64,768]{1,0:T(8,128)(2,1)S(1)} %add_convert_fusion.2), channel_id=1, source_target_pairs={{0,448},{32,480},{64,0},{96,32},{128,64},{160,96},{192,128},{224,1... | collective-permute-start | bytes 294920 | tf_op jit(solution)/shard_map/ppermute | solution.py:375
  79.3 1.9 %collective-permute-start.9 = (bf16[64,768]{1,0:T(8,128)(2,1)S(1)}, bf16[64,768]{1,0:T(8,128)(2,1)S(1)}, u32[]{:S(2)}, u32[]{:S(2)}) collective-permute-start(bf16[64,768]{1,0:T(8,128)(2,1)S(1)} %add_convert_fusion.3), channel_id=1, source_target_pairs={{0,64},{32,96},{64,128},{96,160},{128,192},{160,224},{192,256},{22... | collective-permute-start | bytes 294920 | tf_op jit(solution)/shard_map/ppermute | solution.py:375
  81.3 5.2 %collective-permute-start.19 = (bf16[32,768]{1,0:T(8,128)(2,1)S(1)}, bf16[32,768]{1,0:T(8,128)(2,1)S(1)}, u32[]{:S(2)}, u32[]{:S(2)}) collective-permute-start(bf16[32,768]{1,0:T(8,128)(2,1)S(1)} %add_convert_fusion.5), channel_id=1, source_target_pairs={{0,384},{32,416},{64,448},{96,480},{128,0},{160,32},{192,64},{224,... | collective-permute-start | bytes 147464 | tf_op jit(solution)/shard_map/ppermute | solution.py:375
  86.5 4.1 %collective-permute-start.16 = (bf16[32,768]{1,0:T(8,128)(2,1)S(1)}, bf16[32,768]{1,0:T(8,128)(2,1)S(1)}, u32[]{:S(2)}, u32[]{:S(2)}) collective-permute-start(bf16[32,768]{1,0:T(8,128)(2,1)S(1)} %add_convert_fusion.7), channel_id=1, source_target_pairs={{0,128},{32,160},{64,192},{96,224},{128,256},{160,288},{192,320},{... | collective-permute-start | bytes 147464 | tf_op jit(solution)/shard_map/ppermute | solution.py:375
  90.7 5.2 %collective-permute-start.13 = (bf16[32,768]{1,0:T(8,128)(2,1)S(1)}, bf16[32,768]{1,0:T(8,128)(2,1)S(1)}, u32[]{:S(2)}, u32[]{:S(2)}) collective-permute-start(bf16[32,768]{1,0:T(8,128)(2,1)S(1)} %add_convert_fusion.9), channel_id=1, source_target_pairs={{0,384},{32,416},{64,448},{96,480},{128,0},{160,32},{192,64},{224,... | collective-permute-start | bytes 147464 | tf_op jit(solution)/shard_map/ppermute | solution.py:375
  95.9 4.0 %collective-permute-start.10 = (bf16[32,768]{1,0:T(8,128)(2,1)S(1)}, bf16[32,768]{1,0:T(8,128)(2,1)S(1)}, u32[]{:S(2)}, u32[]{:S(2)}) collective-permute-start(bf16[32,768]{1,0:T(8,128)(2,1)S(1)} %add_convert_fusion.11), channel_id=1, source_target_pairs={{0,128},{32,160},{64,192},{96,224},{128,256},{160,288},{192,320},{... | collective-permute-start | bytes 147464 | tf_op jit(solution)/shard_map/ppermute | solution.py:375
  100.1 4.6 %collective-permute-done.10 = bf16[32,768]{1,0:T(8,128)(2,1)S(1)} collective-permute-done((bf16[32,768]{1,0:T(8,128)(2,1)S(1)}, bf16[32,768]{1,0:T(8,128)(2,1)S(1)}, u32[]{:S(2)}, u32[]{:S(2)}) %collective-permute-start.10) | collective-permute-done | bytes 49184 | tf_op jit(solution)/shard_map/ppermute | solution.py:375
  104.8 11.5 %all-gather = bf16[512,768]{1,0:T(8,128)(2,1)S(1)} all-gather(bf16[128,768]{1,0:T(8,128)(2,1)S(1)} %pad_maximum_fusion.2), channel_id=2, replica_groups=mesh['z'=16,'x'=4,'y'=4,'c'=2] {'x'}, dimensions={0}, use_global_device_ids=true | all-gather | bytes 983040 | tf_op jit(solution)/shard_map/all_gather | solution.py:383
  116.2 1.3 shard_map.126
  117.5 7.4 %all-to-all-start = ((bf16[16,16,512]{2,1,0:T(8,128)(2,1)}), bf16[16,16,512]{2,1,0:T(8,128)(2,1)S(1)}, u32[]{:S(2)}, u32[]{:S(2)}) async-start(bf16[16,16,512]{2,1,0:T(8,128)(2,1)} %bitcast.11), calls=%async_computation | async-start | bytes 524288 | tf_op jit(solution)/shard_map/all_to_all | solution.py:386
  124.9 9.2 %collective-permute-start.21 = (bf16[4,2,2,64,512]{4,3,2,1,0:T(8,128)(2,1)S(1)}, bf16[4,2,2,64,512]{4,3,2,1,0:T(8,128)(2,1)S(1)}, u32[]{:S(2)}, u32[]{:S(2)}) collective-permute-start(bf16[4,2,2,64,512]{4,3,2,1,0:T(8,128)(2,1)S(1)} %pad_maximum_fusion.rm_ref), channel_id=1, source_target_pairs={{0,1},{1,0},{2,3},{3,2},{4,5},{5,4},{6,7},{7,6},{8,9},{9,8},{10,11... | collective-permute-start | bytes 3145736 | tf_op jit(solution)/shard_map/ppermute | solution.py:363
  134.2 0.2 fusion.9
  134.4 3.4 %all-to-all-done = bf16[16,16,512]{2,1,0:T(8,128)(2,1)S(1)} async-done(((bf16[16,16,512]{2,1,0:T(8,128)(2,1)}), bf16[16,16,512]{2,1,0:T(8,128)(2,1)S(1)}, u32[]{:S(2)}, u32[]{:S(2)}) %all-to-all-start) | async-done | bytes 262176 | tf_op jit(solution)/shard_map/all_to_all | solution.py:386
  137.8 1.5 shard_map.127
  139.3 11.1 %all-gather.1 = bf16[576,512]{1,0:T(8,128)(2,1)S(1)} all-gather(bf16[144,512]{1,0:T(8,128)(2,1)S(1)} %get-tuple-element.48), channel_id=3, replica_groups=mesh['z'=16,'x'=4,'y'=4,'c'=2] {'y'}, dimensions={0}, use_global_device_ids=true | all-gather | bytes 737280 | tf_op jit(solution)/shard_map/all_gather | solution.py:393
  150.4 12.9 %collective-permute-start.20 = (bf16[4,144,512]{2,1,0:T(8,128)(2,1)S(1)}, bf16[4,144,512]{2,1,0:T(8,128)(2,1)}, u32[]{:S(2)}, u32[]{:S(2)}) collective-permute-start(bf16[4,144,512]{2,1,0:T(8,128)(2,1)S(1)} %bitcast.48), channel_id=1, source_target_pairs={{0,1},{1,0},{2,3},{3,2},{4,5},{5,4},{6,7},{7,6},{8,9},{9,8},{10,11... | collective-permute-start | bytes 1769480 | tf_op jit(solution)/shard_map/ppermute | solution.py:394
  163.3 0.2 compare_reduce_fusion
  163.6 1.5 collective-permute-done.20.o_ref
  165.0 5.1 %shard_map.128 = (f32[2,64,512]{2,1,0:T(8,128)}, f32[2,64,512]{2,1,0:T(8,128)}, bf16[2,512,512]{2,1,0:T(8,128)(2,1)}) custom-call(s32[7]{0:T(128)S(1)} %concatenate.13.f_ref, bf16[4,144,512]{2,1,0:T(8,128)(2,1)S(1)} %bitcast.49, bf16[4,144,512]{2,1,0:T(8,128)(2,1)} %collective-permute-done.20.o_ref, bf16[4,2,2,64,512]{4,3,2,1,0:T(8,128)(2,1)S(1)} %pad_maximum_fusion.rm_ref, ...), custom_call_target="tpu_custom_call" | custom-call | tf_op jit(solution)/shard_map/pallas_call | solution.py:298
  (59 shorter events, 0.8 us)
Async XLA Ops:
  0.6 15.1 %copy-start.7 = (s32[96]{0:T(128)S(1)}, s32[96]{0:T(128)}, u32[]{:S(2)}) copy-start(s32[96]{0:T(128)} %param.11) | copy-start | bytes 1156
  4.7 14.7 %copy-start.4 = (bf16[1,2,64,512]{3,2,1,0:T(8,128)(2,1)S(1)}, bf16[1,2,64,512]{3,2,1,0:T(8,128)(2,1)}, u32[]{:S(2)}) copy-start(bf16[1,2,64,512]{3,2,1,0:T(8,128)(2,1)} %param.16) | copy-start | bytes 393220
  4.8 14.7 %copy-start.5 = (bf16[1,2,64,512]{3,2,1,0:T(8,128)(2,1)S(1)}, bf16[1,2,64,512]{3,2,1,0:T(8,128)(2,1)}, u32[]{:S(2)}) copy-start(bf16[1,2,64,512]{3,2,1,0:T(8,128)(2,1)} %param.15) | copy-start | bytes 393220
  4.8 27.9 %collective-permute-start.2 = (bf16[1280,256]{1,0:T(8,128)(2,1)}, bf16[1280,256]{1,0:T(8,128)(2,1)S(1)}, u32[]{:S(2)}, u32[]{:S(2)}) collective-permute-start(bf16[1280,256]{1,0:T(8,128)(2,1)} %get-tuple-element.33.p_ref), channel_id=1, source_target_pairs={{0,16},{8,24},{16,0},{24,8},{1,17},{9,25},{17,1},{25,9},{2,18},{10... | collective-permute-start | bytes 1966088 | tf_op jit(solution)/shard_map/ppermute | solution.py:340
  10.4 28.8 %collective-permute-start.3 = (bf16[1280,256]{1,0:T(8,128)(2,1)}, bf16[1280,256]{1,0:T(8,128)(2,1)S(1)}, u32[]{:S(2)}, u32[]{:S(2)}) collective-permute-start(bf16[1280,256]{1,0:T(8,128)(2,1)} %get-tuple-element.38), channel_id=1, source_target_pairs={{0,24},{8,0},{16,8},{24,16},{1,25},{9,1},{17,9},{25,17},{2,26},{10... | collective-permute-start | bytes 1966088 | tf_op jit(solution)/shard_map/ppermute | solution.py:340
  13.2 29.4 %collective-permute-start.4 = (bf16[1280,256]{1,0:T(8,128)(2,1)}, bf16[1280,256]{1,0:T(8,128)(2,1)S(1)}, u32[]{:S(2)}, u32[]{:S(2)}) collective-permute-start(bf16[1280,256]{1,0:T(8,128)(2,1)} %get-tuple-element.39), channel_id=1, source_target_pairs={{0,8},{8,16},{16,24},{24,0},{1,9},{9,17},{17,25},{25,1},{2,10},{10... | collective-permute-start | bytes 1966088 | tf_op jit(solution)/shard_map/ppermute | solution.py:340
  19.5 27.1 %copy-start = (bf16[2048,256]{1,0:T(8,128)(2,1)S(1)}, bf16[2048,256]{1,0:T(8,128)(2,1)}, u32[]{:S(2)}) copy-start(bf16[2048,256]{1,0:T(8,128)(2,1)} %shard_map.121.refs_0_.refs_4_) | copy-start | bytes 3145732
  19.5 7.5 %collective-permute-start = (bf16[1,2,2,64,512]{4,3,2,1,0:T(8,128)(2,1)S(1)}, bf16[1,2,2,64,512]{4,3,2,1,0:T(8,128)(2,1)S(1)}, u32[]{:S(2)}, u32[]{:S(2)}) collective-permute-start(bf16[1,2,2,64,512]{4,3,2,1,0:T(8,128)(2,1)S(1)} %maximum_bitcast_fusion), channel_id=1, source_target_pairs={{0,2},{2,0},{4,6},{6,4},{1,3},{3,1},{5,7},{7,5},{8,10},{10,8},{12,... | collective-permute-start | bytes 786440 | tf_op jit(solution)/shard_map/ppermute | solution.py:359
  27.1 17.4 %collective-permute-start.1 = (bf16[2,2,2,64,512]{4,3,2,1,0:T(8,128)(2,1)S(1)}, bf16[2,2,2,64,512]{4,3,2,1,0:T(8,128)(2,1)S(1)}, u32[]{:S(2)}, u32[]{:S(2)}) collective-permute-start(bf16[2,2,2,64,512]{4,3,2,1,0:T(8,128)(2,1)S(1)} %pad_maximum_fusion.1), channel_id=1, source_target_pairs={{0,4},{2,6},{4,0},{6,2},{1,5},{3,7},{5,1},{7,3},{8,12},{10,14},{12... | collective-permute-start | bytes 1572872 | tf_op jit(solution)/shard_map/ppermute | solution.py:359
  32.7 11.9 %collective-permute-start.5 = (bf16[1280,256]{1,0:T(8,128)(2,1)S(1)}, bf16[1280,256]{1,0:T(8,128)(2,1)S(1)}, u32[]{:S(2)}, u32[]{:S(2)}) collective-permute-start(bf16[1280,256]{1,0:T(8,128)(2,1)S(1)} %collective-permute-done.2.refs_1_.refs_5_), channel_id=1, source_target_pairs={{0,1},{1,0},{2,3},{3,2},{4,5},{5,4},{6,7},{7,6},{8,9},{9,8},{10,11... | collective-permute-start | bytes 1966088 | tf_op jit(solution)/shard_map/ppermute | solution.py:362
  39.2 5.4 %collective-permute-start.6 = (bf16[1280,256]{1,0:T(8,128)(2,1)S(1)}, bf16[1280,256]{1,0:T(8,128)(2,1)S(1)}, u32[]{:S(2)}, u32[]{:S(2)}) collective-permute-start(bf16[1280,256]{1,0:T(8,128)(2,1)S(1)} %collective-permute-done.3.refs_2_.refs_6_), channel_id=1, source_target_pairs={{0,1},{1,0},{2,3},{3,2},{4,5},{5,4},{6,7},{7,6},{8,9},{9,8},{10,11... | collective-permute-start | bytes 1966088 | tf_op jit(solution)/shard_map/ppermute | solution.py:362
  42.6 4.0 %collective-permute-start.7 = (bf16[1280,256]{1,0:T(8,128)(2,1)S(1)}, bf16[1280,256]{1,0:T(8,128)(2,1)S(1)}, u32[]{:S(2)}, u32[]{:S(2)}) collective-permute-start(bf16[1280,256]{1,0:T(8,128)(2,1)S(1)} %collective-permute-done.4.refs_3_.refs_7_), channel_id=1, source_target_pairs={{0,1},{1,0},{2,3},{3,2},{4,5},{5,4},{6,7},{7,6},{8,9},{9,8},{10,11... | collective-permute-start | bytes 1966088 | tf_op jit(solution)/shard_map/ppermute | solution.py:362
  47.2 21.3 %collective-permute-start.17 = (bf16[128,768]{1,0:T(8,128)(2,1)S(1)}, bf16[128,768]{1,0:T(8,128)(2,1)S(1)}, u32[]{:S(2)}, u32[]{:S(2)}) collective-permute-start(bf16[128,768]{1,0:T(8,128)(2,1)S(1)} %get-tuple-element.47), channel_id=1, source_target_pairs={{0,480},{32,0},{64,32},{96,64},{128,96},{160,128},{192,160},{224,1... | collective-permute-start | bytes 589832 | tf_op jit(solution)/shard_map/ppermute | solution.py:369
  58.3 13.3 %collective-permute-start.14 = (bf16[128,768]{1,0:T(8,128)(2,1)S(1)}, bf16[128,768]{1,0:T(8,128)(2,1)S(1)}, u32[]{:S(2)}, u32[]{:S(2)}) collective-permute-start(bf16[128,768]{1,0:T(8,128)(2,1)S(1)} %get-tuple-element.45), channel_id=1, source_target_pairs={{0,32},{32,64},{64,96},{96,128},{128,160},{160,192},{192,224},{224... | collective-permute-start | bytes 589832 | tf_op jit(solution)/shard_map/ppermute | solution.py:369
  60.8 14.0 %collective-permute-start.11 = (bf16[128,768]{1,0:T(8,128)(2,1)S(1)}, bf16[128,768]{1,0:T(8,128)(2,1)S(1)}, u32[]{:S(2)}, u32[]{:S(2)}) collective-permute-start(bf16[128,768]{1,0:T(8,128)(2,1)S(1)} %get-tuple-element.43), channel_id=1, source_target_pairs={{0,480},{32,0},{64,32},{96,64},{128,96},{160,128},{192,160},{224,1... | collective-permute-start | bytes 589832 | tf_op jit(solution)/shard_map/ppermute | solution.py:369
  65.4 13.9 %collective-permute-start.8 = (bf16[128,768]{1,0:T(8,128)(2,1)S(1)}, bf16[128,768]{1,0:T(8,128)(2,1)S(1)}, u32[]{:S(2)}, u32[]{:S(2)}) collective-permute-start(bf16[128,768]{1,0:T(8,128)(2,1)S(1)} %get-tuple-element.41), channel_id=1, source_target_pairs={{0,32},{32,64},{64,96},{96,128},{128,160},{160,192},{192,224},{224... | collective-permute-start | bytes 589832 | tf_op jit(solution)/shard_map/ppermute | solution.py:369
  68.5 12.7 %collective-permute-start.18 = (bf16[64,768]{1,0:T(8,128)(2,1)S(1)}, bf16[64,768]{1,0:T(8,128)(2,1)S(1)}, u32[]{:S(2)}, u32[]{:S(2)}) collective-permute-start(bf16[64,768]{1,0:T(8,128)(2,1)S(1)} %add_convert_fusion), channel_id=1, source_target_pairs={{0,448},{32,480},{64,0},{96,32},{128,64},{160,96},{192,128},{224,1... | collective-permute-start | bytes 294920 | tf_op jit(solution)/shard_map/ppermute | solution.py:375
  71.7 14.8 %collective-permute-start.15 = (bf16[64,768]{1,0:T(8,128)(2,1)S(1)}, bf16[64,768]{1,0:T(8,128)(2,1)S(1)}, u32[]{:S(2)}, u32[]{:S(2)}) collective-permute-start(bf16[64,768]{1,0:T(8,128)(2,1)S(1)} %add_convert_fusion.1), channel_id=1, source_target_pairs={{0,64},{32,96},{64,128},{96,160},{128,192},{160,224},{192,256},{22... | collective-permute-start | bytes 294920 | tf_op jit(solution)/shard_map/ppermute | solution.py:375
  74.8 59.4 %copy-start.6 = (s32[96]{0:T(128)S(1)}, s32[96]{0:T(128)}, u32[]{:S(2)}) copy-start(s32[96]{0:T(128)} %param.12) | copy-start | bytes 1156
  74.8 63.0 %copy-start.3 = (f32[1,2,64,512]{3,2,1,0:T(8,128)S(1)}, f32[1,2,64,512]{3,2,1,0:T(8,128)}, u32[]{:S(2)}) copy-start(f32[1,2,64,512]{3,2,1,0:T(8,128)} %param.17) | copy-start | bytes 786436
  74.8 15.8 %collective-permute-start.12 = (bf16[64,768]{1,0:T(8,128)(2,1)S(1)}, bf16[64,768]{1,0:T(8,128)(2,1)S(1)}, u32[]{:S(2)}, u32[]{:S(2)}) collective-permute-start(bf16[64,768]{1,0:T(8,128)(2,1)S(1)} %add_convert_fusion.2), channel_id=1, source_target_pairs={{0,448},{32,480},{64,0},{96,32},{128,64},{160,96},{192,128},{224,1... | collective-permute-start | bytes 294920 | tf_op jit(solution)/shard_map/ppermute | solution.py:375
  79.3 16.6 %collective-permute-start.9 = (bf16[64,768]{1,0:T(8,128)(2,1)S(1)}, bf16[64,768]{1,0:T(8,128)(2,1)S(1)}, u32[]{:S(2)}, u32[]{:S(2)}) collective-permute-start(bf16[64,768]{1,0:T(8,128)(2,1)S(1)} %add_convert_fusion.3), channel_id=1, source_target_pairs={{0,64},{32,96},{64,128},{96,160},{128,192},{160,224},{192,256},{22... | collective-permute-start | bytes 294920 | tf_op jit(solution)/shard_map/ppermute | solution.py:375
  81.3 18.7 %collective-permute-start.19 = (bf16[32,768]{1,0:T(8,128)(2,1)S(1)}, bf16[32,768]{1,0:T(8,128)(2,1)S(1)}, u32[]{:S(2)}, u32[]{:S(2)}) collective-permute-start(bf16[32,768]{1,0:T(8,128)(2,1)S(1)} %add_convert_fusion.5), channel_id=1, source_target_pairs={{0,384},{32,416},{64,448},{96,480},{128,0},{160,32},{192,64},{224,... | collective-permute-start | bytes 147464 | tf_op jit(solution)/shard_map/ppermute | solution.py:375
  86.5 78.5 %copy-start.1 = (f32[1,2,64,512]{3,2,1,0:T(8,128)S(1)}, f32[1,2,64,512]{3,2,1,0:T(8,128)}, u32[]{:S(2)}) copy-start(f32[1,2,64,512]{3,2,1,0:T(8,128)} %param.13) | copy-start | bytes 786436
  86.5 78.5 %copy-start.2 = (f32[1,2,64,512]{3,2,1,0:T(8,128)S(1)}, f32[1,2,64,512]{3,2,1,0:T(8,128)}, u32[]{:S(2)}) copy-start(f32[1,2,64,512]{3,2,1,0:T(8,128)} %param.14) | copy-start | bytes 786436
  86.5 13.5 %collective-permute-start.16 = (bf16[32,768]{1,0:T(8,128)(2,1)S(1)}, bf16[32,768]{1,0:T(8,128)(2,1)S(1)}, u32[]{:S(2)}, u32[]{:S(2)}) collective-permute-start(bf16[32,768]{1,0:T(8,128)(2,1)S(1)} %add_convert_fusion.7), channel_id=1, source_target_pairs={{0,128},{32,160},{64,192},{96,224},{128,256},{160,288},{192,320},{... | collective-permute-start | bytes 147464 | tf_op jit(solution)/shard_map/ppermute | solution.py:375
  90.7 9.3 %collective-permute-start.13 = (bf16[32,768]{1,0:T(8,128)(2,1)S(1)}, bf16[32,768]{1,0:T(8,128)(2,1)S(1)}, u32[]{:S(2)}, u32[]{:S(2)}) collective-permute-start(bf16[32,768]{1,0:T(8,128)(2,1)S(1)} %add_convert_fusion.9), channel_id=1, source_target_pairs={{0,384},{32,416},{64,448},{96,480},{128,0},{160,32},{192,64},{224,... | collective-permute-start | bytes 147464 | tf_op jit(solution)/shard_map/ppermute | solution.py:375
  95.9 8.8 %collective-permute-start.10 = (bf16[32,768]{1,0:T(8,128)(2,1)S(1)}, bf16[32,768]{1,0:T(8,128)(2,1)S(1)}, u32[]{:S(2)}, u32[]{:S(2)}) collective-permute-start(bf16[32,768]{1,0:T(8,128)(2,1)S(1)} %add_convert_fusion.11), channel_id=1, source_target_pairs={{0,128},{32,160},{64,192},{96,224},{128,256},{160,288},{192,320},{... | collective-permute-start | bytes 147464 | tf_op jit(solution)/shard_map/ppermute | solution.py:375
  117.5 20.3 %all-to-all-start = ((bf16[16,16,512]{2,1,0:T(8,128)(2,1)}), bf16[16,16,512]{2,1,0:T(8,128)(2,1)S(1)}, u32[]{:S(2)}, u32[]{:S(2)}) async-start(bf16[16,16,512]{2,1,0:T(8,128)(2,1)} %bitcast.11), calls=%async_computation | async-start | bytes 524288 | tf_op jit(solution)/shard_map/all_to_all | solution.py:386
  124.9 38.6 %collective-permute-start.21 = (bf16[4,2,2,64,512]{4,3,2,1,0:T(8,128)(2,1)S(1)}, bf16[4,2,2,64,512]{4,3,2,1,0:T(8,128)(2,1)S(1)}, u32[]{:S(2)}, u32[]{:S(2)}) collective-permute-start(bf16[4,2,2,64,512]{4,3,2,1,0:T(8,128)(2,1)S(1)} %pad_maximum_fusion.rm_ref), channel_id=1, source_target_pairs={{0,1},{1,0},{2,3},{3,2},{4,5},{5,4},{6,7},{7,6},{8,9},{9,8},{10,11... | collective-permute-start | bytes 3145736 | tf_op jit(solution)/shard_map/ppermute | solution.py:363
  150.4 14.6 %collective-permute-start.20 = (bf16[4,144,512]{2,1,0:T(8,128)(2,1)S(1)}, bf16[4,144,512]{2,1,0:T(8,128)(2,1)}, u32[]{:S(2)}, u32[]{:S(2)}) collective-permute-start(bf16[4,144,512]{2,1,0:T(8,128)(2,1)S(1)} %bitcast.48), channel_id=1, source_target_pairs={{0,1},{1,0},{2,3},{3,2},{4,5},{5,4},{6,7},{7,6},{8,9},{9,8},{10,11... | collective-permute-start | bytes 1769480 | tf_op jit(solution)/shard_map/ppermute | solution.py:394

commit v7 on v5

--- a/solution.py
+++ b/solution.py
@@ -39,10 +39,8 @@
 
 def prepare(activations, out_grads, place):
     block_rows, rows, toks = activations.shape
-    part = block_rows // 2
     per_z = rows // NZ
-    count = part * rows
-    small = count // 2
+    count = block_rows * rows // 2
     half = toks // NC
     width = out_grads.shape[1] // NX
     tile = width // TILES
@@ -60,23 +58,21 @@
                 copies.append(pltpu.make_async_copy(b_ref.at[tok, at], held.at[i, to, :], sems.at[i, n]))
         for copy in copies:
             copy.start()
-        m, k = iota((small, count), 0), iota((small, count), 1)
-        block = m % part
-        row = (m // part) % per_z
-        tail = m // (part * per_z)
+        m, k = iota((count, 2 * count), 0), iota((count, 2 * count), 1)
+        block = m % block_rows
+        row = (m // block_rows) % per_z
+        tail = m // (block_rows * per_z)
         high = 2 * (tail // 4) + 4 * ((tail // 2) % 2) + 8 * (tail % 2)
-        for side in range(2):
-            values = a_ref[side * part : (side + 1) * part].reshape(count, toks)
-            for odd in range(2):
-                dist = high + odd
-                goal = jnp.bitwise_and(z + dist if side == 0 else z - dist, NZ - 1)
-                pick = (block * rows + goal * per_z + row == k).astype(WIDE).astype(HALF)
-                moved = dot(pick, values).astype(HALF)
-                turned = jnp.concatenate([moved[:, half:], moved[:, :half]], axis=1)
-                at = (1 - odd) * count + side * small
-                ordered = jnp.where(c == 1, turned, moved)
-                for i in range(3):
-                    held[i, at : at + small, :] = ordered
+        values = a_ref[...].reshape(2 * count, toks)
+        for odd in range(2):
+            goal = jnp.bitwise_and(z + (1 - 2 * c) * (high + odd), NZ - 1)
+            pick = (block * rows + goal * per_z + row == k).astype(WIDE).astype(HALF)
+            moved = dot(pick, values).astype(HALF)
+            turned = jnp.concatenate([moved[:, half:], moved[:, :half]], axis=1)
+            at = (1 - odd) * count
+            ordered = jnp.where(c == 1, turned, moved)
+            for i in range(3):
+                held[i, at : at + count, :] = ordered
         last = [pltpu.make_async_copy(held.at[i], out_refs[i], out_sems.at[i]) for i in range(3)]
         for i in range(3):
             for copy in copies[i * TILES : (i + 1) * TILES]:
@@ -147,15 +143,14 @@
     group = 2
 
     def kernel(*refs):
-        rows_refs, own_ref, mine, other, (one_ref, two_ref) = refs[:4], refs[4], refs[5:8], refs[8:11], refs[11:]
+        rows_refs, own_ref, mine, other, out_ref = refs[:4], refs[4], refs[5:8], refs[8:11], refs[11]
         for n in range(group):
             at = slice(n * half, (n + 1) * half)
             total = dot(rows_refs[0][...], own_ref[n * toks : (n + 1) * toks, :])
             for rows_ref, m_ref, o_ref in zip(rows_refs[1:], mine, other):
                 total += dot(rows_ref[...], jnp.concatenate([m_ref[at, :], o_ref[at, :]], axis=0))
             to = slice(n * toks, (n + 1) * toks)
-            one_ref[:, to] = total[: count // 2].astype(kind)
-            two_ref[:, to] = total[count // 2 :].astype(kind)
+            out_ref[:, to] = total.astype(kind)
 
     rows = pl.BlockSpec((count, toks), lambda n: (0 if odd else 1, 0))
     columns = pl.BlockSpec((group * half, toks), lambda n: (total_rows // (group * half) + n, 0))
@@ -163,9 +158,9 @@
     return pl.pallas_call(
         kernel,
         grid=(TILES // group,),
-        out_shape=[jax.ShapeDtypeStruct((count // 2, TILES * toks), kind)] * 2,
+        out_shape=jax.ShapeDtypeStruct((count, TILES * toks), kind),
         in_specs=[rows] * 4 + [own_columns] + [columns] * 6,
-        out_specs=[pl.BlockSpec((count // 2, group * toks), lambda n: (0, n))] * 2,
+        out_specs=pl.BlockSpec((count, group * toks), lambda n: (0, n)),
         compiler_params=PARAMS,
     )(own, *arrived, own, *arrived, *swapped)
 
@@ -328,21 +323,20 @@
     block_count = owners.shape[0]
     per_z = rows // NZ
     columns = out_grads.shape[1] // block_size // NX
-    half_rows = block_rows // 2
     my_owner = z * NX + x
     my_mp = y * NC + c
     my_rows = my_mp * rows
 
-    place = jnp.stack([z, x, c] + [jnp.bitwise_and(x + step, NX - 1) for step in (1, 3, 2)]).astype(jnp.int32)
+    place = jnp.stack([z, x, c] + [jnp.bitwise_and(x + step, NX - 1) for step in (3, 2, 1)]).astype(jnp.int32)
     pieces = prepare(activations, out_grads, place)
-    arrived = [lax.ppermute(piece, "x", ring(NX, step)) for piece, step in zip(pieces, (1, -1, 2))]
+    arrived = [lax.ppermute(piece, "x", ring(NX, step)) for piece, step in zip(pieces, (-1, 2, 1))]
 
     piece_own, owners = lax.optimization_barrier((pieces[0], owners))
     targets = slot_targets(owners, slots)
-    by_block = targets.reshape(2, half_rows, NX, columns).transpose(2, 3, 0, 1)[:, :, :, None, None, :]
-    shape = (NX, columns, 2, 2, per_z, half_rows)
+    by_block = targets.reshape(block_rows, NX, columns).transpose(1, 2, 0)[:, :, None, None, :]
+    shape = (NX, columns, 2, per_z, block_rows)
     owner = by_block // slots
-    code = (((owner // NX) * slots + by_block % slots) * 2 + iota(shape, 3)) * per_z + iota(shape, 4)
+    code = (((owner // NX) * slots + by_block % slots) * 2 + iota(shape, 2)) * per_z + iota(shape, 3)
     code = jnp.where(owner % NX == x, code, -1).reshape(1, -1)
     out_rows = NZ * slots * 2 * per_z
     chosen = (code == iota((out_rows, 1), 0)).astype(HALF)
@@ -363,21 +357,17 @@
     sent = partial_products(own, arrived, swapped, True)
     kept = partial_products(own, arrived, swapped, False)
 
-    sums = []
-    for way, out, keep in ((1, sent[0], kept[0]), (-1, sent[1], kept[1])):
-        got = [lax.ppermute(out, "z", ring(NZ, way))]
-        for step in (2, 4):
-            part = got[-1].shape[0] // 2
-            out = keep[part : 2 * part]
-            for rows_in in got:
-                out = out + rows_in[part : 2 * part]
-            got.append(lax.ppermute(out.astype(HALF), "z", ring(NZ, way * step)))
-        part = got[-1].shape[0]
-        total = keep[:part]
+    got = []
+    for step in (1, 2, 4):
+        goals = [((i + (1 - 2 * k) * step) % NZ) * NC + k for i in range(NZ) for k in range(NC)]
+        got.append(lax.ppermute(sent, ("z", "c"), list(enumerate(goals))))
+        part = got[-1].shape[0] // (2 if step < 4 else 1)
+        rows_from = slice(part, 2 * part) if step < 4 else slice(0, part)
+        total = kept[rows_from]
         for rows_in in got:
-            total = total + rows_in[:part]
-        sums.append(total.astype(HALF))
-    sums = lax.all_gather(jnp.concatenate(sums, axis=0), "x", axis=0, tiled=False)
+            total = total + rows_in[rows_from]
+        sent = total.astype(HALF)
+    sums = lax.all_gather(sent, "x", axis=0, tiled=False)
 
     picked = pick_blocks(chosen, sums, block_size).reshape(NZ, out_rows // NZ, block_size)
     arrived = lax.all_to_all(picked, "z", 0, 0, tiled=True).reshape(out_rows, block_size)

time: 167 us -> 163 us (0.976)
  starting transfers between devices: 93.6 us -> 86.4 us
  waiting for transfers between devices: 29.4 us -> 33.5 us
    ppermute x6 -> x3, starting transfers between devices: 29.9 us -> 22.4 us  [body(): got.append(lax.ppermute(sent, ('z', 'c'), list(enumerate(goals))))]
    ppermute x6 -> x3, waiting for transfers between devices: 15.6 us -> 20.4 us  [body(): got.append(lax.ppermute(sent, ('z', 'c'), list(enumerate(goals))))]
    ppermute x3, starting transfers between devices: 13.5 us -> 9.46 us  [body(): swapped = [lax.ppermute(piece, 'c', ring(NC, 1)) for piece in arrived]]
    all_to_all x1, starting transfers between devices: 11.5 us -> 14.2 us  [body(): lax.all_to_all(picked, 'z', 0, 0, tiled=True).reshape(out_rows, block_size)]
    ppermute x3, starting transfers between devices: 10.3 us -> 12 us  [body(): lax.ppermute(piece, 'x', ring(NX, step))]
  transfers between devices with their start and end apart: 17 -> 14, of which waited for: 8 -> 8; matrix products, arithmetic and copies ran while one was open for 1% -> 1% of each run, Pallas kernels for 4% -> 4%
where the time goes in v7:
time: 163 us
  starting transfers between devices  86.4 us (53%)
  waiting for transfers between devices  33.5 us (21%)
  blocking collectives  22.3 us (14%)
  Pallas kernels  17.2 us (11%)
    ppermute x3, starting transfers between devices, body(): got.append(lax.ppermute(sent, ('z', 'c'), list(enumerate(goals))))  22.4 us
    ppermute x3, waiting for transfers between devices, body(): got.append(lax.ppermute(sent, ('z', 'c'), list(enumerate(goals))))  20.4 us
    all_to_all x1, starting transfers between devices, body(): lax.all_to_all(picked, 'z', 0, 0, tiled=True).reshape(out_rows, block_size)  14.2 us
    ppermute x3, starting transfers between devices, body(): lax.ppermute(piece, 'x', ring(NX, step))  12 us
    ppermute x1, starting transfers between devices, body(): rows_other = lax.ppermute(rows_mine, 'c', ring(NC, 1))  11.7 us
    all_gather x1, blocking collectives, body(): sums = lax.all_gather(sent, 'x', axis=0, tiled=False)  11.5 us
    all_gather x1, blocking collectives, body(): rows_mine = lax.all_gather(own_rows, 'y', axis=0, tiled=False)  10.8 us
    ppermute x3, starting transfers between devices, body(): swapped = [lax.ppermute(piece, 'c', ring(NC, 1)) for piece in arrived]  9.46 us
  transfers between devices with their start and end apart: 14, of which 8 were waited for; matrix products, arithmetic and copies ran while one was open for 1% of the time, Pallas kernels for 4%

profile of v7, /device:TPU:1, one launch (start us, length us, event | category | flops | bytes accessed | tf_op | source)
XLA Modules:
  0.0 162.7 jit_solution(2102708012900736755)
XLA Ops:
  0.6 0.7 stack.39.place_ref
  1.3 3.5 %shard_map.120 = (bf16[1280,256]{1,0:T(8,128)(2,1)}, bf16[1280,256]{1,0:T(8,128)(2,1)}, bf16[1280,256]{1,0:T(8,128)(2,1)}) custom-call(s32[6]{0:T(128)} %stack.39.place_ref, bf16[8,64,256]{2,1,0:T(8,128)(2,1)} %a_ref.1, bf16[256,6144]{1,0:T(8,128)(2,1)} %b_ref.3), custom_call_target="tpu_custom_call" | custom-call | tf_op jit(solution)/shard_map/pallas_call | solution.py:86
  4.8 5.5 %collective-permute-start.3 = (bf16[1280,256]{1,0:T(8,128)(2,1)}, bf16[1280,256]{1,0:T(8,128)(2,1)S(1)}, u32[]{:S(2)}, u32[]{:S(2)}) collective-permute-start(bf16[1280,256]{1,0:T(8,128)(2,1)} %get-tuple-element.30), channel_id=1, source_target_pairs={{0,16},{8,24},{16,0},{24,8},{1,17},{9,25},{17,1},{25,9},{2,18},{10... | collective-permute-start | bytes 1966088 | tf_op jit(solution)/shard_map/ppermute | solution.py:332
  10.3 2.2 %collective-permute-start.4 = (bf16[1280,256]{1,0:T(8,128)(2,1)}, bf16[1280,256]{1,0:T(8,128)(2,1)S(1)}, u32[]{:S(2)}, u32[]{:S(2)}) collective-permute-start(bf16[1280,256]{1,0:T(8,128)(2,1)} %get-tuple-element.31), channel_id=1, source_target_pairs={{0,8},{8,16},{16,24},{24,0},{1,9},{9,17},{17,25},{25,1},{2,10},{10... | collective-permute-start | bytes 1966088 | tf_op jit(solution)/shard_map/ppermute | solution.py:332
  12.5 4.3 %collective-permute-start.2 = (bf16[1280,256]{1,0:T(8,128)(2,1)}, bf16[1280,256]{1,0:T(8,128)(2,1)S(1)}, u32[]{:S(2)}, u32[]{:S(2)}) collective-permute-start(bf16[1280,256]{1,0:T(8,128)(2,1)} %get-tuple-element.25.p_ref), channel_id=1, source_target_pairs={{0,24},{8,0},{16,8},{24,16},{1,25},{9,1},{17,9},{25,17},{2,26},{10... | collective-permute-start | bytes 1966088 | tf_op jit(solution)/shard_map/ppermute | solution.py:332
  16.8 0.2 select_reduce_fusion
  17.0 0.1 reshape.110
  17.1 0.1 copy.19
  17.3 0.1 select_n.49
  17.4 0.1 fusion.1.p_ref
  17.5 0.0 copy-start.5
  17.5 3.1 %shard_map.121.refs_0_.refs_4_ = bf16[2048,256]{1,0:T(8,128)(2,1)} custom-call(s32[6]{0:T(128)} %stack.39.place_ref, bf16[1280,256]{1,0:T(8,128)(2,1)} %get-tuple-element.25.p_ref, bf16[256,6144]{1,0:T(8,128)(2,1)} %b_ref.3), custom_call_target="tpu_custom_call" | custom-call | tf_op jit(solution)/shard_map/pallas_call | solution.py:121
  20.6 3.3 %collective-permute-start = (bf16[1,2,2,64,512]{4,3,2,1,0:T(8,128)(2,1)S(1)}, bf16[1,2,2,64,512]{4,3,2,1,0:T(8,128)(2,1)S(1)}, u32[]{:S(2)}, u32[]{:S(2)}) collective-permute-start(bf16[1,2,2,64,512]{4,3,2,1,0:T(8,128)(2,1)S(1)} %maximum_bitcast_fusion), channel_id=1, source_target_pairs={{0,2},{2,0},{4,6},{6,4},{1,3},{3,1},{5,7},{7,5},{8,10},{10,8},{12,... | collective-permute-start | bytes 786440 | tf_op jit(solution)/shard_map/ppermute | solution.py:351
  24.0 4.2 %collective-permute-done = bf16[1,2,2,64,512]{4,3,2,1,0:T(8,128)(2,1)S(1)} collective-permute-done((bf16[1,2,2,64,512]{4,3,2,1,0:T(8,128)(2,1)S(1)}, bf16[1,2,2,64,512]{4,3,2,1,0:T(8,128)(2,1)S(1)}, u32[]{:S(2)}, u32[]{:S(2)}) %collective-permute-start) | collective-permute-done | bytes 262176 | tf_op jit(solution)/shard_map/ppermute | solution.py:351
  28.2 0.1 pad_maximum_fusion.1
  28.2 5.6 %collective-permute-start.1 = (bf16[2,2,2,64,512]{4,3,2,1,0:T(8,128)(2,1)S(1)}, bf16[2,2,2,64,512]{4,3,2,1,0:T(8,128)(2,1)S(1)}, u32[]{:S(2)}, u32[]{:S(2)}) collective-permute-start(bf16[2,2,2,64,512]{4,3,2,1,0:T(8,128)(2,1)S(1)} %pad_maximum_fusion.1), channel_id=1, source_target_pairs={{0,4},{2,6},{4,0},{6,2},{1,5},{3,7},{5,1},{7,3},{8,12},{10,14},{12... | collective-permute-start | bytes 1572872 | tf_op jit(solution)/shard_map/ppermute | solution.py:351
  33.8 4.6 %collective-permute-start.6 = (bf16[1280,256]{1,0:T(8,128)(2,1)S(1)}, bf16[1280,256]{1,0:T(8,128)(2,1)S(1)}, u32[]{:S(2)}, u32[]{:S(2)}) collective-permute-start(bf16[1280,256]{1,0:T(8,128)(2,1)S(1)} %collective-permute-done.3.refs_2_.refs_6_), channel_id=1, source_target_pairs={{0,1},{1,0},{2,3},{3,2},{4,5},{5,4},{6,7},{7,6},{8,9},{9,8},{10,11... | collective-permute-start | bytes 1966088 | tf_op jit(solution)/shard_map/ppermute | solution.py:354
  38.5 0.7 collective-permute-done.4.refs_3_.refs_7_
  39.2 2.9 %collective-permute-start.7 = (bf16[1280,256]{1,0:T(8,128)(2,1)S(1)}, bf16[1280,256]{1,0:T(8,128)(2,1)S(1)}, u32[]{:S(2)}, u32[]{:S(2)}) collective-permute-start(bf16[1280,256]{1,0:T(8,128)(2,1)S(1)} %collective-permute-done.4.refs_3_.refs_7_), channel_id=1, source_target_pairs={{0,1},{1,0},{2,3},{3,2},{4,5},{5,4},{6,7},{7,6},{8,9},{9,8},{10,11... | collective-permute-start | bytes 1966088 | tf_op jit(solution)/shard_map/ppermute | solution.py:354
  42.1 1.9 %collective-permute-start.5 = (bf16[1280,256]{1,0:T(8,128)(2,1)S(1)}, bf16[1280,256]{1,0:T(8,128)(2,1)S(1)}, u32[]{:S(2)}, u32[]{:S(2)}) collective-permute-start(bf16[1280,256]{1,0:T(8,128)(2,1)S(1)} %collective-permute-done.2.refs_1_.refs_5_), channel_id=1, source_target_pairs={{0,1},{1,0},{2,3},{3,2},{4,5},{5,4},{6,7},{7,6},{8,9},{9,8},{10,11... | collective-permute-start | bytes 1966088 | tf_op jit(solution)/shard_map/ppermute | solution.py:354
  44.1 0.1 pad_maximum_fusion.rm_ref
  44.2 1.9 %collective-permute-done.5.refs_8_ = bf16[1280,256]{1,0:T(8,128)(2,1)S(1)} collective-permute-done((bf16[1280,256]{1,0:T(8,128)(2,1)S(1)}, bf16[1280,256]{1,0:T(8,128)(2,1)S(1)}, u32[]{:S(2)}, u32[]{:S(2)}) %collective-permute-start.5) | collective-permute-done | bytes 655392 | tf_op jit(solution)/shard_map/ppermute | solution.py:354
  46.1 1.4 shard_map.123
  47.5 11.3 %collective-permute-start.8 = (bf16[256,1536]{1,0:T(8,128)(2,1)S(1)}, bf16[256,1536]{1,0:T(8,128)(2,1)S(1)}, u32[]{:S(2)}, u32[]{:S(2)}) collective-permute-start(bf16[256,1536]{1,0:T(8,128)(2,1)S(1)} %shard_map.123), channel_id=1, source_target_pairs={{0,32},{1,481},{32,64},{33,1},{64,96},{65,33},{96,128},{97,65},{12... | collective-permute-start | bytes 2359304 | tf_op jit(solution)/shard_map/ppermute | solution.py:363
  58.8 1.5 shard_map.122
  60.3 7.4 %collective-permute-done.8 = bf16[256,1536]{1,0:T(8,128)(2,1)S(1)} collective-permute-done((bf16[256,1536]{1,0:T(8,128)(2,1)S(1)}, bf16[256,1536]{1,0:T(8,128)(2,1)S(1)}, u32[]{:S(2)}, u32[]{:S(2)}) %collective-permute-start.8) | collective-permute-done | bytes 786464 | tf_op jit(solution)/shard_map/ppermute | solution.py:363
  67.7 0.1 fusion
  67.8 4.6 %collective-permute-start.9 = (bf16[128,1536]{1,0:T(8,128)(2,1)S(1)}, bf16[128,1536]{1,0:T(8,128)(2,1)S(1)}, u32[]{:S(2)}, u32[]{:S(2)}) collective-permute-start(bf16[128,1536]{1,0:T(8,128)(2,1)S(1)} %fusion), channel_id=1, source_target_pairs={{0,64},{1,449},{32,96},{33,481},{64,128},{65,1},{96,160},{97,33},{... | collective-permute-start | bytes 1179656 | tf_op jit(solution)/shard_map/ppermute | solution.py:363
  72.4 7.2 %collective-permute-done.9 = bf16[128,1536]{1,0:T(8,128)(2,1)S(1)} collective-permute-done((bf16[128,1536]{1,0:T(8,128)(2,1)S(1)}, bf16[128,1536]{1,0:T(8,128)(2,1)S(1)}, u32[]{:S(2)}, u32[]{:S(2)}) %collective-permute-start.9) | collective-permute-done | bytes 393248 | tf_op jit(solution)/shard_map/ppermute | solution.py:363
  79.6 0.1 fusion.3
  79.7 6.5 %collective-permute-start.10 = (bf16[64,1536]{1,0:T(8,128)(2,1)S(1)}, bf16[64,1536]{1,0:T(8,128)(2,1)S(1)}, u32[]{:S(2)}, u32[]{:S(2)}) collective-permute-start(bf16[64,1536]{1,0:T(8,128)(2,1)S(1)} %fusion.3), channel_id=1, source_target_pairs={{0,128},{1,385},{32,160},{33,417},{64,192},{65,449},{96,224},{97,4... | collective-permute-start | bytes 589832 | tf_op jit(solution)/shard_map/ppermute | solution.py:363
  86.2 5.8 %collective-permute-done.10 = bf16[64,1536]{1,0:T(8,128)(2,1)S(1)} collective-permute-done((bf16[64,1536]{1,0:T(8,128)(2,1)S(1)}, bf16[64,1536]{1,0:T(8,128)(2,1)S(1)}, u32[]{:S(2)}, u32[]{:S(2)}) %collective-permute-start.10) | collective-permute-done | bytes 196640 | tf_op jit(solution)/shard_map/ppermute | solution.py:363
  92.0 0.1 fusion.6
  92.0 0.0 copy-start.6
  92.1 0.0 copy-start.3
  92.1 11.5 %all-gather = bf16[256,1536]{1,0:T(8,128)(2,1)S(1)} all-gather(bf16[64,1536]{1,0:T(8,128)(2,1)S(1)} %fusion.6), channel_id=2, replica_groups=mesh['z'=16,'x'=4,'y'=4,'c'=2] {'x'}, dimensions={0}, use_global_device_ids=true | all-gather | bytes 983040 | tf_op jit(solution)/shard_map/all_gather | solution.py:370
  103.6 1.3 shard_map.124
  104.8 14.2 %all-to-all-start = ((bf16[16,16,512]{2,1,0:T(8,128)(2,1)}), bf16[16,16,512]{2,1,0:T(8,128)(2,1)S(1)}, u32[]{:S(2)}, u32[]{:S(2)}) async-start(bf16[16,16,512]{2,1,0:T(8,128)(2,1)} %bitcast.11), calls=%async_computation | async-start | bytes 524288 | tf_op jit(solution)/shard_map/all_to_all | solution.py:373
  119.0 7.8 %collective-permute-start.12 = (bf16[4,2,2,64,512]{4,3,2,1,0:T(8,128)(2,1)S(1)}, bf16[4,2,2,64,512]{4,3,2,1,0:T(8,128)(2,1)S(1)}, u32[]{:S(2)}, u32[]{:S(2)}) collective-permute-start(bf16[4,2,2,64,512]{4,3,2,1,0:T(8,128)(2,1)S(1)} %pad_maximum_fusion.rm_ref), channel_id=1, source_target_pairs={{0,1},{1,0},{2,3},{3,2},{4,5},{5,4},{6,7},{7,6},{8,9},{9,8},{10,11... | collective-permute-start | bytes 3145736 | tf_op jit(solution)/shard_map/ppermute | solution.py:355
  126.8 0.2 fusion.15
  127.0 4.8 %all-to-all-done = bf16[16,16,512]{2,1,0:T(8,128)(2,1)S(1)} async-done(((bf16[16,16,512]{2,1,0:T(8,128)(2,1)}), bf16[16,16,512]{2,1,0:T(8,128)(2,1)S(1)}, u32[]{:S(2)}, u32[]{:S(2)}) %all-to-all-start) | async-done | bytes 262176 | tf_op jit(solution)/shard_map/all_to_all | solution.py:373
  131.8 1.5 shard_map.125
  133.4 10.8 %all-gather.1 = bf16[576,512]{1,0:T(8,128)(2,1)S(1)} all-gather(bf16[144,512]{1,0:T(8,128)(2,1)S(1)} %get-tuple-element.32), channel_id=3, replica_groups=mesh['z'=16,'x'=4,'y'=4,'c'=2] {'y'}, dimensions={0}, use_global_device_ids=true | all-gather | bytes 737280 | tf_op jit(solution)/shard_map/all_gather | solution.py:380
  144.2 11.7 %collective-permute-start.11 = (bf16[4,144,512]{2,1,0:T(8,128)(2,1)S(1)}, bf16[4,144,512]{2,1,0:T(8,128)(2,1)}, u32[]{:S(2)}, u32[]{:S(2)}) collective-permute-start(bf16[4,144,512]{2,1,0:T(8,128)(2,1)S(1)} %bitcast.48), channel_id=1, source_target_pairs={{0,1},{1,0},{2,3},{3,2},{4,5},{5,4},{6,7},{7,6},{8,9},{9,8},{10,11... | collective-permute-start | bytes 1769480 | tf_op jit(solution)/shard_map/ppermute | solution.py:381
  155.8 0.2 compare_reduce_fusion
  156.0 0.1 concatenate.10.f_ref
  156.1 1.5 collective-permute-done.11.o_ref
  157.6 5.1 %shard_map.126 = (f32[2,64,512]{2,1,0:T(8,128)}, f32[2,64,512]{2,1,0:T(8,128)}, bf16[2,512,512]{2,1,0:T(8,128)(2,1)}) custom-call(s32[7]{0:T(128)S(1)} %concatenate.10.f_ref, bf16[4,144,512]{2,1,0:T(8,128)(2,1)S(1)} %bitcast.49, bf16[4,144,512]{2,1,0:T(8,128)(2,1)} %collective-permute-done.11.o_ref, bf16[4,2,2,64,512]{4,3,2,1,0:T(8,128)(2,1)S(1)} %pad_maximum_fusion.rm_ref, ...), custom_call_target="tpu_custom_call" | custom-call | tf_op jit(solution)/shard_map/pallas_call | solution.py:291
  (29 shorter events, 0.2 us)
Async XLA Ops:
  1.3 15.5 %copy-start.7 = (s32[96]{0:T(128)S(1)}, s32[96]{0:T(128)}, u32[]{:S(2)}) copy-start(s32[96]{0:T(128)} %param.11) | copy-start | bytes 1156
  4.8 29.1 %collective-permute-start.3 = (bf16[1280,256]{1,0:T(8,128)(2,1)}, bf16[1280,256]{1,0:T(8,128)(2,1)S(1)}, u32[]{:S(2)}, u32[]{:S(2)}) collective-permute-start(bf16[1280,256]{1,0:T(8,128)(2,1)} %get-tuple-element.30), channel_id=1, source_target_pairs={{0,16},{8,24},{16,0},{24,8},{1,17},{9,25},{17,1},{25,9},{2,18},{10... | collective-permute-start | bytes 1966088 | tf_op jit(solution)/shard_map/ppermute | solution.py:332
  10.3 28.9 %collective-permute-start.4 = (bf16[1280,256]{1,0:T(8,128)(2,1)}, bf16[1280,256]{1,0:T(8,128)(2,1)S(1)}, u32[]{:S(2)}, u32[]{:S(2)}) collective-permute-start(bf16[1280,256]{1,0:T(8,128)(2,1)} %get-tuple-element.31), channel_id=1, source_target_pairs={{0,8},{8,16},{16,24},{24,0},{1,9},{9,17},{17,25},{25,1},{2,10},{10... | collective-permute-start | bytes 1966088 | tf_op jit(solution)/shard_map/ppermute | solution.py:332
  12.5 29.6 %collective-permute-start.2 = (bf16[1280,256]{1,0:T(8,128)(2,1)}, bf16[1280,256]{1,0:T(8,128)(2,1)S(1)}, u32[]{:S(2)}, u32[]{:S(2)}) collective-permute-start(bf16[1280,256]{1,0:T(8,128)(2,1)} %get-tuple-element.25.p_ref), channel_id=1, source_target_pairs={{0,24},{8,0},{16,8},{24,16},{1,25},{9,1},{17,9},{25,17},{2,26},{10... | collective-permute-start | bytes 1966088 | tf_op jit(solution)/shard_map/ppermute | solution.py:332
  17.5 3.1 %copy-start.4 = (bf16[1,2,64,512]{3,2,1,0:T(8,128)(2,1)S(1)}, bf16[1,2,64,512]{3,2,1,0:T(8,128)(2,1)}, u32[]{:S(2)}) copy-start(bf16[1,2,64,512]{3,2,1,0:T(8,128)(2,1)} %param.16) | copy-start | bytes 393220
  17.5 3.1 %copy-start.5 = (bf16[1,2,64,512]{3,2,1,0:T(8,128)(2,1)S(1)}, bf16[1,2,64,512]{3,2,1,0:T(8,128)(2,1)}, u32[]{:S(2)}) copy-start(bf16[1,2,64,512]{3,2,1,0:T(8,128)(2,1)} %param.15) | copy-start | bytes 393220
  20.6 25.5 %copy-start = (bf16[2048,256]{1,0:T(8,128)(2,1)S(1)}, bf16[2048,256]{1,0:T(8,128)(2,1)}, u32[]{:S(2)}) copy-start(bf16[2048,256]{1,0:T(8,128)(2,1)} %shard_map.121.refs_0_.refs_4_) | copy-start | bytes 3145732
  20.6 7.5 %collective-permute-start = (bf16[1,2,2,64,512]{4,3,2,1,0:T(8,128)(2,1)S(1)}, bf16[1,2,2,64,512]{4,3,2,1,0:T(8,128)(2,1)S(1)}, u32[]{:S(2)}, u32[]{:S(2)}) collective-permute-start(bf16[1,2,2,64,512]{4,3,2,1,0:T(8,128)(2,1)S(1)} %maximum_bitcast_fusion), channel_id=1, source_target_pairs={{0,2},{2,0},{4,6},{6,4},{1,3},{3,1},{5,7},{7,5},{8,10},{10,8},{12,... | collective-permute-start | bytes 786440 | tf_op jit(solution)/shard_map/ppermute | solution.py:351
  28.2 15.8 %collective-permute-start.1 = (bf16[2,2,2,64,512]{4,3,2,1,0:T(8,128)(2,1)S(1)}, bf16[2,2,2,64,512]{4,3,2,1,0:T(8,128)(2,1)S(1)}, u32[]{:S(2)}, u32[]{:S(2)}) collective-permute-start(bf16[2,2,2,64,512]{4,3,2,1,0:T(8,128)(2,1)S(1)} %pad_maximum_fusion.1), channel_id=1, source_target_pairs={{0,4},{2,6},{4,0},{6,2},{1,5},{3,7},{5,1},{7,3},{8,12},{10,14},{12... | collective-permute-start | bytes 1572872 | tf_op jit(solution)/shard_map/ppermute | solution.py:351
  33.8 10.3 %collective-permute-start.6 = (bf16[1280,256]{1,0:T(8,128)(2,1)S(1)}, bf16[1280,256]{1,0:T(8,128)(2,1)S(1)}, u32[]{:S(2)}, u32[]{:S(2)}) collective-permute-start(bf16[1280,256]{1,0:T(8,128)(2,1)S(1)} %collective-permute-done.3.refs_2_.refs_6_), channel_id=1, source_target_pairs={{0,1},{1,0},{2,3},{3,2},{4,5},{5,4},{6,7},{7,6},{8,9},{9,8},{10,11... | collective-permute-start | bytes 1966088 | tf_op jit(solution)/shard_map/ppermute | solution.py:354
  39.2 5.0 %collective-permute-start.7 = (bf16[1280,256]{1,0:T(8,128)(2,1)S(1)}, bf16[1280,256]{1,0:T(8,128)(2,1)S(1)}, u32[]{:S(2)}, u32[]{:S(2)}) collective-permute-start(bf16[1280,256]{1,0:T(8,128)(2,1)S(1)} %collective-permute-done.4.refs_3_.refs_7_), channel_id=1, source_target_pairs={{0,1},{1,0},{2,3},{3,2},{4,5},{5,4},{6,7},{7,6},{8,9},{9,8},{10,11... | collective-permute-start | bytes 1966088 | tf_op jit(solution)/shard_map/ppermute | solution.py:354
  42.1 4.0 %collective-permute-start.5 = (bf16[1280,256]{1,0:T(8,128)(2,1)S(1)}, bf16[1280,256]{1,0:T(8,128)(2,1)S(1)}, u32[]{:S(2)}, u32[]{:S(2)}) collective-permute-start(bf16[1280,256]{1,0:T(8,128)(2,1)S(1)} %collective-permute-done.2.refs_1_.refs_5_), channel_id=1, source_target_pairs={{0,1},{1,0},{2,3},{3,2},{4,5},{5,4},{6,7},{7,6},{8,9},{9,8},{10,11... | collective-permute-start | bytes 1966088 | tf_op jit(solution)/shard_map/ppermute | solution.py:354
  47.5 20.3 %collective-permute-start.8 = (bf16[256,1536]{1,0:T(8,128)(2,1)S(1)}, bf16[256,1536]{1,0:T(8,128)(2,1)S(1)}, u32[]{:S(2)}, u32[]{:S(2)}) collective-permute-start(bf16[256,1536]{1,0:T(8,128)(2,1)S(1)} %shard_map.123), channel_id=1, source_target_pairs={{0,32},{1,481},{32,64},{33,1},{64,96},{65,33},{96,128},{97,65},{12... | collective-permute-start | bytes 2359304 | tf_op jit(solution)/shard_map/ppermute | solution.py:363
  67.8 11.8 %collective-permute-start.9 = (bf16[128,1536]{1,0:T(8,128)(2,1)S(1)}, bf16[128,1536]{1,0:T(8,128)(2,1)S(1)}, u32[]{:S(2)}, u32[]{:S(2)}) collective-permute-start(bf16[128,1536]{1,0:T(8,128)(2,1)S(1)} %fusion), channel_id=1, source_target_pairs={{0,64},{1,449},{32,96},{33,481},{64,128},{65,1},{96,160},{97,33},{... | collective-permute-start | bytes 1179656 | tf_op jit(solution)/shard_map/ppermute | solution.py:363
  79.7 12.3 %collective-permute-start.10 = (bf16[64,1536]{1,0:T(8,128)(2,1)S(1)}, bf16[64,1536]{1,0:T(8,128)(2,1)S(1)}, u32[]{:S(2)}, u32[]{:S(2)}) collective-permute-start(bf16[64,1536]{1,0:T(8,128)(2,1)S(1)} %fusion.3), channel_id=1, source_target_pairs={{0,128},{1,385},{32,160},{33,417},{64,192},{65,449},{96,224},{97,4... | collective-permute-start | bytes 589832 | tf_op jit(solution)/shard_map/ppermute | solution.py:363
  92.0 34.8 %copy-start.6 = (s32[96]{0:T(128)S(1)}, s32[96]{0:T(128)}, u32[]{:S(2)}) copy-start(s32[96]{0:T(128)} %param.12) | copy-start | bytes 1156
  92.1 39.8 %copy-start.3 = (f32[1,2,64,512]{3,2,1,0:T(8,128)S(1)}, f32[1,2,64,512]{3,2,1,0:T(8,128)}, u32[]{:S(2)}) copy-start(f32[1,2,64,512]{3,2,1,0:T(8,128)} %param.17) | copy-start | bytes 786436
  103.6 54.0 %copy-start.1 = (f32[1,2,64,512]{3,2,1,0:T(8,128)S(1)}, f32[1,2,64,512]{3,2,1,0:T(8,128)}, u32[]{:S(2)}) copy-start(f32[1,2,64,512]{3,2,1,0:T(8,128)} %param.13) | copy-start | bytes 786436
  103.6 54.0 %copy-start.2 = (f32[1,2,64,512]{3,2,1,0:T(8,128)S(1)}, f32[1,2,64,512]{3,2,1,0:T(8,128)}, u32[]{:S(2)}) copy-start(f32[1,2,64,512]{3,2,1,0:T(8,128)} %param.14) | copy-start | bytes 786436
  104.8 27.0 %all-to-all-start = ((bf16[16,16,512]{2,1,0:T(8,128)(2,1)}), bf16[16,16,512]{2,1,0:T(8,128)(2,1)S(1)}, u32[]{:S(2)}, u32[]{:S(2)}) async-start(bf16[16,16,512]{2,1,0:T(8,128)(2,1)} %bitcast.11), calls=%async_computation | async-start | bytes 524288 | tf_op jit(solution)/shard_map/all_to_all | solution.py:373
  119.0 37.1 %collective-permute-start.12 = (bf16[4,2,2,64,512]{4,3,2,1,0:T(8,128)(2,1)S(1)}, bf16[4,2,2,64,512]{4,3,2,1,0:T(8,128)(2,1)S(1)}, u32[]{:S(2)}, u32[]{:S(2)}) collective-permute-start(bf16[4,2,2,64,512]{4,3,2,1,0:T(8,128)(2,1)S(1)} %pad_maximum_fusion.rm_ref), channel_id=1, source_target_pairs={{0,1},{1,0},{2,3},{3,2},{4,5},{5,4},{6,7},{7,6},{8,9},{9,8},{10,11... | collective-permute-start | bytes 3145736 | tf_op jit(solution)/shard_map/ppermute | solution.py:355
  144.2 13.4 %collective-permute-start.11 = (bf16[4,144,512]{2,1,0:T(8,128)(2,1)S(1)}, bf16[4,144,512]{2,1,0:T(8,128)(2,1)}, u32[]{:S(2)}, u32[]{:S(2)}) collective-permute-start(bf16[4,144,512]{2,1,0:T(8,128)(2,1)S(1)} %bitcast.48), channel_id=1, source_target_pairs={{0,1},{1,0},{2,3},{3,2},{4,5},{5,4},{6,7},{7,6},{8,9},{9,8},{10,11... | collective-permute-start | bytes 1769480 | tf_op jit(solution)/shard_map/ppermute | solution.py:381

commit v8 on v7

--- a/solution.py
+++ b/solution.py
@@ -10,6 +10,7 @@
 HALF = jnp.bfloat16
 WIDE = jnp.float32
 NZ, NX, NC = 16, 4, 2
+NL = 4
 TILES = 6
 ROOMY = pltpu.CompilerParams(vmem_limit_bytes=60 * 1024 * 1024)
 PARAMS = pltpu.CompilerParams(vmem_limit_bytes=8 * 1024 * 1024)
@@ -316,7 +317,8 @@
     right_root,
     grad_acc,
 ):
-    z, x, y, c = (lax.axis_index(name) for name in ("z", "x", "y", "c"))
+    zh, zl, x, y, c = (lax.axis_index(name) for name in ("zh", "zl", "x", "y", "c"))
+    z = zh * NL + zl
     block_rows, rows, toks = activations.shape
     block_size = left_stat.shape[3]
     slots = left_stat.shape[1]
@@ -336,7 +338,9 @@
     by_block = targets.reshape(block_rows, NX, columns).transpose(1, 2, 0)[:, :, None, None, :]
     shape = (NX, columns, 2, per_z, block_rows)
     owner = by_block // slots
-    code = (((owner // NX) * slots + by_block % slots) * 2 + iota(shape, 2)) * per_z + iota(shape, 3)
+    owner_z = owner // NX
+    owner_z = owner_z % NL * (NZ // NL) + owner_z // NL
+    code = ((owner_z * slots + by_block % slots) * 2 + iota(shape, 2)) * per_z + iota(shape, 3)
     code = jnp.where(owner % NX == x, code, -1).reshape(1, -1)
     out_rows = NZ * slots * 2 * per_z
     chosen = (code == iota((out_rows, 1), 0)).astype(HALF)
@@ -360,7 +364,7 @@
     got = []
     for step in (1, 2, 4):
         goals = [((i + (1 - 2 * k) * step) % NZ) * NC + k for i in range(NZ) for k in range(NC)]
-        got.append(lax.ppermute(sent, ("z", "c"), list(enumerate(goals))))
+        got.append(lax.ppermute(sent, ("zh", "zl", "c"), list(enumerate(goals))))
         part = got[-1].shape[0] // (2 if step < 4 else 1)
         rows_from = slice(part, 2 * part) if step < 4 else slice(0, part)
         total = kept[rows_from]
@@ -369,8 +373,9 @@
         sent = total.astype(HALF)
     sums = lax.all_gather(sent, "x", axis=0, tiled=False)
 
-    picked = pick_blocks(chosen, sums, block_size).reshape(NZ, out_rows // NZ, block_size)
-    arrived = lax.all_to_all(picked, "z", 0, 0, tiled=True).reshape(out_rows, block_size)
+    picked = pick_blocks(chosen, sums, block_size).reshape(NL, NZ // NL, out_rows // NZ, block_size)
+    picked = lax.all_to_all(picked, "zl", 0, 0, tiled=True).transpose(1, 0, 2, 3)
+    arrived = lax.all_to_all(picked, "zh", 0, 0, tiled=True).reshape(out_rows, block_size)
 
     wanted = my_owner * slots + iota((slots, block_count), 0)
     matched = targets[None, :] == wanted
@@ -387,9 +392,10 @@
 
 
 def solution(mesh):
-    dp, mp = mesh.devices.shape
-    parts = Mesh(mesh.devices.reshape(NZ, NX, mp // NC, NC), ("z", "x", "y", "c"))
-    owner, strip = ("z", "x"), ("y", "c")
+    mp = mesh.devices.shape[1]
+    names = ("zh", "zl", "x", "y", "c")
+    parts = Mesh(mesh.devices.reshape(NZ // NL, NL, NX, mp // NC, NC), names)
+    owner, strip = names[:3], names[3:]
     state = P(owner, None, strip, None)
     return jax.shard_map(
         body,

time: 163 us -> 174 us (1.067)
  blocking collectives: 22.3 us -> 34.6 us
  starting transfers between devices: 86.4 us -> 84.4 us
    all_to_all x0 -> x1, blocking collectives: none -> 12.4 us  [body(): lax.all_to_all(picked, 'zl', 0, 0, tiled=True).transpose(1, 0, 2, 3)]
    all_to_all x1, starting transfers between devices: 14.2 us -> 10.1 us  [body(): lax.all_to_all(picked, 'zh', 0, 0, tiled=True).reshape(out_rows, block_size)]
where the time goes in v8:
time: 174 us; the launch traced here: 172 us
  starting transfers between devices  84.4 us (49%)
  blocking collectives  34.6 us (20%)
  waiting for transfers between devices  32.8 us (19%)
  Pallas kernels  16.6 us (10%)
  local copies, waits for them, and re-layouts  1.84 us (1%)
    ppermute x3, starting transfers between devices, body(): got.append(lax.ppermute(sent, ('zh', 'zl', 'c'), list(enumerate(goals))))  22.4 us
    ppermute x3, waiting for transfers between devices, body(): got.append(lax.ppermute(sent, ('zh', 'zl', 'c'), list(enumerate(goals))))  20.4 us
    ppermute x1, starting transfers between devices, body(): rows_other = lax.ppermute(rows_mine, 'c', ring(NC, 1))  12.6 us
    all_to_all x1, blocking collectives, body(): lax.all_to_all(picked, 'zl', 0, 0, tiled=True).transpose(1, 0, 2, 3)  12.4 us
    ppermute x3, starting transfers between devices, body(): lax.ppermute(piece, 'x', ring(NX, step))  12 us
    all_gather x1, blocking collectives, body(): sums = lax.all_gather(sent, 'x', axis=0, tiled=False)  11.4 us
    all_gather x1, blocking collectives, body(): rows_mine = lax.all_gather(own_rows, 'y', axis=0, tiled=False)  10.8 us
    all_to_all x1, starting transfers between devices, body(): lax.all_to_all(picked, 'zh', 0, 0, tiled=True).reshape(out_rows, block_size)  10.1 us
  transfers between devices with their start and end apart: 14, of which 8 were waited for; matrix products, arithmetic and copies ran while one was open for 1% of the time, Pallas kernels for 4%

profile of v8, /device:TPU:1, one launch (start us, length us, event | category | flops | bytes accessed | tf_op | source)
XLA Modules:
  0.0 172.3 jit_solution(17204385114462573548)
XLA Ops:
  0.6 0.7 stack.39.place_ref
  1.3 3.5 %shard_map.120 = (bf16[1280,256]{1,0:T(8,128)(2,1)}, bf16[1280,256]{1,0:T(8,128)(2,1)}, bf16[1280,256]{1,0:T(8,128)(2,1)}) custom-call(s32[6]{0:T(128)} %stack.39.place_ref, bf16[8,64,256]{2,1,0:T(8,128)(2,1)} %a_ref.1, bf16[256,6144]{1,0:T(8,128)(2,1)} %b_ref.3), custom_call_target="tpu_custom_call" | custom-call | tf_op jit(solution)/shard_map/pallas_call | solution.py:87
  4.8 5.5 %collective-permute-start.3 = (bf16[1280,256]{1,0:T(8,128)(2,1)}, bf16[1280,256]{1,0:T(8,128)(2,1)S(1)}, u32[]{:S(2)}, u32[]{:S(2)}) collective-permute-start(bf16[1280,256]{1,0:T(8,128)(2,1)} %get-tuple-element.30), channel_id=1, source_target_pairs={{0,16},{8,24},{16,0},{24,8},{1,17},{9,25},{17,1},{25,9},{2,18},{10... | collective-permute-start | bytes 1966088 | tf_op jit(solution)/shard_map/ppermute | solution.py:334
  10.3 2.2 %collective-permute-start.4 = (bf16[1280,256]{1,0:T(8,128)(2,1)}, bf16[1280,256]{1,0:T(8,128)(2,1)S(1)}, u32[]{:S(2)}, u32[]{:S(2)}) collective-permute-start(bf16[1280,256]{1,0:T(8,128)(2,1)} %get-tuple-element.31), channel_id=1, source_target_pairs={{0,8},{8,16},{16,24},{24,0},{1,9},{9,17},{17,25},{25,1},{2,10},{10... | collective-permute-start | bytes 1966088 | tf_op jit(solution)/shard_map/ppermute | solution.py:334
  12.5 4.3 %collective-permute-start.2 = (bf16[1280,256]{1,0:T(8,128)(2,1)}, bf16[1280,256]{1,0:T(8,128)(2,1)S(1)}, u32[]{:S(2)}, u32[]{:S(2)}) collective-permute-start(bf16[1280,256]{1,0:T(8,128)(2,1)} %get-tuple-element.25.p_ref), channel_id=1, source_target_pairs={{0,24},{8,0},{16,8},{24,16},{1,25},{9,1},{17,9},{25,17},{2,26},{10... | collective-permute-start | bytes 1966088 | tf_op jit(solution)/shard_map/ppermute | solution.py:334
  16.8 0.2 select_reduce_fusion
  17.0 0.1 reshape.136
  17.1 0.1 copy.28
  17.3 0.1 select_n.60
  17.4 0.1 fusion.1.p_ref
  17.5 0.0 copy-start.5
  17.6 3.1 %shard_map.121.refs_0_.refs_4_ = bf16[2048,256]{1,0:T(8,128)(2,1)} custom-call(s32[6]{0:T(128)} %stack.39.place_ref, bf16[1280,256]{1,0:T(8,128)(2,1)} %get-tuple-element.25.p_ref, bf16[256,6144]{1,0:T(8,128)(2,1)} %b_ref.3), custom_call_target="tpu_custom_call" | custom-call | tf_op jit(solution)/shard_map/pallas_call | solution.py:122
  20.7 3.3 %collective-permute-start = (bf16[1,2,2,64,512]{4,3,2,1,0:T(8,128)(2,1)S(1)}, bf16[1,2,2,64,512]{4,3,2,1,0:T(8,128)(2,1)S(1)}, u32[]{:S(2)}, u32[]{:S(2)}) collective-permute-start(bf16[1,2,2,64,512]{4,3,2,1,0:T(8,128)(2,1)S(1)} %maximum_bitcast_fusion), channel_id=1, source_target_pairs={{0,2},{2,0},{4,6},{6,4},{1,3},{3,1},{5,7},{7,5},{8,10},{10,8},{12,... | collective-permute-start | bytes 786440 | tf_op jit(solution)/shard_map/ppermute | solution.py:355
  24.0 4.2 %collective-permute-done = bf16[1,2,2,64,512]{4,3,2,1,0:T(8,128)(2,1)S(1)} collective-permute-done((bf16[1,2,2,64,512]{4,3,2,1,0:T(8,128)(2,1)S(1)}, bf16[1,2,2,64,512]{4,3,2,1,0:T(8,128)(2,1)S(1)}, u32[]{:S(2)}, u32[]{:S(2)}) %collective-permute-start) | collective-permute-done | bytes 262176 | tf_op jit(solution)/shard_map/ppermute | solution.py:355
  28.2 0.1 pad_maximum_fusion.1
  28.3 5.6 %collective-permute-start.1 = (bf16[2,2,2,64,512]{4,3,2,1,0:T(8,128)(2,1)S(1)}, bf16[2,2,2,64,512]{4,3,2,1,0:T(8,128)(2,1)S(1)}, u32[]{:S(2)}, u32[]{:S(2)}) collective-permute-start(bf16[2,2,2,64,512]{4,3,2,1,0:T(8,128)(2,1)S(1)} %pad_maximum_fusion.1), channel_id=1, source_target_pairs={{0,4},{2,6},{4,0},{6,2},{1,5},{3,7},{5,1},{7,3},{8,12},{10,14},{12... | collective-permute-start | bytes 1572872 | tf_op jit(solution)/shard_map/ppermute | solution.py:355
  33.9 4.6 %collective-permute-start.6 = (bf16[1280,256]{1,0:T(8,128)(2,1)S(1)}, bf16[1280,256]{1,0:T(8,128)(2,1)S(1)}, u32[]{:S(2)}, u32[]{:S(2)}) collective-permute-start(bf16[1280,256]{1,0:T(8,128)(2,1)S(1)} %collective-permute-done.3.refs_2_.refs_6_), channel_id=1, source_target_pairs={{0,1},{1,0},{2,3},{3,2},{4,5},{5,4},{6,7},{7,6},{8,9},{9,8},{10,11... | collective-permute-start | bytes 1966088 | tf_op jit(solution)/shard_map/ppermute | solution.py:358
  38.5 0.7 collective-permute-done.4.refs_3_.refs_7_
  39.2 2.9 %collective-permute-start.7 = (bf16[1280,256]{1,0:T(8,128)(2,1)S(1)}, bf16[1280,256]{1,0:T(8,128)(2,1)S(1)}, u32[]{:S(2)}, u32[]{:S(2)}) collective-permute-start(bf16[1280,256]{1,0:T(8,128)(2,1)S(1)} %collective-permute-done.4.refs_3_.refs_7_), channel_id=1, source_target_pairs={{0,1},{1,0},{2,3},{3,2},{4,5},{5,4},{6,7},{7,6},{8,9},{9,8},{10,11... | collective-permute-start | bytes 1966088 | tf_op jit(solution)/shard_map/ppermute | solution.py:358
  42.1 1.9 %collective-permute-start.5 = (bf16[1280,256]{1,0:T(8,128)(2,1)S(1)}, bf16[1280,256]{1,0:T(8,128)(2,1)S(1)}, u32[]{:S(2)}, u32[]{:S(2)}) collective-permute-start(bf16[1280,256]{1,0:T(8,128)(2,1)S(1)} %collective-permute-done.2.refs_1_.refs_5_), channel_id=1, source_target_pairs={{0,1},{1,0},{2,3},{3,2},{4,5},{5,4},{6,7},{7,6},{8,9},{9,8},{10,11... | collective-permute-start | bytes 1966088 | tf_op jit(solution)/shard_map/ppermute | solution.py:358
  44.1 0.1 pad_maximum_fusion.rm_ref
  44.2 1.9 %collective-permute-done.5.refs_8_ = bf16[1280,256]{1,0:T(8,128)(2,1)S(1)} collective-permute-done((bf16[1280,256]{1,0:T(8,128)(2,1)S(1)}, bf16[1280,256]{1,0:T(8,128)(2,1)S(1)}, u32[]{:S(2)}, u32[]{:S(2)}) %collective-permute-start.5) | collective-permute-done | bytes 655392 | tf_op jit(solution)/shard_map/ppermute | solution.py:358
  46.1 1.4 shard_map.123
  47.5 11.3 %collective-permute-start.8 = (bf16[256,1536]{1,0:T(8,128)(2,1)S(1)}, bf16[256,1536]{1,0:T(8,128)(2,1)S(1)}, u32[]{:S(2)}, u32[]{:S(2)}) collective-permute-start(bf16[256,1536]{1,0:T(8,128)(2,1)S(1)} %shard_map.123), channel_id=1, source_target_pairs={{0,32},{1,481},{32,64},{33,1},{64,96},{65,33},{96,128},{97,65},{12... | collective-permute-start | bytes 2359304 | tf_op jit(solution)/shard_map/ppermute | solution.py:367
  58.8 1.5 shard_map.122
  60.3 7.4 %collective-permute-done.8 = bf16[256,1536]{1,0:T(8,128)(2,1)S(1)} collective-permute-done((bf16[256,1536]{1,0:T(8,128)(2,1)S(1)}, bf16[256,1536]{1,0:T(8,128)(2,1)S(1)}, u32[]{:S(2)}, u32[]{:S(2)}) %collective-permute-start.8) | collective-permute-done | bytes 786464 | tf_op jit(solution)/shard_map/ppermute | solution.py:367
  67.7 0.1 fusion
  67.8 4.6 %collective-permute-start.9 = (bf16[128,1536]{1,0:T(8,128)(2,1)S(1)}, bf16[128,1536]{1,0:T(8,128)(2,1)S(1)}, u32[]{:S(2)}, u32[]{:S(2)}) collective-permute-start(bf16[128,1536]{1,0:T(8,128)(2,1)S(1)} %fusion), channel_id=1, source_target_pairs={{0,64},{1,449},{32,96},{33,481},{64,128},{65,1},{96,160},{97,33},{... | collective-permute-start | bytes 1179656 | tf_op jit(solution)/shard_map/ppermute | solution.py:367
  72.4 7.2 %collective-permute-done.9 = bf16[128,1536]{1,0:T(8,128)(2,1)S(1)} collective-permute-done((bf16[128,1536]{1,0:T(8,128)(2,1)S(1)}, bf16[128,1536]{1,0:T(8,128)(2,1)S(1)}, u32[]{:S(2)}, u32[]{:S(2)}) %collective-permute-start.9) | collective-permute-done | bytes 393248 | tf_op jit(solution)/shard_map/ppermute | solution.py:367
  79.6 0.1 fusion.3
  79.7 6.5 %collective-permute-start.10 = (bf16[64,1536]{1,0:T(8,128)(2,1)S(1)}, bf16[64,1536]{1,0:T(8,128)(2,1)S(1)}, u32[]{:S(2)}, u32[]{:S(2)}) collective-permute-start(bf16[64,1536]{1,0:T(8,128)(2,1)S(1)} %fusion.3), channel_id=1, source_target_pairs={{0,128},{1,385},{32,160},{33,417},{64,192},{65,449},{96,224},{97,4... | collective-permute-start | bytes 589832 | tf_op jit(solution)/shard_map/ppermute | solution.py:367
  86.2 5.8 %collective-permute-done.10 = bf16[64,1536]{1,0:T(8,128)(2,1)S(1)} collective-permute-done((bf16[64,1536]{1,0:T(8,128)(2,1)S(1)}, bf16[64,1536]{1,0:T(8,128)(2,1)S(1)}, u32[]{:S(2)}, u32[]{:S(2)}) %collective-permute-start.10) | collective-permute-done | bytes 196640 | tf_op jit(solution)/shard_map/ppermute | solution.py:367
  92.0 0.1 fusion.6
  92.0 11.4 %all-gather = bf16[256,1536]{1,0:T(8,128)(2,1)S(1)} all-gather(bf16[64,1536]{1,0:T(8,128)(2,1)S(1)} %fusion.6), channel_id=2, replica_groups=mesh['zh'=4,'zl'=4,'x'=4,'y'=4,'c'=2] {'x'}, dimensions={0}, use_global_device_ids=true | all-gather | bytes 983040 | tf_op jit(solution)/shard_map/all_gather | solution.py:374
  103.4 0.6 shard_map.124
  104.1 12.4 %all_to_all.10 = bf16[4,4,16,512]{3,2,1,0:T(8,128)(2,1)S(1)} all-to-all(bf16[4,4,16,512]{3,2,1,0:T(8,128)(2,1)S(1)} %bitcast.52), channel_id=1, replica_groups=mesh['zh'=4,'zl'=4,'x'=4,'y'=4,'c'=2] {'zl'}, dimensions={0} | all-to-all | bytes 524288 | tf_op jit(solution)/shard_map/all_to_all | solution.py:377
  116.5 0.7 copy.31
  117.2 10.1 %all-to-all-start.1 = ((bf16[4,4,16,512]{3,2,1,0:T(8,128)(2,1)}), bf16[4,4,16,512]{3,2,1,0:T(8,128)(2,1)S(1)}, u32[]{:S(2)}, u32[]{:S(2)}) async-start(bf16[4,4,16,512]{3,2,1,0:T(8,128)(2,1)} %copy.31), calls=%async_computation.1 | async-start | bytes 524288 | tf_op jit(solution)/shard_map/all_to_all | solution.py:378
  127.3 9.0 %collective-permute-start.12 = (bf16[4,2,2,64,512]{4,3,2,1,0:T(8,128)(2,1)S(1)}, bf16[4,2,2,64,512]{4,3,2,1,0:T(8,128)(2,1)S(1)}, u32[]{:S(2)}, u32[]{:S(2)}) collective-permute-start(bf16[4,2,2,64,512]{4,3,2,1,0:T(8,128)(2,1)S(1)} %pad_maximum_fusion.rm_ref), channel_id=1, source_target_pairs={{0,1},{1,0},{2,3},{3,2},{4,5},{5,4},{6,7},{7,6},{8,9},{9,8},{10,11... | collective-permute-start | bytes 3145736 | tf_op jit(solution)/shard_map/ppermute | solution.py:359
  136.3 0.2 fusion.19
  136.5 4.1 %all-to-all-done.1 = bf16[4,4,16,512]{3,2,1,0:T(8,128)(2,1)S(1)} async-done(((bf16[4,4,16,512]{3,2,1,0:T(8,128)(2,1)}), bf16[4,4,16,512]{3,2,1,0:T(8,128)(2,1)S(1)}, u32[]{:S(2)}, u32[]{:S(2)}) %all-to-all-start.1) | async-done | bytes 262176 | tf_op jit(solution)/shard_map/all_to_all | solution.py:378
  140.6 1.5 shard_map.125
  142.1 10.8 %all-gather.1 = bf16[576,512]{1,0:T(8,128)(2,1)S(1)} all-gather(bf16[144,512]{1,0:T(8,128)(2,1)S(1)} %get-tuple-element.32), channel_id=3, replica_groups=mesh['zh'=4,'zl'=4,'x'=4,'y'=4,'c'=2] {'y'}, dimensions={0}, use_global_device_ids=true | all-gather | bytes 737280 | tf_op jit(solution)/shard_map/all_gather | solution.py:385
  152.9 12.6 %collective-permute-start.11 = (bf16[4,144,512]{2,1,0:T(8,128)(2,1)S(1)}, bf16[4,144,512]{2,1,0:T(8,128)(2,1)}, u32[]{:S(2)}, u32[]{:S(2)}) collective-permute-start(bf16[4,144,512]{2,1,0:T(8,128)(2,1)S(1)} %bitcast.49), channel_id=1, source_target_pairs={{0,1},{1,0},{2,3},{3,2},{4,5},{5,4},{6,7},{7,6},{8,9},{9,8},{10,11... | collective-permute-start | bytes 1769480 | tf_op jit(solution)/shard_map/ppermute | solution.py:386
  165.5 0.2 compare_reduce_fusion
  165.7 0.1 concatenate.10.f_ref
  165.8 1.5 collective-permute-done.11.o_ref
  167.3 5.1 %shard_map.126 = (f32[2,64,512]{2,1,0:T(8,128)}, f32[2,64,512]{2,1,0:T(8,128)}, bf16[2,512,512]{2,1,0:T(8,128)(2,1)}) custom-call(s32[7]{0:T(128)S(1)} %concatenate.10.f_ref, bf16[4,144,512]{2,1,0:T(8,128)(2,1)S(1)} %bitcast.50, bf16[4,144,512]{2,1,0:T(8,128)(2,1)} %collective-permute-done.11.o_ref, bf16[4,2,2,64,512]{4,3,2,1,0:T(8,128)(2,1)S(1)} %pad_maximum_fusion.rm_ref, ...), custom_call_target="tpu_custom_call" | custom-call | tf_op jit(solution)/shard_map/pallas_call | solution.py:292
  (31 shorter events, 0.2 us)
Async XLA Ops:
  1.3 15.5 %copy-start.7 = (s32[96]{0:T(128)S(1)}, s32[96]{0:T(128)}, u32[]{:S(2)}) copy-start(s32[96]{0:T(128)} %param.11) | copy-start | bytes 1156
  4.8 29.1 %collective-permute-start.3 = (bf16[1280,256]{1,0:T(8,128)(2,1)}, bf16[1280,256]{1,0:T(8,128)(2,1)S(1)}, u32[]{:S(2)}, u32[]{:S(2)}) collective-permute-start(bf16[1280,256]{1,0:T(8,128)(2,1)} %get-tuple-element.30), channel_id=1, source_target_pairs={{0,16},{8,24},{16,0},{24,8},{1,17},{9,25},{17,1},{25,9},{2,18},{10... | collective-permute-start | bytes 1966088 | tf_op jit(solution)/shard_map/ppermute | solution.py:334
  10.3 28.9 %collective-permute-start.4 = (bf16[1280,256]{1,0:T(8,128)(2,1)}, bf16[1280,256]{1,0:T(8,128)(2,1)S(1)}, u32[]{:S(2)}, u32[]{:S(2)}) collective-permute-start(bf16[1280,256]{1,0:T(8,128)(2,1)} %get-tuple-element.31), channel_id=1, source_target_pairs={{0,8},{8,16},{16,24},{24,0},{1,9},{9,17},{17,25},{25,1},{2,10},{10... | collective-permute-start | bytes 1966088 | tf_op jit(solution)/shard_map/ppermute | solution.py:334
  12.5 29.6 %collective-permute-start.2 = (bf16[1280,256]{1,0:T(8,128)(2,1)}, bf16[1280,256]{1,0:T(8,128)(2,1)S(1)}, u32[]{:S(2)}, u32[]{:S(2)}) collective-permute-start(bf16[1280,256]{1,0:T(8,128)(2,1)} %get-tuple-element.25.p_ref), channel_id=1, source_target_pairs={{0,24},{8,0},{16,8},{24,16},{1,25},{9,1},{17,9},{25,17},{2,26},{10... | collective-permute-start | bytes 1966088 | tf_op jit(solution)/shard_map/ppermute | solution.py:334
  17.5 3.1 %copy-start.4 = (bf16[1,2,64,512]{3,2,1,0:T(8,128)(2,1)S(1)}, bf16[1,2,64,512]{3,2,1,0:T(8,128)(2,1)}, u32[]{:S(2)}) copy-start(bf16[1,2,64,512]{3,2,1,0:T(8,128)(2,1)} %param.16) | copy-start | bytes 393220
  17.5 3.1 %copy-start.5 = (bf16[1,2,64,512]{3,2,1,0:T(8,128)(2,1)S(1)}, bf16[1,2,64,512]{3,2,1,0:T(8,128)(2,1)}, u32[]{:S(2)}) copy-start(bf16[1,2,64,512]{3,2,1,0:T(8,128)(2,1)} %param.15) | copy-start | bytes 393220
  20.6 25.5 %copy-start = (bf16[2048,256]{1,0:T(8,128)(2,1)S(1)}, bf16[2048,256]{1,0:T(8,128)(2,1)}, u32[]{:S(2)}) copy-start(bf16[2048,256]{1,0:T(8,128)(2,1)} %shard_map.121.refs_0_.refs_4_) | copy-start | bytes 3145732
  20.7 7.5 %collective-permute-start = (bf16[1,2,2,64,512]{4,3,2,1,0:T(8,128)(2,1)S(1)}, bf16[1,2,2,64,512]{4,3,2,1,0:T(8,128)(2,1)S(1)}, u32[]{:S(2)}, u32[]{:S(2)}) collective-permute-start(bf16[1,2,2,64,512]{4,3,2,1,0:T(8,128)(2,1)S(1)} %maximum_bitcast_fusion), channel_id=1, source_target_pairs={{0,2},{2,0},{4,6},{6,4},{1,3},{3,1},{5,7},{7,5},{8,10},{10,8},{12,... | collective-permute-start | bytes 786440 | tf_op jit(solution)/shard_map/ppermute | solution.py:355
  28.3 15.8 %collective-permute-start.1 = (bf16[2,2,2,64,512]{4,3,2,1,0:T(8,128)(2,1)S(1)}, bf16[2,2,2,64,512]{4,3,2,1,0:T(8,128)(2,1)S(1)}, u32[]{:S(2)}, u32[]{:S(2)}) collective-permute-start(bf16[2,2,2,64,512]{4,3,2,1,0:T(8,128)(2,1)S(1)} %pad_maximum_fusion.1), channel_id=1, source_target_pairs={{0,4},{2,6},{4,0},{6,2},{1,5},{3,7},{5,1},{7,3},{8,12},{10,14},{12... | collective-permute-start | bytes 1572872 | tf_op jit(solution)/shard_map/ppermute | solution.py:355
  33.9 10.3 %collective-permute-start.6 = (bf16[1280,256]{1,0:T(8,128)(2,1)S(1)}, bf16[1280,256]{1,0:T(8,128)(2,1)S(1)}, u32[]{:S(2)}, u32[]{:S(2)}) collective-permute-start(bf16[1280,256]{1,0:T(8,128)(2,1)S(1)} %collective-permute-done.3.refs_2_.refs_6_), channel_id=1, source_target_pairs={{0,1},{1,0},{2,3},{3,2},{4,5},{5,4},{6,7},{7,6},{8,9},{9,8},{10,11... | collective-permute-start | bytes 1966088 | tf_op jit(solution)/shard_map/ppermute | solution.py:358
  39.2 5.0 %collective-permute-start.7 = (bf16[1280,256]{1,0:T(8,128)(2,1)S(1)}, bf16[1280,256]{1,0:T(8,128)(2,1)S(1)}, u32[]{:S(2)}, u32[]{:S(2)}) collective-permute-start(bf16[1280,256]{1,0:T(8,128)(2,1)S(1)} %collective-permute-done.4.refs_3_.refs_7_), channel_id=1, source_target_pairs={{0,1},{1,0},{2,3},{3,2},{4,5},{5,4},{6,7},{7,6},{8,9},{9,8},{10,11... | collective-permute-start | bytes 1966088 | tf_op jit(solution)/shard_map/ppermute | solution.py:358
  42.1 4.0 %collective-permute-start.5 = (bf16[1280,256]{1,0:T(8,128)(2,1)S(1)}, bf16[1280,256]{1,0:T(8,128)(2,1)S(1)}, u32[]{:S(2)}, u32[]{:S(2)}) collective-permute-start(bf16[1280,256]{1,0:T(8,128)(2,1)S(1)} %collective-permute-done.2.refs_1_.refs_5_), channel_id=1, source_target_pairs={{0,1},{1,0},{2,3},{3,2},{4,5},{5,4},{6,7},{7,6},{8,9},{9,8},{10,11... | collective-permute-start | bytes 1966088 | tf_op jit(solution)/shard_map/ppermute | solution.py:358
  47.5 20.3 %collective-permute-start.8 = (bf16[256,1536]{1,0:T(8,128)(2,1)S(1)}, bf16[256,1536]{1,0:T(8,128)(2,1)S(1)}, u32[]{:S(2)}, u32[]{:S(2)}) collective-permute-start(bf16[256,1536]{1,0:T(8,128)(2,1)S(1)} %shard_map.123), channel_id=1, source_target_pairs={{0,32},{1,481},{32,64},{33,1},{64,96},{65,33},{96,128},{97,65},{12... | collective-permute-start | bytes 2359304 | tf_op jit(solution)/shard_map/ppermute | solution.py:367
  67.8 11.8 %collective-permute-start.9 = (bf16[128,1536]{1,0:T(8,128)(2,1)S(1)}, bf16[128,1536]{1,0:T(8,128)(2,1)S(1)}, u32[]{:S(2)}, u32[]{:S(2)}) collective-permute-start(bf16[128,1536]{1,0:T(8,128)(2,1)S(1)} %fusion), channel_id=1, source_target_pairs={{0,64},{1,449},{32,96},{33,481},{64,128},{65,1},{96,160},{97,33},{... | collective-permute-start | bytes 1179656 | tf_op jit(solution)/shard_map/ppermute | solution.py:367
  79.7 12.3 %collective-permute-start.10 = (bf16[64,1536]{1,0:T(8,128)(2,1)S(1)}, bf16[64,1536]{1,0:T(8,128)(2,1)S(1)}, u32[]{:S(2)}, u32[]{:S(2)}) collective-permute-start(bf16[64,1536]{1,0:T(8,128)(2,1)S(1)} %fusion.3), channel_id=1, source_target_pairs={{0,128},{1,385},{32,160},{33,417},{64,192},{65,449},{96,224},{97,4... | collective-permute-start | bytes 589832 | tf_op jit(solution)/shard_map/ppermute | solution.py:367
  103.4 32.9 %copy-start.6 = (s32[96]{0:T(128)S(1)}, s32[96]{0:T(128)}, u32[]{:S(2)}) copy-start(s32[96]{0:T(128)} %param.12) | copy-start | bytes 1156
  103.4 37.2 %copy-start.3 = (f32[1,2,64,512]{3,2,1,0:T(8,128)S(1)}, f32[1,2,64,512]{3,2,1,0:T(8,128)}, u32[]{:S(2)}) copy-start(f32[1,2,64,512]{3,2,1,0:T(8,128)} %param.17) | copy-start | bytes 786436
  104.0 63.2 %copy-start.1 = (f32[1,2,64,512]{3,2,1,0:T(8,128)S(1)}, f32[1,2,64,512]{3,2,1,0:T(8,128)}, u32[]{:S(2)}) copy-start(f32[1,2,64,512]{3,2,1,0:T(8,128)} %param.13) | copy-start | bytes 786436
  104.0 63.2 %copy-start.2 = (f32[1,2,64,512]{3,2,1,0:T(8,128)S(1)}, f32[1,2,64,512]{3,2,1,0:T(8,128)}, u32[]{:S(2)}) copy-start(f32[1,2,64,512]{3,2,1,0:T(8,128)} %param.14) | copy-start | bytes 786436
  117.2 23.4 %all-to-all-start.1 = ((bf16[4,4,16,512]{3,2,1,0:T(8,128)(2,1)}), bf16[4,4,16,512]{3,2,1,0:T(8,128)(2,1)S(1)}, u32[]{:S(2)}, u32[]{:S(2)}) async-start(bf16[4,4,16,512]{3,2,1,0:T(8,128)(2,1)} %copy.31), calls=%async_computation.1 | async-start | bytes 524288 | tf_op jit(solution)/shard_map/all_to_all | solution.py:378
  127.3 38.5 %collective-permute-start.12 = (bf16[4,2,2,64,512]{4,3,2,1,0:T(8,128)(2,1)S(1)}, bf16[4,2,2,64,512]{4,3,2,1,0:T(8,128)(2,1)S(1)}, u32[]{:S(2)}, u32[]{:S(2)}) collective-permute-start(bf16[4,2,2,64,512]{4,3,2,1,0:T(8,128)(2,1)S(1)} %pad_maximum_fusion.rm_ref), channel_id=1, source_target_pairs={{0,1},{1,0},{2,3},{3,2},{4,5},{5,4},{6,7},{7,6},{8,9},{9,8},{10,11... | collective-permute-start | bytes 3145736 | tf_op jit(solution)/shard_map/ppermute | solution.py:359
  152.9 14.3 %collective-permute-start.11 = (bf16[4,144,512]{2,1,0:T(8,128)(2,1)S(1)}, bf16[4,144,512]{2,1,0:T(8,128)(2,1)}, u32[]{:S(2)}, u32[]{:S(2)}) collective-permute-start(bf16[4,144,512]{2,1,0:T(8,128)(2,1)S(1)} %bitcast.49), channel_id=1, source_target_pairs={{0,1},{1,0},{2,3},{3,2},{4,5},{5,4},{6,7},{7,6},{8,9},{9,8},{10,11... | collective-permute-start | bytes 1769480 | tf_op jit(solution)/shard_map/ppermute | solution.py:386

commit v9 on v7

--- a/solution.py
+++ b/solution.py
@@ -11,6 +11,7 @@
 WIDE = jnp.float32
 NZ, NX, NC = 16, 4, 2
 TILES = 6
+CHUNKS = 2
 ROOMY = pltpu.CompilerParams(vmem_limit_bytes=60 * 1024 * 1024)
 PARAMS = pltpu.CompilerParams(vmem_limit_bytes=8 * 1024 * 1024)
 
@@ -134,13 +135,13 @@
     )(place, piece, out_grads)
 
 
-def partial_products(own, arrived, swapped, odd):
+def partial_products(own, arrived, swapped, odd, chunk):
     toks = own.shape[1]
     half = toks // NC
     total_rows = own.shape[0] - TILES * toks
     count = total_rows // 2
     kind = HALF if odd else WIDE
-    group = 2
+    group = TILES // CHUNKS
 
     def kernel(*refs):
         rows_refs, own_ref, mine, other, out_ref = refs[:4], refs[4], refs[5:8], refs[8:11], refs[11]
@@ -152,22 +153,24 @@
             to = slice(n * toks, (n + 1) * toks)
             out_ref[:, to] = total.astype(kind)
 
+    def block(skip, size):
+        first = pl.Element(size)
+        return pl.BlockSpec((first, pl.Element(toks)), lambda n: (skip + chunk * size, 0))
+
     rows = pl.BlockSpec((count, toks), lambda n: (0 if odd else 1, 0))
-    columns = pl.BlockSpec((group * half, toks), lambda n: (total_rows // (group * half) + n, 0))
-    own_columns = pl.BlockSpec((group * toks, toks), lambda n: (total_rows // (group * toks) + n, 0))
-    return pl.pallas_call(
-        kernel,
-        grid=(TILES // group,),
-        out_shape=jax.ShapeDtypeStruct((count, TILES * toks), kind),
-        in_specs=[rows] * 4 + [own_columns] + [columns] * 6,
-        out_specs=pl.BlockSpec((count, group * toks), lambda n: (0, n)),
+    return pl.pallas_call(
+        kernel,
+        grid=(1,),
+        out_shape=jax.ShapeDtypeStruct((count, group * toks), kind),
+        in_specs=[rows] * 4 + [block(total_rows, group * toks)] + [block(total_rows, group * half)] * 6,
+        out_specs=pl.BlockSpec((count, group * toks), lambda n: (0, 0)),
         compiler_params=PARAMS,
     )(own, *arrived, own, *arrived, *swapped)
 
 
 def pick_blocks(chosen, sums, block_size):
-    sources, rows, width = sums.shape
-    columns = width // block_size
+    sources, rows, width = sums.shape[0], sums.shape[1] // CHUNKS, sums.shape[2]
+    columns = CHUNKS * width // block_size
     out_rows = chosen.shape[0]
     tile = out_rows // 2
 
@@ -175,11 +178,10 @@
         total = None
         for pair in range(sources // 2):
             depth = 2 * columns * rows
-            pieces = [
-                s_ref[x, :, j * block_size : (j + 1) * block_size]
-                for x in (2 * pair, 2 * pair + 1)
-                for j in range(columns)
-            ]
+            pieces = []
+            for x in (2 * pair, 2 * pair + 1):
+                whole = jnp.concatenate([s_ref[x, k * rows : (k + 1) * rows, :] for k in range(CHUNKS)], axis=1)
+                pieces += [whole[:, j * block_size : (j + 1) * block_size] for j in range(columns)]
             term = dot(p_ref[:, pair * depth : (pair + 1) * depth], jnp.concatenate(pieces, axis=0))
             total = term if total is None else total + term
         o_ref[...] = total.astype(HALF)
@@ -327,9 +329,9 @@
     my_mp = y * NC + c
     my_rows = my_mp * rows
 
-    place = jnp.stack([z, x, c] + [jnp.bitwise_and(x + step, NX - 1) for step in (3, 2, 1)]).astype(jnp.int32)
+    place = jnp.stack([z, x, c] + [jnp.bitwise_and(x + step, NX - 1) for step in (2, 3, 1)]).astype(jnp.int32)
     pieces = prepare(activations, out_grads, place)
-    arrived = [lax.ppermute(piece, "x", ring(NX, step)) for piece, step in zip(pieces, (-1, 2, 1))]
+    arrived = [lax.ppermute(piece, "x", ring(NX, step)) for piece, step in zip(pieces, (2, -1, 1))]
 
     piece_own, owners = lax.optimization_barrier((pieces[0], owners))
     targets = slot_targets(owners, slots)
@@ -354,20 +356,23 @@
     swapped = [lax.ppermute(piece, "c", ring(NC, 1)) for piece in arrived]
     roots_other = lax.ppermute(roots, "c", ring(NC, 1))
 
-    sent = partial_products(own, arrived, swapped, True)
-    kept = partial_products(own, arrived, swapped, False)
-
-    got = []
-    for step in (1, 2, 4):
-        goals = [((i + (1 - 2 * k) * step) % NZ) * NC + k for i in range(NZ) for k in range(NC)]
-        got.append(lax.ppermute(sent, ("z", "c"), list(enumerate(goals))))
-        part = got[-1].shape[0] // (2 if step < 4 else 1)
-        rows_from = slice(part, 2 * part) if step < 4 else slice(0, part)
-        total = kept[rows_from]
-        for rows_in in got:
-            total = total + rows_in[rows_from]
-        sent = total.astype(HALF)
-    sums = lax.all_gather(sent, "x", axis=0, tiled=False)
+    sent = [partial_products(own, arrived, swapped, True, chunk) for chunk in range(CHUNKS)]
+    kept = [partial_products(own, arrived, swapped, False, chunk) for chunk in range(CHUNKS)]
+
+    sums = []
+    for out, keep in zip(sent, kept):
+        got = []
+        for step in (1, 2, 4):
+            goals = [((i + (1 - 2 * k) * step) % NZ) * NC + k for i in range(NZ) for k in range(NC)]
+            got.append(lax.ppermute(out, ("z", "c"), list(enumerate(goals))))
+            part = got[-1].shape[0] // (2 if step < 4 else 1)
+            rows_from = slice(part, 2 * part) if step < 4 else slice(0, part)
+            total = keep[rows_from]
+            for rows_in in got:
+                total = total + rows_in[rows_from]
+            out = total.astype(HALF)
+        sums.append(out)
+    sums = lax.all_gather(jnp.concatenate(sums, axis=0), "x", axis=0, tiled=False)
 
     picked = pick_blocks(chosen, sums, block_size).reshape(NZ, out_rows // NZ, block_size)
     arrived = lax.all_to_all(picked, "z", 0, 0, tiled=True).reshape(out_rows, block_size)

time: 163 us -> 156 us (0.957)
  waiting for transfers between devices: 33.5 us -> 20 us
  starting transfers between devices: 86.4 us -> 93 us
    ppermute x3 -> x6, waiting for transfers between devices: 20.4 us -> 6.8 us  [body(): got.append(lax.ppermute(out, ('z', 'c'), list(enumerate(goals))))]
    ppermute x3 -> x6, starting transfers between devices: 22.4 us -> 33.2 us  [body(): got.append(lax.ppermute(out, ('z', 'c'), list(enumerate(goals))))]
    all_to_all x1, starting transfers between devices: 14.2 us -> 8.38 us  [body(): lax.all_to_all(picked, 'z', 0, 0, tiled=True).reshape(out_rows, block_size)]
  transfers between devices with their start and end apart: 14 -> 17, of which waited for: 8 -> 8; matrix products, arithmetic and copies ran while one was open for 1% -> 1% of each run, Pallas kernels for 4% -> 4%
where the time goes in v9:
time: 156 us; the launch traced here: 155 us
  starting transfers between devices  93 us (60%)
  blocking collectives  21.8 us (14%)
  waiting for transfers between devices  20 us (13%)
  Pallas kernels  16.6 us (11%)
    ppermute x6, starting transfers between devices, body(): got.append(lax.ppermute(out, ('z', 'c'), list(enumerate(goals))))  33.2 us
    ppermute x1, starting transfers between devices, body(): rows_other = lax.ppermute(rows_mine, 'c', ring(NC, 1))  12.8 us
    all_gather x1, blocking collectives, body(): lax.all_gather(jnp.concatenate(sums, axis=0), 'x', axis=0, tiled=False)  11 us
    ppermute x3, starting transfers between devices, body(): lax.ppermute(piece, 'x', ring(NX, step))  10.9 us
    all_gather x1, blocking collectives, body(): rows_mine = lax.all_gather(own_rows, 'y', axis=0, tiled=False)  10.8 us
    ppermute x3, starting transfers between devices, body(): swapped = [lax.ppermute(piece, 'c', ring(NC, 1)) for piece in arrived]  9.9 us
    ppermute x1, starting transfers between devices, body(): roots_other = lax.ppermute(roots, 'c', ring(NC, 1))  8.99 us
    ppermute x2, starting transfers between devices, body(): came = lax.ppermute(roots, 'y', [(i, i ^ step) for i in range(ny)])  8.92 us
  transfers between devices with their start and end apart: 17, of which 8 were waited for; matrix products, arithmetic and copies ran while one was open for 1% of the time, Pallas kernels for 4%

profile of v9, /device:TPU:1, one launch (start us, length us, event | category | flops | bytes accessed | tf_op | source)
XLA Modules:
  0.0 154.8 jit_solution(9511611903800079492)
XLA Ops:
  0.7 0.6 stack.39.place_ref
  1.3 3.4 %shard_map.120 = (bf16[1280,256]{1,0:T(8,128)(2,1)}, bf16[1280,256]{1,0:T(8,128)(2,1)}, bf16[1280,256]{1,0:T(8,128)(2,1)}) custom-call(s32[6]{0:T(128)} %stack.39.place_ref, bf16[8,64,256]{2,1,0:T(8,128)(2,1)} %a_ref.1, bf16[256,6144]{1,0:T(8,128)(2,1)} %b_ref.3), custom_call_target="tpu_custom_call" | custom-call | tf_op jit(solution)/shard_map/pallas_call | solution.py:87
  4.8 5.6 %collective-permute-start.2 = (bf16[1280,256]{1,0:T(8,128)(2,1)}, bf16[1280,256]{1,0:T(8,128)(2,1)S(1)}, u32[]{:S(2)}, u32[]{:S(2)}) collective-permute-start(bf16[1280,256]{1,0:T(8,128)(2,1)} %get-tuple-element.25.p_ref), channel_id=1, source_target_pairs={{0,16},{8,24},{16,0},{24,8},{1,17},{9,25},{17,1},{25,9},{2,18},{10... | collective-permute-start | bytes 1966088 | tf_op jit(solution)/shard_map/ppermute | solution.py:334
  10.4 2.8 %collective-permute-start.3 = (bf16[1280,256]{1,0:T(8,128)(2,1)}, bf16[1280,256]{1,0:T(8,128)(2,1)S(1)}, u32[]{:S(2)}, u32[]{:S(2)}) collective-permute-start(bf16[1280,256]{1,0:T(8,128)(2,1)} %get-tuple-element.30), channel_id=1, source_target_pairs={{0,24},{8,0},{16,8},{24,16},{1,25},{9,1},{17,9},{25,17},{2,26},{10... | collective-permute-start | bytes 1966088 | tf_op jit(solution)/shard_map/ppermute | solution.py:334
  13.2 2.5 %collective-permute-start.4 = (bf16[1280,256]{1,0:T(8,128)(2,1)}, bf16[1280,256]{1,0:T(8,128)(2,1)S(1)}, u32[]{:S(2)}, u32[]{:S(2)}) collective-permute-start(bf16[1280,256]{1,0:T(8,128)(2,1)} %get-tuple-element.31), channel_id=1, source_target_pairs={{0,8},{8,16},{16,24},{24,0},{1,9},{9,17},{17,25},{25,1},{2,10},{10... | collective-permute-start | bytes 1966088 | tf_op jit(solution)/shard_map/ppermute | solution.py:334
  15.7 0.2 select_reduce_fusion
  15.9 0.1 reshape.110
  16.0 0.1 copy.19
  16.2 0.1 select_n.49
  16.3 0.1 fusion.p_ref
  16.4 2.9 %shard_map.121.refs_0_.refs_4_ = bf16[2048,256]{1,0:T(8,128)(2,1)} custom-call(s32[6]{0:T(128)} %stack.39.place_ref, bf16[1280,256]{1,0:T(8,128)(2,1)} %get-tuple-element.25.p_ref, bf16[256,6144]{1,0:T(8,128)(2,1)} %b_ref.3), custom_call_target="tpu_custom_call" | custom-call | tf_op jit(solution)/shard_map/pallas_call | solution.py:122
  19.4 3.3 %collective-permute-start = (bf16[1,2,2,64,512]{4,3,2,1,0:T(8,128)(2,1)S(1)}, bf16[1,2,2,64,512]{4,3,2,1,0:T(8,128)(2,1)S(1)}, u32[]{:S(2)}, u32[]{:S(2)}) collective-permute-start(bf16[1,2,2,64,512]{4,3,2,1,0:T(8,128)(2,1)S(1)} %maximum_bitcast_fusion), channel_id=1, source_target_pairs={{0,2},{2,0},{4,6},{6,4},{1,3},{3,1},{5,7},{7,5},{8,10},{10,8},{12,... | collective-permute-start | bytes 786440 | tf_op jit(solution)/shard_map/ppermute | solution.py:353
  22.7 4.2 %collective-permute-done = bf16[1,2,2,64,512]{4,3,2,1,0:T(8,128)(2,1)S(1)} collective-permute-done((bf16[1,2,2,64,512]{4,3,2,1,0:T(8,128)(2,1)S(1)}, bf16[1,2,2,64,512]{4,3,2,1,0:T(8,128)(2,1)S(1)}, u32[]{:S(2)}, u32[]{:S(2)}) %collective-permute-start) | collective-permute-done | bytes 262176 | tf_op jit(solution)/shard_map/ppermute | solution.py:353
  26.9 0.1 pad_maximum_fusion.1
  27.0 5.6 %collective-permute-start.1 = (bf16[2,2,2,64,512]{4,3,2,1,0:T(8,128)(2,1)S(1)}, bf16[2,2,2,64,512]{4,3,2,1,0:T(8,128)(2,1)S(1)}, u32[]{:S(2)}, u32[]{:S(2)}) collective-permute-start(bf16[2,2,2,64,512]{4,3,2,1,0:T(8,128)(2,1)S(1)} %pad_maximum_fusion.1), channel_id=1, source_target_pairs={{0,4},{2,6},{4,0},{6,2},{1,5},{3,7},{5,1},{7,3},{8,12},{10,14},{12... | collective-permute-start | bytes 1572872 | tf_op jit(solution)/shard_map/ppermute | solution.py:353
  32.6 4.6 %collective-permute-start.5 = (bf16[1280,256]{1,0:T(8,128)(2,1)S(1)}, bf16[1280,256]{1,0:T(8,128)(2,1)S(1)}, u32[]{:S(2)}, u32[]{:S(2)}) collective-permute-start(bf16[1280,256]{1,0:T(8,128)(2,1)S(1)} %collective-permute-done.2.refs_1_.refs_5_), channel_id=1, source_target_pairs={{0,1},{1,0},{2,3},{3,2},{4,5},{5,4},{6,7},{7,6},{8,9},{9,8},{10,11... | collective-permute-start | bytes 1966088 | tf_op jit(solution)/shard_map/ppermute | solution.py:356
  37.2 2.0 %collective-permute-done.3.refs_2_.refs_6_ = bf16[1280,256]{1,0:T(8,128)(2,1)S(1)} collective-permute-done((bf16[1280,256]{1,0:T(8,128)(2,1)}, bf16[1280,256]{1,0:T(8,128)(2,1)S(1)}, u32[]{:S(2)}, u32[]{:S(2)}) %collective-permute-start.3) | collective-permute-done | bytes 655392 | tf_op jit(solution)/shard_map/ppermute | solution.py:334
  39.2 3.3 %collective-permute-start.6 = (bf16[1280,256]{1,0:T(8,128)(2,1)S(1)}, bf16[1280,256]{1,0:T(8,128)(2,1)S(1)}, u32[]{:S(2)}, u32[]{:S(2)}) collective-permute-start(bf16[1280,256]{1,0:T(8,128)(2,1)S(1)} %collective-permute-done.3.refs_2_.refs_6_), channel_id=1, source_target_pairs={{0,1},{1,0},{2,3},{3,2},{4,5},{5,4},{6,7},{7,6},{8,9},{9,8},{10,11... | collective-permute-start | bytes 1966088 | tf_op jit(solution)/shard_map/ppermute | solution.py:356
  42.6 1.9 %collective-permute-start.7 = (bf16[1280,256]{1,0:T(8,128)(2,1)S(1)}, bf16[1280,256]{1,0:T(8,128)(2,1)S(1)}, u32[]{:S(2)}, u32[]{:S(2)}) collective-permute-start(bf16[1280,256]{1,0:T(8,128)(2,1)S(1)} %collective-permute-done.4.refs_3_.refs_7_), channel_id=1, source_target_pairs={{0,1},{1,0},{2,3},{3,2},{4,5},{5,4},{6,7},{7,6},{8,9},{9,8},{10,11... | collective-permute-start | bytes 1966088 | tf_op jit(solution)/shard_map/ppermute | solution.py:356
  44.5 0.1 pad_maximum_fusion.rm_ref
  44.6 1.9 %collective-permute-done.7.refs_10_ = bf16[1280,256]{1,0:T(8,128)(2,1)S(1)} collective-permute-done((bf16[1280,256]{1,0:T(8,128)(2,1)S(1)}, bf16[1280,256]{1,0:T(8,128)(2,1)S(1)}, u32[]{:S(2)}, u32[]{:S(2)}) %collective-permute-start.7) | collective-permute-done | bytes 655392 | tf_op jit(solution)/shard_map/ppermute | solution.py:356
  46.6 0.6 shard_map.125
  47.1 11.1 %collective-permute-start.11 = (bf16[256,768]{1,0:T(8,128)(2,1)S(1)}, bf16[256,768]{1,0:T(8,128)(2,1)S(1)}, u32[]{:S(2)}, u32[]{:S(2)}) collective-permute-start(bf16[256,768]{1,0:T(8,128)(2,1)S(1)} %shard_map.125), channel_id=1, source_target_pairs={{0,32},{1,481},{32,64},{33,1},{64,96},{65,33},{96,128},{97,65},{12... | collective-permute-start | bytes 1179656 | tf_op jit(solution)/shard_map/ppermute | solution.py:367
  58.3 0.6 shard_map.123
  58.9 2.6 %collective-permute-start.8 = (bf16[256,768]{1,0:T(8,128)(2,1)S(1)}, bf16[256,768]{1,0:T(8,128)(2,1)S(1)}, u32[]{:S(2)}, u32[]{:S(2)}) collective-permute-start(bf16[256,768]{1,0:T(8,128)(2,1)S(1)} %shard_map.123), channel_id=1, source_target_pairs={{0,32},{1,481},{32,64},{33,1},{64,96},{65,33},{96,128},{97,65},{12... | collective-permute-start | bytes 1179656 | tf_op jit(solution)/shard_map/ppermute | solution.py:367
  61.5 0.6 shard_map.124
  62.1 0.6 shard_map.122
  62.7 0.3 collective-permute-done.11
  63.0 4.7 %collective-permute-start.12 = (bf16[128,768]{1,0:T(8,128)(2,1)S(1)}, bf16[128,768]{1,0:T(8,128)(2,1)S(1)}, u32[]{:S(2)}, u32[]{:S(2)}) collective-permute-start(bf16[128,768]{1,0:T(8,128)(2,1)S(1)} %fusion.1), channel_id=1, source_target_pairs={{0,64},{1,449},{32,96},{33,481},{64,128},{65,1},{96,160},{97,33},{... | collective-permute-start | bytes 589832 | tf_op jit(solution)/shard_map/ppermute | solution.py:367
  67.8 4.0 %collective-permute-start.9 = (bf16[128,768]{1,0:T(8,128)(2,1)S(1)}, bf16[128,768]{1,0:T(8,128)(2,1)S(1)}, u32[]{:S(2)}, u32[]{:S(2)}) collective-permute-start(bf16[128,768]{1,0:T(8,128)(2,1)S(1)} %fusion.2), channel_id=1, source_target_pairs={{0,64},{1,449},{32,96},{33,481},{64,128},{65,1},{96,160},{97,33},{... | collective-permute-start | bytes 589832 | tf_op jit(solution)/shard_map/ppermute | solution.py:367
  71.8 1.1 collective-permute-done.12
  73.0 5.6 %collective-permute-start.13 = (bf16[64,768]{1,0:T(8,128)(2,1)S(1)}, bf16[64,768]{1,0:T(8,128)(2,1)S(1)}, u32[]{:S(2)}, u32[]{:S(2)}) collective-permute-start(bf16[64,768]{1,0:T(8,128)(2,1)S(1)} %fusion.4), channel_id=1, source_target_pairs={{0,128},{1,385},{32,160},{33,417},{64,192},{65,449},{96,224},{97,4... | collective-permute-start | bytes 294920 | tf_op jit(solution)/shard_map/ppermute | solution.py:367
  78.6 5.2 %collective-permute-start.10 = (bf16[64,768]{1,0:T(8,128)(2,1)S(1)}, bf16[64,768]{1,0:T(8,128)(2,1)S(1)}, u32[]{:S(2)}, u32[]{:S(2)}) collective-permute-start(bf16[64,768]{1,0:T(8,128)(2,1)S(1)} %fusion.9), channel_id=1, source_target_pairs={{0,128},{1,385},{32,160},{33,417},{64,192},{65,449},{96,224},{97,4... | collective-permute-start | bytes 294920 | tf_op jit(solution)/shard_map/ppermute | solution.py:367
  83.8 0.1 fusion.7
  83.9 5.4 %collective-permute-done.10 = bf16[64,768]{1,0:T(8,128)(2,1)S(1)} collective-permute-done((bf16[64,768]{1,0:T(8,128)(2,1)S(1)}, bf16[64,768]{1,0:T(8,128)(2,1)S(1)}, u32[]{:S(2)}, u32[]{:S(2)}) %collective-permute-start.10) | collective-permute-done | bytes 98336 | tf_op jit(solution)/shard_map/ppermute | solution.py:367
  89.3 11.0 %all-gather = bf16[512,768]{1,0:T(8,128)(2,1)S(1)} all-gather(bf16[128,768]{1,0:T(8,128)(2,1)S(1)} %pad_maximum_fusion.2), channel_id=2, replica_groups=mesh['z'=16,'x'=4,'y'=4,'c'=2] {'x'}, dimensions={0}, use_global_device_ids=true | all-gather | bytes 983040 | tf_op jit(solution)/shard_map/all_gather | solution.py:375
  100.3 1.3 shard_map.126
  101.6 8.4 %all-to-all-start = ((bf16[16,16,512]{2,1,0:T(8,128)(2,1)}), bf16[16,16,512]{2,1,0:T(8,128)(2,1)S(1)}, u32[]{:S(2)}, u32[]{:S(2)}) async-start(bf16[16,16,512]{2,1,0:T(8,128)(2,1)} %bitcast.11), calls=%async_computation | async-start | bytes 524288 | tf_op jit(solution)/shard_map/all_to_all | solution.py:378
  110.0 9.0 %collective-permute-start.15 = (bf16[4,2,2,64,512]{4,3,2,1,0:T(8,128)(2,1)S(1)}, bf16[4,2,2,64,512]{4,3,2,1,0:T(8,128)(2,1)S(1)}, u32[]{:S(2)}, u32[]{:S(2)}) collective-permute-start(bf16[4,2,2,64,512]{4,3,2,1,0:T(8,128)(2,1)S(1)} %pad_maximum_fusion.rm_ref), channel_id=1, source_target_pairs={{0,1},{1,0},{2,3},{3,2},{4,5},{5,4},{6,7},{7,6},{8,9},{9,8},{10,11... | collective-permute-start | bytes 3145736 | tf_op jit(solution)/shard_map/ppermute | solution.py:357
  119.0 0.2 fusion.21
  119.2 3.6 %all-to-all-done = bf16[16,16,512]{2,1,0:T(8,128)(2,1)S(1)} async-done(((bf16[16,16,512]{2,1,0:T(8,128)(2,1)}), bf16[16,16,512]{2,1,0:T(8,128)(2,1)S(1)}, u32[]{:S(2)}, u32[]{:S(2)}) %all-to-all-start) | async-done | bytes 262176 | tf_op jit(solution)/shard_map/all_to_all | solution.py:378
  122.8 1.5 shard_map.127
  124.4 10.8 %all-gather.1 = bf16[576,512]{1,0:T(8,128)(2,1)S(1)} all-gather(bf16[144,512]{1,0:T(8,128)(2,1)S(1)} %get-tuple-element.32), channel_id=3, replica_groups=mesh['z'=16,'x'=4,'y'=4,'c'=2] {'y'}, dimensions={0}, use_global_device_ids=true | all-gather | bytes 737280 | tf_op jit(solution)/shard_map/all_gather | solution.py:385
  135.2 12.8 %collective-permute-start.14 = (bf16[4,144,512]{2,1,0:T(8,128)(2,1)S(1)}, bf16[4,144,512]{2,1,0:T(8,128)(2,1)}, u32[]{:S(2)}, u32[]{:S(2)}) collective-permute-start(bf16[4,144,512]{2,1,0:T(8,128)(2,1)S(1)} %bitcast.48), channel_id=1, source_target_pairs={{0,1},{1,0},{2,3},{3,2},{4,5},{5,4},{6,7},{7,6},{8,9},{9,8},{10,11... | collective-permute-start | bytes 1769480 | tf_op jit(solution)/shard_map/ppermute | solution.py:386
  148.0 0.2 compare_reduce_fusion
  148.1 0.1 concatenate.13.f_ref
  148.2 1.5 collective-permute-done.14.o_ref
  149.7 5.1 %shard_map.128 = (f32[2,64,512]{2,1,0:T(8,128)}, f32[2,64,512]{2,1,0:T(8,128)}, bf16[2,512,512]{2,1,0:T(8,128)(2,1)}) custom-call(s32[7]{0:T(128)S(1)} %concatenate.13.f_ref, bf16[4,144,512]{2,1,0:T(8,128)(2,1)S(1)} %bitcast.49, bf16[4,144,512]{2,1,0:T(8,128)(2,1)} %collective-permute-done.14.o_ref, bf16[4,2,2,64,512]{4,3,2,1,0:T(8,128)(2,1)S(1)} %pad_maximum_fusion.rm_ref, ...), custom_call_target="tpu_custom_call" | custom-call | tf_op jit(solution)/shard_map/pallas_call | solution.py:293
  (41 shorter events, 0.4 us)
Async XLA Ops:
  0.6 15.0 %copy-start.7 = (s32[96]{0:T(128)S(1)}, s32[96]{0:T(128)}, u32[]{:S(2)}) copy-start(s32[96]{0:T(128)} %param.11) | copy-start | bytes 1156
  4.7 14.6 %copy-start.4 = (bf16[1,2,64,512]{3,2,1,0:T(8,128)(2,1)S(1)}, bf16[1,2,64,512]{3,2,1,0:T(8,128)(2,1)}, u32[]{:S(2)}) copy-start(bf16[1,2,64,512]{3,2,1,0:T(8,128)(2,1)} %param.16) | copy-start | bytes 393220
  4.7 14.6 %copy-start.5 = (bf16[1,2,64,512]{3,2,1,0:T(8,128)(2,1)S(1)}, bf16[1,2,64,512]{3,2,1,0:T(8,128)(2,1)}, u32[]{:S(2)}) copy-start(bf16[1,2,64,512]{3,2,1,0:T(8,128)(2,1)} %param.15) | copy-start | bytes 393220
  4.8 27.8 %collective-permute-start.2 = (bf16[1280,256]{1,0:T(8,128)(2,1)}, bf16[1280,256]{1,0:T(8,128)(2,1)S(1)}, u32[]{:S(2)}, u32[]{:S(2)}) collective-permute-start(bf16[1280,256]{1,0:T(8,128)(2,1)} %get-tuple-element.25.p_ref), channel_id=1, source_target_pairs={{0,16},{8,24},{16,0},{24,8},{1,17},{9,25},{17,1},{25,9},{2,18},{10... | collective-permute-start | bytes 1966088 | tf_op jit(solution)/shard_map/ppermute | solution.py:334
  10.4 28.8 %collective-permute-start.3 = (bf16[1280,256]{1,0:T(8,128)(2,1)}, bf16[1280,256]{1,0:T(8,128)(2,1)S(1)}, u32[]{:S(2)}, u32[]{:S(2)}) collective-permute-start(bf16[1280,256]{1,0:T(8,128)(2,1)} %get-tuple-element.30), channel_id=1, source_target_pairs={{0,24},{8,0},{16,8},{24,16},{1,25},{9,1},{17,9},{25,17},{2,26},{10... | collective-permute-start | bytes 1966088 | tf_op jit(solution)/shard_map/ppermute | solution.py:334
  13.2 29.4 %collective-permute-start.4 = (bf16[1280,256]{1,0:T(8,128)(2,1)}, bf16[1280,256]{1,0:T(8,128)(2,1)S(1)}, u32[]{:S(2)}, u32[]{:S(2)}) collective-permute-start(bf16[1280,256]{1,0:T(8,128)(2,1)} %get-tuple-element.31), channel_id=1, source_target_pairs={{0,8},{8,16},{16,24},{24,0},{1,9},{9,17},{17,25},{25,1},{2,10},{10... | collective-permute-start | bytes 1966088 | tf_op jit(solution)/shard_map/ppermute | solution.py:334
  19.3 27.2 %copy-start = (bf16[2048,256]{1,0:T(8,128)(2,1)S(1)}, bf16[2048,256]{1,0:T(8,128)(2,1)}, u32[]{:S(2)}) copy-start(bf16[2048,256]{1,0:T(8,128)(2,1)} %shard_map.121.refs_0_.refs_4_) | copy-start | bytes 3145732
  19.4 7.5 %collective-permute-start = (bf16[1,2,2,64,512]{4,3,2,1,0:T(8,128)(2,1)S(1)}, bf16[1,2,2,64,512]{4,3,2,1,0:T(8,128)(2,1)S(1)}, u32[]{:S(2)}, u32[]{:S(2)}) collective-permute-start(bf16[1,2,2,64,512]{4,3,2,1,0:T(8,128)(2,1)S(1)} %maximum_bitcast_fusion), channel_id=1, source_target_pairs={{0,2},{2,0},{4,6},{6,4},{1,3},{3,1},{5,7},{7,5},{8,10},{10,8},{12,... | collective-permute-start | bytes 786440 | tf_op jit(solution)/shard_map/ppermute | solution.py:353
  27.0 17.5 %collective-permute-start.1 = (bf16[2,2,2,64,512]{4,3,2,1,0:T(8,128)(2,1)S(1)}, bf16[2,2,2,64,512]{4,3,2,1,0:T(8,128)(2,1)S(1)}, u32[]{:S(2)}, u32[]{:S(2)}) collective-permute-start(bf16[2,2,2,64,512]{4,3,2,1,0:T(8,128)(2,1)S(1)} %pad_maximum_fusion.1), channel_id=1, source_target_pairs={{0,4},{2,6},{4,0},{6,2},{1,5},{3,7},{5,1},{7,3},{8,12},{10,14},{12... | collective-permute-start | bytes 1572872 | tf_op jit(solution)/shard_map/ppermute | solution.py:353
  32.6 12.0 %collective-permute-start.5 = (bf16[1280,256]{1,0:T(8,128)(2,1)S(1)}, bf16[1280,256]{1,0:T(8,128)(2,1)S(1)}, u32[]{:S(2)}, u32[]{:S(2)}) collective-permute-start(bf16[1280,256]{1,0:T(8,128)(2,1)S(1)} %collective-permute-done.2.refs_1_.refs_5_), channel_id=1, source_target_pairs={{0,1},{1,0},{2,3},{3,2},{4,5},{5,4},{6,7},{7,6},{8,9},{9,8},{10,11... | collective-permute-start | bytes 1966088 | tf_op jit(solution)/shard_map/ppermute | solution.py:356
  39.2 5.4 %collective-permute-start.6 = (bf16[1280,256]{1,0:T(8,128)(2,1)S(1)}, bf16[1280,256]{1,0:T(8,128)(2,1)S(1)}, u32[]{:S(2)}, u32[]{:S(2)}) collective-permute-start(bf16[1280,256]{1,0:T(8,128)(2,1)S(1)} %collective-permute-done.3.refs_2_.refs_6_), channel_id=1, source_target_pairs={{0,1},{1,0},{2,3},{3,2},{4,5},{5,4},{6,7},{7,6},{8,9},{9,8},{10,11... | collective-permute-start | bytes 1966088 | tf_op jit(solution)/shard_map/ppermute | solution.py:356
  42.6 4.0 %collective-permute-start.7 = (bf16[1280,256]{1,0:T(8,128)(2,1)S(1)}, bf16[1280,256]{1,0:T(8,128)(2,1)S(1)}, u32[]{:S(2)}, u32[]{:S(2)}) collective-permute-start(bf16[1280,256]{1,0:T(8,128)(2,1)S(1)} %collective-permute-done.4.refs_3_.refs_7_), channel_id=1, source_target_pairs={{0,1},{1,0},{2,3},{3,2},{4,5},{5,4},{6,7},{7,6},{8,9},{9,8},{10,11... | collective-permute-start | bytes 1966088 | tf_op jit(solution)/shard_map/ppermute | solution.py:356
  47.1 15.8 %collective-permute-start.11 = (bf16[256,768]{1,0:T(8,128)(2,1)S(1)}, bf16[256,768]{1,0:T(8,128)(2,1)S(1)}, u32[]{:S(2)}, u32[]{:S(2)}) collective-permute-start(bf16[256,768]{1,0:T(8,128)(2,1)S(1)} %shard_map.125), channel_id=1, source_target_pairs={{0,32},{1,481},{32,64},{33,1},{64,96},{65,33},{96,128},{97,65},{12... | collective-permute-start | bytes 1179656 | tf_op jit(solution)/shard_map/ppermute | solution.py:367
  58.9 8.9 %collective-permute-start.8 = (bf16[256,768]{1,0:T(8,128)(2,1)S(1)}, bf16[256,768]{1,0:T(8,128)(2,1)S(1)}, u32[]{:S(2)}, u32[]{:S(2)}) collective-permute-start(bf16[256,768]{1,0:T(8,128)(2,1)S(1)} %shard_map.123), channel_id=1, source_target_pairs={{0,32},{1,481},{32,64},{33,1},{64,96},{65,33},{96,128},{97,65},{12... | collective-permute-start | bytes 1179656 | tf_op jit(solution)/shard_map/ppermute | solution.py:367
  63.0 56.0 %copy-start.6 = (s32[96]{0:T(128)S(1)}, s32[96]{0:T(128)}, u32[]{:S(2)}) copy-start(s32[96]{0:T(128)} %param.12) | copy-start | bytes 1156
  63.0 59.8 %copy-start.3 = (f32[1,2,64,512]{3,2,1,0:T(8,128)S(1)}, f32[1,2,64,512]{3,2,1,0:T(8,128)}, u32[]{:S(2)}) copy-start(f32[1,2,64,512]{3,2,1,0:T(8,128)} %param.17) | copy-start | bytes 786436
  63.0 9.9 %collective-permute-start.12 = (bf16[128,768]{1,0:T(8,128)(2,1)S(1)}, bf16[128,768]{1,0:T(8,128)(2,1)S(1)}, u32[]{:S(2)}, u32[]{:S(2)}) collective-permute-start(bf16[128,768]{1,0:T(8,128)(2,1)S(1)} %fusion.1), channel_id=1, source_target_pairs={{0,64},{1,449},{32,96},{33,481},{64,128},{65,1},{96,160},{97,33},{... | collective-permute-start | bytes 589832 | tf_op jit(solution)/shard_map/ppermute | solution.py:367
  67.8 10.8 %collective-permute-start.9 = (bf16[128,768]{1,0:T(8,128)(2,1)S(1)}, bf16[128,768]{1,0:T(8,128)(2,1)S(1)}, u32[]{:S(2)}, u32[]{:S(2)}) collective-permute-start(bf16[128,768]{1,0:T(8,128)(2,1)S(1)} %fusion.2), channel_id=1, source_target_pairs={{0,64},{1,449},{32,96},{33,481},{64,128},{65,1},{96,160},{97,33},{... | collective-permute-start | bytes 589832 | tf_op jit(solution)/shard_map/ppermute | solution.py:367
  73.0 76.7 %copy-start.1 = (f32[1,2,64,512]{3,2,1,0:T(8,128)S(1)}, f32[1,2,64,512]{3,2,1,0:T(8,128)}, u32[]{:S(2)}) copy-start(f32[1,2,64,512]{3,2,1,0:T(8,128)} %param.13) | copy-start | bytes 786436
  73.0 76.7 %copy-start.2 = (f32[1,2,64,512]{3,2,1,0:T(8,128)S(1)}, f32[1,2,64,512]{3,2,1,0:T(8,128)}, u32[]{:S(2)}) copy-start(f32[1,2,64,512]{3,2,1,0:T(8,128)} %param.14) | copy-start | bytes 786436
  73.0 10.8 %collective-permute-start.13 = (bf16[64,768]{1,0:T(8,128)(2,1)S(1)}, bf16[64,768]{1,0:T(8,128)(2,1)S(1)}, u32[]{:S(2)}, u32[]{:S(2)}) collective-permute-start(bf16[64,768]{1,0:T(8,128)(2,1)S(1)} %fusion.4), channel_id=1, source_target_pairs={{0,128},{1,385},{32,160},{33,417},{64,192},{65,449},{96,224},{97,4... | collective-permute-start | bytes 294920 | tf_op jit(solution)/shard_map/ppermute | solution.py:367
  78.6 10.6 %collective-permute-start.10 = (bf16[64,768]{1,0:T(8,128)(2,1)S(1)}, bf16[64,768]{1,0:T(8,128)(2,1)S(1)}, u32[]{:S(2)}, u32[]{:S(2)}) collective-permute-start(bf16[64,768]{1,0:T(8,128)(2,1)S(1)} %fusion.9), channel_id=1, source_target_pairs={{0,128},{1,385},{32,160},{33,417},{64,192},{65,449},{96,224},{97,4... | collective-permute-start | bytes 294920 | tf_op jit(solution)/shard_map/ppermute | solution.py:367
  101.6 21.3 %all-to-all-start = ((bf16[16,16,512]{2,1,0:T(8,128)(2,1)}), bf16[16,16,512]{2,1,0:T(8,128)(2,1)S(1)}, u32[]{:S(2)}, u32[]{:S(2)}) async-start(bf16[16,16,512]{2,1,0:T(8,128)(2,1)} %bitcast.11), calls=%async_computation | async-start | bytes 524288 | tf_op jit(solution)/shard_map/all_to_all | solution.py:378
  110.0 38.2 %collective-permute-start.15 = (bf16[4,2,2,64,512]{4,3,2,1,0:T(8,128)(2,1)S(1)}, bf16[4,2,2,64,512]{4,3,2,1,0:T(8,128)(2,1)S(1)}, u32[]{:S(2)}, u32[]{:S(2)}) collective-permute-start(bf16[4,2,2,64,512]{4,3,2,1,0:T(8,128)(2,1)S(1)} %pad_maximum_fusion.rm_ref), channel_id=1, source_target_pairs={{0,1},{1,0},{2,3},{3,2},{4,5},{5,4},{6,7},{7,6},{8,9},{9,8},{10,11... | collective-permute-start | bytes 3145736 | tf_op jit(solution)/shard_map/ppermute | solution.py:357
  135.2 14.5 %collective-permute-start.14 = (bf16[4,144,512]{2,1,0:T(8,128)(2,1)S(1)}, bf16[4,144,512]{2,1,0:T(8,128)(2,1)}, u32[]{:S(2)}, u32[]{:S(2)}) collective-permute-start(bf16[4,144,512]{2,1,0:T(8,128)(2,1)S(1)} %bitcast.48), channel_id=1, source_target_pairs={{0,1},{1,0},{2,3},{3,2},{4,5},{5,4},{6,7},{7,6},{8,9},{9,8},{10,11... | collective-permute-start | bytes 1769480 | tf_op jit(solution)/shard_map/ppermute | solution.py:386

commit v10 on v9

--- a/solution.py
+++ b/solution.py
@@ -12,6 +12,7 @@
 NZ, NX, NC = 16, 4, 2
 TILES = 6
 CHUNKS = 2
+X_CHUNKS = 1
 ROOMY = pltpu.CompilerParams(vmem_limit_bytes=60 * 1024 * 1024)
 PARAMS = pltpu.CompilerParams(vmem_limit_bytes=8 * 1024 * 1024)
 
@@ -38,76 +39,86 @@
     return lax.dot_general(a, b, (dims, ((), ())), preferred_element_type=WIDE)
 
 
-def prepare(activations, out_grads, place):
-    block_rows, rows, toks = activations.shape
+def ordered_rows(values, z, way, odd, block_rows, rows):
     per_z = rows // NZ
+    count = block_rows * rows // 2
+    m, k = iota((count, 2 * count), 0), iota((count, 2 * count), 1)
+    block = m % block_rows
+    row = (m // block_rows) % per_z
+    tail = m // (block_rows * per_z)
+    high = 2 * (tail // 4) + 4 * ((tail // 2) % 2) + 8 * (tail % 2)
+    goal = jnp.bitwise_and(z + way * (high + odd), NZ - 1)
+    pick = (block * rows + goal * per_z + row == k).astype(WIDE).astype(HALF)
+    return dot(pick, values).astype(HALF)
+
+
+def send_pieces(kernel, shapes, place, arrays, copies):
+    any_place = pl.BlockSpec(memory_space=pl.ANY)
+    return pl.pallas_call(
+        kernel,
+        out_shape=[jax.ShapeDtypeStruct(shape, HALF) for shape in shapes],
+        in_specs=[pl.BlockSpec(memory_space=pltpu.SMEM)]
+        + [pl.BlockSpec(memory_space=pltpu.VMEM)] * (len(arrays) - 1)
+        + [any_place],
+        out_specs=[any_place] * len(shapes),
+        scratch_shapes=[pltpu.VMEM(shape, HALF) for shape in shapes]
+        + [pltpu.SemaphoreType.DMA((copies,)), pltpu.SemaphoreType.DMA((len(shapes),))],
+        compiler_params=ROOMY,
+    )(place, *arrays)
+
+
+def prepare(sources, out_grads, place, far):
+    block_rows, rows, toks = sources[0].shape
     count = block_rows * rows // 2
     half = toks // NC
     width = out_grads.shape[1] // NX
     tile = width // TILES
-
-    def kernel(place_ref, a_ref, b_ref, *refs):
-        out_refs, (held, sems, out_sems) = refs[:3], refs[3:]
-        z, c = place_ref[0], place_ref[2]
-        tok = pl.ds(pl.multiple_of(c * half, half), half)
+    size = half if far else toks
+    group = TILES // X_CHUNKS
+    skip = 2 * count * (1 if far else NC)
+    shapes = [((skip if k == 0 else 0) + group * size, toks) for k in range(X_CHUNKS)]
+
+    def kernel(place_ref, *refs):
+        a_refs, refs = refs[: len(sources)], refs[len(sources) :]
+        b_ref, out_refs, refs = refs[0], refs[1 : 1 + X_CHUNKS], refs[1 + X_CHUNKS :]
+        held, (sems, out_sems) = refs[:X_CHUNKS], refs[X_CHUNKS:]
+        z, x, c = place_ref[0], place_ref[1], place_ref[2]
+        goal_x = jnp.bitwise_and(x + 2 if far else x + 1 - 2 * c, NX - 1)
+        tok = pl.ds(pl.multiple_of(c * half, half) if far else 0, size)
         copies = []
-        for i in range(3):
-            begin = place_ref[3 + i] * width
-            for n in range(TILES):
-                at = pl.ds(pl.multiple_of(begin + n * tile, tile), tile)
-                to = pl.ds(2 * count + n * half, half)
-                copies.append(pltpu.make_async_copy(b_ref.at[tok, at], held.at[i, to, :], sems.at[i, n]))
-        for copy in copies:
-            copy.start()
-        m, k = iota((count, 2 * count), 0), iota((count, 2 * count), 1)
-        block = m % block_rows
-        row = (m // block_rows) % per_z
-        tail = m // (block_rows * per_z)
-        high = 2 * (tail // 4) + 4 * ((tail // 2) % 2) + 8 * (tail % 2)
-        values = a_ref[...].reshape(2 * count, toks)
-        for odd in range(2):
-            goal = jnp.bitwise_and(z + (1 - 2 * c) * (high + odd), NZ - 1)
-            pick = (block * rows + goal * per_z + row == k).astype(WIDE).astype(HALF)
-            moved = dot(pick, values).astype(HALF)
-            turned = jnp.concatenate([moved[:, half:], moved[:, :half]], axis=1)
-            at = (1 - odd) * count
-            ordered = jnp.where(c == 1, turned, moved)
-            for i in range(3):
-                held[i, at : at + count, :] = ordered
-        last = [pltpu.make_async_copy(held.at[i], out_refs[i], out_sems.at[i]) for i in range(3)]
-        for i in range(3):
-            for copy in copies[i * TILES : (i + 1) * TILES]:
+        for n in range(TILES):
+            at = pl.ds(pl.multiple_of(goal_x * width + n * tile, tile), tile)
+            first = (skip if n < group else 0) + n % group * size
+            copies.append(pltpu.make_async_copy(b_ref.at[tok, at], held[n // group].at[pl.ds(first, size), :], sems.at[n]))
+            copies[-1].start()
+        for i, ref in enumerate(a_refs):
+            core = c if i == 0 else 1 - c
+            values = ref[...].reshape(2 * count, toks)
+            for odd in range(2):
+                moved = ordered_rows(values, z, 1 - 2 * core, odd, block_rows, rows)
+                if far:
+                    turned = jnp.concatenate([moved[:, half:], moved[:, :half]], axis=1)
+                    held[0][(1 - odd) * count : (2 - odd) * count, :] = jnp.where(c == 1, turned, moved)
+                else:
+                    to = pl.ds(pl.multiple_of((2 * core + 1 - odd) * count, count), count)
+                    held[0][to, :] = moved
+        last = []
+        for k in range(X_CHUNKS):
+            for copy in copies[k * group : (k + 1) * group]:
                 copy.wait()
-            last[i].start()
+            last.append(pltpu.make_async_copy(held[k], out_refs[k], out_sems.at[k]))
+            last[k].start()
         for copy in last:
             copy.wait()
 
-    piece = (2 * count + TILES * half, toks)
-    any_place = pl.BlockSpec(memory_space=pl.ANY)
-    return pl.pallas_call(
-        kernel,
-        out_shape=[jax.ShapeDtypeStruct(piece, HALF)] * 3,
-        in_specs=[
-            pl.BlockSpec(memory_space=pltpu.SMEM),
-            pl.BlockSpec(memory_space=pltpu.VMEM),
-            any_place,
-        ],
-        out_specs=[any_place] * 3,
-        scratch_shapes=[
-            pltpu.VMEM((3, *piece), HALF),
-            pltpu.SemaphoreType.DMA((3, TILES)),
-            pltpu.SemaphoreType.DMA((3,)),
-        ],
-        compiler_params=ROOMY,
-    )(place, activations, out_grads)
-
-
-def own_part(piece, out_grads, place):
+    return send_pieces(kernel, shapes, place, (*sources, out_grads), TILES)
+
+
+def own_part(piece, count, out_grads, place):
     toks = out_grads.shape[0]
     half = toks // NC
     width = out_grads.shape[1] // NX
     tile = width // TILES
-    count = piece.shape[0] - TILES * half
 
     def kernel(place_ref, p_ref, b_ref, o_ref):
         c = place_ref[2]
@@ -135,37 +146,46 @@
     )(place, piece, out_grads)
 
 
-def partial_products(own, arrived, swapped, odd, chunk):
+def partial_products(place, own, far, near, odd, chunk):
     toks = own.shape[1]
     half = toks // NC
     total_rows = own.shape[0] - TILES * toks
     count = total_rows // 2
     kind = HALF if odd else WIDE
     group = TILES // CHUNKS
-
-    def kernel(*refs):
-        rows_refs, own_ref, mine, other, out_ref = refs[:4], refs[4], refs[5:8], refs[8:11], refs[11]
+    row_block = 0 if odd else 1
+
+    def kernel(place_ref, *refs):
+        rows_refs, own_ref, (mine, other), near_refs, out_ref = refs[:4], refs[4], refs[5:7], refs[7:9], refs[9]
         for n in range(group):
             at = slice(n * half, (n + 1) * half)
-            total = dot(rows_refs[0][...], own_ref[n * toks : (n + 1) * toks, :])
-            for rows_ref, m_ref, o_ref in zip(rows_refs[1:], mine, other):
-                total += dot(rows_ref[...], jnp.concatenate([m_ref[at, :], o_ref[at, :]], axis=0))
             to = slice(n * toks, (n + 1) * toks)
+            total = dot(rows_refs[0][...], own_ref[to, :])
+            total += dot(rows_refs[1][...], jnp.concatenate([mine[at, :], other[at, :]], axis=0))
+            for rows_ref, ref in zip(rows_refs[2:], near_refs):
+                total += dot(rows_ref[...], ref[to, :])
             out_ref[:, to] = total.astype(kind)
 
     def block(skip, size):
-        first = pl.Element(size)
-        return pl.BlockSpec((first, pl.Element(toks)), lambda n: (skip + chunk * size, 0))
-
-    rows = pl.BlockSpec((count, toks), lambda n: (0 if odd else 1, 0))
-    return pl.pallas_call(
-        kernel,
-        grid=(1,),
+        return pl.BlockSpec((pl.Element(size), pl.Element(toks)), lambda n, place_ref: (skip, 0))
+
+    rows = pl.BlockSpec((count, toks), lambda n, place_ref: (row_block, 0))
+    rows_of_core = pl.BlockSpec((count, toks), lambda n, place_ref: (2 * place_ref[2] + row_block, 0))
+    return pl.pallas_call(
+        kernel,
         out_shape=jax.ShapeDtypeStruct((count, group * toks), kind),
-        in_specs=[rows] * 4 + [block(total_rows, group * toks)] + [block(total_rows, group * half)] * 6,
-        out_specs=pl.BlockSpec((count, group * toks), lambda n: (0, 0)),
+        grid_spec=pltpu.PrefetchScalarGridSpec(
+            num_scalar_prefetch=1,
+            grid=(1,),
+            in_specs=[rows] * 2
+            + [rows_of_core] * 2
+            + [block(total_rows + chunk * group * toks, group * toks)]
+            + [block(total_rows + chunk * group * half, group * half)] * 2
+            + [block(NC * total_rows + chunk * group * toks, group * toks)] * 2,
+            out_specs=pl.BlockSpec((count, group * toks), lambda n, place_ref: (0, 0)),
+        ),
         compiler_params=PARAMS,
-    )(own, *arrived, own, *arrived, *swapped)
+    )(place, own, far[0][0], near[0][0], near[1][0], own, *[part[0] for part in far], *[part[0] for part in near])
 
 
 def pick_blocks(chosen, sums, block_size):
@@ -329,9 +349,14 @@
     my_mp = y * NC + c
     my_rows = my_mp * rows
 
-    place = jnp.stack([z, x, c] + [jnp.bitwise_and(x + step, NX - 1) for step in (2, 3, 1)]).astype(jnp.int32)
-    pieces = prepare(activations, out_grads, place)
-    arrived = [lax.ppermute(piece, "x", ring(NX, step)) for piece, step in zip(pieces, (2, -1, 1))]
+    place = jnp.stack([z, x, c]).astype(jnp.int32)
+    swap = ring(NC, 1)
+    other_rows = lax.ppermute(activations, "c", swap)
+    goals = [(i + (1 - 2 * k)) % NX * NC + k for i in range(NX) for k in range(NC)]
+    pieces = prepare((activations,), out_grads, place, True)
+    far_mine = [lax.ppermute(piece, "x", ring(NX, 2)) for piece in pieces]
+    near_pieces = prepare((activations, other_rows), out_grads, place, False)
+    near_mine = [lax.ppermute(piece, ("x", "c"), list(enumerate(goals))) for piece in near_pieces]
 
     piece_own, owners = lax.optimization_barrier((pieces[0], owners))
     targets = slot_targets(owners, slots)
@@ -343,9 +368,9 @@
     out_rows = NZ * slots * 2 * per_z
     chosen = (code == iota((out_rows, 1), 0)).astype(HALF)
     piece_own, chosen = lax.optimization_barrier((piece_own, chosen))
-    own = own_part(piece_own, out_grads, place)
-
-    own, left_root, right_root = lax.optimization_barrier((own, left_root, right_root))
+    own = own_part(piece_own, block_rows * rows, out_grads, place)
+
+    piece_far, left_root, right_root = lax.optimization_barrier((pieces[0], left_root, right_root))
     ny = lax.axis_size("y")
     roots = jnp.stack([left_root[0], right_root[0]])[None]
     for step in (1, 2):
@@ -353,11 +378,12 @@
             came = lax.ppermute(roots, "y", [(i, i ^ step) for i in range(ny)])
             roots = jnp.concatenate([roots, came], axis=0)
     own, roots = lax.optimization_barrier((own, roots))
-    swapped = [lax.ppermute(piece, "c", ring(NC, 1)) for piece in arrived]
-    roots_other = lax.ppermute(roots, "c", ring(NC, 1))
-
-    sent = [partial_products(own, arrived, swapped, True, chunk) for chunk in range(CHUNKS)]
-    kept = [partial_products(own, arrived, swapped, False, chunk) for chunk in range(CHUNKS)]
+    roots_other = lax.ppermute(roots, "c", swap)
+    far = [far_mine, [lax.ppermute(piece, "c", swap) for piece in far_mine]]
+    near_mine[0], own = lax.optimization_barrier((near_mine[0], own))
+    near = [near_mine, [lax.ppermute(piece, "c", swap) for piece in near_mine]]
+    sent = [partial_products(place, own, far, near, True, chunk) for chunk in range(CHUNKS)]
+    kept = [partial_products(place, own, far, near, False, chunk) for chunk in range(CHUNKS)]
 
     sums = []
     for out, keep in zip(sent, kept):

time: 156 us -> 158 us (1.013)
  starting transfers between devices: 93 us -> 76.5 us
  waiting for transfers between devices: 20 us -> 29.4 us
  Pallas kernels: 16.6 us -> 21.6 us
  blocking collectives: 21.8 us -> 25.1 us
  other arithmetic: 1.16 us -> 2.75 us
    ppermute x6, starting transfers between devices: 33.2 us -> 24.6 us  [body(): got.append(lax.ppermute(out, ('z', 'c'), list(enumerate(goals))))]
    ppermute x2, waiting for transfers between devices: 4.2 us -> 11.7 us  [body(): came = lax.ppermute(roots, 'y', [(i, i ^ step) for i in range(ny)])]
    pallas_call x5 -> x6, Pallas kernels: 5.76 us -> 10.8 us  [the longest x2 6.33 us: send_pieces(): pl.pallas_call(kernel, out_shape=[jax.ShapeDtypeStruct(shape, HALF) for s...]
    ppermute x2, starting transfers between devices: 8.92 us -> 4.58 us  [body(): came = lax.ppermute(roots, 'y', [(i, i ^ step) for i in range(ny)])]
    all_gather x1, blocking collectives: 11 us -> 14.3 us  [body(): lax.all_gather(jnp.concatenate(sums, axis=0), 'x', axis=0, tiled=False)]
    all_to_all x1, starting transfers between devices: 8.38 us -> 5.72 us  [body(): lax.all_to_all(picked, 'z', 0, 0, tiled=True).reshape(out_rows, block_size)]
    ppermute x6, waiting for transfers between devices: 6.8 us -> 9.38 us  [body(): got.append(lax.ppermute(out, ('z', 'c'), list(enumerate(goals))))]
    ppermute x7 -> x6, waiting for transfers between devices: 3.91 us -> 2.18 us  [the longest x1 2.06 us: body(): far = [far_mine, [lax.ppermute(piece, 'c', swap) for piece in far_mine]]]
  transfers between devices with their start and end apart: 17 -> 16, of which waited for: 8 -> 11; matrix products, arithmetic and copies ran while one was open for 1% -> 2% of each run, Pallas kernels for 4% -> 9%
where the time goes in v10:
time: 158 us; the launch traced here: 157 us
  starting transfers between devices  76.5 us (48%)
  waiting for transfers between devices  29.4 us (19%)
  blocking collectives  25.1 us (16%)
  Pallas kernels  21.6 us (14%)
  other arithmetic  2.75 us (2%)
    ppermute x6, starting transfers between devices, body(): got.append(lax.ppermute(out, ('z', 'c'), list(enumerate(goals))))  24.6 us
    all_gather x1, blocking collectives, body(): lax.all_gather(jnp.concatenate(sums, axis=0), 'x', axis=0, tiled=False)  14.3 us
    ppermute x1, starting transfers between devices, body(): rows_other = lax.ppermute(rows_mine, 'c', ring(NC, 1))  11.7 us
    ppermute x2, waiting for transfers between devices, body(): came = lax.ppermute(roots, 'y', [(i, i ^ step) for i in range(ny)])  11.7 us
    all_gather x1, blocking collectives, body(): rows_mine = lax.all_gather(own_rows, 'y', axis=0, tiled=False)  10.7 us
    ppermute x6, waiting for transfers between devices, body(): got.append(lax.ppermute(out, ('z', 'c'), list(enumerate(goals))))  9.38 us
    ppermute x1, starting transfers between devices, body(): other_rows = lax.ppermute(activations, 'c', swap)  8.79 us
    ppermute x1, starting transfers between devices, body(): roots_other = lax.ppermute(roots, 'c', swap)  7.92 us
  transfers between devices with their start and end apart: 16, of which 11 were waited for; matrix products, arithmetic and copies ran while one was open for 2% of the time, Pallas kernels for 9%

profile of v10, /device:TPU:1, one launch (start us, length us, event | category | flops | bytes accessed | tf_op | source)
XLA Modules:
  0.0 157.5 jit_solution(11774508388395739237)
XLA Ops:
  0.6 8.8 %collective-permute-start = (bf16[8,64,256]{2,1,0:T(8,128)(2,1)}, bf16[8,64,256]{2,1,0:T(8,128)(2,1)S(1)}, u32[]{:S(2)}, u32[]{:S(2)}) collective-permute-start(bf16[8,64,256]{2,1,0:T(8,128)(2,1)} %refs_0_.3), channel_id=1, source_target_pairs={{0,1},{1,0},{2,3},{3,2},{4,5},{5,4},{6,7},{7,6},{8,9},{9,8},{10,11... | collective-permute-start | bytes 786440 | tf_op jit(solution)/shard_map/ppermute | solution.py:354
  9.4 0.6 pad_add_fusion.place_ref
  10.0 2.9 %shard_map.120.p_ref = bf16[1280,256]{1,0:T(8,128)(2,1)} custom-call(s32[3]{0:T(128)} %pad_add_fusion.place_ref, bf16[8,64,256]{2,1,0:T(8,128)(2,1)} %refs_0_.3, bf16[256,6144]{1,0:T(8,128)(2,1)} %b_ref.1), custom_call_target="tpu_custom_call" | custom-call | tf_op jit(solution)/shard_map/pallas_call | solution.py:57
  12.9 1.9 %collective-permute-start.4 = (bf16[1280,256]{1,0:T(8,128)(2,1)}, bf16[1280,256]{1,0:T(8,128)(2,1)S(1)}, u32[]{:S(2)}, u32[]{:S(2)}) collective-permute-start(bf16[1280,256]{1,0:T(8,128)(2,1)} %shard_map.120.p_ref), channel_id=1, source_target_pairs={{0,16},{8,24},{16,0},{24,8},{1,17},{9,25},{17,1},{25,9},{2,18},{10... | collective-permute-start | bytes 1966088 | tf_op jit(solution)/shard_map/ppermute | solution.py:357
  14.9 1.9 %collective-permute-start.2 = (bf16[1,2,2,64,512]{4,3,2,1,0:T(8,128)(2,1)S(1)}, bf16[1,2,2,64,512]{4,3,2,1,0:T(8,128)(2,1)S(1)}, u32[]{:S(2)}, u32[]{:S(2)}) collective-permute-start(bf16[1,2,2,64,512]{4,3,2,1,0:T(8,128)(2,1)S(1)} %maximum_bitcast_fusion), channel_id=1, source_target_pairs={{0,2},{2,0},{4,6},{6,4},{1,3},{3,1},{5,7},{7,5},{8,10},{10,8},{12,... | collective-permute-start | bytes 786440 | tf_op jit(solution)/shard_map/ppermute | solution.py:378
  16.8 0.2 select_reduce_fusion
  17.0 0.7 copy-done.5
  17.7 3.4 %shard_map.121 = bf16[2560,256]{1,0:T(8,128)(2,1)} custom-call(s32[3]{0:T(128)} %pad_add_fusion.place_ref, bf16[8,64,256]{2,1,0:T(8,128)(2,1)} %refs_0_.3, bf16[8,64,256]{2,1,0:T(8,128)(2,1)} %copy-done.5, bf16[256,6144]{1,0:T(8,128)(2,1)} %b_ref.1), custom_call_target="tpu_custom_call" | custom-call | tf_op jit(solution)/shard_map/pallas_call | solution.py:57
  21.2 1.9 %collective-permute-start.1 = (bf16[2560,256]{1,0:T(8,128)(2,1)}, bf16[2560,256]{1,0:T(8,128)(2,1)S(1)}, u32[]{:S(2)}, u32[]{:S(2)}) collective-permute-start(bf16[2560,256]{1,0:T(8,128)(2,1)} %shard_map.121), channel_id=1, source_target_pairs={{0,8},{1,25},{8,16},{9,1},{16,24},{17,9},{24,0},{25,17},{2,10},{3,... | collective-permute-start | bytes 3932168 | tf_op jit(solution)/shard_map/ppermute | solution.py:359
  23.1 0.1 reshape.110
  23.2 0.1 copy.19
  23.4 1.4 collective-permute-done.2
  24.8 2.7 %collective-permute-start.3 = (bf16[2,2,2,64,512]{4,3,2,1,0:T(8,128)(2,1)S(1)}, bf16[2,2,2,64,512]{4,3,2,1,0:T(8,128)(2,1)}, u32[]{:S(2)}, u32[]{:S(2)}) collective-permute-start(bf16[2,2,2,64,512]{4,3,2,1,0:T(8,128)(2,1)S(1)} %pad_maximum_fusion.1), channel_id=1, source_target_pairs={{0,4},{2,6},{4,0},{6,2},{1,5},{3,7},{5,1},{7,3},{8,12},{10,14},{12... | collective-permute-start | bytes 1572872 | tf_op jit(solution)/shard_map/ppermute | solution.py:378
  27.5 0.1 select_n.49
  27.7 2.9 %shard_map.122.refs_0_.refs_4_ = bf16[2048,256]{1,0:T(8,128)(2,1)} custom-call(s32[3]{0:T(128)} %pad_add_fusion.place_ref, bf16[1280,256]{1,0:T(8,128)(2,1)} %shard_map.120.p_ref, bf16[256,6144]{1,0:T(8,128)(2,1)} %b_ref.1), custom_call_target="tpu_custom_call" | custom-call | tf_op jit(solution)/shard_map/pallas_call | solution.py:133
  30.6 10.3 %collective-permute-done.3 = bf16[2,2,2,64,512]{4,3,2,1,0:T(8,128)(2,1)} collective-permute-done((bf16[2,2,2,64,512]{4,3,2,1,0:T(8,128)(2,1)S(1)}, bf16[2,2,2,64,512]{4,3,2,1,0:T(8,128)(2,1)}, u32[]{:S(2)}, u32[]{:S(2)}) %collective-permute-start.3) | collective-permute-done | bytes 524320 | tf_op jit(solution)/shard_map/ppermute | solution.py:378
  40.9 1.1 pad_maximum_fusion.rm_ref
  42.1 0.1 collective-permute-done.1.refs_2_.refs_7_
  42.2 7.4 %collective-permute-start.5 = (bf16[2560,256]{1,0:T(8,128)(2,1)S(1)}, bf16[2560,256]{1,0:T(8,128)(2,1)S(1)}, u32[]{:S(2)}, u32[]{:S(2)}) collective-permute-start(bf16[2560,256]{1,0:T(8,128)(2,1)S(1)} %collective-permute-done.1.refs_2_.refs_7_), channel_id=1, source_target_pairs={{0,1},{1,0},{2,3},{3,2},{4,5},{5,4},{6,7},{7,6},{8,9},{9,8},{10,11... | collective-permute-start | bytes 3932168 | tf_op jit(solution)/shard_map/ppermute | solution.py:384
  49.6 1.9 %collective-permute-start.6 = (bf16[1280,256]{1,0:T(8,128)(2,1)S(1)}, bf16[1280,256]{1,0:T(8,128)(2,1)S(1)}, u32[]{:S(2)}, u32[]{:S(2)}) collective-permute-start(bf16[1280,256]{1,0:T(8,128)(2,1)S(1)} %collective-permute-done.4.refs_1_.refs_5_), channel_id=1, source_target_pairs={{0,1},{1,0},{2,3},{3,2},{4,5},{5,4},{6,7},{7,6},{8,9},{9,8},{10,11... | collective-permute-start | bytes 1966088 | tf_op jit(solution)/shard_map/ppermute | solution.py:382
  51.6 2.1 %collective-permute-done.6.refs_6_ = bf16[1280,256]{1,0:T(8,128)(2,1)S(1)} collective-permute-done((bf16[1280,256]{1,0:T(8,128)(2,1)S(1)}, bf16[1280,256]{1,0:T(8,128)(2,1)S(1)}, u32[]{:S(2)}, u32[]{:S(2)}) %collective-permute-start.6) | collective-permute-done | bytes 655392 | tf_op jit(solution)/shard_map/ppermute | solution.py:382
  53.6 1.1 shard_map.126
  54.8 5.7 %collective-permute-start.10 = (bf16[256,768]{1,0:T(8,128)(2,1)S(1)}, bf16[256,768]{1,0:T(8,128)(2,1)S(1)}, u32[]{:S(2)}, u32[]{:S(2)}) collective-permute-start(bf16[256,768]{1,0:T(8,128)(2,1)S(1)} %shard_map.126), channel_id=1, source_target_pairs={{0,32},{1,481},{32,64},{33,1},{64,96},{65,33},{96,128},{97,65},{12... | collective-permute-start | bytes 1179656 | tf_op jit(solution)/shard_map/ppermute | solution.py:393
  60.5 1.1 shard_map.124
  61.7 2.6 %collective-permute-start.7 = (bf16[256,768]{1,0:T(8,128)(2,1)S(1)}, bf16[256,768]{1,0:T(8,128)(2,1)S(1)}, u32[]{:S(2)}, u32[]{:S(2)}) collective-permute-start(bf16[256,768]{1,0:T(8,128)(2,1)S(1)} %shard_map.124), channel_id=1, source_target_pairs={{0,32},{1,481},{32,64},{33,1},{64,96},{65,33},{96,128},{97,65},{12... | collective-permute-start | bytes 1179656 | tf_op jit(solution)/shard_map/ppermute | solution.py:393
  64.3 1.1 shard_map.125
  65.4 1.1 shard_map.123
  66.6 3.2 %collective-permute-start.11 = (bf16[128,768]{1,0:T(8,128)(2,1)S(1)}, bf16[128,768]{1,0:T(8,128)(2,1)S(1)}, u32[]{:S(2)}, u32[]{:S(2)}) collective-permute-start(bf16[128,768]{1,0:T(8,128)(2,1)S(1)} %fusion.1), channel_id=1, source_target_pairs={{0,64},{1,449},{32,96},{33,481},{64,128},{65,1},{96,160},{97,33},{... | collective-permute-start | bytes 589832 | tf_op jit(solution)/shard_map/ppermute | solution.py:393
  69.8 0.6 collective-permute-done.7
  70.5 3.5 %collective-permute-start.8 = (bf16[128,768]{1,0:T(8,128)(2,1)S(1)}, bf16[128,768]{1,0:T(8,128)(2,1)S(1)}, u32[]{:S(2)}, u32[]{:S(2)}) collective-permute-start(bf16[128,768]{1,0:T(8,128)(2,1)S(1)} %fusion.2), channel_id=1, source_target_pairs={{0,64},{1,449},{32,96},{33,481},{64,128},{65,1},{96,160},{97,33},{... | collective-permute-start | bytes 589832 | tf_op jit(solution)/shard_map/ppermute | solution.py:393
  74.1 2.3 %collective-permute-done.11 = bf16[128,768]{1,0:T(8,128)(2,1)S(1)} collective-permute-done((bf16[128,768]{1,0:T(8,128)(2,1)S(1)}, bf16[128,768]{1,0:T(8,128)(2,1)S(1)}, u32[]{:S(2)}, u32[]{:S(2)}) %collective-permute-start.11) | collective-permute-done | bytes 196640 | tf_op jit(solution)/shard_map/ppermute | solution.py:393
  76.4 3.8 %collective-permute-start.12 = (bf16[64,768]{1,0:T(8,128)(2,1)S(1)}, bf16[64,768]{1,0:T(8,128)(2,1)S(1)}, u32[]{:S(2)}, u32[]{:S(2)}) collective-permute-start(bf16[64,768]{1,0:T(8,128)(2,1)S(1)} %fusion.4), channel_id=1, source_target_pairs={{0,128},{1,385},{32,160},{33,417},{64,192},{65,449},{96,224},{97,4... | collective-permute-start | bytes 294920 | tf_op jit(solution)/shard_map/ppermute | solution.py:393
  80.2 0.4 collective-permute-done.8
  80.6 5.7 %collective-permute-start.9 = (bf16[64,768]{1,0:T(8,128)(2,1)S(1)}, bf16[64,768]{1,0:T(8,128)(2,1)S(1)}, u32[]{:S(2)}, u32[]{:S(2)}) collective-permute-start(bf16[64,768]{1,0:T(8,128)(2,1)S(1)} %fusion.9), channel_id=1, source_target_pairs={{0,128},{1,385},{32,160},{33,417},{64,192},{65,449},{96,224},{97,4... | collective-permute-start | bytes 294920 | tf_op jit(solution)/shard_map/ppermute | solution.py:393
  86.3 1.4 collective-permute-done.12
  87.8 4.7 %collective-permute-done.9 = bf16[64,768]{1,0:T(8,128)(2,1)S(1)} collective-permute-done((bf16[64,768]{1,0:T(8,128)(2,1)S(1)}, bf16[64,768]{1,0:T(8,128)(2,1)S(1)}, u32[]{:S(2)}, u32[]{:S(2)}) %collective-permute-start.9) | collective-permute-done | bytes 98336 | tf_op jit(solution)/shard_map/ppermute | solution.py:393
  92.5 14.3 %all-gather = bf16[512,768]{1,0:T(8,128)(2,1)S(1)} all-gather(bf16[128,768]{1,0:T(8,128)(2,1)S(1)} %pad_maximum_fusion.2), channel_id=2, replica_groups=mesh['z'=16,'x'=4,'y'=4,'c'=2] {'x'}, dimensions={0}, use_global_device_ids=true | all-gather | bytes 983040 | tf_op jit(solution)/shard_map/all_gather | solution.py:401
  106.9 1.3 shard_map.127
  108.1 5.7 %all-to-all-start = ((bf16[16,16,512]{2,1,0:T(8,128)(2,1)}), bf16[16,16,512]{2,1,0:T(8,128)(2,1)S(1)}, u32[]{:S(2)}, u32[]{:S(2)}) async-start(bf16[16,16,512]{2,1,0:T(8,128)(2,1)} %bitcast.8), calls=%async_computation | async-start | bytes 524288 | tf_op jit(solution)/shard_map/all_to_all | solution.py:404
  113.9 7.9 %collective-permute-start.14 = (bf16[4,2,2,64,512]{4,3,2,1,0:T(8,128)(2,1)S(1)}, bf16[4,2,2,64,512]{4,3,2,1,0:T(8,128)(2,1)S(1)}, u32[]{:S(2)}, u32[]{:S(2)}) collective-permute-start(bf16[4,2,2,64,512]{4,3,2,1,0:T(8,128)(2,1)S(1)} %pad_maximum_fusion.rm_ref), channel_id=1, source_target_pairs={{0,1},{1,0},{2,3},{3,2},{4,5},{5,4},{6,7},{7,6},{8,9},{9,8},{10,11... | collective-permute-start | bytes 3145736 | tf_op jit(solution)/shard_map/ppermute | solution.py:381
  121.8 0.2 fusion.21
  122.0 4.7 %all-to-all-done = bf16[16,16,512]{2,1,0:T(8,128)(2,1)S(1)} async-done(((bf16[16,16,512]{2,1,0:T(8,128)(2,1)}), bf16[16,16,512]{2,1,0:T(8,128)(2,1)S(1)}, u32[]{:S(2)}, u32[]{:S(2)}) %all-to-all-start) | async-done | bytes 262176 | tf_op jit(solution)/shard_map/all_to_all | solution.py:404
  126.7 1.5 shard_map.128
  128.2 10.7 %all-gather.1 = bf16[576,512]{1,0:T(8,128)(2,1)S(1)} all-gather(bf16[144,512]{1,0:T(8,128)(2,1)S(1)} %get-tuple-element.28), channel_id=3, replica_groups=mesh['z'=16,'x'=4,'y'=4,'c'=2] {'y'}, dimensions={0}, use_global_device_ids=true | all-gather | bytes 737280 | tf_op jit(solution)/shard_map/all_gather | solution.py:411
  139.0 11.7 %collective-permute-start.13 = (bf16[4,144,512]{2,1,0:T(8,128)(2,1)S(1)}, bf16[4,144,512]{2,1,0:T(8,128)(2,1)}, u32[]{:S(2)}, u32[]{:S(2)}) collective-permute-start(bf16[4,144,512]{2,1,0:T(8,128)(2,1)S(1)} %bitcast.45), channel_id=1, source_target_pairs={{0,1},{1,0},{2,3},{3,2},{4,5},{5,4},{6,7},{7,6},{8,9},{9,8},{10,11... | collective-permute-start | bytes 1769480 | tf_op jit(solution)/shard_map/ppermute | solution.py:412
  150.7 0.2 compare_reduce_fusion
  150.9 1.5 collective-permute-done.13.o_ref
  152.4 5.1 %shard_map.129 = (f32[2,64,512]{2,1,0:T(8,128)}, f32[2,64,512]{2,1,0:T(8,128)}, bf16[2,512,512]{2,1,0:T(8,128)(2,1)}) custom-call(s32[7]{0:T(128)S(1)} %concatenate.13.f_ref, bf16[4,144,512]{2,1,0:T(8,128)(2,1)S(1)} %bitcast.46, bf16[4,144,512]{2,1,0:T(8,128)(2,1)} %collective-permute-done.13.o_ref, bf16[4,2,2,64,512]{4,3,2,1,0:T(8,128)(2,1)S(1)} %pad_maximum_fusion.rm_ref, ...), custom_call_target="tpu_custom_call" | custom-call | tf_op jit(solution)/shard_map/pallas_call | solution.py:313
  (44 shorter events, 0.7 us)
Async XLA Ops:
  0.6 16.4 %collective-permute-start = (bf16[8,64,256]{2,1,0:T(8,128)(2,1)}, bf16[8,64,256]{2,1,0:T(8,128)(2,1)S(1)}, u32[]{:S(2)}, u32[]{:S(2)}) collective-permute-start(bf16[8,64,256]{2,1,0:T(8,128)(2,1)} %refs_0_.3), channel_id=1, source_target_pairs={{0,1},{1,0},{2,3},{3,2},{4,5},{5,4},{6,7},{7,6},{8,9},{9,8},{10,11... | collective-permute-start | bytes 786440 | tf_op jit(solution)/shard_map/ppermute | solution.py:354
  10.0 4.9 %copy-start.6 = (bf16[1,2,64,512]{3,2,1,0:T(8,128)(2,1)S(1)}, bf16[1,2,64,512]{3,2,1,0:T(8,128)(2,1)}, u32[]{:S(2)}) copy-start(bf16[1,2,64,512]{3,2,1,0:T(8,128)(2,1)} %param.16) | copy-start | bytes 393220
  10.0 4.9 %copy-start.7 = (bf16[1,2,64,512]{3,2,1,0:T(8,128)(2,1)S(1)}, bf16[1,2,64,512]{3,2,1,0:T(8,128)(2,1)}, u32[]{:S(2)}) copy-start(bf16[1,2,64,512]{3,2,1,0:T(8,128)(2,1)} %param.15) | copy-start | bytes 393220
  10.0 6.8 %copy-start.9 = (s32[96]{0:T(128)S(1)}, s32[96]{0:T(128)}, u32[]{:S(2)}) copy-start(s32[96]{0:T(128)} %param.11) | copy-start | bytes 1156
  12.9 36.7 %collective-permute-start.4 = (bf16[1280,256]{1,0:T(8,128)(2,1)}, bf16[1280,256]{1,0:T(8,128)(2,1)S(1)}, u32[]{:S(2)}, u32[]{:S(2)}) collective-permute-start(bf16[1280,256]{1,0:T(8,128)(2,1)} %shard_map.120.p_ref), channel_id=1, source_target_pairs={{0,16},{8,24},{16,0},{24,8},{1,17},{9,25},{17,1},{25,9},{2,18},{10... | collective-permute-start | bytes 1966088 | tf_op jit(solution)/shard_map/ppermute | solution.py:357
  14.9 9.8 %collective-permute-start.2 = (bf16[1,2,2,64,512]{4,3,2,1,0:T(8,128)(2,1)S(1)}, bf16[1,2,2,64,512]{4,3,2,1,0:T(8,128)(2,1)S(1)}, u32[]{:S(2)}, u32[]{:S(2)}) collective-permute-start(bf16[1,2,2,64,512]{4,3,2,1,0:T(8,128)(2,1)S(1)} %maximum_bitcast_fusion), channel_id=1, source_target_pairs={{0,2},{2,0},{4,6},{6,4},{1,3},{3,1},{5,7},{7,5},{8,10},{10,8},{12,... | collective-permute-start | bytes 786440 | tf_op jit(solution)/shard_map/ppermute | solution.py:378
  17.0 0.7 copy-start.5
  21.2 21.0 %collective-permute-start.1 = (bf16[2560,256]{1,0:T(8,128)(2,1)}, bf16[2560,256]{1,0:T(8,128)(2,1)S(1)}, u32[]{:S(2)}, u32[]{:S(2)}) collective-permute-start(bf16[2560,256]{1,0:T(8,128)(2,1)} %shard_map.121), channel_id=1, source_target_pairs={{0,8},{1,25},{8,16},{9,1},{16,24},{17,9},{24,0},{25,17},{2,10},{3,... | collective-permute-start | bytes 3932168 | tf_op jit(solution)/shard_map/ppermute | solution.py:359
  24.8 16.2 %collective-permute-start.3 = (bf16[2,2,2,64,512]{4,3,2,1,0:T(8,128)(2,1)S(1)}, bf16[2,2,2,64,512]{4,3,2,1,0:T(8,128)(2,1)}, u32[]{:S(2)}, u32[]{:S(2)}) collective-permute-start(bf16[2,2,2,64,512]{4,3,2,1,0:T(8,128)(2,1)S(1)} %pad_maximum_fusion.1), channel_id=1, source_target_pairs={{0,4},{2,6},{4,0},{6,2},{1,5},{3,7},{5,1},{7,3},{8,12},{10,14},{12... | collective-permute-start | bytes 1572872 | tf_op jit(solution)/shard_map/ppermute | solution.py:378
  30.6 23.0 %copy-start = (bf16[2048,256]{1,0:T(8,128)(2,1)S(1)}, bf16[2048,256]{1,0:T(8,128)(2,1)}, u32[]{:S(2)}) copy-start(bf16[2048,256]{1,0:T(8,128)(2,1)} %shard_map.122.refs_0_.refs_4_) | copy-start | bytes 3145732
  30.6 23.0 %copy-start.4 = (s32[3]{0:T(128)S(1)}, s32[3]{0:T(128)}, u32[]{:S(2)}) copy-start(s32[3]{0:T(128)} %pad_add_fusion.place_ref) | copy-start | bytes 40
  42.2 11.4 %collective-permute-start.5 = (bf16[2560,256]{1,0:T(8,128)(2,1)S(1)}, bf16[2560,256]{1,0:T(8,128)(2,1)S(1)}, u32[]{:S(2)}, u32[]{:S(2)}) collective-permute-start(bf16[2560,256]{1,0:T(8,128)(2,1)S(1)} %collective-permute-done.1.refs_2_.refs_7_), channel_id=1, source_target_pairs={{0,1},{1,0},{2,3},{3,2},{4,5},{5,4},{6,7},{7,6},{8,9},{9,8},{10,11... | collective-permute-start | bytes 3932168 | tf_op jit(solution)/shard_map/ppermute | solution.py:384
  49.6 4.0 %collective-permute-start.6 = (bf16[1280,256]{1,0:T(8,128)(2,1)S(1)}, bf16[1280,256]{1,0:T(8,128)(2,1)S(1)}, u32[]{:S(2)}, u32[]{:S(2)}) collective-permute-start(bf16[1280,256]{1,0:T(8,128)(2,1)S(1)} %collective-permute-done.4.refs_1_.refs_5_), channel_id=1, source_target_pairs={{0,1},{1,0},{2,3},{3,2},{4,5},{5,4},{6,7},{7,6},{8,9},{9,8},{10,11... | collective-permute-start | bytes 1966088 | tf_op jit(solution)/shard_map/ppermute | solution.py:382
  54.8 11.8 %collective-permute-start.10 = (bf16[256,768]{1,0:T(8,128)(2,1)S(1)}, bf16[256,768]{1,0:T(8,128)(2,1)S(1)}, u32[]{:S(2)}, u32[]{:S(2)}) collective-permute-start(bf16[256,768]{1,0:T(8,128)(2,1)S(1)} %shard_map.126), channel_id=1, source_target_pairs={{0,32},{1,481},{32,64},{33,1},{64,96},{65,33},{96,128},{97,65},{12... | collective-permute-start | bytes 1179656 | tf_op jit(solution)/shard_map/ppermute | solution.py:393
  61.7 8.8 %collective-permute-start.7 = (bf16[256,768]{1,0:T(8,128)(2,1)S(1)}, bf16[256,768]{1,0:T(8,128)(2,1)S(1)}, u32[]{:S(2)}, u32[]{:S(2)}) collective-permute-start(bf16[256,768]{1,0:T(8,128)(2,1)S(1)} %shard_map.124), channel_id=1, source_target_pairs={{0,32},{1,481},{32,64},{33,1},{64,96},{65,33},{96,128},{97,65},{12... | collective-permute-start | bytes 1179656 | tf_op jit(solution)/shard_map/ppermute | solution.py:393
  66.6 9.7 %collective-permute-start.11 = (bf16[128,768]{1,0:T(8,128)(2,1)S(1)}, bf16[128,768]{1,0:T(8,128)(2,1)S(1)}, u32[]{:S(2)}, u32[]{:S(2)}) collective-permute-start(bf16[128,768]{1,0:T(8,128)(2,1)S(1)} %fusion.1), channel_id=1, source_target_pairs={{0,64},{1,449},{32,96},{33,481},{64,128},{65,1},{96,160},{97,33},{... | collective-permute-start | bytes 589832 | tf_op jit(solution)/shard_map/ppermute | solution.py:393
  70.5 10.0 %collective-permute-start.8 = (bf16[128,768]{1,0:T(8,128)(2,1)S(1)}, bf16[128,768]{1,0:T(8,128)(2,1)S(1)}, u32[]{:S(2)}, u32[]{:S(2)}) collective-permute-start(bf16[128,768]{1,0:T(8,128)(2,1)S(1)} %fusion.2), channel_id=1, source_target_pairs={{0,64},{1,449},{32,96},{33,481},{64,128},{65,1},{96,160},{97,33},{... | collective-permute-start | bytes 589832 | tf_op jit(solution)/shard_map/ppermute | solution.py:393
  76.4 11.3 %collective-permute-start.12 = (bf16[64,768]{1,0:T(8,128)(2,1)S(1)}, bf16[64,768]{1,0:T(8,128)(2,1)S(1)}, u32[]{:S(2)}, u32[]{:S(2)}) collective-permute-start(bf16[64,768]{1,0:T(8,128)(2,1)S(1)} %fusion.4), channel_id=1, source_target_pairs={{0,128},{1,385},{32,160},{33,417},{64,192},{65,449},{96,224},{97,4... | collective-permute-start | bytes 294920 | tf_op jit(solution)/shard_map/ppermute | solution.py:393
  80.6 11.8 %collective-permute-start.9 = (bf16[64,768]{1,0:T(8,128)(2,1)S(1)}, bf16[64,768]{1,0:T(8,128)(2,1)S(1)}, u32[]{:S(2)}, u32[]{:S(2)}) collective-permute-start(bf16[64,768]{1,0:T(8,128)(2,1)S(1)} %fusion.9), channel_id=1, source_target_pairs={{0,128},{1,385},{32,160},{33,417},{64,192},{65,449},{96,224},{97,4... | collective-permute-start | bytes 294920 | tf_op jit(solution)/shard_map/ppermute | solution.py:393
  92.5 29.3 %copy-start.8 = (s32[96]{0:T(128)S(1)}, s32[96]{0:T(128)}, u32[]{:S(2)}) copy-start(s32[96]{0:T(128)} %param.12) | copy-start | bytes 1156
  92.5 34.2 %copy-start.3 = (f32[1,2,64,512]{3,2,1,0:T(8,128)S(1)}, f32[1,2,64,512]{3,2,1,0:T(8,128)}, u32[]{:S(2)}) copy-start(f32[1,2,64,512]{3,2,1,0:T(8,128)} %param.17) | copy-start | bytes 786436
  106.8 45.5 %copy-start.1 = (f32[1,2,64,512]{3,2,1,0:T(8,128)S(1)}, f32[1,2,64,512]{3,2,1,0:T(8,128)}, u32[]{:S(2)}) copy-start(f32[1,2,64,512]{3,2,1,0:T(8,128)} %param.13) | copy-start | bytes 786436
  106.9 45.6 %copy-start.2 = (f32[1,2,64,512]{3,2,1,0:T(8,128)S(1)}, f32[1,2,64,512]{3,2,1,0:T(8,128)}, u32[]{:S(2)}) copy-start(f32[1,2,64,512]{3,2,1,0:T(8,128)} %param.14) | copy-start | bytes 786436
  108.1 18.6 %all-to-all-start = ((bf16[16,16,512]{2,1,0:T(8,128)(2,1)}), bf16[16,16,512]{2,1,0:T(8,128)(2,1)S(1)}, u32[]{:S(2)}, u32[]{:S(2)}) async-start(bf16[16,16,512]{2,1,0:T(8,128)(2,1)} %bitcast.8), calls=%async_computation | async-start | bytes 524288 | tf_op jit(solution)/shard_map/all_to_all | solution.py:404
  113.9 37.1 %collective-permute-start.14 = (bf16[4,2,2,64,512]{4,3,2,1,0:T(8,128)(2,1)S(1)}, bf16[4,2,2,64,512]{4,3,2,1,0:T(8,128)(2,1)S(1)}, u32[]{:S(2)}, u32[]{:S(2)}) collective-permute-start(bf16[4,2,2,64,512]{4,3,2,1,0:T(8,128)(2,1)S(1)} %pad_maximum_fusion.rm_ref), channel_id=1, source_target_pairs={{0,1},{1,0},{2,3},{3,2},{4,5},{5,4},{6,7},{7,6},{8,9},{9,8},{10,11... | collective-permute-start | bytes 3145736 | tf_op jit(solution)/shard_map/ppermute | solution.py:381
  139.0 13.4 %collective-permute-start.13 = (bf16[4,144,512]{2,1,0:T(8,128)(2,1)S(1)}, bf16[4,144,512]{2,1,0:T(8,128)(2,1)}, u32[]{:S(2)}, u32[]{:S(2)}) collective-permute-start(bf16[4,144,512]{2,1,0:T(8,128)(2,1)S(1)} %bitcast.45), channel_id=1, source_target_pairs={{0,1},{1,0},{2,3},{3,2},{4,5},{5,4},{6,7},{7,6},{8,9},{9,8},{10,11... | collective-permute-start | bytes 1769480 | tf_op jit(solution)/shard_map/ppermute | solution.py:412

commit v11 on v9

--- a/solution.py
+++ b/solution.py
@@ -26,6 +26,11 @@
     return owners * slot_count + ranked
 
 
+def position(place_ref, ny):
+    index = place_ref[0]
+    return index // (NX * ny * NC), index // (ny * NC) % NX, index % NC
+
+
 def ring(count, step):
     return [(i, (i + step) % count) for i in range(count)]
 
@@ -38,7 +43,7 @@
     return lax.dot_general(a, b, (dims, ((), ())), preferred_element_type=WIDE)
 
 
-def prepare(activations, out_grads, place):
+def prepare(activations, out_grads, place, ny):
     block_rows, rows, toks = activations.shape
     per_z = rows // NZ
     count = block_rows * rows // 2
@@ -47,12 +52,14 @@
     tile = width // TILES
 
     def kernel(place_ref, a_ref, b_ref, *refs):
-        out_refs, (held, sems, out_sems) = refs[:3], refs[3:]
-        z, c = place_ref[0], place_ref[2]
+        out_refs, (held, rows_in, sems, out_sems, rows_sem) = refs[:3], refs[3:]
+        z, x, c = position(place_ref, ny)
+        rows_copy = pltpu.make_async_copy(a_ref, rows_in, rows_sem)
+        rows_copy.start()
         tok = pl.ds(pl.multiple_of(c * half, half), half)
         copies = []
         for i in range(3):
-            begin = place_ref[3 + i] * width
+            begin = jnp.bitwise_and(x + (2, 3, 1)[i], NX - 1) * width
             for n in range(TILES):
                 at = pl.ds(pl.multiple_of(begin + n * tile, tile), tile)
                 to = pl.ds(2 * count + n * half, half)
@@ -64,11 +71,14 @@
         row = (m // block_rows) % per_z
         tail = m // (block_rows * per_z)
         high = 2 * (tail // 4) + 4 * ((tail // 2) % 2) + 8 * (tail % 2)
-        values = a_ref[...].reshape(2 * count, toks)
+        picks = []
         for odd in range(2):
             goal = jnp.bitwise_and(z + (1 - 2 * c) * (high + odd), NZ - 1)
-            pick = (block * rows + goal * per_z + row == k).astype(WIDE).astype(HALF)
-            moved = dot(pick, values).astype(HALF)
+            picks.append((block * rows + goal * per_z + row == k).astype(WIDE).astype(HALF))
+        rows_copy.wait()
+        values = rows_in[...].reshape(2 * count, toks)
+        for odd in range(2):
+            moved = dot(picks[odd], values).astype(HALF)
             turned = jnp.concatenate([moved[:, half:], moved[:, :half]], axis=1)
             at = (1 - odd) * count
             ordered = jnp.where(c == 1, turned, moved)
@@ -89,20 +99,22 @@
         out_shape=[jax.ShapeDtypeStruct(piece, HALF)] * 3,
         in_specs=[
             pl.BlockSpec(memory_space=pltpu.SMEM),
-            pl.BlockSpec(memory_space=pltpu.VMEM),
+            any_place,
             any_place,
         ],
         out_specs=[any_place] * 3,
         scratch_shapes=[
             pltpu.VMEM((3, *piece), HALF),
+            pltpu.VMEM(activations.shape, HALF),
             pltpu.SemaphoreType.DMA((3, TILES)),
             pltpu.SemaphoreType.DMA((3,)),
+            pltpu.SemaphoreType.DMA,
         ],
         compiler_params=ROOMY,
     )(place, activations, out_grads)
 
 
-def own_part(piece, out_grads, place):
+def own_part(piece, out_grads, place, ny):
     toks = out_grads.shape[0]
     half = toks // NC
     width = out_grads.shape[1] // NX
@@ -110,7 +122,7 @@
     count = piece.shape[0] - TILES * half
 
     def kernel(place_ref, p_ref, b_ref, o_ref):
-        c = place_ref[2]
+        c = position(place_ref, ny)[2]
         o_ref[:count, :] = p_ref[...]
         for n in range(TILES):
             for side, who in enumerate((c, 1 - c)):
@@ -127,7 +139,7 @@
             grid=(1,),
             in_specs=[
                 pl.BlockSpec((count, tile), lambda i, place_ref: (0, 0)),
-                pl.BlockSpec((toks, width), lambda i, place_ref: (0, place_ref[1])),
+                pl.BlockSpec((toks, width), lambda i, place_ref: (0, position(place_ref, ny)[1])),
             ],
             out_specs=pl.BlockSpec(own, lambda i, place_ref: (0, 0)),
         ),
@@ -329,8 +341,9 @@
     my_mp = y * NC + c
     my_rows = my_mp * rows
 
-    place = jnp.stack([z, x, c] + [jnp.bitwise_and(x + step, NX - 1) for step in (2, 3, 1)]).astype(jnp.int32)
-    pieces = prepare(activations, out_grads, place)
+    ny = lax.axis_size("y")
+    place = lax.axis_index(("z", "x", "y", "c")).reshape(1).astype(jnp.int32)
+    pieces = prepare(activations, out_grads, place, ny)
     arrived = [lax.ppermute(piece, "x", ring(NX, step)) for piece, step in zip(pieces, (2, -1, 1))]
 
     piece_own, owners = lax.optimization_barrier((pieces[0], owners))
@@ -343,10 +356,9 @@
     out_rows = NZ * slots * 2 * per_z
     chosen = (code == iota((out_rows, 1), 0)).astype(HALF)
     piece_own, chosen = lax.optimization_barrier((piece_own, chosen))
-    own = own_part(piece_own, out_grads, place)
+    own = own_part(piece_own, out_grads, place, ny)
 
     own, left_root, right_root = lax.optimization_barrier((own, left_root, right_root))
-    ny = lax.axis_size("y")
     roots = jnp.stack([left_root[0], right_root[0]])[None]
     for step in (1, 2):
         if step < ny:
@@ -359,20 +371,24 @@
     sent = [partial_products(own, arrived, swapped, True, chunk) for chunk in range(CHUNKS)]
     kept = [partial_products(own, arrived, swapped, False, chunk) for chunk in range(CHUNKS)]
 
-    sums = []
+    def along(out, step):
+        goals = [((i + (1 - 2 * k) * step) % NZ) * NC + k for i in range(NZ) for k in range(NC)]
+        return lax.ppermute(out, ("z", "c"), list(enumerate(goals)))
+
+    lasts, sums = [], []
     for out, keep in zip(sent, kept):
-        got = []
-        for step in (1, 2, 4):
-            goals = [((i + (1 - 2 * k) * step) % NZ) * NC + k for i in range(NZ) for k in range(NC)]
-            got.append(lax.ppermute(out, ("z", "c"), list(enumerate(goals))))
-            part = got[-1].shape[0] // (2 if step < 4 else 1)
-            rows_from = slice(part, 2 * part) if step < 4 else slice(0, part)
-            total = keep[rows_from]
-            for rows_in in got:
-                total = total + rows_in[rows_from]
-            out = total.astype(HALF)
-        sums.append(out)
-    sums = lax.all_gather(jnp.concatenate(sums, axis=0), "x", axis=0, tiled=False)
+        first = along(out, 1)
+        part = first.shape[0] // 2
+        second = along((keep[part:] + first[part:]).astype(HALF), 2)
+        half = part // 2
+        lasts.append((keep[half:part] + first[half:part] + second[half:]).astype(HALF))
+        sums.append((keep[:half], first[:half], second[:half]))
+    third = along(jnp.concatenate(lasts, axis=0), 4)
+    sums = [
+        (a + b + d + third[k * half : (k + 1) * half]).astype(HALF) for k, (a, b, d) in enumerate(sums)
+    ]
+    sums = jnp.concatenate(sums, axis=0)
+    sums = lax.all_gather(sums, "x", axis=0, tiled=False)
 
     picked = pick_blocks(chosen, sums, block_size).reshape(NZ, out_rows // NZ, block_size)
     arrived = lax.all_to_all(picked, "z", 0, 0, tiled=True).reshape(out_rows, block_size)

time: 156 us -> 163 us (1.045)
  waiting for transfers between devices: 20 us -> 31.2 us
  starting transfers between devices: 93 us -> 89.4 us
    ppermute x6 -> x5, waiting for transfers between devices: 6.8 us -> 17.8 us  [along(): return lax.ppermute(out, ('z', 'c'), list(enumerate(goals)))]
    ppermute x6 -> x5, starting transfers between devices: 33.2 us -> 26.4 us  [along(): return lax.ppermute(out, ('z', 'c'), list(enumerate(goals)))]
    ppermute x3, starting transfers between devices: 9.9 us -> 16.5 us  [body(): swapped = [lax.ppermute(piece, 'c', ring(NC, 1)) for piece in arrived]]
    ppermute x1, starting transfers between devices: 8.99 us -> 6.82 us  [body(): roots_other = lax.ppermute(roots, 'c', ring(NC, 1))]
    all_to_all x1, waiting for transfers between devices: 3.63 us -> 5.74 us  [body(): lax.all_to_all(picked, 'z', 0, 0, tiled=True).reshape(out_rows, block_size)]
    ppermute x3, waiting for transfers between devices: 1.99 us -> 0.01 us  [body(): lax.ppermute(piece, 'x', ring(NX, step))]
  transfers between devices with their start and end apart: 17 -> 16, of which waited for: 8 -> 9; matrix products, arithmetic and copies ran while one was open for 1% -> 1% of each run, Pallas kernels for 4% -> 3%
where the time goes in v11:
time: 163 us; the launch traced here: 162 us
  starting transfers between devices  89.4 us (55%)
  waiting for transfers between devices  31.2 us (19%)
  blocking collectives  23.4 us (14%)
  Pallas kernels  15.7 us (10%)
    ppermute x5, starting transfers between devices, along(): return lax.ppermute(out, ('z', 'c'), list(enumerate(goals)))  26.4 us
    ppermute x5, waiting for transfers between devices, along(): return lax.ppermute(out, ('z', 'c'), list(enumerate(goals)))  17.8 us
    ppermute x3, starting transfers between devices, body(): swapped = [lax.ppermute(piece, 'c', ring(NC, 1)) for piece in arrived]  16.5 us
    ppermute x1, starting transfers between devices, body(): rows_other = lax.ppermute(rows_mine, 'c', ring(NC, 1))  12.8 us
    all_gather x1, blocking collectives, body(): sums = lax.all_gather(sums, 'x', axis=0, tiled=False)  12.3 us
    all_gather x1, blocking collectives, body(): rows_mine = lax.all_gather(own_rows, 'y', axis=0, tiled=False)  11.1 us
    ppermute x3, starting transfers between devices, body(): lax.ppermute(piece, 'x', ring(NX, step))  10.9 us
    ppermute x2, starting transfers between devices, body(): came = lax.ppermute(roots, 'y', [(i, i ^ step) for i in range(ny)])  8.92 us
  transfers between devices with their start and end apart: 16, of which 9 were waited for; matrix products, arithmetic and copies ran while one was open for 1% of the time, Pallas kernels for 3%

profile of v11, /device:TPU:1, one launch (start us, length us, event | category | flops | bytes accessed | tf_op | source)
XLA Modules:
  0.0 162.4 jit_solution(3708521118707447323)
XLA Ops:
  0.7 3.3 %shard_map.120 = (bf16[1280,256]{1,0:T(8,128)(2,1)}, bf16[1280,256]{1,0:T(8,128)(2,1)}, bf16[1280,256]{1,0:T(8,128)(2,1)}) custom-call(s32[1]{0:T(128)} %bitcast.3.place_ref, bf16[8,64,256]{2,1,0:T(8,128)(2,1)} %a_ref.1, bf16[256,6144]{1,0:T(8,128)(2,1)} %b_ref.3), custom_call_target="tpu_custom_call" | custom-call | tf_op jit(solution)/shard_map/pallas_call | solution.py:97
  3.9 0.0 copy-start.4
  4.0 5.3 %collective-permute-start.3 = (bf16[1280,256]{1,0:T(8,128)(2,1)}, bf16[1280,256]{1,0:T(8,128)(2,1)S(1)}, u32[]{:S(2)}, u32[]{:S(2)}) collective-permute-start(bf16[1280,256]{1,0:T(8,128)(2,1)} %get-tuple-element.30), channel_id=1, source_target_pairs={{0,24},{8,0},{16,8},{24,16},{1,25},{9,1},{17,9},{25,17},{2,26},{10... | collective-permute-start | bytes 1966088 | tf_op jit(solution)/shard_map/ppermute | solution.py:347
  9.3 1.9 %collective-permute-start.4 = (bf16[1280,256]{1,0:T(8,128)(2,1)}, bf16[1280,256]{1,0:T(8,128)(2,1)S(1)}, u32[]{:S(2)}, u32[]{:S(2)}) collective-permute-start(bf16[1280,256]{1,0:T(8,128)(2,1)} %get-tuple-element.31), channel_id=1, source_target_pairs={{0,8},{8,16},{16,24},{24,0},{1,9},{9,17},{17,25},{25,1},{2,10},{10... | collective-permute-start | bytes 1966088 | tf_op jit(solution)/shard_map/ppermute | solution.py:347
  11.2 3.6 %collective-permute-start.2 = (bf16[1280,256]{1,0:T(8,128)(2,1)}, bf16[1280,256]{1,0:T(8,128)(2,1)S(1)}, u32[]{:S(2)}, u32[]{:S(2)}) collective-permute-start(bf16[1280,256]{1,0:T(8,128)(2,1)} %get-tuple-element.25.p_ref), channel_id=1, source_target_pairs={{0,16},{8,24},{16,0},{24,8},{1,17},{9,25},{17,1},{25,9},{2,18},{10... | collective-permute-start | bytes 1966088 | tf_op jit(solution)/shard_map/ppermute | solution.py:347
  14.9 0.2 select_reduce_fusion
  15.1 0.1 reshape.114
  15.2 0.1 copy.19
  15.4 0.1 select_n.49
  15.5 0.1 fusion.p_ref
  15.6 2.3 %shard_map.121.refs_0_.refs_4_ = bf16[2048,256]{1,0:T(8,128)(2,1)} custom-call(s32[1]{0:T(128)} %bitcast.3.place_ref, bf16[1280,256]{1,0:T(8,128)(2,1)} %get-tuple-element.25.p_ref, bf16[256,6144]{1,0:T(8,128)(2,1)} %b_ref.3), custom_call_target="tpu_custom_call" | custom-call | tf_op jit(solution)/shard_map/pallas_call | solution.py:134
  17.9 3.3 %collective-permute-start = (bf16[1,2,2,64,512]{4,3,2,1,0:T(8,128)(2,1)S(1)}, bf16[1,2,2,64,512]{4,3,2,1,0:T(8,128)(2,1)S(1)}, u32[]{:S(2)}, u32[]{:S(2)}) collective-permute-start(bf16[1,2,2,64,512]{4,3,2,1,0:T(8,128)(2,1)S(1)} %maximum_bitcast_fusion), channel_id=1, source_target_pairs={{0,2},{2,0},{4,6},{6,4},{1,3},{3,1},{5,7},{7,5},{8,10},{10,8},{12,... | collective-permute-start | bytes 786440 | tf_op jit(solution)/shard_map/ppermute | solution.py:365
  21.3 4.2 %collective-permute-done = bf16[1,2,2,64,512]{4,3,2,1,0:T(8,128)(2,1)S(1)} collective-permute-done((bf16[1,2,2,64,512]{4,3,2,1,0:T(8,128)(2,1)S(1)}, bf16[1,2,2,64,512]{4,3,2,1,0:T(8,128)(2,1)S(1)}, u32[]{:S(2)}, u32[]{:S(2)}) %collective-permute-start) | collective-permute-done | bytes 262176 | tf_op jit(solution)/shard_map/ppermute | solution.py:365
  25.5 0.1 pad_maximum_fusion.1
  25.5 5.6 %collective-permute-start.1 = (bf16[2,2,2,64,512]{4,3,2,1,0:T(8,128)(2,1)S(1)}, bf16[2,2,2,64,512]{4,3,2,1,0:T(8,128)(2,1)S(1)}, u32[]{:S(2)}, u32[]{:S(2)}) collective-permute-start(bf16[2,2,2,64,512]{4,3,2,1,0:T(8,128)(2,1)S(1)} %pad_maximum_fusion.1), channel_id=1, source_target_pairs={{0,4},{2,6},{4,0},{6,2},{1,5},{3,7},{5,1},{7,3},{8,12},{10,14},{12... | collective-permute-start | bytes 1572872 | tf_op jit(solution)/shard_map/ppermute | solution.py:365
  31.1 9.4 %collective-permute-start.6 = (bf16[1280,256]{1,0:T(8,128)(2,1)S(1)}, bf16[1280,256]{1,0:T(8,128)(2,1)S(1)}, u32[]{:S(2)}, u32[]{:S(2)}) collective-permute-start(bf16[1280,256]{1,0:T(8,128)(2,1)S(1)} %collective-permute-done.3.refs_2_.refs_6_), channel_id=1, source_target_pairs={{0,1},{1,0},{2,3},{3,2},{4,5},{5,4},{6,7},{7,6},{8,9},{9,8},{10,11... | collective-permute-start | bytes 1966088 | tf_op jit(solution)/shard_map/ppermute | solution.py:368
  40.5 5.2 %collective-permute-start.7 = (bf16[1280,256]{1,0:T(8,128)(2,1)S(1)}, bf16[1280,256]{1,0:T(8,128)(2,1)S(1)}, u32[]{:S(2)}, u32[]{:S(2)}) collective-permute-start(bf16[1280,256]{1,0:T(8,128)(2,1)S(1)} %collective-permute-done.4.refs_3_.refs_7_), channel_id=1, source_target_pairs={{0,1},{1,0},{2,3},{3,2},{4,5},{5,4},{6,7},{7,6},{8,9},{9,8},{10,11... | collective-permute-start | bytes 1966088 | tf_op jit(solution)/shard_map/ppermute | solution.py:368
  45.7 1.9 %collective-permute-start.5 = (bf16[1280,256]{1,0:T(8,128)(2,1)S(1)}, bf16[1280,256]{1,0:T(8,128)(2,1)S(1)}, u32[]{:S(2)}, u32[]{:S(2)}) collective-permute-start(bf16[1280,256]{1,0:T(8,128)(2,1)S(1)} %collective-permute-done.2.refs_1_.refs_5_), channel_id=1, source_target_pairs={{0,1},{1,0},{2,3},{3,2},{4,5},{5,4},{6,7},{7,6},{8,9},{9,8},{10,11... | collective-permute-start | bytes 1966088 | tf_op jit(solution)/shard_map/ppermute | solution.py:368
  47.7 0.1 pad_maximum_fusion.rm_ref
  47.8 1.9 %collective-permute-done.5.refs_8_ = bf16[1280,256]{1,0:T(8,128)(2,1)S(1)} collective-permute-done((bf16[1280,256]{1,0:T(8,128)(2,1)S(1)}, bf16[1280,256]{1,0:T(8,128)(2,1)S(1)}, u32[]{:S(2)}, u32[]{:S(2)}) %collective-permute-start.5) | collective-permute-done | bytes 655392 | tf_op jit(solution)/shard_map/ppermute | solution.py:368
  49.7 0.6 shard_map.125
  50.3 11.1 %collective-permute-start.10 = (bf16[256,768]{1,0:T(8,128)(2,1)S(1)}, bf16[256,768]{1,0:T(8,128)(2,1)S(1)}, u32[]{:S(2)}, u32[]{:S(2)}) collective-permute-start(bf16[256,768]{1,0:T(8,128)(2,1)S(1)} %shard_map.125), channel_id=1, source_target_pairs={{0,32},{1,481},{32,64},{33,1},{64,96},{65,33},{96,128},{97,65},{12... | collective-permute-start | bytes 1179656 | tf_op jit(solution)/shard_map/ppermute | solution.py:376
  61.5 0.6 shard_map.123
  62.0 2.6 %collective-permute-start.8 = (bf16[256,768]{1,0:T(8,128)(2,1)S(1)}, bf16[256,768]{1,0:T(8,128)(2,1)S(1)}, u32[]{:S(2)}, u32[]{:S(2)}) collective-permute-start(bf16[256,768]{1,0:T(8,128)(2,1)S(1)} %shard_map.123), channel_id=1, source_target_pairs={{0,32},{1,481},{32,64},{33,1},{64,96},{65,33},{96,128},{97,65},{12... | collective-permute-start | bytes 1179656 | tf_op jit(solution)/shard_map/ppermute | solution.py:376
  64.7 0.6 shard_map.124
  65.3 0.6 shard_map.122
  65.9 0.3 collective-permute-done.10
  66.2 4.6 %collective-permute-start.11 = (bf16[128,768]{1,0:T(8,128)(2,1)S(1)}, bf16[128,768]{1,0:T(8,128)(2,1)S(1)}, u32[]{:S(2)}, u32[]{:S(2)}) collective-permute-start(bf16[128,768]{1,0:T(8,128)(2,1)S(1)} %fusion.1), channel_id=1, source_target_pairs={{0,64},{1,449},{32,96},{33,481},{64,128},{65,1},{96,160},{97,33},{... | collective-permute-start | bytes 589832 | tf_op jit(solution)/shard_map/ppermute | solution.py:376
  70.7 0.1 collective-permute-done.8
  70.9 4.2 %collective-permute-start.9 = (bf16[128,768]{1,0:T(8,128)(2,1)S(1)}, bf16[128,768]{1,0:T(8,128)(2,1)S(1)}, u32[]{:S(2)}, u32[]{:S(2)}) collective-permute-start(bf16[128,768]{1,0:T(8,128)(2,1)S(1)} %fusion.2), channel_id=1, source_target_pairs={{0,64},{1,449},{32,96},{33,481},{64,128},{65,1},{96,160},{97,33},{... | collective-permute-start | bytes 589832 | tf_op jit(solution)/shard_map/ppermute | solution.py:376
  75.1 0.8 collective-permute-done.11
  76.0 4.8 %collective-permute-done.9 = bf16[128,768]{1,0:T(8,128)(2,1)S(1)} collective-permute-done((bf16[128,768]{1,0:T(8,128)(2,1)S(1)}, bf16[128,768]{1,0:T(8,128)(2,1)S(1)}, u32[]{:S(2)}, u32[]{:S(2)}) %collective-permute-start.9) | collective-permute-done | bytes 196640 | tf_op jit(solution)/shard_map/ppermute | solution.py:376
  80.9 3.9 %collective-permute-start.12 = (bf16[128,768]{1,0:T(8,128)(2,1)S(1)}, bf16[128,768]{1,0:T(8,128)(2,1)S(1)}, u32[]{:S(2)}, u32[]{:S(2)}) collective-permute-start(bf16[128,768]{1,0:T(8,128)(2,1)S(1)} %pad_maximum_fusion.2), channel_id=1, source_target_pairs={{0,128},{1,385},{32,160},{33,417},{64,192},{65,449},{96,224},{97,4... | collective-permute-start | bytes 589832 | tf_op jit(solution)/shard_map/ppermute | solution.py:376
  84.8 11.8 %collective-permute-done.12 = bf16[128,768]{1,0:T(8,128)(2,1)S(1)} collective-permute-done((bf16[128,768]{1,0:T(8,128)(2,1)S(1)}, bf16[128,768]{1,0:T(8,128)(2,1)S(1)}, u32[]{:S(2)}, u32[]{:S(2)}) %collective-permute-start.12) | collective-permute-done | bytes 196640 | tf_op jit(solution)/shard_map/ppermute | solution.py:376
  96.6 0.1 fusion.12
  96.7 12.3 %all-gather = bf16[512,768]{1,0:T(8,128)(2,1)S(1)} all-gather(bf16[128,768]{1,0:T(8,128)(2,1)S(1)} %pad_maximum_fusion.3), channel_id=2, replica_groups=mesh['z'=16,'x'=4,'y'=4,'c'=2] {'x'}, dimensions={0}, use_global_device_ids=true | all-gather | bytes 983040 | tf_op jit(solution)/shard_map/all_gather | solution.py:391
  109.0 1.3 shard_map.126
  110.3 7.1 %all-to-all-start = ((bf16[16,16,512]{2,1,0:T(8,128)(2,1)}), bf16[16,16,512]{2,1,0:T(8,128)(2,1)S(1)}, u32[]{:S(2)}, u32[]{:S(2)}) async-start(bf16[16,16,512]{2,1,0:T(8,128)(2,1)} %bitcast.7), calls=%async_computation | async-start | bytes 524288 | tf_op jit(solution)/shard_map/all_to_all | solution.py:394
  117.4 6.8 %collective-permute-start.14 = (bf16[4,2,2,64,512]{4,3,2,1,0:T(8,128)(2,1)S(1)}, bf16[4,2,2,64,512]{4,3,2,1,0:T(8,128)(2,1)S(1)}, u32[]{:S(2)}, u32[]{:S(2)}) collective-permute-start(bf16[4,2,2,64,512]{4,3,2,1,0:T(8,128)(2,1)S(1)} %pad_maximum_fusion.rm_ref), channel_id=1, source_target_pairs={{0,1},{1,0},{2,3},{3,2},{4,5},{5,4},{6,7},{7,6},{8,9},{9,8},{10,11... | collective-permute-start | bytes 3145736 | tf_op jit(solution)/shard_map/ppermute | solution.py:369
  124.2 0.2 fusion.21
  124.4 5.7 %all-to-all-done = bf16[16,16,512]{2,1,0:T(8,128)(2,1)S(1)} async-done(((bf16[16,16,512]{2,1,0:T(8,128)(2,1)}), bf16[16,16,512]{2,1,0:T(8,128)(2,1)S(1)}, u32[]{:S(2)}, u32[]{:S(2)}) %all-to-all-start) | async-done | bytes 262176 | tf_op jit(solution)/shard_map/all_to_all | solution.py:394
  130.1 1.5 shard_map.127
  131.7 11.1 %all-gather.1 = bf16[576,512]{1,0:T(8,128)(2,1)S(1)} all-gather(bf16[144,512]{1,0:T(8,128)(2,1)S(1)} %get-tuple-element.32), channel_id=3, replica_groups=mesh['z'=16,'x'=4,'y'=4,'c'=2] {'y'}, dimensions={0}, use_global_device_ids=true | all-gather | bytes 737280 | tf_op jit(solution)/shard_map/all_gather | solution.py:401
  142.8 12.8 %collective-permute-start.13 = (bf16[4,144,512]{2,1,0:T(8,128)(2,1)S(1)}, bf16[4,144,512]{2,1,0:T(8,128)(2,1)}, u32[]{:S(2)}, u32[]{:S(2)}) collective-permute-start(bf16[4,144,512]{2,1,0:T(8,128)(2,1)S(1)} %bitcast.44), channel_id=1, source_target_pairs={{0,1},{1,0},{2,3},{3,2},{4,5},{5,4},{6,7},{7,6},{8,9},{9,8},{10,11... | collective-permute-start | bytes 1769480 | tf_op jit(solution)/shard_map/ppermute | solution.py:402
  155.6 0.2 compare_reduce_fusion
  155.8 0.1 concatenate.16.f_ref
  155.9 1.5 collective-permute-done.13.o_ref
  157.3 5.1 %shard_map.128 = (f32[2,64,512]{2,1,0:T(8,128)}, f32[2,64,512]{2,1,0:T(8,128)}, bf16[2,512,512]{2,1,0:T(8,128)(2,1)}) custom-call(s32[7]{0:T(128)S(1)} %concatenate.16.f_ref, bf16[4,144,512]{2,1,0:T(8,128)(2,1)S(1)} %bitcast.45, bf16[4,144,512]{2,1,0:T(8,128)(2,1)} %collective-permute-done.13.o_ref, bf16[4,2,2,64,512]{4,3,2,1,0:T(8,128)(2,1)S(1)} %pad_maximum_fusion.rm_ref, ...), custom_call_target="tpu_custom_call" | custom-call | tf_op jit(solution)/shard_map/pallas_call | solution.py:305
  (38 shorter events, 0.4 us)
Async XLA Ops:
  0.6 14.3 %copy-start.7 = (s32[96]{0:T(128)S(1)}, s32[96]{0:T(128)}, u32[]{:S(2)}) copy-start(s32[96]{0:T(128)} %param.11) | copy-start | bytes 1156
  3.9 13.9 %copy-start.4 = (bf16[1,2,64,512]{3,2,1,0:T(8,128)(2,1)S(1)}, bf16[1,2,64,512]{3,2,1,0:T(8,128)(2,1)}, u32[]{:S(2)}) copy-start(bf16[1,2,64,512]{3,2,1,0:T(8,128)(2,1)} %param.16) | copy-start | bytes 393220
  3.9 13.9 %copy-start.5 = (bf16[1,2,64,512]{3,2,1,0:T(8,128)(2,1)S(1)}, bf16[1,2,64,512]{3,2,1,0:T(8,128)(2,1)}, u32[]{:S(2)}) copy-start(bf16[1,2,64,512]{3,2,1,0:T(8,128)(2,1)} %param.15) | copy-start | bytes 393220
  4.0 27.2 %collective-permute-start.3 = (bf16[1280,256]{1,0:T(8,128)(2,1)}, bf16[1280,256]{1,0:T(8,128)(2,1)S(1)}, u32[]{:S(2)}, u32[]{:S(2)}) collective-permute-start(bf16[1280,256]{1,0:T(8,128)(2,1)} %get-tuple-element.30), channel_id=1, source_target_pairs={{0,24},{8,0},{16,8},{24,16},{1,25},{9,1},{17,9},{25,17},{2,26},{10... | collective-permute-start | bytes 1966088 | tf_op jit(solution)/shard_map/ppermute | solution.py:347
  9.3 31.2 %collective-permute-start.4 = (bf16[1280,256]{1,0:T(8,128)(2,1)}, bf16[1280,256]{1,0:T(8,128)(2,1)S(1)}, u32[]{:S(2)}, u32[]{:S(2)}) collective-permute-start(bf16[1280,256]{1,0:T(8,128)(2,1)} %get-tuple-element.31), channel_id=1, source_target_pairs={{0,8},{8,16},{16,24},{24,0},{1,9},{9,17},{17,25},{25,1},{2,10},{10... | collective-permute-start | bytes 1966088 | tf_op jit(solution)/shard_map/ppermute | solution.py:347
  11.2 34.5 %collective-permute-start.2 = (bf16[1280,256]{1,0:T(8,128)(2,1)}, bf16[1280,256]{1,0:T(8,128)(2,1)S(1)}, u32[]{:S(2)}, u32[]{:S(2)}) collective-permute-start(bf16[1280,256]{1,0:T(8,128)(2,1)} %get-tuple-element.25.p_ref), channel_id=1, source_target_pairs={{0,16},{8,24},{16,0},{24,8},{1,17},{9,25},{17,1},{25,9},{2,18},{10... | collective-permute-start | bytes 1966088 | tf_op jit(solution)/shard_map/ppermute | solution.py:347
  17.9 31.8 %copy-start = (bf16[2048,256]{1,0:T(8,128)(2,1)S(1)}, bf16[2048,256]{1,0:T(8,128)(2,1)}, u32[]{:S(2)}) copy-start(bf16[2048,256]{1,0:T(8,128)(2,1)} %shard_map.121.refs_0_.refs_4_) | copy-start | bytes 3145732
  17.9 7.5 %collective-permute-start = (bf16[1,2,2,64,512]{4,3,2,1,0:T(8,128)(2,1)S(1)}, bf16[1,2,2,64,512]{4,3,2,1,0:T(8,128)(2,1)S(1)}, u32[]{:S(2)}, u32[]{:S(2)}) collective-permute-start(bf16[1,2,2,64,512]{4,3,2,1,0:T(8,128)(2,1)S(1)} %maximum_bitcast_fusion), channel_id=1, source_target_pairs={{0,2},{2,0},{4,6},{6,4},{1,3},{3,1},{5,7},{7,5},{8,10},{10,8},{12,... | collective-permute-start | bytes 786440 | tf_op jit(solution)/shard_map/ppermute | solution.py:365
  25.5 22.1 %collective-permute-start.1 = (bf16[2,2,2,64,512]{4,3,2,1,0:T(8,128)(2,1)S(1)}, bf16[2,2,2,64,512]{4,3,2,1,0:T(8,128)(2,1)S(1)}, u32[]{:S(2)}, u32[]{:S(2)}) collective-permute-start(bf16[2,2,2,64,512]{4,3,2,1,0:T(8,128)(2,1)S(1)} %pad_maximum_fusion.1), channel_id=1, source_target_pairs={{0,4},{2,6},{4,0},{6,2},{1,5},{3,7},{5,1},{7,3},{8,12},{10,14},{12... | collective-permute-start | bytes 1572872 | tf_op jit(solution)/shard_map/ppermute | solution.py:365
  31.1 16.7 %collective-permute-start.6 = (bf16[1280,256]{1,0:T(8,128)(2,1)S(1)}, bf16[1280,256]{1,0:T(8,128)(2,1)S(1)}, u32[]{:S(2)}, u32[]{:S(2)}) collective-permute-start(bf16[1280,256]{1,0:T(8,128)(2,1)S(1)} %collective-permute-done.3.refs_2_.refs_6_), channel_id=1, source_target_pairs={{0,1},{1,0},{2,3},{3,2},{4,5},{5,4},{6,7},{7,6},{8,9},{9,8},{10,11... | collective-permute-start | bytes 1966088 | tf_op jit(solution)/shard_map/ppermute | solution.py:368
  40.5 7.3 %collective-permute-start.7 = (bf16[1280,256]{1,0:T(8,128)(2,1)S(1)}, bf16[1280,256]{1,0:T(8,128)(2,1)S(1)}, u32[]{:S(2)}, u32[]{:S(2)}) collective-permute-start(bf16[1280,256]{1,0:T(8,128)(2,1)S(1)} %collective-permute-done.4.refs_3_.refs_7_), channel_id=1, source_target_pairs={{0,1},{1,0},{2,3},{3,2},{4,5},{5,4},{6,7},{7,6},{8,9},{9,8},{10,11... | collective-permute-start | bytes 1966088 | tf_op jit(solution)/shard_map/ppermute | solution.py:368
  45.7 4.0 %collective-permute-start.5 = (bf16[1280,256]{1,0:T(8,128)(2,1)S(1)}, bf16[1280,256]{1,0:T(8,128)(2,1)S(1)}, u32[]{:S(2)}, u32[]{:S(2)}) collective-permute-start(bf16[1280,256]{1,0:T(8,128)(2,1)S(1)} %collective-permute-done.2.refs_1_.refs_5_), channel_id=1, source_target_pairs={{0,1},{1,0},{2,3},{3,2},{4,5},{5,4},{6,7},{7,6},{8,9},{9,8},{10,11... | collective-permute-start | bytes 1966088 | tf_op jit(solution)/shard_map/ppermute | solution.py:368
  50.3 15.8 %collective-permute-start.10 = (bf16[256,768]{1,0:T(8,128)(2,1)S(1)}, bf16[256,768]{1,0:T(8,128)(2,1)S(1)}, u32[]{:S(2)}, u32[]{:S(2)}) collective-permute-start(bf16[256,768]{1,0:T(8,128)(2,1)S(1)} %shard_map.125), channel_id=1, source_target_pairs={{0,32},{1,481},{32,64},{33,1},{64,96},{65,33},{96,128},{97,65},{12... | collective-permute-start | bytes 1179656 | tf_op jit(solution)/shard_map/ppermute | solution.py:376
  62.0 8.8 %collective-permute-start.8 = (bf16[256,768]{1,0:T(8,128)(2,1)S(1)}, bf16[256,768]{1,0:T(8,128)(2,1)S(1)}, u32[]{:S(2)}, u32[]{:S(2)}) collective-permute-start(bf16[256,768]{1,0:T(8,128)(2,1)S(1)} %shard_map.123), channel_id=1, source_target_pairs={{0,32},{1,481},{32,64},{33,1},{64,96},{65,33},{96,128},{97,65},{12... | collective-permute-start | bytes 1179656 | tf_op jit(solution)/shard_map/ppermute | solution.py:376
  66.2 9.8 %collective-permute-start.11 = (bf16[128,768]{1,0:T(8,128)(2,1)S(1)}, bf16[128,768]{1,0:T(8,128)(2,1)S(1)}, u32[]{:S(2)}, u32[]{:S(2)}) collective-permute-start(bf16[128,768]{1,0:T(8,128)(2,1)S(1)} %fusion.1), channel_id=1, source_target_pairs={{0,64},{1,449},{32,96},{33,481},{64,128},{65,1},{96,160},{97,33},{... | collective-permute-start | bytes 589832 | tf_op jit(solution)/shard_map/ppermute | solution.py:376
  70.9 53.3 %copy-start.6 = (s32[96]{0:T(128)S(1)}, s32[96]{0:T(128)}, u32[]{:S(2)}) copy-start(s32[96]{0:T(128)} %param.12) | copy-start | bytes 1156
  70.9 59.2 %copy-start.3 = (f32[1,2,64,512]{3,2,1,0:T(8,128)S(1)}, f32[1,2,64,512]{3,2,1,0:T(8,128)}, u32[]{:S(2)}) copy-start(f32[1,2,64,512]{3,2,1,0:T(8,128)} %param.17) | copy-start | bytes 786436
  70.9 9.9 %collective-permute-start.9 = (bf16[128,768]{1,0:T(8,128)(2,1)S(1)}, bf16[128,768]{1,0:T(8,128)(2,1)S(1)}, u32[]{:S(2)}, u32[]{:S(2)}) collective-permute-start(bf16[128,768]{1,0:T(8,128)(2,1)S(1)} %fusion.2), channel_id=1, source_target_pairs={{0,64},{1,449},{32,96},{33,481},{64,128},{65,1},{96,160},{97,33},{... | collective-permute-start | bytes 589832 | tf_op jit(solution)/shard_map/ppermute | solution.py:376
  80.8 76.5 %copy-start.1 = (f32[1,2,64,512]{3,2,1,0:T(8,128)S(1)}, f32[1,2,64,512]{3,2,1,0:T(8,128)}, u32[]{:S(2)}) copy-start(f32[1,2,64,512]{3,2,1,0:T(8,128)} %param.13) | copy-start | bytes 786436
  80.9 76.5 %copy-start.2 = (f32[1,2,64,512]{3,2,1,0:T(8,128)S(1)}, f32[1,2,64,512]{3,2,1,0:T(8,128)}, u32[]{:S(2)}) copy-start(f32[1,2,64,512]{3,2,1,0:T(8,128)} %param.14) | copy-start | bytes 786436
  80.9 15.7 %collective-permute-start.12 = (bf16[128,768]{1,0:T(8,128)(2,1)S(1)}, bf16[128,768]{1,0:T(8,128)(2,1)S(1)}, u32[]{:S(2)}, u32[]{:S(2)}) collective-permute-start(bf16[128,768]{1,0:T(8,128)(2,1)S(1)} %pad_maximum_fusion.2), channel_id=1, source_target_pairs={{0,128},{1,385},{32,160},{33,417},{64,192},{65,449},{96,224},{97,4... | collective-permute-start | bytes 589832 | tf_op jit(solution)/shard_map/ppermute | solution.py:376
  110.3 19.9 %all-to-all-start = ((bf16[16,16,512]{2,1,0:T(8,128)(2,1)}), bf16[16,16,512]{2,1,0:T(8,128)(2,1)S(1)}, u32[]{:S(2)}, u32[]{:S(2)}) async-start(bf16[16,16,512]{2,1,0:T(8,128)(2,1)} %bitcast.7), calls=%async_computation | async-start | bytes 524288 | tf_op jit(solution)/shard_map/all_to_all | solution.py:394
  117.4 38.5 %collective-permute-start.14 = (bf16[4,2,2,64,512]{4,3,2,1,0:T(8,128)(2,1)S(1)}, bf16[4,2,2,64,512]{4,3,2,1,0:T(8,128)(2,1)S(1)}, u32[]{:S(2)}, u32[]{:S(2)}) collective-permute-start(bf16[4,2,2,64,512]{4,3,2,1,0:T(8,128)(2,1)S(1)} %pad_maximum_fusion.rm_ref), channel_id=1, source_target_pairs={{0,1},{1,0},{2,3},{3,2},{4,5},{5,4},{6,7},{7,6},{8,9},{9,8},{10,11... | collective-permute-start | bytes 3145736 | tf_op jit(solution)/shard_map/ppermute | solution.py:369
  142.8 14.6 %collective-permute-start.13 = (bf16[4,144,512]{2,1,0:T(8,128)(2,1)S(1)}, bf16[4,144,512]{2,1,0:T(8,128)(2,1)}, u32[]{:S(2)}, u32[]{:S(2)}) collective-permute-start(bf16[4,144,512]{2,1,0:T(8,128)(2,1)S(1)} %bitcast.44), channel_id=1, source_target_pairs={{0,1},{1,0},{2,3},{3,2},{4,5},{5,4},{6,7},{7,6},{8,9},{9,8},{10,11... | collective-permute-start | bytes 1769480 | tf_op jit(solution)/shard_map/ppermute | solution.py:402

commit v12 on v11

--- a/solution.py
+++ b/solution.py
@@ -371,24 +371,20 @@
     sent = [partial_products(own, arrived, swapped, True, chunk) for chunk in range(CHUNKS)]
     kept = [partial_products(own, arrived, swapped, False, chunk) for chunk in range(CHUNKS)]
 
-    def along(out, step):
-        goals = [((i + (1 - 2 * k) * step) % NZ) * NC + k for i in range(NZ) for k in range(NC)]
-        return lax.ppermute(out, ("z", "c"), list(enumerate(goals)))
-
-    lasts, sums = [], []
+    sums = []
     for out, keep in zip(sent, kept):
-        first = along(out, 1)
-        part = first.shape[0] // 2
-        second = along((keep[part:] + first[part:]).astype(HALF), 2)
-        half = part // 2
-        lasts.append((keep[half:part] + first[half:part] + second[half:]).astype(HALF))
-        sums.append((keep[:half], first[:half], second[:half]))
-    third = along(jnp.concatenate(lasts, axis=0), 4)
-    sums = [
-        (a + b + d + third[k * half : (k + 1) * half]).astype(HALF) for k, (a, b, d) in enumerate(sums)
-    ]
-    sums = jnp.concatenate(sums, axis=0)
-    sums = lax.all_gather(sums, "x", axis=0, tiled=False)
+        got = []
+        for step in (1, 2, 4):
+            goals = [((i + (1 - 2 * k) * step) % NZ) * NC + k for i in range(NZ) for k in range(NC)]
+            got.append(lax.ppermute(out, ("z", "c"), list(enumerate(goals))))
+            part = got[-1].shape[0] // (2 if step < 4 else 1)
+            rows_from = slice(part, 2 * part) if step < 4 else slice(0, part)
+            total = keep[rows_from]
+            for rows_in in got:
+                total = total + rows_in[rows_from]
+            out = total.astype(HALF)
+        sums.append(out)
+    sums = lax.all_gather(jnp.concatenate(sums, axis=0), "x", axis=0, tiled=False)
 
     picked = pick_blocks(chosen, sums, block_size).reshape(NZ, out_rows // NZ, block_size)
     arrived = lax.all_to_all(picked, "z", 0, 0, tiled=True).reshape(out_rows, block_size)

time: 163 us -> 155 us (0.951)
  waiting for transfers between devices: 31.2 us -> 20.7 us
  starting transfers between devices: 89.4 us -> 93 us
    ppermute x5 -> x6, waiting for transfers between devices: 17.8 us -> 6.8 us  [body(): got.append(lax.ppermute(out, ('z', 'c'), list(enumerate(goals))))]
    ppermute x5 -> x6, starting transfers between devices: 26.4 us -> 33.2 us  [body(): got.append(lax.ppermute(out, ('z', 'c'), list(enumerate(goals))))]
    ppermute x3, starting transfers between devices: 16.5 us -> 9.9 us  [body(): swapped = [lax.ppermute(piece, 'c', ring(NC, 1)) for piece in arrived]]
    ppermute x3, waiting for transfers between devices: 0.01 us -> 2.64 us  [body(): lax.ppermute(piece, 'x', ring(NX, step))]
    ppermute x1, starting transfers between devices: 6.82 us -> 9 us  [body(): roots_other = lax.ppermute(roots, 'c', ring(NC, 1))]
    all_to_all x1, waiting for transfers between devices: 5.74 us -> 3.64 us  [body(): lax.all_to_all(picked, 'z', 0, 0, tiled=True).reshape(out_rows, block_size)]
  transfers between devices with their start and end apart: 16 -> 17, of which waited for: 9 -> 8; matrix products, arithmetic and copies ran while one was open for 1% -> 1% of each run, Pallas kernels for 3% -> 4%
where the time goes in v12:
time: 155 us; the launch traced here: 154 us
  starting transfers between devices  93 us (60%)
  blocking collectives  21.8 us (14%)
  waiting for transfers between devices  20.7 us (13%)
  Pallas kernels  15.7 us (10%)
    ppermute x6, starting transfers between devices, body(): got.append(lax.ppermute(out, ('z', 'c'), list(enumerate(goals))))  33.2 us
    ppermute x1, starting transfers between devices, body(): rows_other = lax.ppermute(rows_mine, 'c', ring(NC, 1))  12.8 us
    all_gather x1, blocking collectives, body(): lax.all_gather(jnp.concatenate(sums, axis=0), 'x', axis=0, tiled=False)  11 us
    ppermute x3, starting transfers between devices, body(): lax.ppermute(piece, 'x', ring(NX, step))  10.9 us
    all_gather x1, blocking collectives, body(): rows_mine = lax.all_gather(own_rows, 'y', axis=0, tiled=False)  10.8 us
    ppermute x3, starting transfers between devices, body(): swapped = [lax.ppermute(piece, 'c', ring(NC, 1)) for piece in arrived]  9.9 us
    ppermute x1, starting transfers between devices, body(): roots_other = lax.ppermute(roots, 'c', ring(NC, 1))  9 us
    ppermute x2, starting transfers between devices, body(): came = lax.ppermute(roots, 'y', [(i, i ^ step) for i in range(ny)])  8.92 us
  transfers between devices with their start and end apart: 17, of which 8 were waited for; matrix products, arithmetic and copies ran while one was open for 1% of the time, Pallas kernels for 4%

profile of v12, /device:TPU:1, one launch (start us, length us, event | category | flops | bytes accessed | tf_op | source)
XLA Modules:
  0.0 154.0 jit_solution(1248826745445082521)
XLA Ops:
  0.7 3.3 %shard_map.120 = (bf16[1280,256]{1,0:T(8,128)(2,1)}, bf16[1280,256]{1,0:T(8,128)(2,1)}, bf16[1280,256]{1,0:T(8,128)(2,1)}) custom-call(s32[1]{0:T(128)} %bitcast.3.place_ref, bf16[8,64,256]{2,1,0:T(8,128)(2,1)} %a_ref.1, bf16[256,6144]{1,0:T(8,128)(2,1)} %b_ref.3), custom_call_target="tpu_custom_call" | custom-call | tf_op jit(solution)/shard_map/pallas_call | solution.py:97
  3.9 0.0 copy-start.5
  4.0 5.6 %collective-permute-start.2 = (bf16[1280,256]{1,0:T(8,128)(2,1)}, bf16[1280,256]{1,0:T(8,128)(2,1)S(1)}, u32[]{:S(2)}, u32[]{:S(2)}) collective-permute-start(bf16[1280,256]{1,0:T(8,128)(2,1)} %get-tuple-element.25.p_ref), channel_id=1, source_target_pairs={{0,16},{8,24},{16,0},{24,8},{1,17},{9,25},{17,1},{25,9},{2,18},{10... | collective-permute-start | bytes 1966088 | tf_op jit(solution)/shard_map/ppermute | solution.py:347
  9.6 2.8 %collective-permute-start.3 = (bf16[1280,256]{1,0:T(8,128)(2,1)}, bf16[1280,256]{1,0:T(8,128)(2,1)S(1)}, u32[]{:S(2)}, u32[]{:S(2)}) collective-permute-start(bf16[1280,256]{1,0:T(8,128)(2,1)} %get-tuple-element.30), channel_id=1, source_target_pairs={{0,24},{8,0},{16,8},{24,16},{1,25},{9,1},{17,9},{25,17},{2,26},{10... | collective-permute-start | bytes 1966088 | tf_op jit(solution)/shard_map/ppermute | solution.py:347
  12.4 2.5 %collective-permute-start.4 = (bf16[1280,256]{1,0:T(8,128)(2,1)}, bf16[1280,256]{1,0:T(8,128)(2,1)S(1)}, u32[]{:S(2)}, u32[]{:S(2)}) collective-permute-start(bf16[1280,256]{1,0:T(8,128)(2,1)} %get-tuple-element.31), channel_id=1, source_target_pairs={{0,8},{8,16},{16,24},{24,0},{1,9},{9,17},{17,25},{25,1},{2,10},{10... | collective-permute-start | bytes 1966088 | tf_op jit(solution)/shard_map/ppermute | solution.py:347
  14.9 0.2 select_reduce_fusion
  15.1 0.1 reshape.114
  15.2 0.1 copy.19
  15.4 0.1 select_n.49
  15.5 0.1 fusion.p_ref
  15.6 2.3 %shard_map.121.refs_0_.refs_4_ = bf16[2048,256]{1,0:T(8,128)(2,1)} custom-call(s32[1]{0:T(128)} %bitcast.3.place_ref, bf16[1280,256]{1,0:T(8,128)(2,1)} %get-tuple-element.25.p_ref, bf16[256,6144]{1,0:T(8,128)(2,1)} %b_ref.3), custom_call_target="tpu_custom_call" | custom-call | tf_op jit(solution)/shard_map/pallas_call | solution.py:134
  17.9 3.3 %collective-permute-start = (bf16[1,2,2,64,512]{4,3,2,1,0:T(8,128)(2,1)S(1)}, bf16[1,2,2,64,512]{4,3,2,1,0:T(8,128)(2,1)S(1)}, u32[]{:S(2)}, u32[]{:S(2)}) collective-permute-start(bf16[1,2,2,64,512]{4,3,2,1,0:T(8,128)(2,1)S(1)} %maximum_bitcast_fusion), channel_id=1, source_target_pairs={{0,2},{2,0},{4,6},{6,4},{1,3},{3,1},{5,7},{7,5},{8,10},{10,8},{12,... | collective-permute-start | bytes 786440 | tf_op jit(solution)/shard_map/ppermute | solution.py:365
  21.3 4.2 %collective-permute-done = bf16[1,2,2,64,512]{4,3,2,1,0:T(8,128)(2,1)S(1)} collective-permute-done((bf16[1,2,2,64,512]{4,3,2,1,0:T(8,128)(2,1)S(1)}, bf16[1,2,2,64,512]{4,3,2,1,0:T(8,128)(2,1)S(1)}, u32[]{:S(2)}, u32[]{:S(2)}) %collective-permute-start) | collective-permute-done | bytes 262176 | tf_op jit(solution)/shard_map/ppermute | solution.py:365
  25.5 0.1 pad_maximum_fusion.1
  25.5 5.6 %collective-permute-start.1 = (bf16[2,2,2,64,512]{4,3,2,1,0:T(8,128)(2,1)S(1)}, bf16[2,2,2,64,512]{4,3,2,1,0:T(8,128)(2,1)S(1)}, u32[]{:S(2)}, u32[]{:S(2)}) collective-permute-start(bf16[2,2,2,64,512]{4,3,2,1,0:T(8,128)(2,1)S(1)} %pad_maximum_fusion.1), channel_id=1, source_target_pairs={{0,4},{2,6},{4,0},{6,2},{1,5},{3,7},{5,1},{7,3},{8,12},{10,14},{12... | collective-permute-start | bytes 1572872 | tf_op jit(solution)/shard_map/ppermute | solution.py:365
  31.1 4.6 %collective-permute-start.5 = (bf16[1280,256]{1,0:T(8,128)(2,1)S(1)}, bf16[1280,256]{1,0:T(8,128)(2,1)S(1)}, u32[]{:S(2)}, u32[]{:S(2)}) collective-permute-start(bf16[1280,256]{1,0:T(8,128)(2,1)S(1)} %collective-permute-done.2.refs_1_.refs_5_), channel_id=1, source_target_pairs={{0,1},{1,0},{2,3},{3,2},{4,5},{5,4},{6,7},{7,6},{8,9},{9,8},{10,11... | collective-permute-start | bytes 1966088 | tf_op jit(solution)/shard_map/ppermute | solution.py:368
  35.8 2.6 %collective-permute-done.3.refs_2_.refs_6_ = bf16[1280,256]{1,0:T(8,128)(2,1)S(1)} collective-permute-done((bf16[1280,256]{1,0:T(8,128)(2,1)}, bf16[1280,256]{1,0:T(8,128)(2,1)S(1)}, u32[]{:S(2)}, u32[]{:S(2)}) %collective-permute-start.3) | collective-permute-done | bytes 655392 | tf_op jit(solution)/shard_map/ppermute | solution.py:347
  38.4 3.3 %collective-permute-start.6 = (bf16[1280,256]{1,0:T(8,128)(2,1)S(1)}, bf16[1280,256]{1,0:T(8,128)(2,1)S(1)}, u32[]{:S(2)}, u32[]{:S(2)}) collective-permute-start(bf16[1280,256]{1,0:T(8,128)(2,1)S(1)} %collective-permute-done.3.refs_2_.refs_6_), channel_id=1, source_target_pairs={{0,1},{1,0},{2,3},{3,2},{4,5},{5,4},{6,7},{7,6},{8,9},{9,8},{10,11... | collective-permute-start | bytes 1966088 | tf_op jit(solution)/shard_map/ppermute | solution.py:368
  41.8 1.9 %collective-permute-start.7 = (bf16[1280,256]{1,0:T(8,128)(2,1)S(1)}, bf16[1280,256]{1,0:T(8,128)(2,1)S(1)}, u32[]{:S(2)}, u32[]{:S(2)}) collective-permute-start(bf16[1280,256]{1,0:T(8,128)(2,1)S(1)} %collective-permute-done.4.refs_3_.refs_7_), channel_id=1, source_target_pairs={{0,1},{1,0},{2,3},{3,2},{4,5},{5,4},{6,7},{7,6},{8,9},{9,8},{10,11... | collective-permute-start | bytes 1966088 | tf_op jit(solution)/shard_map/ppermute | solution.py:368
  43.7 0.1 pad_maximum_fusion.rm_ref
  43.8 1.9 %collective-permute-done.7.refs_10_ = bf16[1280,256]{1,0:T(8,128)(2,1)S(1)} collective-permute-done((bf16[1280,256]{1,0:T(8,128)(2,1)S(1)}, bf16[1280,256]{1,0:T(8,128)(2,1)S(1)}, u32[]{:S(2)}, u32[]{:S(2)}) %collective-permute-start.7) | collective-permute-done | bytes 655392 | tf_op jit(solution)/shard_map/ppermute | solution.py:368
  45.8 0.6 shard_map.125
  46.3 11.1 %collective-permute-start.11 = (bf16[256,768]{1,0:T(8,128)(2,1)S(1)}, bf16[256,768]{1,0:T(8,128)(2,1)S(1)}, u32[]{:S(2)}, u32[]{:S(2)}) collective-permute-start(bf16[256,768]{1,0:T(8,128)(2,1)S(1)} %shard_map.125), channel_id=1, source_target_pairs={{0,32},{1,481},{32,64},{33,1},{64,96},{65,33},{96,128},{97,65},{12... | collective-permute-start | bytes 1179656 | tf_op jit(solution)/shard_map/ppermute | solution.py:379
  57.5 0.6 shard_map.123
  58.1 2.6 %collective-permute-start.8 = (bf16[256,768]{1,0:T(8,128)(2,1)S(1)}, bf16[256,768]{1,0:T(8,128)(2,1)S(1)}, u32[]{:S(2)}, u32[]{:S(2)}) collective-permute-start(bf16[256,768]{1,0:T(8,128)(2,1)S(1)} %shard_map.123), channel_id=1, source_target_pairs={{0,32},{1,481},{32,64},{33,1},{64,96},{65,33},{96,128},{97,65},{12... | collective-permute-start | bytes 1179656 | tf_op jit(solution)/shard_map/ppermute | solution.py:379
  60.7 0.6 shard_map.124
  61.3 0.6 shard_map.122
  61.9 0.3 collective-permute-done.11
  62.2 4.7 %collective-permute-start.12 = (bf16[128,768]{1,0:T(8,128)(2,1)S(1)}, bf16[128,768]{1,0:T(8,128)(2,1)S(1)}, u32[]{:S(2)}, u32[]{:S(2)}) collective-permute-start(bf16[128,768]{1,0:T(8,128)(2,1)S(1)} %fusion.1), channel_id=1, source_target_pairs={{0,64},{1,449},{32,96},{33,481},{64,128},{65,1},{96,160},{97,33},{... | collective-permute-start | bytes 589832 | tf_op jit(solution)/shard_map/ppermute | solution.py:379
  67.0 4.0 %collective-permute-start.9 = (bf16[128,768]{1,0:T(8,128)(2,1)S(1)}, bf16[128,768]{1,0:T(8,128)(2,1)S(1)}, u32[]{:S(2)}, u32[]{:S(2)}) collective-permute-start(bf16[128,768]{1,0:T(8,128)(2,1)S(1)} %fusion.2), channel_id=1, source_target_pairs={{0,64},{1,449},{32,96},{33,481},{64,128},{65,1},{96,160},{97,33},{... | collective-permute-start | bytes 589832 | tf_op jit(solution)/shard_map/ppermute | solution.py:379
  71.0 1.1 collective-permute-done.12
  72.2 5.6 %collective-permute-start.13 = (bf16[64,768]{1,0:T(8,128)(2,1)S(1)}, bf16[64,768]{1,0:T(8,128)(2,1)S(1)}, u32[]{:S(2)}, u32[]{:S(2)}) collective-permute-start(bf16[64,768]{1,0:T(8,128)(2,1)S(1)} %fusion.4), channel_id=1, source_target_pairs={{0,128},{1,385},{32,160},{33,417},{64,192},{65,449},{96,224},{97,4... | collective-permute-start | bytes 294920 | tf_op jit(solution)/shard_map/ppermute | solution.py:379
  77.8 5.2 %collective-permute-start.10 = (bf16[64,768]{1,0:T(8,128)(2,1)S(1)}, bf16[64,768]{1,0:T(8,128)(2,1)S(1)}, u32[]{:S(2)}, u32[]{:S(2)}) collective-permute-start(bf16[64,768]{1,0:T(8,128)(2,1)S(1)} %fusion.9), channel_id=1, source_target_pairs={{0,128},{1,385},{32,160},{33,417},{64,192},{65,449},{96,224},{97,4... | collective-permute-start | bytes 294920 | tf_op jit(solution)/shard_map/ppermute | solution.py:379
  83.0 0.1 fusion.7
  83.1 5.4 %collective-permute-done.10 = bf16[64,768]{1,0:T(8,128)(2,1)S(1)} collective-permute-done((bf16[64,768]{1,0:T(8,128)(2,1)S(1)}, bf16[64,768]{1,0:T(8,128)(2,1)S(1)}, u32[]{:S(2)}, u32[]{:S(2)}) %collective-permute-start.10) | collective-permute-done | bytes 98336 | tf_op jit(solution)/shard_map/ppermute | solution.py:379
  88.5 11.0 %all-gather = bf16[512,768]{1,0:T(8,128)(2,1)S(1)} all-gather(bf16[128,768]{1,0:T(8,128)(2,1)S(1)} %pad_maximum_fusion.2), channel_id=2, replica_groups=mesh['z'=16,'x'=4,'y'=4,'c'=2] {'x'}, dimensions={0}, use_global_device_ids=true | all-gather | bytes 983040 | tf_op jit(solution)/shard_map/all_gather | solution.py:387
  99.5 1.3 shard_map.126
  100.8 8.4 %all-to-all-start = ((bf16[16,16,512]{2,1,0:T(8,128)(2,1)}), bf16[16,16,512]{2,1,0:T(8,128)(2,1)S(1)}, u32[]{:S(2)}, u32[]{:S(2)}) async-start(bf16[16,16,512]{2,1,0:T(8,128)(2,1)} %bitcast.7), calls=%async_computation | async-start | bytes 524288 | tf_op jit(solution)/shard_map/all_to_all | solution.py:390
  109.2 9.0 %collective-permute-start.15 = (bf16[4,2,2,64,512]{4,3,2,1,0:T(8,128)(2,1)S(1)}, bf16[4,2,2,64,512]{4,3,2,1,0:T(8,128)(2,1)S(1)}, u32[]{:S(2)}, u32[]{:S(2)}) collective-permute-start(bf16[4,2,2,64,512]{4,3,2,1,0:T(8,128)(2,1)S(1)} %pad_maximum_fusion.rm_ref), channel_id=1, source_target_pairs={{0,1},{1,0},{2,3},{3,2},{4,5},{5,4},{6,7},{7,6},{8,9},{9,8},{10,11... | collective-permute-start | bytes 3145736 | tf_op jit(solution)/shard_map/ppermute | solution.py:369
  118.2 0.2 fusion.21
  118.4 3.6 %all-to-all-done = bf16[16,16,512]{2,1,0:T(8,128)(2,1)S(1)} async-done(((bf16[16,16,512]{2,1,0:T(8,128)(2,1)}), bf16[16,16,512]{2,1,0:T(8,128)(2,1)S(1)}, u32[]{:S(2)}, u32[]{:S(2)}) %all-to-all-start) | async-done | bytes 262176 | tf_op jit(solution)/shard_map/all_to_all | solution.py:390
  122.0 1.5 shard_map.127
  123.6 10.8 %all-gather.1 = bf16[576,512]{1,0:T(8,128)(2,1)S(1)} all-gather(bf16[144,512]{1,0:T(8,128)(2,1)S(1)} %get-tuple-element.32), channel_id=3, replica_groups=mesh['z'=16,'x'=4,'y'=4,'c'=2] {'y'}, dimensions={0}, use_global_device_ids=true | all-gather | bytes 737280 | tf_op jit(solution)/shard_map/all_gather | solution.py:397
  134.4 12.8 %collective-permute-start.14 = (bf16[4,144,512]{2,1,0:T(8,128)(2,1)S(1)}, bf16[4,144,512]{2,1,0:T(8,128)(2,1)}, u32[]{:S(2)}, u32[]{:S(2)}) collective-permute-start(bf16[4,144,512]{2,1,0:T(8,128)(2,1)S(1)} %bitcast.44), channel_id=1, source_target_pairs={{0,1},{1,0},{2,3},{3,2},{4,5},{5,4},{6,7},{7,6},{8,9},{9,8},{10,11... | collective-permute-start | bytes 1769480 | tf_op jit(solution)/shard_map/ppermute | solution.py:398
  147.2 0.2 compare_reduce_fusion
  147.4 0.1 concatenate.13.f_ref
  147.4 1.5 collective-permute-done.14.o_ref
  148.9 5.1 %shard_map.128 = (f32[2,64,512]{2,1,0:T(8,128)}, f32[2,64,512]{2,1,0:T(8,128)}, bf16[2,512,512]{2,1,0:T(8,128)(2,1)}) custom-call(s32[7]{0:T(128)S(1)} %concatenate.13.f_ref, bf16[4,144,512]{2,1,0:T(8,128)(2,1)S(1)} %bitcast.45, bf16[4,144,512]{2,1,0:T(8,128)(2,1)} %collective-permute-done.14.o_ref, bf16[4,2,2,64,512]{4,3,2,1,0:T(8,128)(2,1)S(1)} %pad_maximum_fusion.rm_ref, ...), custom_call_target="tpu_custom_call" | custom-call | tf_op jit(solution)/shard_map/pallas_call | solution.py:305
  (40 shorter events, 0.4 us)
Async XLA Ops:
  0.6 14.3 %copy-start.7 = (s32[96]{0:T(128)S(1)}, s32[96]{0:T(128)}, u32[]{:S(2)}) copy-start(s32[96]{0:T(128)} %param.11) | copy-start | bytes 1156
  3.9 13.9 %copy-start.4 = (bf16[1,2,64,512]{3,2,1,0:T(8,128)(2,1)S(1)}, bf16[1,2,64,512]{3,2,1,0:T(8,128)(2,1)}, u32[]{:S(2)}) copy-start(bf16[1,2,64,512]{3,2,1,0:T(8,128)(2,1)} %param.16) | copy-start | bytes 393220
  3.9 13.9 %copy-start.5 = (bf16[1,2,64,512]{3,2,1,0:T(8,128)(2,1)S(1)}, bf16[1,2,64,512]{3,2,1,0:T(8,128)(2,1)}, u32[]{:S(2)}) copy-start(bf16[1,2,64,512]{3,2,1,0:T(8,128)(2,1)} %param.15) | copy-start | bytes 393220
  4.0 27.2 %collective-permute-start.2 = (bf16[1280,256]{1,0:T(8,128)(2,1)}, bf16[1280,256]{1,0:T(8,128)(2,1)S(1)}, u32[]{:S(2)}, u32[]{:S(2)}) collective-permute-start(bf16[1280,256]{1,0:T(8,128)(2,1)} %get-tuple-element.25.p_ref), channel_id=1, source_target_pairs={{0,16},{8,24},{16,0},{24,8},{1,17},{9,25},{17,1},{25,9},{2,18},{10... | collective-permute-start | bytes 1966088 | tf_op jit(solution)/shard_map/ppermute | solution.py:347
  9.6 28.8 %collective-permute-start.3 = (bf16[1280,256]{1,0:T(8,128)(2,1)}, bf16[1280,256]{1,0:T(8,128)(2,1)S(1)}, u32[]{:S(2)}, u32[]{:S(2)}) collective-permute-start(bf16[1280,256]{1,0:T(8,128)(2,1)} %get-tuple-element.30), channel_id=1, source_target_pairs={{0,24},{8,0},{16,8},{24,16},{1,25},{9,1},{17,9},{25,17},{2,26},{10... | collective-permute-start | bytes 1966088 | tf_op jit(solution)/shard_map/ppermute | solution.py:347
  12.4 29.4 %collective-permute-start.4 = (bf16[1280,256]{1,0:T(8,128)(2,1)}, bf16[1280,256]{1,0:T(8,128)(2,1)S(1)}, u32[]{:S(2)}, u32[]{:S(2)}) collective-permute-start(bf16[1280,256]{1,0:T(8,128)(2,1)} %get-tuple-element.31), channel_id=1, source_target_pairs={{0,8},{8,16},{16,24},{24,0},{1,9},{9,17},{17,25},{25,1},{2,10},{10... | collective-permute-start | bytes 1966088 | tf_op jit(solution)/shard_map/ppermute | solution.py:347
  17.9 27.9 %copy-start = (bf16[2048,256]{1,0:T(8,128)(2,1)S(1)}, bf16[2048,256]{1,0:T(8,128)(2,1)}, u32[]{:S(2)}) copy-start(bf16[2048,256]{1,0:T(8,128)(2,1)} %shard_map.121.refs_0_.refs_4_) | copy-start | bytes 3145732
  17.9 7.5 %collective-permute-start = (bf16[1,2,2,64,512]{4,3,2,1,0:T(8,128)(2,1)S(1)}, bf16[1,2,2,64,512]{4,3,2,1,0:T(8,128)(2,1)S(1)}, u32[]{:S(2)}, u32[]{:S(2)}) collective-permute-start(bf16[1,2,2,64,512]{4,3,2,1,0:T(8,128)(2,1)S(1)} %maximum_bitcast_fusion), channel_id=1, source_target_pairs={{0,2},{2,0},{4,6},{6,4},{1,3},{3,1},{5,7},{7,5},{8,10},{10,8},{12,... | collective-permute-start | bytes 786440 | tf_op jit(solution)/shard_map/ppermute | solution.py:365
  25.5 18.2 %collective-permute-start.1 = (bf16[2,2,2,64,512]{4,3,2,1,0:T(8,128)(2,1)S(1)}, bf16[2,2,2,64,512]{4,3,2,1,0:T(8,128)(2,1)S(1)}, u32[]{:S(2)}, u32[]{:S(2)}) collective-permute-start(bf16[2,2,2,64,512]{4,3,2,1,0:T(8,128)(2,1)S(1)} %pad_maximum_fusion.1), channel_id=1, source_target_pairs={{0,4},{2,6},{4,0},{6,2},{1,5},{3,7},{5,1},{7,3},{8,12},{10,14},{12... | collective-permute-start | bytes 1572872 | tf_op jit(solution)/shard_map/ppermute | solution.py:365
  31.1 12.7 %collective-permute-start.5 = (bf16[1280,256]{1,0:T(8,128)(2,1)S(1)}, bf16[1280,256]{1,0:T(8,128)(2,1)S(1)}, u32[]{:S(2)}, u32[]{:S(2)}) collective-permute-start(bf16[1280,256]{1,0:T(8,128)(2,1)S(1)} %collective-permute-done.2.refs_1_.refs_5_), channel_id=1, source_target_pairs={{0,1},{1,0},{2,3},{3,2},{4,5},{5,4},{6,7},{7,6},{8,9},{9,8},{10,11... | collective-permute-start | bytes 1966088 | tf_op jit(solution)/shard_map/ppermute | solution.py:368
  38.4 5.4 %collective-permute-start.6 = (bf16[1280,256]{1,0:T(8,128)(2,1)S(1)}, bf16[1280,256]{1,0:T(8,128)(2,1)S(1)}, u32[]{:S(2)}, u32[]{:S(2)}) collective-permute-start(bf16[1280,256]{1,0:T(8,128)(2,1)S(1)} %collective-permute-done.3.refs_2_.refs_6_), channel_id=1, source_target_pairs={{0,1},{1,0},{2,3},{3,2},{4,5},{5,4},{6,7},{7,6},{8,9},{9,8},{10,11... | collective-permute-start | bytes 1966088 | tf_op jit(solution)/shard_map/ppermute | solution.py:368
  41.8 4.0 %collective-permute-start.7 = (bf16[1280,256]{1,0:T(8,128)(2,1)S(1)}, bf16[1280,256]{1,0:T(8,128)(2,1)S(1)}, u32[]{:S(2)}, u32[]{:S(2)}) collective-permute-start(bf16[1280,256]{1,0:T(8,128)(2,1)S(1)} %collective-permute-done.4.refs_3_.refs_7_), channel_id=1, source_target_pairs={{0,1},{1,0},{2,3},{3,2},{4,5},{5,4},{6,7},{7,6},{8,9},{9,8},{10,11... | collective-permute-start | bytes 1966088 | tf_op jit(solution)/shard_map/ppermute | solution.py:368
  46.3 15.8 %collective-permute-start.11 = (bf16[256,768]{1,0:T(8,128)(2,1)S(1)}, bf16[256,768]{1,0:T(8,128)(2,1)S(1)}, u32[]{:S(2)}, u32[]{:S(2)}) collective-permute-start(bf16[256,768]{1,0:T(8,128)(2,1)S(1)} %shard_map.125), channel_id=1, source_target_pairs={{0,32},{1,481},{32,64},{33,1},{64,96},{65,33},{96,128},{97,65},{12... | collective-permute-start | bytes 1179656 | tf_op jit(solution)/shard_map/ppermute | solution.py:379
  58.1 8.9 %collective-permute-start.8 = (bf16[256,768]{1,0:T(8,128)(2,1)S(1)}, bf16[256,768]{1,0:T(8,128)(2,1)S(1)}, u32[]{:S(2)}, u32[]{:S(2)}) collective-permute-start(bf16[256,768]{1,0:T(8,128)(2,1)S(1)} %shard_map.123), channel_id=1, source_target_pairs={{0,32},{1,481},{32,64},{33,1},{64,96},{65,33},{96,128},{97,65},{12... | collective-permute-start | bytes 1179656 | tf_op jit(solution)/shard_map/ppermute | solution.py:379
  62.2 56.0 %copy-start.6 = (s32[96]{0:T(128)S(1)}, s32[96]{0:T(128)}, u32[]{:S(2)}) copy-start(s32[96]{0:T(128)} %param.12) | copy-start | bytes 1156
  62.2 59.8 %copy-start.3 = (f32[1,2,64,512]{3,2,1,0:T(8,128)S(1)}, f32[1,2,64,512]{3,2,1,0:T(8,128)}, u32[]{:S(2)}) copy-start(f32[1,2,64,512]{3,2,1,0:T(8,128)} %param.17) | copy-start | bytes 786436
  62.2 9.9 %collective-permute-start.12 = (bf16[128,768]{1,0:T(8,128)(2,1)S(1)}, bf16[128,768]{1,0:T(8,128)(2,1)S(1)}, u32[]{:S(2)}, u32[]{:S(2)}) collective-permute-start(bf16[128,768]{1,0:T(8,128)(2,1)S(1)} %fusion.1), channel_id=1, source_target_pairs={{0,64},{1,449},{32,96},{33,481},{64,128},{65,1},{96,160},{97,33},{... | collective-permute-start | bytes 589832 | tf_op jit(solution)/shard_map/ppermute | solution.py:379
  67.0 10.8 %collective-permute-start.9 = (bf16[128,768]{1,0:T(8,128)(2,1)S(1)}, bf16[128,768]{1,0:T(8,128)(2,1)S(1)}, u32[]{:S(2)}, u32[]{:S(2)}) collective-permute-start(bf16[128,768]{1,0:T(8,128)(2,1)S(1)} %fusion.2), channel_id=1, source_target_pairs={{0,64},{1,449},{32,96},{33,481},{64,128},{65,1},{96,160},{97,33},{... | collective-permute-start | bytes 589832 | tf_op jit(solution)/shard_map/ppermute | solution.py:379
  72.2 76.7 %copy-start.1 = (f32[1,2,64,512]{3,2,1,0:T(8,128)S(1)}, f32[1,2,64,512]{3,2,1,0:T(8,128)}, u32[]{:S(2)}) copy-start(f32[1,2,64,512]{3,2,1,0:T(8,128)} %param.13) | copy-start | bytes 786436
  72.2 76.7 %copy-start.2 = (f32[1,2,64,512]{3,2,1,0:T(8,128)S(1)}, f32[1,2,64,512]{3,2,1,0:T(8,128)}, u32[]{:S(2)}) copy-start(f32[1,2,64,512]{3,2,1,0:T(8,128)} %param.14) | copy-start | bytes 786436
  72.2 10.8 %collective-permute-start.13 = (bf16[64,768]{1,0:T(8,128)(2,1)S(1)}, bf16[64,768]{1,0:T(8,128)(2,1)S(1)}, u32[]{:S(2)}, u32[]{:S(2)}) collective-permute-start(bf16[64,768]{1,0:T(8,128)(2,1)S(1)} %fusion.4), channel_id=1, source_target_pairs={{0,128},{1,385},{32,160},{33,417},{64,192},{65,449},{96,224},{97,4... | collective-permute-start | bytes 294920 | tf_op jit(solution)/shard_map/ppermute | solution.py:379
  77.8 10.6 %collective-permute-start.10 = (bf16[64,768]{1,0:T(8,128)(2,1)S(1)}, bf16[64,768]{1,0:T(8,128)(2,1)S(1)}, u32[]{:S(2)}, u32[]{:S(2)}) collective-permute-start(bf16[64,768]{1,0:T(8,128)(2,1)S(1)} %fusion.9), channel_id=1, source_target_pairs={{0,128},{1,385},{32,160},{33,417},{64,192},{65,449},{96,224},{97,4... | collective-permute-start | bytes 294920 | tf_op jit(solution)/shard_map/ppermute | solution.py:379
  100.8 21.2 %all-to-all-start = ((bf16[16,16,512]{2,1,0:T(8,128)(2,1)}), bf16[16,16,512]{2,1,0:T(8,128)(2,1)S(1)}, u32[]{:S(2)}, u32[]{:S(2)}) async-start(bf16[16,16,512]{2,1,0:T(8,128)(2,1)} %bitcast.7), calls=%async_computation | async-start | bytes 524288 | tf_op jit(solution)/shard_map/all_to_all | solution.py:390
  109.2 38.2 %collective-permute-start.15 = (bf16[4,2,2,64,512]{4,3,2,1,0:T(8,128)(2,1)S(1)}, bf16[4,2,2,64,512]{4,3,2,1,0:T(8,128)(2,1)S(1)}, u32[]{:S(2)}, u32[]{:S(2)}) collective-permute-start(bf16[4,2,2,64,512]{4,3,2,1,0:T(8,128)(2,1)S(1)} %pad_maximum_fusion.rm_ref), channel_id=1, source_target_pairs={{0,1},{1,0},{2,3},{3,2},{4,5},{5,4},{6,7},{7,6},{8,9},{9,8},{10,11... | collective-permute-start | bytes 3145736 | tf_op jit(solution)/shard_map/ppermute | solution.py:369
  134.4 14.5 %collective-permute-start.14 = (bf16[4,144,512]{2,1,0:T(8,128)(2,1)S(1)}, bf16[4,144,512]{2,1,0:T(8,128)(2,1)}, u32[]{:S(2)}, u32[]{:S(2)}) collective-permute-start(bf16[4,144,512]{2,1,0:T(8,128)(2,1)S(1)} %bitcast.44), channel_id=1, source_target_pairs={{0,1},{1,0},{2,3},{3,2},{4,5},{5,4},{6,7},{7,6},{8,9},{9,8},{10,11... | collective-permute-start | bytes 1769480 | tf_op jit(solution)/shard_map/ppermute | solution.py:398

commit v13 on v12

--- a/solution.py
+++ b/solution.py
@@ -363,8 +363,8 @@
     for step in (1, 2):
         if step < ny:
             came = lax.ppermute(roots, "y", [(i, i ^ step) for i in range(ny)])
+            own, came = lax.optimization_barrier((own, came)) if step == 2 else (own, came)
             roots = jnp.concatenate([roots, came], axis=0)
-    own, roots = lax.optimization_barrier((own, roots))
     swapped = [lax.ppermute(piece, "c", ring(NC, 1)) for piece in arrived]
     roots_other = lax.ppermute(roots, "c", ring(NC, 1))
 

time: 155 us -> 172 us (1.11)
  starting transfers between devices: 93 us -> 102 us
  waiting for transfers between devices: 20.7 us -> 26.4 us
  local copies, waits for them, and re-layouts: 0.45 us -> 2.61 us
    ppermute x3, starting transfers between devices: 9.9 us -> 18.3 us  [body(): swapped = [lax.ppermute(piece, 'c', ring(NC, 1)) for piece in arrived]]
    ppermute x2, waiting for transfers between devices: 4.2 us -> 11.6 us  [body(): came = lax.ppermute(roots, 'y', [(i, i ^ step) for i in range(ny)])]
    unnamed x16, local copies, waits for them, and re-layouts: 0.05 us -> 2.21 us
    ppermute x3, waiting for transfers between devices: 1.92 us -> 0.01 us  [body(): swapped = [lax.ppermute(piece, 'c', ring(NC, 1)) for piece in arrived]]
  transfers between devices with their start and end apart: 17 -> 17, of which waited for: 8 -> 8; matrix products, arithmetic and copies ran while one was open for 1% -> 1% of each run, Pallas kernels for 4% -> 3%
where the time goes in v13:
time: 172 us; the launch traced here: 171 us
  starting transfers between devices  102 us (59%)
  waiting for transfers between devices  26.4 us (15%)
  blocking collectives  22.8 us (13%)
  Pallas kernels  15.2 us (9%)
  local copies, waits for them, and re-layouts  2.61 us (2%)
    ppermute x6, starting transfers between devices, body(): got.append(lax.ppermute(out, ('z', 'c'), list(enumerate(goals))))  32.9 us
    ppermute x3, starting transfers between devices, body(): swapped = [lax.ppermute(piece, 'c', ring(NC, 1)) for piece in arrived]  18.3 us
    ppermute x1, starting transfers between devices, body(): rows_other = lax.ppermute(rows_mine, 'c', ring(NC, 1))  13 us
    all_gather x1, blocking collectives, body(): lax.all_gather(jnp.concatenate(sums, axis=0), 'x', axis=0, tiled=False)  11.7 us
    ppermute x2, waiting for transfers between devices, body(): came = lax.ppermute(roots, 'y', [(i, i ^ step) for i in range(ny)])  11.6 us
    all_gather x1, blocking collectives, body(): rows_mine = lax.all_gather(own_rows, 'y', axis=0, tiled=False)  11.1 us
    ppermute x3, starting transfers between devices, body(): lax.ppermute(piece, 'x', ring(NX, step))  10.9 us
    ppermute x1, starting transfers between devices, body(): roots_other = lax.ppermute(roots, 'c', ring(NC, 1))  9.59 us
  transfers between devices with their start and end apart: 17, of which 8 were waited for; matrix products, arithmetic and copies ran while one was open for 1% of the time, Pallas kernels for 3%

profile of v13, /device:TPU:1, one launch (start us, length us, event | category | flops | bytes accessed | tf_op | source)
XLA Modules:
  0.0 171.0 jit_solution(14422125272222155960)
XLA Ops:
  0.7 3.3 %shard_map.120 = (bf16[1280,256]{1,0:T(8,128)(2,1)}, bf16[1280,256]{1,0:T(8,128)(2,1)}, bf16[1280,256]{1,0:T(8,128)(2,1)}) custom-call(s32[1]{0:T(128)} %bitcast.3.place_ref, bf16[8,64,256]{2,1,0:T(8,128)(2,1)} %a_ref.1, bf16[256,6144]{1,0:T(8,128)(2,1)} %b_ref.3), custom_call_target="tpu_custom_call" | custom-call | tf_op jit(solution)/shard_map/pallas_call | solution.py:97
  4.0 5.6 %collective-permute-start.2 = (bf16[1280,256]{1,0:T(8,128)(2,1)}, bf16[1280,256]{1,0:T(8,128)(2,1)S(1)}, u32[]{:S(2)}, u32[]{:S(2)}) collective-permute-start(bf16[1280,256]{1,0:T(8,128)(2,1)} %get-tuple-element.25.p_ref), channel_id=1, source_target_pairs={{0,16},{8,24},{16,0},{24,8},{1,17},{9,25},{17,1},{25,9},{2,18},{10... | collective-permute-start | bytes 1966088 | tf_op jit(solution)/shard_map/ppermute | solution.py:347
  9.6 2.8 %collective-permute-start.3 = (bf16[1280,256]{1,0:T(8,128)(2,1)}, bf16[1280,256]{1,0:T(8,128)(2,1)S(1)}, u32[]{:S(2)}, u32[]{:S(2)}) collective-permute-start(bf16[1280,256]{1,0:T(8,128)(2,1)} %get-tuple-element.30), channel_id=1, source_target_pairs={{0,24},{8,0},{16,8},{24,16},{1,25},{9,1},{17,9},{25,17},{2,26},{10... | collective-permute-start | bytes 1966088 | tf_op jit(solution)/shard_map/ppermute | solution.py:347
  12.4 2.5 %collective-permute-start.4 = (bf16[1280,256]{1,0:T(8,128)(2,1)}, bf16[1280,256]{1,0:T(8,128)(2,1)S(1)}, u32[]{:S(2)}, u32[]{:S(2)}) collective-permute-start(bf16[1280,256]{1,0:T(8,128)(2,1)} %get-tuple-element.31), channel_id=1, source_target_pairs={{0,8},{8,16},{16,24},{24,0},{1,9},{9,17},{17,25},{25,1},{2,10},{10... | collective-permute-start | bytes 1966088 | tf_op jit(solution)/shard_map/ppermute | solution.py:347
  14.9 0.2 select_reduce_fusion
  15.1 0.1 reshape.114
  15.2 0.1 copy.19
  15.4 0.1 select_n.49
  15.5 0.1 fusion.p_ref
  15.6 2.3 %shard_map.121.refs_0_.refs_4_ = bf16[2048,256]{1,0:T(8,128)(2,1)} custom-call(s32[1]{0:T(128)} %bitcast.3.place_ref, bf16[1280,256]{1,0:T(8,128)(2,1)} %get-tuple-element.25.p_ref, bf16[256,6144]{1,0:T(8,128)(2,1)} %b_ref.3), custom_call_target="tpu_custom_call" | custom-call | tf_op jit(solution)/shard_map/pallas_call | solution.py:134
  17.9 3.2 %collective-permute-start = (bf16[1,2,2,64,512]{4,3,2,1,0:T(8,128)(2,1)S(1)}, bf16[1,2,2,64,512]{4,3,2,1,0:T(8,128)(2,1)S(1)}, u32[]{:S(2)}, u32[]{:S(2)}) collective-permute-start(bf16[1,2,2,64,512]{4,3,2,1,0:T(8,128)(2,1)S(1)} %maximum_bitcast_fusion), channel_id=1, source_target_pairs={{0,2},{2,0},{4,6},{6,4},{1,3},{3,1},{5,7},{7,5},{8,10},{10,8},{12,... | collective-permute-start | bytes 786440 | tf_op jit(solution)/shard_map/ppermute | solution.py:365
  21.1 13.0 %collective-permute-start.5 = (bf16[1280,256]{1,0:T(8,128)(2,1)S(1)}, bf16[1280,256]{1,0:T(8,128)(2,1)S(1)}, u32[]{:S(2)}, u32[]{:S(2)}) collective-permute-start(bf16[1280,256]{1,0:T(8,128)(2,1)S(1)} %collective-permute-done.2.refs_1_.refs_5_), channel_id=1, source_target_pairs={{0,1},{1,0},{2,3},{3,2},{4,5},{5,4},{6,7},{7,6},{8,9},{9,8},{10,11... | collective-permute-start | bytes 1966088 | tf_op jit(solution)/shard_map/ppermute | solution.py:368
  34.2 4.2 %collective-permute-done.3.refs_2_.refs_6_ = bf16[1280,256]{1,0:T(8,128)(2,1)S(1)} collective-permute-done((bf16[1280,256]{1,0:T(8,128)(2,1)}, bf16[1280,256]{1,0:T(8,128)(2,1)S(1)}, u32[]{:S(2)}, u32[]{:S(2)}) %collective-permute-start.3) | collective-permute-done | bytes 655392 | tf_op jit(solution)/shard_map/ppermute | solution.py:347
  38.4 3.3 %collective-permute-start.6 = (bf16[1280,256]{1,0:T(8,128)(2,1)S(1)}, bf16[1280,256]{1,0:T(8,128)(2,1)S(1)}, u32[]{:S(2)}, u32[]{:S(2)}) collective-permute-start(bf16[1280,256]{1,0:T(8,128)(2,1)S(1)} %collective-permute-done.3.refs_2_.refs_6_), channel_id=1, source_target_pairs={{0,1},{1,0},{2,3},{3,2},{4,5},{5,4},{6,7},{7,6},{8,9},{9,8},{10,11... | collective-permute-start | bytes 1966088 | tf_op jit(solution)/shard_map/ppermute | solution.py:368
  41.8 1.9 %collective-permute-start.7 = (bf16[1280,256]{1,0:T(8,128)(2,1)S(1)}, bf16[1280,256]{1,0:T(8,128)(2,1)S(1)}, u32[]{:S(2)}, u32[]{:S(2)}) collective-permute-start(bf16[1280,256]{1,0:T(8,128)(2,1)S(1)} %collective-permute-done.4.refs_3_.refs_7_), channel_id=1, source_target_pairs={{0,1},{1,0},{2,3},{3,2},{4,5},{5,4},{6,7},{7,6},{8,9},{9,8},{10,11... | collective-permute-start | bytes 1966088 | tf_op jit(solution)/shard_map/ppermute | solution.py:368
  43.7 0.1 pad_maximum_fusion.1
  43.8 4.8 %collective-permute-start.1 = (bf16[2,2,2,64,512]{4,3,2,1,0:T(8,128)(2,1)S(1)}, bf16[2,2,2,64,512]{4,3,2,1,0:T(8,128)(2,1)S(1)}, u32[]{:S(2)}, u32[]{:S(2)}) collective-permute-start(bf16[2,2,2,64,512]{4,3,2,1,0:T(8,128)(2,1)S(1)} %pad_maximum_fusion.1), channel_id=1, source_target_pairs={{0,4},{2,6},{4,0},{6,2},{1,5},{3,7},{5,1},{7,3},{8,12},{10,14},{12... | collective-permute-start | bytes 1572872 | tf_op jit(solution)/shard_map/ppermute | solution.py:365
  48.6 11.6 %collective-permute-done.1 = bf16[2,2,2,64,512]{4,3,2,1,0:T(8,128)(2,1)S(1)} collective-permute-done((bf16[2,2,2,64,512]{4,3,2,1,0:T(8,128)(2,1)S(1)}, bf16[2,2,2,64,512]{4,3,2,1,0:T(8,128)(2,1)S(1)}, u32[]{:S(2)}, u32[]{:S(2)}) %collective-permute-start.1) | collective-permute-done | bytes 524320 | tf_op jit(solution)/shard_map/ppermute | solution.py:365
  60.2 1.2 copy-done
  61.4 0.6 shard_map.125
  62.0 11.1 %collective-permute-start.11 = (bf16[256,768]{1,0:T(8,128)(2,1)S(1)}, bf16[256,768]{1,0:T(8,128)(2,1)S(1)}, u32[]{:S(2)}, u32[]{:S(2)}) collective-permute-start(bf16[256,768]{1,0:T(8,128)(2,1)S(1)} %shard_map.125), channel_id=1, source_target_pairs={{0,32},{1,481},{32,64},{33,1},{64,96},{65,33},{96,128},{97,65},{12... | collective-permute-start | bytes 1179656 | tf_op jit(solution)/shard_map/ppermute | solution.py:379
  73.1 0.6 shard_map.123
  73.7 2.6 %collective-permute-start.8 = (bf16[256,768]{1,0:T(8,128)(2,1)S(1)}, bf16[256,768]{1,0:T(8,128)(2,1)S(1)}, u32[]{:S(2)}, u32[]{:S(2)}) collective-permute-start(bf16[256,768]{1,0:T(8,128)(2,1)S(1)} %shard_map.123), channel_id=1, source_target_pairs={{0,32},{1,481},{32,64},{33,1},{64,96},{65,33},{96,128},{97,65},{12... | collective-permute-start | bytes 1179656 | tf_op jit(solution)/shard_map/ppermute | solution.py:379
  76.3 0.6 shard_map.124
  76.9 0.6 shard_map.122
  77.5 0.3 collective-permute-done.11
  77.8 4.6 %collective-permute-start.12 = (bf16[128,768]{1,0:T(8,128)(2,1)S(1)}, bf16[128,768]{1,0:T(8,128)(2,1)S(1)}, u32[]{:S(2)}, u32[]{:S(2)}) collective-permute-start(bf16[128,768]{1,0:T(8,128)(2,1)S(1)} %fusion.1), channel_id=1, source_target_pairs={{0,64},{1,449},{32,96},{33,481},{64,128},{65,1},{96,160},{97,33},{... | collective-permute-start | bytes 589832 | tf_op jit(solution)/shard_map/ppermute | solution.py:379
  82.4 0.1 collective-permute-done.8
  82.6 4.1 %collective-permute-start.9 = (bf16[128,768]{1,0:T(8,128)(2,1)S(1)}, bf16[128,768]{1,0:T(8,128)(2,1)S(1)}, u32[]{:S(2)}, u32[]{:S(2)}) collective-permute-start(bf16[128,768]{1,0:T(8,128)(2,1)S(1)} %fusion.2), channel_id=1, source_target_pairs={{0,64},{1,449},{32,96},{33,481},{64,128},{65,1},{96,160},{97,33},{... | collective-permute-start | bytes 589832 | tf_op jit(solution)/shard_map/ppermute | solution.py:379
  86.6 0.7 collective-permute-done.12
  87.4 5.4 %collective-permute-start.13 = (bf16[64,768]{1,0:T(8,128)(2,1)S(1)}, bf16[64,768]{1,0:T(8,128)(2,1)S(1)}, u32[]{:S(2)}, u32[]{:S(2)}) collective-permute-start(bf16[64,768]{1,0:T(8,128)(2,1)S(1)} %fusion.4), channel_id=1, source_target_pairs={{0,128},{1,385},{32,160},{33,417},{64,192},{65,449},{96,224},{97,4... | collective-permute-start | bytes 294920 | tf_op jit(solution)/shard_map/ppermute | solution.py:379
  92.8 5.2 %collective-permute-start.10 = (bf16[64,768]{1,0:T(8,128)(2,1)S(1)}, bf16[64,768]{1,0:T(8,128)(2,1)S(1)}, u32[]{:S(2)}, u32[]{:S(2)}) collective-permute-start(bf16[64,768]{1,0:T(8,128)(2,1)S(1)} %fusion.9), channel_id=1, source_target_pairs={{0,128},{1,385},{32,160},{33,417},{64,192},{65,449},{96,224},{97,4... | collective-permute-start | bytes 294920 | tf_op jit(solution)/shard_map/ppermute | solution.py:379
  98.1 5.3 %collective-permute-done.10 = bf16[64,768]{1,0:T(8,128)(2,1)S(1)} collective-permute-done((bf16[64,768]{1,0:T(8,128)(2,1)S(1)}, bf16[64,768]{1,0:T(8,128)(2,1)S(1)}, u32[]{:S(2)}, u32[]{:S(2)}) %collective-permute-start.10) | collective-permute-done | bytes 98336 | tf_op jit(solution)/shard_map/ppermute | solution.py:379
  103.5 11.7 %all-gather = bf16[512,768]{1,0:T(8,128)(2,1)S(1)} all-gather(bf16[128,768]{1,0:T(8,128)(2,1)S(1)} %pad_maximum_fusion.2), channel_id=2, replica_groups=mesh['z'=16,'x'=4,'y'=4,'c'=2] {'x'}, dimensions={0}, use_global_device_ids=true | all-gather | bytes 983040 | tf_op jit(solution)/shard_map/all_gather | solution.py:387
  115.2 1.3 shard_map.126
  116.5 9.0 %all-to-all-start = ((bf16[16,16,512]{2,1,0:T(8,128)(2,1)}), bf16[16,16,512]{2,1,0:T(8,128)(2,1)S(1)}, u32[]{:S(2)}, u32[]{:S(2)}) async-start(bf16[16,16,512]{2,1,0:T(8,128)(2,1)} %bitcast.7), calls=%async_computation | async-start | bytes 524288 | tf_op jit(solution)/shard_map/all_to_all | solution.py:390
  125.5 0.1 pad_maximum_fusion.rm_ref
  125.6 9.6 %collective-permute-start.15 = (bf16[4,2,2,64,512]{4,3,2,1,0:T(8,128)(2,1)S(1)}, bf16[4,2,2,64,512]{4,3,2,1,0:T(8,128)(2,1)S(1)}, u32[]{:S(2)}, u32[]{:S(2)}) collective-permute-start(bf16[4,2,2,64,512]{4,3,2,1,0:T(8,128)(2,1)S(1)} %pad_maximum_fusion.rm_ref), channel_id=1, source_target_pairs={{0,1},{1,0},{2,3},{3,2},{4,5},{5,4},{6,7},{7,6},{8,9},{9,8},{10,11... | collective-permute-start | bytes 3145736 | tf_op jit(solution)/shard_map/ppermute | solution.py:369
  135.3 0.2 fusion.21
  135.4 2.8 %all-to-all-done = bf16[16,16,512]{2,1,0:T(8,128)(2,1)S(1)} async-done(((bf16[16,16,512]{2,1,0:T(8,128)(2,1)}), bf16[16,16,512]{2,1,0:T(8,128)(2,1)S(1)}, u32[]{:S(2)}, u32[]{:S(2)}) %all-to-all-start) | async-done | bytes 262176 | tf_op jit(solution)/shard_map/all_to_all | solution.py:390
  138.3 1.5 shard_map.127
  139.8 11.1 %all-gather.1 = bf16[576,512]{1,0:T(8,128)(2,1)S(1)} all-gather(bf16[144,512]{1,0:T(8,128)(2,1)S(1)} %get-tuple-element.32), channel_id=3, replica_groups=mesh['z'=16,'x'=4,'y'=4,'c'=2] {'y'}, dimensions={0}, use_global_device_ids=true | all-gather | bytes 737280 | tf_op jit(solution)/shard_map/all_gather | solution.py:397
  150.9 13.0 %collective-permute-start.14 = (bf16[4,144,512]{2,1,0:T(8,128)(2,1)S(1)}, bf16[4,144,512]{2,1,0:T(8,128)(2,1)S(1)}, u32[]{:S(2)}, u32[]{:S(2)}) collective-permute-start(bf16[4,144,512]{2,1,0:T(8,128)(2,1)S(1)} %bitcast.44), channel_id=1, source_target_pairs={{0,1},{1,0},{2,3},{3,2},{4,5},{5,4},{6,7},{7,6},{8,9},{9,8},{10,11... | collective-permute-start | bytes 1769480 | tf_op jit(solution)/shard_map/ppermute | solution.py:398
  164.0 0.2 compare_reduce_fusion
  164.1 0.1 concatenate.13.f_ref
  164.2 1.3 collective-permute-done.14.o_ref
  165.6 0.9 copy-done.2
  166.5 4.5 %shard_map.128 = (f32[2,64,512]{2,1,0:T(8,128)}, f32[2,64,512]{2,1,0:T(8,128)}, bf16[2,512,512]{2,1,0:T(8,128)(2,1)}) custom-call(s32[7]{0:T(128)S(1)} %concatenate.13.f_ref, bf16[4,144,512]{2,1,0:T(8,128)(2,1)S(1)} %bitcast.45, bf16[4,144,512]{2,1,0:T(8,128)(2,1)S(1)} %collective-permute-done.14.o_ref, ...), custom_call_target="tpu_custom_call" | custom-call | tf_op jit(solution)/shard_map/pallas_call | solution.py:305
  (40 shorter events, 0.5 us)
Async XLA Ops:
  0.6 14.3 %copy-start.7 = (s32[96]{0:T(128)S(1)}, s32[96]{0:T(128)}, u32[]{:S(2)}) copy-start(s32[96]{0:T(128)} %param.11) | copy-start | bytes 1156
  3.9 13.9 %copy-start.4 = (bf16[1,2,64,512]{3,2,1,0:T(8,128)(2,1)S(1)}, bf16[1,2,64,512]{3,2,1,0:T(8,128)(2,1)}, u32[]{:S(2)}) copy-start(bf16[1,2,64,512]{3,2,1,0:T(8,128)(2,1)} %param.16) | copy-start | bytes 393220
  3.9 13.9 %copy-start.5 = (bf16[1,2,64,512]{3,2,1,0:T(8,128)(2,1)S(1)}, bf16[1,2,64,512]{3,2,1,0:T(8,128)(2,1)}, u32[]{:S(2)}) copy-start(bf16[1,2,64,512]{3,2,1,0:T(8,128)(2,1)} %param.15) | copy-start | bytes 393220
  4.0 17.2 %collective-permute-start.2 = (bf16[1280,256]{1,0:T(8,128)(2,1)}, bf16[1280,256]{1,0:T(8,128)(2,1)S(1)}, u32[]{:S(2)}, u32[]{:S(2)}) collective-permute-start(bf16[1280,256]{1,0:T(8,128)(2,1)} %get-tuple-element.25.p_ref), channel_id=1, source_target_pairs={{0,16},{8,24},{16,0},{24,8},{1,17},{9,25},{17,1},{25,9},{2,18},{10... | collective-permute-start | bytes 1966088 | tf_op jit(solution)/shard_map/ppermute | solution.py:347
  9.6 28.8 %collective-permute-start.3 = (bf16[1280,256]{1,0:T(8,128)(2,1)}, bf16[1280,256]{1,0:T(8,128)(2,1)S(1)}, u32[]{:S(2)}, u32[]{:S(2)}) collective-permute-start(bf16[1280,256]{1,0:T(8,128)(2,1)} %get-tuple-element.30), channel_id=1, source_target_pairs={{0,24},{8,0},{16,8},{24,16},{1,25},{9,1},{17,9},{25,17},{2,26},{10... | collective-permute-start | bytes 1966088 | tf_op jit(solution)/shard_map/ppermute | solution.py:347
  12.4 29.4 %collective-permute-start.4 = (bf16[1280,256]{1,0:T(8,128)(2,1)}, bf16[1280,256]{1,0:T(8,128)(2,1)S(1)}, u32[]{:S(2)}, u32[]{:S(2)}) collective-permute-start(bf16[1280,256]{1,0:T(8,128)(2,1)} %get-tuple-element.31), channel_id=1, source_target_pairs={{0,8},{8,16},{16,24},{24,0},{1,9},{9,17},{17,25},{25,1},{2,10},{10... | collective-permute-start | bytes 1966088 | tf_op jit(solution)/shard_map/ppermute | solution.py:347
  17.9 25.8 %collective-permute-start = (bf16[1,2,2,64,512]{4,3,2,1,0:T(8,128)(2,1)S(1)}, bf16[1,2,2,64,512]{4,3,2,1,0:T(8,128)(2,1)S(1)}, u32[]{:S(2)}, u32[]{:S(2)}) collective-permute-start(bf16[1,2,2,64,512]{4,3,2,1,0:T(8,128)(2,1)S(1)} %maximum_bitcast_fusion), channel_id=1, source_target_pairs={{0,2},{2,0},{4,6},{6,4},{1,3},{3,1},{5,7},{7,5},{8,10},{10,8},{12,... | collective-permute-start | bytes 786440 | tf_op jit(solution)/shard_map/ppermute | solution.py:365
  21.1 39.0 %collective-permute-start.5 = (bf16[1280,256]{1,0:T(8,128)(2,1)S(1)}, bf16[1280,256]{1,0:T(8,128)(2,1)S(1)}, u32[]{:S(2)}, u32[]{:S(2)}) collective-permute-start(bf16[1280,256]{1,0:T(8,128)(2,1)S(1)} %collective-permute-done.2.refs_1_.refs_5_), channel_id=1, source_target_pairs={{0,1},{1,0},{2,3},{3,2},{4,5},{5,4},{6,7},{7,6},{8,9},{9,8},{10,11... | collective-permute-start | bytes 1966088 | tf_op jit(solution)/shard_map/ppermute | solution.py:368
  38.4 21.8 %collective-permute-start.6 = (bf16[1280,256]{1,0:T(8,128)(2,1)S(1)}, bf16[1280,256]{1,0:T(8,128)(2,1)S(1)}, u32[]{:S(2)}, u32[]{:S(2)}) collective-permute-start(bf16[1280,256]{1,0:T(8,128)(2,1)S(1)} %collective-permute-done.3.refs_2_.refs_6_), channel_id=1, source_target_pairs={{0,1},{1,0},{2,3},{3,2},{4,5},{5,4},{6,7},{7,6},{8,9},{9,8},{10,11... | collective-permute-start | bytes 1966088 | tf_op jit(solution)/shard_map/ppermute | solution.py:368
  41.8 18.4 %collective-permute-start.7 = (bf16[1280,256]{1,0:T(8,128)(2,1)S(1)}, bf16[1280,256]{1,0:T(8,128)(2,1)S(1)}, u32[]{:S(2)}, u32[]{:S(2)}) collective-permute-start(bf16[1280,256]{1,0:T(8,128)(2,1)S(1)} %collective-permute-done.4.refs_3_.refs_7_), channel_id=1, source_target_pairs={{0,1},{1,0},{2,3},{3,2},{4,5},{5,4},{6,7},{7,6},{8,9},{9,8},{10,11... | collective-permute-start | bytes 1966088 | tf_op jit(solution)/shard_map/ppermute | solution.py:368
  43.8 16.4 %collective-permute-start.1 = (bf16[2,2,2,64,512]{4,3,2,1,0:T(8,128)(2,1)S(1)}, bf16[2,2,2,64,512]{4,3,2,1,0:T(8,128)(2,1)S(1)}, u32[]{:S(2)}, u32[]{:S(2)}) collective-permute-start(bf16[2,2,2,64,512]{4,3,2,1,0:T(8,128)(2,1)S(1)} %pad_maximum_fusion.1), channel_id=1, source_target_pairs={{0,4},{2,6},{4,0},{6,2},{1,5},{3,7},{5,1},{7,3},{8,12},{10,14},{12... | collective-permute-start | bytes 1572872 | tf_op jit(solution)/shard_map/ppermute | solution.py:365
  60.2 1.2 copy-start
  62.0 15.8 %collective-permute-start.11 = (bf16[256,768]{1,0:T(8,128)(2,1)S(1)}, bf16[256,768]{1,0:T(8,128)(2,1)S(1)}, u32[]{:S(2)}, u32[]{:S(2)}) collective-permute-start(bf16[256,768]{1,0:T(8,128)(2,1)S(1)} %shard_map.125), channel_id=1, source_target_pairs={{0,32},{1,481},{32,64},{33,1},{64,96},{65,33},{96,128},{97,65},{12... | collective-permute-start | bytes 1179656 | tf_op jit(solution)/shard_map/ppermute | solution.py:379
  73.7 8.8 %collective-permute-start.8 = (bf16[256,768]{1,0:T(8,128)(2,1)S(1)}, bf16[256,768]{1,0:T(8,128)(2,1)S(1)}, u32[]{:S(2)}, u32[]{:S(2)}) collective-permute-start(bf16[256,768]{1,0:T(8,128)(2,1)S(1)} %shard_map.123), channel_id=1, source_target_pairs={{0,32},{1,481},{32,64},{33,1},{64,96},{65,33},{96,128},{97,65},{12... | collective-permute-start | bytes 1179656 | tf_op jit(solution)/shard_map/ppermute | solution.py:379
  77.8 9.5 %collective-permute-start.12 = (bf16[128,768]{1,0:T(8,128)(2,1)S(1)}, bf16[128,768]{1,0:T(8,128)(2,1)S(1)}, u32[]{:S(2)}, u32[]{:S(2)}) collective-permute-start(bf16[128,768]{1,0:T(8,128)(2,1)S(1)} %fusion.1), channel_id=1, source_target_pairs={{0,64},{1,449},{32,96},{33,481},{64,128},{65,1},{96,160},{97,33},{... | collective-permute-start | bytes 589832 | tf_op jit(solution)/shard_map/ppermute | solution.py:379
  82.6 10.2 %collective-permute-start.9 = (bf16[128,768]{1,0:T(8,128)(2,1)S(1)}, bf16[128,768]{1,0:T(8,128)(2,1)S(1)}, u32[]{:S(2)}, u32[]{:S(2)}) collective-permute-start(bf16[128,768]{1,0:T(8,128)(2,1)S(1)} %fusion.2), channel_id=1, source_target_pairs={{0,64},{1,449},{32,96},{33,481},{64,128},{65,1},{96,160},{97,33},{... | collective-permute-start | bytes 589832 | tf_op jit(solution)/shard_map/ppermute | solution.py:379
  87.4 10.6 %collective-permute-start.13 = (bf16[64,768]{1,0:T(8,128)(2,1)S(1)}, bf16[64,768]{1,0:T(8,128)(2,1)S(1)}, u32[]{:S(2)}, u32[]{:S(2)}) collective-permute-start(bf16[64,768]{1,0:T(8,128)(2,1)S(1)} %fusion.4), channel_id=1, source_target_pairs={{0,128},{1,385},{32,160},{33,417},{64,192},{65,449},{96,224},{97,4... | collective-permute-start | bytes 294920 | tf_op jit(solution)/shard_map/ppermute | solution.py:379
  92.8 10.5 %collective-permute-start.10 = (bf16[64,768]{1,0:T(8,128)(2,1)S(1)}, bf16[64,768]{1,0:T(8,128)(2,1)S(1)}, u32[]{:S(2)}, u32[]{:S(2)}) collective-permute-start(bf16[64,768]{1,0:T(8,128)(2,1)S(1)} %fusion.9), channel_id=1, source_target_pairs={{0,128},{1,385},{32,160},{33,417},{64,192},{65,449},{96,224},{97,4... | collective-permute-start | bytes 294920 | tf_op jit(solution)/shard_map/ppermute | solution.py:379
  98.1 37.1 %copy-start.6 = (s32[96]{0:T(128)S(1)}, s32[96]{0:T(128)}, u32[]{:S(2)}) copy-start(s32[96]{0:T(128)} %param.12) | copy-start | bytes 1156
  98.1 40.2 %copy-start.3 = (f32[1,2,64,512]{3,2,1,0:T(8,128)S(1)}, f32[1,2,64,512]{3,2,1,0:T(8,128)}, u32[]{:S(2)}) copy-start(f32[1,2,64,512]{3,2,1,0:T(8,128)} %param.17) | copy-start | bytes 786436
  103.5 62.1 %copy-start.1 = (f32[1,2,64,512]{3,2,1,0:T(8,128)S(1)}, f32[1,2,64,512]{3,2,1,0:T(8,128)}, u32[]{:S(2)}) copy-start(f32[1,2,64,512]{3,2,1,0:T(8,128)} %param.13) | copy-start | bytes 786436
  116.5 21.8 %all-to-all-start = ((bf16[16,16,512]{2,1,0:T(8,128)(2,1)}), bf16[16,16,512]{2,1,0:T(8,128)(2,1)S(1)}, u32[]{:S(2)}, u32[]{:S(2)}) async-start(bf16[16,16,512]{2,1,0:T(8,128)(2,1)} %bitcast.7), calls=%async_computation | async-start | bytes 524288 | tf_op jit(solution)/shard_map/all_to_all | solution.py:390
  125.6 38.6 %collective-permute-start.15 = (bf16[4,2,2,64,512]{4,3,2,1,0:T(8,128)(2,1)S(1)}, bf16[4,2,2,64,512]{4,3,2,1,0:T(8,128)(2,1)S(1)}, u32[]{:S(2)}, u32[]{:S(2)}) collective-permute-start(bf16[4,2,2,64,512]{4,3,2,1,0:T(8,128)(2,1)S(1)} %pad_maximum_fusion.rm_ref), channel_id=1, source_target_pairs={{0,1},{1,0},{2,3},{3,2},{4,5},{5,4},{6,7},{7,6},{8,9},{9,8},{10,11... | collective-permute-start | bytes 3145736 | tf_op jit(solution)/shard_map/ppermute | solution.py:369
  150.9 14.6 %collective-permute-start.14 = (bf16[4,144,512]{2,1,0:T(8,128)(2,1)S(1)}, bf16[4,144,512]{2,1,0:T(8,128)(2,1)S(1)}, u32[]{:S(2)}, u32[]{:S(2)}) collective-permute-start(bf16[4,144,512]{2,1,0:T(8,128)(2,1)S(1)} %bitcast.44), channel_id=1, source_target_pairs={{0,1},{1,0},{2,3},{3,2},{4,5},{5,4},{6,7},{7,6},{8,9},{9,8},{10,11... | collective-permute-start | bytes 1769480 | tf_op jit(solution)/shard_map/ppermute | solution.py:398
  165.6 1.0 copy-start.2
